TPU v7x, 256 devices: a whole 4x4x8 slice. The times are simulated.
256 devices in a mesh: worker: 32 (over x, z_hi, core), fsdp: 8 (over z_lo, y).
Axes of the slice: x: 4, y: 4, z: 8 (z_hi: 4, z_lo: 2; z = z_hi * 2 + z_lo), core: 2. Of those that a mesh axis runs over, the one named last changes fastest.
Arguments:
- token_ids: int32 [65536], P(('worker', 'fsdp')), may hold values from 0 to 128255, as said below
- layer_inputs: bfloat16 [2, 65536, 8192], P(None, ('worker', 'fsdp')), may hold values from -6 to 6
- key_grads: bfloat16 [2, 65536, 512], P(None, ('worker', 'fsdp')), may hold values from -0.125 to 0.125
- weights: bfloat16 [32, 2, 8192, 512], P('worker', None, 'fsdp'), may hold values from -6 to 6
- anchors: float32 [2, 8192, 512], P(None, ('fsdp', 'worker')), may hold values from -6 to 6
- momentum: float32 [8192, 512], P(('fsdp', 'worker')), may hold values from -3 to 3
- plan: int32 [1], replicated, may hold values from 0 to 1023
Outputs:
- weights_new: bfloat16 [32, 2, 8192, 512], P('worker', None, 'fsdp')
- anchor_new: float32 [8192, 512], P(('fsdp', 'worker'))
- momentum_new: float32 [8192, 512], P(('fsdp', 'worker'))
- pending: float32 [8192, 512], P(('fsdp', 'worker'))
Inputs may be any that keep to these rules, and one draw needn't show every extreme that they name: `token_ids`: 0 marks a token left out of the loss; other values are vocabulary ids.
All inputs are finite; a program needn't handle non-finite values.
Results may differ from a plain program's by a relative error of at most 0.01.
Values may be sent and summed in bfloat16 or wider, within the bound.
No kernel may reach another device: no remote copies, remote signals or barrier semaphores. Data moves between devices by JAX's collectives and lax.ppermute only.
A program may use at most 128 MiB of HBM per device.

v0:
```python
import jax
import jax.numpy as jnp
from jax import lax
from jax.sharding import PartitionSpec as P

inner_rate = 0.25
decay_rate = 0.1
outer_rate = 0.7
outer_beta = 0.9
mix_weight = 0.5


def body(token_ids, layer_inputs, key_grads, weights, anchors, momentum, plan):
    chosen = jnp.remainder(plan[0], 2)
    other = 1 - chosen
    kept_mask = (token_ids != 0).astype(jnp.bfloat16)
    masked = key_grads * kept_mask[None, :, None]
    summed_rows = lax.psum_scatter(
        jnp.einsum("ltr,ltc->rlc", layer_inputs, masked, preferred_element_type=jnp.float32).astype(
            jnp.bfloat16
        ),
        "fsdp",
        scatter_dimension=0,
        tiled=True,
    ).astype(jnp.float32)
    gradient = jnp.transpose(summed_rows, (1, 0, 2))
    own_rows = weights[0]
    inner_new = (
        own_rows.astype(jnp.float32) * (1.0 - inner_rate * decay_rate) - inner_rate * gradient
    ).astype(jnp.bfloat16)
    synced = lax.dynamic_index_in_dim(inner_new, chosen, 0, keepdims=False)
    waiting = lax.dynamic_index_in_dim(inner_new, other, 0, keepdims=False)
    workers = lax.axis_size("worker")
    anchor_now = lax.dynamic_index_in_dim(anchors, chosen, 0, keepdims=False)
    anchor_other = lax.dynamic_index_in_dim(anchors, other, 0, keepdims=False)
    sync_sum = lax.psum_scatter(
        synced.astype(jnp.float32).astype(jnp.bfloat16), "worker", scatter_dimension=0, tiled=True
    ).astype(jnp.float32)
    outer_grad = anchor_now - sync_sum / workers
    moment_next = outer_beta * momentum + outer_grad
    anchor_next = anchor_now - outer_rate * (outer_grad + outer_beta * moment_next)
    other_sum = lax.psum_scatter(
        waiting.astype(jnp.float32).astype(jnp.bfloat16), "worker", scatter_dimension=0, tiled=True
    ).astype(jnp.float32)
    pending = anchor_other - other_sum / workers
    full_anchor = lax.all_gather(
        anchor_next.astype(jnp.bfloat16), "worker", axis=0, tiled=True
    ).astype(anchor_next.dtype)
    mixed_rows = (
        mix_weight * synced.astype(jnp.float32) + (1.0 - mix_weight) * full_anchor
    ).astype(jnp.bfloat16)
    is_synced = jnp.arange(2, dtype=jnp.int32) == chosen
    weights_new = jnp.where(is_synced[:, None, None], mixed_rows[None], inner_new)[None]
    return (weights_new, anchor_next, moment_next, pending)


def solution(mesh):
    return jax.shard_map(
        body,
        mesh=mesh,
        in_specs=(
            P(("worker", "fsdp")),
            P(None, ("worker", "fsdp"), None),
            P(None, ("worker", "fsdp"), None),
            P("worker", None, "fsdp", None),
            P(None, ("fsdp", "worker"), None),
            P(("fsdp", "worker"), None),
            P(),
        ),
        out_specs=(
            P("worker", None, "fsdp", None),
            P(("fsdp", "worker"), None),
            P(("fsdp", "worker"), None),
            P(("fsdp", "worker"), None),
        ),
        check_vma=False,
    )
```

profile of v0, /device:TPU:8, one launch (start us, length us, event | category | flops | bytes accessed | tf_op | source)
XLA Modules:
  0.0 449.8 jit_solution(16494790172867395569)
XLA Ops:
  7.2 0.0 reduce-scatter.4.cloned.1.call-start
  7.2 0.7 compare_convert_fusion
  7.9 11.6 %convert_bitcast_fusion = bf16[8192,2,512]{0,2,1:T(8,128)(2,1)} fusion(bf16[2,256,8192]{2,1,0:T(8,128)(2,1)} %param.8, bf16[2,256,512]{2,1,0:T(8,128)(2,1)} %param.9, bf16[256]{0:T(256)(128)(2,1)S(1)} %compare_convert_fusion), kind=kOutput, calls=%fused_computation | convolution fusion | flops 4303618048 | bytes 25690624 | tf_op jit(solution)/shard_map/ltr,ltc->rlc/dot_general | solution.py:19
  19.5 0.0 copy-start.1
  19.5 0.0 reduce-scatter.4.cloned.1.call-update
  19.5 0.0 reduce-scatter.6.cloned.1.call-start
  20.4 0.7 copy-done.1
  21.1 2.4 copy.15
  23.5 170.8 %reduce-scatter.4.cloned.1.call-done = bf16[1024,2,512]{0,2,1:T(8,128)(2,1)} async-done(((bf16[8192,2,512]{0,2,1:T(8,128)(2,1)}), bf16[1024,2,512]{0,2,1:T(8,128)(2,1)}) %reduce-scatter.4.cloned.1.call-update) | async-done | bytes 2097168 | tf_op jit(solution)/shard_map/reduce_scatter | solution.py:18
  194.3 3.3 fusion
  197.6 1.1 constant_dynamic-slice_fusion
  198.7 1.3 copy.17
  200.0 0.0 copy-start.2
  200.0 0.0 copy-start.3
  200.0 0.0 reduce-scatter.6.cloned.1.call-update
  200.0 0.0 copy-start
  200.0 0.0 reduce-scatter.8.cloned.1.call-start
  200.1 2.4 copy.19
  202.5 0.0 reduce-scatter.8.cloned.1.call-update
  202.5 0.0 all-gather.2.cloned.1.call-start
  202.5 87.6 %reduce-scatter.6.cloned.1.call-done = bf16[32,512]{1,0:T(8,128)(2,1)} async-done(((bf16[1024,512]{1,0:T(8,128)(2,1)}), bf16[32,512]{1,0:T(8,128)(2,1)}) %reduce-scatter.6.cloned.1.call-update) | async-done | bytes 32784 | tf_op jit(solution)/shard_map/reduce_scatter | solution.py:36
  290.1 90.9 %reduce-scatter.8.cloned.1.call-done = bf16[32,512]{1,0:T(8,128)(2,1)} async-done(((bf16[1024,512]{1,0:T(8,128)(2,1)}), bf16[32,512]{1,0:T(8,128)(2,1)}) %reduce-scatter.8.cloned.1.call-update) | async-done | bytes 32784 | tf_op jit(solution)/shard_map/reduce_scatter | solution.py:42
  381.0 0.0 copy-done.2
  381.0 0.0 copy-done.3
  381.1 1.5 fusion.3
  382.5 0.0 all-gather.2.cloned.1.call-update
  382.6 51.1 %all-gather.2.cloned.1.call-done = bf16[1024,512]{1,0:T(8,128)(2,1)} async-done(((bf16[32,512]{1,0:T(8,128)(2,1)}), bf16[1024,512]{1,0:T(8,128)(2,1)}) %all-gather.2.cloned.1.call-update) | async-done | bytes 1048592 | tf_op jit(solution)/shard_map/all_gather | solution.py:46
  433.7 0.0 copy-done
  433.7 2.5 multiply_convert_fusion
  436.2 1.5 copy.18
  437.7 1.6 select_bitcast_fusion
  439.3 3.9 copy.20
  (1 shorter events, 0.0 us)
Async XLA Ops:
  7.2 187.1 %reduce-scatter.4.cloned.1.call-start = ((), (), s32[]{:S(2)}) async-start(), calls=%async_computation.3 | async-start | bytes 18874368 | tf_op jit(solution)/shard_map/reduce_scatter | solution.py:18
  19.5 1.6 copy-start.1
  19.5 270.6 %reduce-scatter.6.cloned.1.call-start = ((), (), s32[]{:S(2)}) async-start(), calls=%async_computation.4 | async-start | bytes 1081344 | tf_op jit(solution)/shard_map/reduce_scatter | solution.py:36
  200.0 181.0 %copy-start.2 = (f32[2,32,512]{2,1,0:T(8,128)S(1)}, f32[2,32,512]{2,1,0:T(8,128)}, u32[]{:S(2)}) copy-start(f32[2,32,512]{2,1,0:T(8,128)} %param.11) | copy-start | bytes 393220
  200.0 181.0 %copy-start.3 = (f32[32,512]{1,0:T(8,128)S(1)}, f32[32,512]{1,0:T(8,128)}, u32[]{:S(2)}) copy-start(f32[32,512]{1,0:T(8,128)} %param.12) | copy-start | bytes 196612
  200.0 233.6 %copy-start = (bf16[1,1024,512]{2,1,0:T(8,128)(2,1)S(1)}, bf16[1,1024,512]{2,1,0:T(8,128)(2,1)}, u32[]{:S(2)}) copy-start(bf16[1,1024,512]{2,1,0:T(8,128)(2,1)} %copy.17) | copy-start | bytes 3145732
  200.0 181.0 %reduce-scatter.8.cloned.1.call-start = ((), (), s32[]{:S(2)}) async-start(), calls=%async_computation.6 | async-start | bytes 1081344 | tf_op jit(solution)/shard_map/reduce_scatter | solution.py:42
  202.5 231.2 %all-gather.2.cloned.1.call-start = ((), (), s32[]{:S(2)}) async-start(), calls=%async_computation.5 | async-start | bytes 1081344 | tf_op jit(solution)/shard_map/all_gather | solution.py:46
Sparse Core Ops, SparseCore 0:
  19.7 174.5 reduce-scatter.3
  200.2 89.9 reduce-scatter.5
  294.4 86.6 reduce-scatter.7
  384.0 49.5 all-gather.1
where the time goes:
time: 451 us; the launch traced here: 450 us
  waiting for transfers between devices  400 us (89%)
  between operations  14.6 us (3%)
  local copies, waits for them, and re-layouts  13.3 us (3%)
  matrix products  11.6 us (3%)
  other arithmetic  9.58 us (2%)
    reduce_scatter x1, waiting for transfers between devices, body(): lax.psum_scatter(jnp.einsum('ltr,ltc->rlc', layer_inputs, masked, preferr...  171 us
    reduce_scatter x1, waiting for transfers between devices, body(): lax.psum_scatter(waiting.astype(jnp.float32).astype(jnp.bfloat16), 'worke...  90.9 us
    reduce_scatter x1, waiting for transfers between devices, body(): lax.psum_scatter(synced.astype(jnp.float32).astype(jnp.bfloat16), 'worker...  87.6 us
    all_gather x1, waiting for transfers between devices, body(): lax.all_gather(anchor_next.astype(jnp.bfloat16), 'worker', axis=0, tiled=...  51.1 us
    dot_general x1, matrix products, body(): jnp.einsum('ltr,ltc->rlc', layer_inputs, masked, preferred_element_type=j...  11.6 us
  transfers between devices with their start and end apart: 4, of which 4 were waited for; matrix products, arithmetic and copies ran while one was open for 1% of the time, Pallas kernels for 0%

commit v1 on v0

v1 whole, which is shorter than its diff:
```python
import jax
import jax.numpy as jnp
from jax import lax
from jax.experimental import pallas as pl
from jax.experimental.pallas import tpu as pltpu
from jax.sharding import PartitionSpec as P

inner_rate = 0.25
decay_rate = 0.1
outer_rate = 0.7
outer_beta = 0.9
mix_weight = 0.5

TOK = 256
KV = 512
ROWS = 1024
HALF = 512
F32 = jnp.float32
BF16 = jnp.bfloat16

ANY = pl.BlockSpec(memory_space=pl.ANY)
VM = pl.BlockSpec(memory_space=pltpu.VMEM)
SM = pl.BlockSpec(memory_space=pltpu.SMEM)
PARAMS = pltpu.CompilerParams(vmem_limit_bytes=40 * 1024 * 1024)


def place():
    w = lax.axis_index("worker")
    f = lax.axis_index("fsdp")
    return w // 8, (w // 2) % 4, w % 2, f // 4, f % 4


def cost(flops, nbytes):
    return pl.CostEstimate(flops=flops, bytes_accessed=nbytes, transcendentals=0)


def shape(*dims, dtype=BF16):
    return jax.ShapeDtypeStruct(dims, dtype)


def call(kernel, outs, args, specs, out_specs, scratch=(), flops=0, nbytes=0, aliases=None, name=None):
    return pl.pallas_call(
        kernel,
        out_shape=outs,
        in_specs=specs,
        out_specs=out_specs,
        scratch_shapes=list(scratch),
        compiler_params=PARAMS,
        cost_estimate=cost(flops, nbytes),
        input_output_aliases=aliases or {},
        name=name,
    )(*args)


def columns(start, width):
    return pl.ds(pl.multiple_of(start, width), width)


def pack_kernel(plan, tok, x, g, buf_a, buf_b, buf_z, gt_out, gin, gt, sems, gsems):
    _, _, _, z, y = place()
    s = lax.rem(plan[0], 2)
    copies = []

    def send(layer, col, width, dst, at):
        copies.append(
            pltpu.make_async_copy(
                x.at[layer, :, columns(col, width)], dst.at[:, pl.ds(at, width)], sems.at[len(copies)]
            )
        )
        copies[-1].start()

    g_copies = [pltpu.make_async_copy(g.at[layer], gin.at[i], gsems.at[i]) for i, layer in enumerate((s, 1 - s))]
    for c in g_copies:
        c.start()
    for buf, first, second, offset in ((buf_a, y ^ 1, y ^ 2, 0), (buf_b, y ^ 3, y ^ 2, HALF)):
        for i, (zz, yy) in enumerate(((z, first), (1 - z, first), (z, second), (1 - z, second))):
            send(s, (zz * 4 + yy) * ROWS + offset, HALF, buf, i * HALF)
    for j in range(4):
        send(1 - s, ((1 - z) * 4 + (y ^ j)) * ROWS, ROWS, buf_z, j * ROWS)
    kept = (tok[...] != 0).astype(F32)
    for i in range(2):
        g_copies[i].wait()
        gt[i] = (gin[i].astype(F32).T * kept).astype(BF16)
    last = []

    def put(src, dst):
        last.append(pltpu.make_async_copy(src, dst, gsems.at[2 + len(last)]))
        last[-1].start()

    for i, bufs, at in ((0, (buf_a, buf_b), 4 * HALF), (1, (buf_z,), 4 * ROWS)):
        for buf in bufs:
            for h in range(2):
                put(gt.at[i, pl.ds(h * TOK, TOK)], buf.at[:, pl.ds(at + h * TOK, TOK)])
    put(gt, gt_out)
    for c in copies + last:
        c.wait()


def pack(plan, tok, x, g):
    return call(
        pack_kernel,
        (shape(TOK, 5 * HALF), shape(TOK, 5 * HALF), shape(TOK, 4 * ROWS + KV), shape(2, KV, TOK)),
        (plan, tok, x, g),
        [SM, VM, ANY, ANY],
        [ANY] * 4,
        [
            pltpu.VMEM((2, TOK, KV), BF16),
            pltpu.VMEM((2, KV, TOK), BF16),
            pltpu.SemaphoreType.DMA((12,)),
            pltpu.SemaphoreType.DMA((9,)),
        ],
        nbytes=10 * 2**20,
        name="pack",
    )


def product(name, fragment, pieces, out_shapes, g_at, plan, x, gt, recv):
    width = pieces[0][2]
    count = len(pieces)

    def kernel(plan_ref, x_ref, gt_ref, recv_ref, *rest):
        outs = rest[: len(out_shapes)]
        stage = rest[len(out_shapes) : 2 * len(out_shapes)]
        gts, xs, rs, sems, out_sems = rest[2 * len(out_shapes) :]
        _, _, _, z, y = place()
        s = lax.rem(plan_ref[0], 2)
        layer = s if fragment == 0 else 1 - s
        g_copies = [
            pltpu.make_async_copy(gt_ref.at[fragment], gts.at[:, pl.ds(0, TOK)], sems.at[2 * count]),
            *(
                pltpu.make_async_copy(
                    recv_ref.at[:, pl.ds(g_at + h * TOK, TOK)],
                    gts.at[pl.ds(h * TOK, TOK), pl.ds(TOK, TOK)],
                    sems.at[2 * count + 1 + h],
                )
                for h in range(2)
            ),
        ]
        copies = []
        for p, (own, at, _, _) in enumerate(pieces):
            copies.append(
                (
                    pltpu.make_async_copy(x_ref.at[layer, :, columns(own(z, y), width)], xs.at[p, pl.ds(0, TOK)], sems.at[2 * p]),
                    pltpu.make_async_copy(recv_ref.at[:, pl.ds(at, width)], xs.at[p, pl.ds(TOK, TOK)], sems.at[2 * p + 1]),
                )
            )
        for c in g_copies:
            c.start()
        for pair in copies:
            for c in pair:
                c.start()
        for c in g_copies:
            c.wait()
        done = []
        for p, (_, _, _, targets) in enumerate(pieces):
            for c in copies[p]:
                c.wait()
            for out, slot, k0, k1 in targets:
                stage[out][slot] = jnp.dot(gts[k0:k1], xs[p], preferred_element_type=F32).astype(BF16)
                c = pltpu.make_async_copy(stage[out].at[slot], outs[out].at[slot], out_sems.at[len(done)])
                c.start()
                done.append(c)
        for c in done:
            c.wait()

    total = sum(len(p[3]) for p in pieces)
    return call(
        kernel,
        tuple(shape(*d) for d in out_shapes),
        (plan, x, gt, recv),
        [SM, ANY, ANY, ANY],
        [ANY] * len(out_shapes),
        [
            *(pltpu.VMEM(d, BF16) for d in out_shapes),
            pltpu.VMEM((KV, 2 * TOK), BF16),
            pltpu.VMEM((count, 2 * TOK, width), BF16),
            pltpu.VMEM((8, 128), BF16),
            pltpu.SemaphoreType.DMA((2 * count + 3,)),
            pltpu.SemaphoreType.DMA((total,)),
        ],
        flops=sum(2 * 2 * TOK * width * (k1 - k0) for p in pieces for _, _, k0, k1 in p[3]),
        nbytes=sum(2 * 2 * TOK * width for _ in pieces) + sum(2 * a * b * c for a, b, c in out_shapes),
        name=name,
    )


def flip(*terms):
    return sum(t.astype(F32) for t in terms).T


def stepped(w, gradient):
    return (w.astype(F32) * (1.0 - inner_rate * decay_rate) - inner_rate * gradient).astype(BF16)


def inner_sync(plan, w, ka, ra, kb, rb):
    def kernel(plan_ref, w_ref, ka_ref, ra_ref, kb_ref, rb_ref, inner_ref, send_ref, wv, sem, sem2):
        s = lax.rem(plan_ref[0], 2)
        core = place()[2]
        load = pltpu.make_async_copy(w_ref.at[s], wv, sem)
        load.start()
        load.wait()
        for h, (k_ref, r_ref) in enumerate(((ka_ref, ra_ref), (kb_ref, rb_ref))):
            for q in range(4):
                cols = pl.ds(q * 128, 128)
                i = h * 8 + q * 2
                new = stepped(wv[i : i + 2].reshape(128, KV), flip(k_ref[:, cols], r_ref[:, cols]))
                inner_ref[i : i + 2] = new.reshape(2, 2, 32, KV)
        out = pltpu.make_async_copy(inner_ref.at[:, 1 - core], send_ref, sem2)
        out.start()
        out.wait()

    return call(
        kernel,
        (shape(16, 2, 32, KV), shape(16, 32, KV)),
        (plan, w, ka, ra, kb, rb),
        [SM, ANY, VM, VM, VM, VM],
        [VM, ANY],
        [pltpu.VMEM((16, 2, 32, KV), BF16), pltpu.SemaphoreType.DMA, pltpu.SemaphoreType.DMA],
        nbytes=5 * 2**20,
        name="inner_sync",
    )


def inner_other(plan, w, k0, r0, k1, r1):
    def kernel(plan_ref, w_ref, k0_ref, r0_ref, k1_ref, r1_ref, inner_ref, send_ref, new_ref, wv, sem, sem2):
        other = 1 - lax.rem(plan_ref[0], 2)
        core = place()[2]
        load = pltpu.make_async_copy(w_ref.at[other], wv, sem)
        load.start()
        load.wait()
        for q in range(8):
            cols = pl.ds(q * 128, 128)
            i = q * 2
            gradient = jnp.concatenate(
                [flip(k0_ref[:, cols], r0_ref[:, cols]), flip(k1_ref[:, cols], r1_ref[:, cols])], axis=1
            )
            inner_ref[i : i + 2] = stepped(wv[i : i + 2].reshape(128, KV), gradient).reshape(2, 2, 32, KV)
        out = pltpu.make_async_copy(inner_ref.at[:, 1 - core], send_ref, sem2.at[0])
        keep = pltpu.make_async_copy(inner_ref, new_ref.at[other], sem2.at[1])
        out.start()
        keep.start()
        out.wait()
        keep.wait()

    return call(
        kernel,
        (shape(16, 2, 32, KV), shape(16, 32, KV), shape(2, 16, 2, 32, KV)),
        (plan, w, k0, r0, k1, r1),
        [SM, ANY, VM, VM, VM, VM],
        [VM, ANY, ANY],
        [pltpu.VMEM((16, 2, 32, KV), BF16), pltpu.SemaphoreType.DMA, pltpu.SemaphoreType.DMA((2,))],
        nbytes=6 * 2**20,
        name="inner_other",
    )


def add_cores(inner, recv, name):
    def kernel(inner_ref, recv_ref, *outs):
        x, _, core, _, _ = place()
        for d in range(4):
            block = pl.ds(lax.rem(x + d, 4) * 4, 4)
            outs[d][...] = (inner_ref[block, core].astype(F32) + recv_ref[block].astype(F32)).astype(BF16)

    return call(
        kernel, (shape(4, 32, KV),) * 4, (inner, recv), [VM, VM], [VM] * 4, nbytes=2 * 2**20, name=name
    )


def add_x(parts, name):
    def kernel(a, b, c, d, *outs):
        zh = place()[1]
        for i in range(4):
            at = lax.rem(zh + i, 4)
            outs[i][...] = sum(t[at].astype(F32) for t in (a, b, c, d)).astype(BF16)

    return call(kernel, (shape(32, KV),) * 4, parts, [VM] * 4, [VM] * 4, nbytes=2**20, name=name)


def outer_sync(plan, anchors, momentum, parts):
    def kernel(plan_ref, anchor_ref, momentum_ref, a, b, c, d, new_ref, moment_ref, short_ref):
        s = lax.rem(plan_ref[0], 2)
        mean = sum(t[...].astype(F32) for t in (a, b, c, d)) / 32
        anchor = anchor_ref[s]
        outer_grad = anchor - mean
        moment = outer_beta * momentum_ref[...] + outer_grad
        new = anchor - outer_rate * (outer_grad + outer_beta * moment)
        new_ref[...] = new
        moment_ref[...] = moment
        short_ref[...] = new.astype(BF16)

    return call(
        kernel,
        (shape(32, KV, dtype=F32), shape(32, KV, dtype=F32), shape(32, KV)),
        (plan, anchors, momentum, *parts),
        [SM] + [VM] * 6,
        [VM] * 3,
        nbytes=2**19,
        name="outer_sync",
    )


def outer_other(plan, anchors, parts):
    def kernel(plan_ref, anchor_ref, a, b, c, d, out_ref):
        other = 1 - lax.rem(plan_ref[0], 2)
        out_ref[...] = anchor_ref[other] - sum(t[...].astype(F32) for t in (a, b, c, d)) / 32

    return call(
        kernel, shape(32, KV, dtype=F32), (plan, anchors, *parts), [SM] + [VM] * 5, VM, nbytes=2**19, name="outer_other"
    )


def gather_z(parts):
    def kernel(a, b, c, d, out_ref):
        zh = place()[1]
        for i, t in enumerate((a, b, c, d)):
            out_ref[lax.rem(zh + 4 - i, 4)] = t[...]

    return call(kernel, shape(4, 32, KV), parts, [VM] * 4, VM, nbytes=2**18, name="gather_z")


def gather_x(parts):
    def kernel(a, b, c, d, out_ref):
        x = place()[0]
        for i, t in enumerate((a, b, c, d)):
            out_ref[pl.ds(lax.rem(x + 4 - i, 4) * 4, 4)] = t[...]

    return call(kernel, shape(16, 32, KV), parts, [VM] * 4, VM, nbytes=2**20, name="gather_x")


def mix(plan, inner, own, recv, new):
    def kernel(plan_ref, inner_ref, own_ref, recv_ref, _, out_ref, stage, sems):
        s = lax.rem(plan_ref[0], 2)
        core = place()[2]
        for i, (t, c) in enumerate(((own_ref, core), (recv_ref, 1 - core))):
            stage[:, c] = (
                mix_weight * inner_ref[:, c].astype(F32) + (1.0 - mix_weight) * t[...].astype(F32)
            ).astype(BF16)
        out = pltpu.make_async_copy(stage, out_ref.at[s], sems)
        out.start()
        out.wait()

    return call(
        kernel,
        shape(2, 16, 2, 32, KV),
        (plan, inner, own, recv, new),
        [SM, VM, VM, VM, ANY],
        ANY,
        [pltpu.VMEM((16, 2, 32, KV), BF16), pltpu.SemaphoreType.DMA],
        nbytes=4 * 2**20,
        aliases={4: 0},
        name="mix",
    )


def along_fsdp(move):
    return [(z * 4 + y, move(z, y)) for z in range(2) for y in range(4)]


TO_A = along_fsdp(lambda z, y: z * 4 + (y ^ 1))
TO_B = along_fsdp(lambda z, y: z * 4 + (y ^ 3))
TO_Z = along_fsdp(lambda z, y: (1 - z) * 4 + y)


def along_worker(dx, dz, dc):
    return [
        ((x * 4 + z) * 2 + c, (((x + dx) % 4) * 4 + (z + dz) % 4) * 2 + (c + dc) % 2)
        for x in range(4)
        for z in range(4)
        for c in range(2)
    ]


def from_x(parts):
    return [lax.ppermute(parts[d - 1], "worker", along_worker(d, 0, 0)) for d in (1, 2, 3)]


def from_z(parts):
    return [lax.ppermute(parts[d - 1], "worker", along_worker(0, d, 0)) for d in (1, 2, 3)]


def add(a, b):
    return (a.astype(F32) + b.astype(F32)).astype(BF16)


def over_workers(inner, send, tag):
    recv = lax.ppermute(send, "worker", along_worker(0, 0, 1))
    parts = add_cores(inner, recv, "add_cores_" + tag)
    sums = add_x((parts[0], *from_x(parts[1:])), "add_x_" + tag)
    return (sums[0], *from_z(sums[1:]))


def body(token_ids, layer_inputs, key_grads, weights, anchors, momentum, plan):
    x = layer_inputs
    w = weights.reshape(2, 16, 2, 32, KV)
    buf_a, buf_b, buf_z, gt = pack(plan, token_ids.reshape(1, TOK), x, key_grads)
    got_a = lax.ppermute(buf_a, "fsdp", TO_A)
    got_b = lax.ppermute(buf_b, "fsdp", TO_B)
    got_z = lax.ppermute(buf_z, "fsdp", TO_Z)

    def pieces(flip_y, offset, first):
        return [
            (lambda z, y: (z * 4 + (y ^ flip_y)) * ROWS + offset, first * HALF, HALF, [(0, 0, 0, KV)]),
            (lambda z, y: ((1 - z) * 4 + (y ^ flip_y)) * ROWS + offset, (first + 1) * HALF, HALF, [(0, 1, 0, KV)]),
        ]

    sync = [(2, KV, HALF)]
    (send_a,) = product("send_a", 0, pieces(3, 0, 2), sync, 4 * HALF, plan, x, gt, got_a)
    next_a = lax.ppermute(send_a, "fsdp", TO_B)
    (send_b,) = product("send_b", 0, pieces(1, HALF, 2), sync, 4 * HALF, plan, x, gt, got_b)
    next_b = lax.ppermute(send_b, "fsdp", TO_A)
    (keep_a,) = product("keep_a", 0, pieces(0, 0, 0), sync, 4 * HALF, plan, x, gt, got_a)
    (keep_b,) = product("keep_b", 0, pieces(0, HALF, 0), sync, 4 * HALF, plan, x, gt, got_b)
    last_a = lax.ppermute(add(keep_a[1], next_a[1]), "fsdp", TO_Z)
    last_b = lax.ppermute(add(keep_b[1], next_b[1]), "fsdp", TO_Z)
    inner_s, send_s = inner_sync(plan, w, add(keep_a[0], next_a[0]), last_a, add(keep_b[0], next_b[0]), last_b)

    def dest(j, targets):
        return (lambda z, y: (z * 4 + (y ^ j)) * ROWS, j * ROWS, ROWS, targets)

    other = [(2, 256, ROWS), (2, 256, ROWS)]
    send_0, send_1 = product(
        "send_o",
        1,
        [dest(1, [(0, 0, 0, 256)]), dest(2, [(0, 1, 0, 256), (1, 1, 256, 512)]), dest(3, [(1, 0, 256, 512)])],
        other, 4 * ROWS, plan, x, gt, got_z,
    )
    got_0 = lax.ppermute(send_0, "fsdp", TO_A)
    got_1 = lax.ppermute(send_1, "fsdp", TO_B)
    keep_0, keep_1 = product(
        "keep_o",
        1,
        [dest(3, [(0, 1, 0, 256)]), dest(1, [(1, 1, 256, 512)]), dest(0, [(0, 0, 0, 256), (1, 0, 256, 512)])],
        other, 4 * ROWS, plan, x, gt, got_z,
    )
    last_0 = lax.ppermute(add(keep_0[1], got_0[1]), "fsdp", TO_B)
    last_1 = lax.ppermute(add(keep_1[1], got_1[1]), "fsdp", TO_A)
    inner_o, send_o, new = inner_other(
        plan, w, add(keep_0[0], got_0[0]), last_0, add(keep_1[0], got_1[0]), last_1
    )

    anchor_new, momentum_new, short = outer_sync(plan, anchors, momentum, over_workers(inner_s, send_s, "s"))
    pending = outer_other(plan, anchors, over_workers(inner_o, send_o, "o"))
    row = gather_z((short, *from_z((short,) * 3)))
    block = gather_x((row, *from_x((row,) * 3)))
    across = lax.ppermute(block, "worker", along_worker(0, 0, 1))
    new = mix(plan, inner_s, block, across, new)
    return (new.reshape(1, 2, ROWS, KV), anchor_new, momentum_new, pending)


def solution(mesh):
    return jax.shard_map(
        body,
        mesh=mesh,
        in_specs=(
            P(("worker", "fsdp")),
            P(None, ("worker", "fsdp"), None),
            P(None, ("worker", "fsdp"), None),
            P("worker", None, "fsdp", None),
            P(None, ("fsdp", "worker"), None),
            P(("fsdp", "worker"), None),
            P(),
        ),
        out_specs=(
            P("worker", None, "fsdp", None),
            P(("fsdp", "worker"), None),
            P(("fsdp", "worker"), None),
            P(("fsdp", "worker"), None),
        ),
        check_vma=False,
    )
```

time: 451 us -> 165 us (0.37)
  waiting for transfers between devices: 400 us -> 82.6 us
  starting transfers between devices: 0.16 us -> 55.2 us
  Pallas kernels: 0 us -> 16.8 us
  between operations: 14.6 us -> 1.55 us
  matrix products: 11.6 us -> 0 us
  local copies, waits for them, and re-layouts: 13.3 us -> 5.11 us
  other arithmetic: 9.58 us -> 2.57 us
    reduce_scatter x3 -> x0, waiting for transfers between devices: 349 us -> none  [the longest x1 171 us: body(): lax.psum_scatter(jnp.einsum('ltr,ltc->rlc', layer_inputs, masked, preferr...]
    ppermute x0 -> x32, waiting for transfers between devices: none -> 82.6 us  [the longest x1 27.4 us: body(): got_a = lax.ppermute(buf_a, 'fsdp', TO_A)]
    ppermute x0 -> x32, starting transfers between devices: none -> 55.2 us  [the longest x9 24.7 us: from_z(): lax.ppermute(parts[d - 1], 'worker', along_worker(0, d, 0))]
    all_gather x1 -> x0, waiting for transfers between devices: 51.1 us -> none  [body(): lax.all_gather(anchor_next.astype(jnp.bfloat16), 'worker', axis=0, tiled=...]
    pallas_call x0 -> x18, Pallas kernels: none -> 16.8 us  [call(): pl.pallas_call(kernel, out_shape=outs, in_specs=specs, out_specs=out_spec...]
    dot_general x1 -> x0, matrix products: 11.6 us -> none  [body(): jnp.einsum('ltr,ltc->rlc', layer_inputs, masked, preferred_element_type=j...]
    convert_element_type x4, other arithmetic: 7.95 us -> 2.57 us  [add(): return (a.astype(F32) + b.astype(F32)).astype(BF16)]
    dynamic_slice x3 -> x0, local copies, waits for them, and re-layouts: 4.82 us -> none  [the longest x2 3.52 us: body(): waiting = lax.dynamic_index_in_dim(inner_new, other, 0, keepdims=False)]
  transfers between devices with their start and end apart: 4 -> 32, of which waited for: 4 -> 18; matrix products, arithmetic and copies ran while one was open for 1% -> 2% of each run, Pallas kernels for 0% -> 9%
where the time goes in v1:
time: 165 us; the launch traced here: 164 us
  waiting for transfers between devices  82.6 us (50%)
  starting transfers between devices  55.2 us (33%)
  Pallas kernels  16.8 us (10%)
  local copies, waits for them, and re-layouts  5.11 us (3%)
  other arithmetic  2.57 us (2%)
    ppermute x1, waiting for transfers between devices, body(): got_a = lax.ppermute(buf_a, 'fsdp', TO_A)  27.4 us
    ppermute x9, starting transfers between devices, from_z(): lax.ppermute(parts[d - 1], 'worker', along_worker(0, d, 0))  24.7 us
    ppermute x9, waiting for transfers between devices, from_x(): lax.ppermute(parts[d - 1], 'worker', along_worker(d, 0, 0))  17.5 us
    pallas_call x18, Pallas kernels, call(): pl.pallas_call(kernel, out_shape=outs, in_specs=specs, out_specs=out_spec...  16.8 us
    ppermute x9, starting transfers between devices, from_x(): lax.ppermute(parts[d - 1], 'worker', along_worker(d, 0, 0))  13.7 us
    ppermute x1, waiting for transfers between devices, body(): got_z = lax.ppermute(buf_z, 'fsdp', TO_Z)  12.9 us
    ppermute x1, waiting for transfers between devices, body(): last_b = lax.ppermute(add(keep_b[1], next_b[1]), 'fsdp', TO_Z)  8.09 us
    ppermute x1, waiting for transfers between devices, body(): last_a = lax.ppermute(add(keep_a[1], next_a[1]), 'fsdp', TO_Z)  7.31 us
  transfers between devices with their start and end apart: 32, of which 18 were waited for; matrix products, arithmetic and copies ran while one was open for 2% of the time, Pallas kernels for 9%

profile of v1, /device:TPU:8, one launch (start us, length us, event | category | flops | bytes accessed | tf_op | source)
XLA Modules:
  0.0 163.8 jit_solution(4825229964111731943)
XLA Ops:
  1.3 3.4 %copy-done = bf16[2,256,8192]{2,1,0:T(8,128)(2,1)S(1)} copy-done((bf16[2,256,8192]{2,1,0:T(8,128)(2,1)S(1)}, bf16[2,256,8192]{2,1,0:T(8,128)(2,1)}, u32[]{:S(2)}) %copy-start) | copy-done | bytes 8388632
  4.7 1.0 copy-done.3
  6.4 1.9 %pack.1 = (bf16[256,2560]{1,0:T(8,128)(2,1)S(1)}, bf16[256,2560]{1,0:T(8,128)(2,1)S(1)}, bf16[256,4608]{1,0:T(8,128)(2,1)}, bf16[2,512,256]{2,1,0:T(8,128)(2,1)S(1)}) custom-call(s32[1]{0:T(128)S(6)} %copy.13.plan.plan_ref, s32[1,256]{1,0:T(1,128)S(1)} %bitcast.21, bf16[2,256,8192]{2,1,0:T(8,128)(2,1)S(1)} %copy-done, bf16[2,256,512]{2,1,0:T(8,128)(2,1)S(1)} %copy-done.3), custom_call_target="tpu_custom_call" | custom-call | bytes 10485760 | tf_op jit(solution)/shard_map/pack/pallas_call | solution.py:42
  8.3 2.0 %collective-permute-start.20 = (bf16[256,4608]{1,0:T(8,128)(2,1)}, bf16[256,4608]{1,0:T(8,128)(2,1)S(1)}, u32[]{:S(2)}, u32[]{:S(2)}) collective-permute-start(bf16[256,4608]{1,0:T(8,128)(2,1)} %get-tuple-element.50), channel_id=1, source_target_pairs={{0,4},{1,5},{2,6},{3,7},{4,0},{5,1},{6,2},{7,3},{8,12},{9,13},{10,... | collective-permute-start | bytes 7077896 | tf_op jit(solution)/shard_map/ppermute | solution.py:398
  10.7 2.4 %collective-permute-start.3 = (bf16[256,2560]{1,0:T(8,128)(2,1)S(1)}, bf16[256,2560]{1,0:T(8,128)(2,1)S(1)}, u32[]{:S(2)}, u32[]{:S(2)}) collective-permute-start(bf16[256,2560]{1,0:T(8,128)(2,1)S(1)} %get-tuple-element.38), channel_id=1, source_target_pairs={{0,3},{1,2},{2,1},{3,0},{4,7},{5,6},{6,5},{7,4},{8,11},{9,10},{10,... | collective-permute-start | bytes 3932168 | tf_op jit(solution)/shard_map/ppermute | solution.py:397
  13.1 27.4 %collective-permute-done.recv_ref = bf16[256,2560]{1,0:T(8,128)(2,1)S(1)} collective-permute-done((bf16[256,2560]{1,0:T(8,128)(2,1)S(1)}, bf16[256,2560]{1,0:T(8,128)(2,1)S(1)}, u32[]{:S(2)}, u32[]{:S(2)}) %collective-permute-start) | collective-permute-done | bytes 1310752 | tf_op jit(solution)/shard_map/ppermute | solution.py:396
  40.5 1.2 send_a.1
  41.7 1.7 %collective-permute-start.1 = (bf16[2,512,512]{2,1,0:T(8,128)(2,1)S(1)}, bf16[2,512,512]{2,1,0:T(8,128)(2,1)S(1)}, u32[]{:S(2)}, u32[]{:S(2)}) collective-permute-start(bf16[2,512,512]{2,1,0:T(8,128)(2,1)S(1)} %send_a.1), channel_id=1, source_target_pairs={{0,3},{1,2},{2,1},{3,0},{4,7},{5,6},{6,5},{7,4},{8,11},{9,10},{10,... | collective-permute-start | bytes 3145736 | tf_op jit(solution)/shard_map/ppermute | solution.py:408
  43.3 1.2 send_b.1
  44.5 2.0 %collective-permute-start.4 = (bf16[2,512,512]{2,1,0:T(8,128)(2,1)S(1)}, bf16[2,512,512]{2,1,0:T(8,128)(2,1)S(1)}, u32[]{:S(2)}, u32[]{:S(2)}) collective-permute-start(bf16[2,512,512]{2,1,0:T(8,128)(2,1)S(1)} %send_b.1), channel_id=1, source_target_pairs={{0,1},{1,0},{2,3},{3,2},{4,5},{5,4},{6,7},{7,6},{8,9},{9,8},{10,11... | collective-permute-start | bytes 3145736 | tf_op jit(solution)/shard_map/ppermute | solution.py:410
  46.5 1.2 keep_a.1
  47.6 1.2 keep_b.1
  48.8 12.9 %collective-permute-done.20.recv_ref = bf16[256,4608]{1,0:T(8,128)(2,1)S(1)} collective-permute-done((bf16[256,4608]{1,0:T(8,128)(2,1)}, bf16[256,4608]{1,0:T(8,128)(2,1)S(1)}, u32[]{:S(2)}, u32[]{:S(2)}) %collective-permute-start.20) | collective-permute-done | bytes 2359328 | tf_op jit(solution)/shard_map/ppermute | solution.py:398
  61.7 2.3 %send_o.1 = (bf16[2,256,1024]{2,1,0:T(8,128)(2,1)S(1)}, bf16[2,256,1024]{2,1,0:T(8,128)(2,1)S(1)}) custom-call(s32[1]{0:T(128)S(6)} %copy.13.plan.plan_ref, bf16[2,256,8192]{2,1,0:T(8,128)(2,1)S(1)} %copy-done.1, bf16[2,512,256]{2,1,0:T(8,128)(2,1)S(1)} %get-tuple-element.36.gt_ref, bf16[256,4608]{1,0:T(8,128)(2,1)S(1)} %collective-permute-done.20.recv_ref), custom_call_target="tpu_custom_call" | custom-call | flops 1073741824 | bytes 5242880 | tf_op jit(solution)/shard_map/send_o/pallas_call | solution.py:42
  64.6 0.9 collective-permute-done.1
  65.8 1.0 collective-permute-start.2
  66.7 2.4 %collective-permute-start.23 = (bf16[2,256,1024]{2,1,0:T(8,128)(2,1)S(1)}, bf16[2,256,1024]{2,1,0:T(8,128)(2,1)}, u32[]{:S(2)}, u32[]{:S(2)}) collective-permute-start(bf16[2,256,1024]{2,1,0:T(8,128)(2,1)S(1)} %get-tuple-element.54), channel_id=1, source_target_pairs={{0,3},{1,2},{2,1},{3,0},{4,7},{5,6},{6,5},{7,4},{8,11},{9,10},{10,... | collective-permute-start | bytes 3145736 | tf_op jit(solution)/shard_map/ppermute | solution.py:428
  69.1 1.2 collective-permute-done.4
  71.0 2.3 %keep_o.1 = (bf16[2,256,1024]{2,1,0:T(8,128)(2,1)S(1)}, bf16[2,256,1024]{2,1,0:T(8,128)(2,1)S(1)}) custom-call(s32[1]{0:T(128)S(6)} %copy.13.plan.plan_ref, bf16[2,256,8192]{2,1,0:T(8,128)(2,1)S(1)} %copy-done.1, bf16[2,512,256]{2,1,0:T(8,128)(2,1)S(1)} %get-tuple-element.36.gt_ref, bf16[256,4608]{1,0:T(8,128)(2,1)S(1)} %collective-permute-done.20.recv_ref), custom_call_target="tpu_custom_call" | custom-call | flops 1073741824 | bytes 5242880 | tf_op jit(solution)/shard_map/keep_o/pallas_call | solution.py:42
  73.4 7.3 %collective-permute-done.2.ra_ref = bf16[512,512]{1,0:T(8,128)(2,1)S(1)} collective-permute-done((bf16[512,512]{1,0:T(8,128)(2,1)S(1)}, bf16[512,512]{1,0:T(8,128)(2,1)S(1)}, u32[]{:S(2)}, u32[]{:S(2)}) %collective-permute-start.2) | collective-permute-done | bytes 524320 | tf_op jit(solution)/shard_map/ppermute | solution.py:413
  80.7 8.1 %collective-permute-done.5.rb_ref = bf16[512,512]{1,0:T(8,128)(2,1)S(1)} collective-permute-done((bf16[512,512]{1,0:T(8,128)(2,1)S(1)}, bf16[512,512]{1,0:T(8,128)(2,1)S(1)}, u32[]{:S(2)}, u32[]{:S(2)}) %collective-permute-start.5) | collective-permute-done | bytes 524320 | tf_op jit(solution)/shard_map/ppermute | solution.py:414
  89.6 1.0 collective-permute-done.21
  91.0 1.7 %collective-permute-start.22 = (bf16[256,1024]{1,0:T(8,128)(2,1)S(1)}, bf16[256,1024]{1,0:T(8,128)(2,1)S(1)}, u32[]{:S(2)}, u32[]{:S(2)}) collective-permute-start(bf16[256,1024]{1,0:T(8,128)(2,1)S(1)} %get-tuple-element.70), channel_id=1, source_target_pairs={{0,3},{1,2},{2,1},{3,0},{4,7},{5,6},{6,5},{7,4},{8,11},{9,10},{10,... | collective-permute-start | bytes 1572872 | tf_op jit(solution)/shard_map/ppermute | solution.py:435
  92.7 1.6 fusion.7
  94.3 2.1 %collective-permute-start.24 = (bf16[256,1024]{1,0:T(8,128)(2,1)S(1)}, bf16[256,1024]{1,0:T(8,128)(2,1)S(1)}, u32[]{:S(2)}, u32[]{:S(2)}) collective-permute-start(bf16[256,1024]{1,0:T(8,128)(2,1)S(1)} %get-tuple-element.68), channel_id=1, source_target_pairs={{0,1},{1,0},{2,3},{3,2},{4,5},{5,4},{6,7},{7,6},{8,9},{9,8},{10,11... | collective-permute-start | bytes 1572872 | tf_op jit(solution)/shard_map/ppermute | solution.py:436
  96.5 1.6 collective-permute-start.7
  98.1 2.7 %collective-permute-start.8 = (bf16[4,32,512]{2,1,0:T(8,128)(2,1)S(1)}, bf16[4,32,512]{2,1,0:T(8,128)(2,1)S(1)}, u32[]{:S(2)}, u32[]{:S(2)}) collective-permute-start(bf16[4,32,512]{2,1,0:T(8,128)(2,1)S(1)} %get-tuple-element.43), channel_id=1, source_target_pairs={{0,128},{8,136},{16,144},{24,152},{32,160},{40,168},{48,176},{56,1... | collective-permute-start | bytes 393224 | tf_op jit(solution)/shard_map/ppermute | solution.py:374
  100.8 1.4 collective-permute-start.9
  102.2 0.9 collective-permute-done.7.b
  103.2 3.7 %collective-permute-done.8.c = bf16[4,32,512]{2,1,0:T(8,128)(2,1)S(1)} collective-permute-done((bf16[4,32,512]{2,1,0:T(8,128)(2,1)S(1)}, bf16[4,32,512]{2,1,0:T(8,128)(2,1)S(1)}, u32[]{:S(2)}, u32[]{:S(2)}) %collective-permute-start.8) | collective-permute-done | bytes 131104 | tf_op jit(solution)/shard_map/ppermute | solution.py:374
  107.0 3.3 %collective-permute-start.10 = (bf16[32,512]{1,0:T(8,128)(2,1)S(1)}, bf16[32,512]{1,0:T(8,128)(2,1)S(1)}, u32[]{:S(2)}, u32[]{:S(2)}) collective-permute-start(bf16[32,512]{1,0:T(8,128)(2,1)S(1)} %get-tuple-element.46), channel_id=1, source_target_pairs={{0,16},{8,24},{16,32},{24,40},{32,48},{40,56},{48,0},{56,8},{64,80... | collective-permute-start | bytes 98312 | tf_op jit(solution)/shard_map/ppermute | solution.py:378
  110.3 4.5 %collective-permute-start.11 = (bf16[32,512]{1,0:T(8,128)(2,1)S(1)}, bf16[32,512]{1,0:T(8,128)(2,1)S(1)}, u32[]{:S(2)}, u32[]{:S(2)}) collective-permute-start(bf16[32,512]{1,0:T(8,128)(2,1)S(1)} %get-tuple-element.47), channel_id=1, source_target_pairs={{0,32},{8,40},{16,48},{24,56},{32,0},{40,8},{48,16},{56,24},{64,96... | collective-permute-start | bytes 98312 | tf_op jit(solution)/shard_map/ppermute | solution.py:378
  114.8 2.7 %collective-permute-start.12 = (bf16[32,512]{1,0:T(8,128)(2,1)S(1)}, bf16[32,512]{1,0:T(8,128)(2,1)S(1)}, u32[]{:S(2)}, u32[]{:S(2)}) collective-permute-start(bf16[32,512]{1,0:T(8,128)(2,1)S(1)} %get-tuple-element.48), channel_id=1, source_target_pairs={{0,48},{8,56},{16,0},{24,8},{32,16},{40,24},{48,32},{56,40},{64,11... | collective-permute-start | bytes 98312 | tf_op jit(solution)/shard_map/ppermute | solution.py:378
  117.5 1.7 %inner_other.1 = (bf16[16,2,32,512]{3,2,1,0:T(8,128)(2,1)S(1)}, bf16[16,32,512]{2,1,0:T(8,128)(2,1)S(1)}, bf16[2,16,2,32,512]{4,3,2,1,0:T(8,128)(2,1)}) custom-call(s32[1]{0:T(128)S(6)} %copy.13.plan.plan_ref, bf16[2,16,2,32,512]{4,3,2,1,0:T(8,128)(2,1)S(1)} %bitcast.20, bf16[256,1024]{1,0:T(8,128)(2,1)S(1)} %get-tuple-element.71.k0_ref, ...), custom_call_target="tpu_custom_call" | custom-call | bytes 6291456 | tf_op jit(solution)/shard_map/inner_other/pallas_call | solution.py:42
  120.4 3.8 %collective-permute-start.15 = (bf16[32,512]{1,0:T(8,128)(2,1)S(1)}, bf16[32,512]{1,0:T(8,128)(2,1)S(1)}, u32[]{:S(2)}, u32[]{:S(2)}) collective-permute-start(bf16[32,512]{1,0:T(8,128)(2,1)S(1)} %get-tuple-element.49.a), channel_id=1, source_target_pairs={{0,48},{8,56},{16,0},{24,8},{32,16},{40,24},{48,32},{56,40},{64,11... | collective-permute-start | bytes 98312 | tf_op jit(solution)/shard_map/ppermute | solution.py:378
  124.2 1.8 %collective-permute-start.14 = (bf16[32,512]{1,0:T(8,128)(2,1)S(1)}, bf16[32,512]{1,0:T(8,128)(2,1)S(1)}, u32[]{:S(2)}, u32[]{:S(2)}) collective-permute-start(bf16[32,512]{1,0:T(8,128)(2,1)S(1)} %get-tuple-element.49.a), channel_id=1, source_target_pairs={{0,32},{8,40},{16,48},{24,56},{32,0},{40,8},{48,16},{56,24},{64,96... | collective-permute-start | bytes 98312 | tf_op jit(solution)/shard_map/ppermute | solution.py:378
  126.6 5.5 %collective-permute-done.14.c = bf16[32,512]{1,0:T(8,128)(2,1)S(1)} collective-permute-done((bf16[32,512]{1,0:T(8,128)(2,1)S(1)}, bf16[32,512]{1,0:T(8,128)(2,1)S(1)}, u32[]{:S(2)}, u32[]{:S(2)}) %collective-permute-start.14) | collective-permute-done | bytes 32800 | tf_op jit(solution)/shard_map/ppermute | solution.py:378
  132.4 2.3 %collective-permute-start.18 = (bf16[4,32,512]{2,1,0:T(8,128)(2,1)S(1)}, bf16[4,32,512]{2,1,0:T(8,128)(2,1)S(1)}, u32[]{:S(2)}, u32[]{:S(2)}) collective-permute-start(bf16[4,32,512]{2,1,0:T(8,128)(2,1)S(1)} %gather_z.1.a), channel_id=1, source_target_pairs={{0,192},{8,200},{16,208},{24,216},{32,224},{40,232},{48,240},{56,2... | collective-permute-start | bytes 393224 | tf_op jit(solution)/shard_map/ppermute | solution.py:374
  134.7 1.1 collective-permute-start.17
  136.6 0.9 collective-permute-done.18.d
  137.4 3.8 %collective-permute-done.17.c = bf16[4,32,512]{2,1,0:T(8,128)(2,1)S(1)} collective-permute-done((bf16[4,32,512]{2,1,0:T(8,128)(2,1)S(1)}, bf16[4,32,512]{2,1,0:T(8,128)(2,1)S(1)}, u32[]{:S(2)}, u32[]{:S(2)}) %collective-permute-start.17) | collective-permute-done | bytes 131104 | tf_op jit(solution)/shard_map/ppermute | solution.py:374
  141.3 1.3 collective-permute-done.16.b
  143.0 2.0 %collective-permute-start.27 = (bf16[4,32,512]{2,1,0:T(8,128)(2,1)S(1)}, bf16[4,32,512]{2,1,0:T(8,128)(2,1)S(1)}, u32[]{:S(2)}, u32[]{:S(2)}) collective-permute-start(bf16[4,32,512]{2,1,0:T(8,128)(2,1)S(1)} %get-tuple-element.62), channel_id=1, source_target_pairs={{0,128},{8,136},{16,144},{24,152},{32,160},{40,168},{48,176},{56,1... | collective-permute-start | bytes 393224 | tf_op jit(solution)/shard_map/ppermute | solution.py:374
  145.0 1.7 %collective-permute-start.28 = (bf16[4,32,512]{2,1,0:T(8,128)(2,1)S(1)}, bf16[4,32,512]{2,1,0:T(8,128)(2,1)S(1)}, u32[]{:S(2)}, u32[]{:S(2)}) collective-permute-start(bf16[4,32,512]{2,1,0:T(8,128)(2,1)S(1)} %get-tuple-element.63), channel_id=1, source_target_pairs={{0,192},{8,200},{16,208},{24,216},{32,224},{40,232},{48,240},{56,2... | collective-permute-start | bytes 393224 | tf_op jit(solution)/shard_map/ppermute | solution.py:374
  146.8 6.1 %collective-permute-done.26.b = bf16[4,32,512]{2,1,0:T(8,128)(2,1)S(1)} collective-permute-done((bf16[4,32,512]{2,1,0:T(8,128)(2,1)S(1)}, bf16[4,32,512]{2,1,0:T(8,128)(2,1)S(1)}, u32[]{:S(2)}, u32[]{:S(2)}) %collective-permute-start.26) | collective-permute-done | bytes 131104 | tf_op jit(solution)/shard_map/ppermute | solution.py:374
  153.7 3.9 %collective-permute-start.30 = (bf16[32,512]{1,0:T(8,128)(2,1)S(1)}, bf16[32,512]{1,0:T(8,128)(2,1)S(1)}, u32[]{:S(2)}, u32[]{:S(2)}) collective-permute-start(bf16[32,512]{1,0:T(8,128)(2,1)S(1)} %get-tuple-element.66), channel_id=1, source_target_pairs={{0,32},{8,40},{16,48},{24,56},{32,0},{40,8},{48,16},{56,24},{64,96... | collective-permute-start | bytes 98312 | tf_op jit(solution)/shard_map/ppermute | solution.py:378
  157.6 4.0 %collective-permute-start.31 = (bf16[32,512]{1,0:T(8,128)(2,1)S(1)}, bf16[32,512]{1,0:T(8,128)(2,1)S(1)}, u32[]{:S(2)}, u32[]{:S(2)}) collective-permute-start(bf16[32,512]{1,0:T(8,128)(2,1)S(1)} %get-tuple-element.67), channel_id=1, source_target_pairs={{0,48},{8,56},{16,0},{24,8},{32,16},{40,24},{48,32},{56,40},{64,11... | collective-permute-start | bytes 98312 | tf_op jit(solution)/shard_map/ppermute | solution.py:378
  161.6 1.4 mix.1
  (52 shorter events, 8.8 us)
Async XLA Ops:
  1.3 3.4 %copy-start = (bf16[2,256,8192]{2,1,0:T(8,128)(2,1)S(1)}, bf16[2,256,8192]{2,1,0:T(8,128)(2,1)}, u32[]{:S(2)}) copy-start(bf16[2,256,8192]{2,1,0:T(8,128)(2,1)} %x_ref.11) | copy-start | bytes 25165828
  4.7 1.0 copy-start.3
  5.7 0.7 copy-start.6
  6.4 34.1 %copy-start.1 = (bf16[2,256,8192]{2,1,0:T(8,128)(2,1)S(1)}, bf16[2,256,8192]{2,1,0:T(8,128)(2,1)}, u32[]{:S(2)}) copy-start(bf16[2,256,8192]{2,1,0:T(8,128)(2,1)} %x_ref.11) | copy-start | bytes 25165828
  8.3 53.5 %collective-permute-start.20 = (bf16[256,4608]{1,0:T(8,128)(2,1)}, bf16[256,4608]{1,0:T(8,128)(2,1)S(1)}, u32[]{:S(2)}, u32[]{:S(2)}) collective-permute-start(bf16[256,4608]{1,0:T(8,128)(2,1)} %get-tuple-element.50), channel_id=1, source_target_pairs={{0,4},{1,5},{2,6},{3,7},{4,0},{5,1},{6,2},{7,3},{8,12},{9,13},{10,... | collective-permute-start | bytes 7077896 | tf_op jit(solution)/shard_map/ppermute | solution.py:398
  10.3 30.2 %collective-permute-start = (bf16[256,2560]{1,0:T(8,128)(2,1)S(1)}, bf16[256,2560]{1,0:T(8,128)(2,1)S(1)}, u32[]{:S(2)}, u32[]{:S(2)}) collective-permute-start(bf16[256,2560]{1,0:T(8,128)(2,1)S(1)} %get-tuple-element.37), channel_id=1, source_target_pairs={{0,1},{1,0},{2,3},{3,2},{4,5},{5,4},{6,7},{7,6},{8,9},{9,8},{10,11... | collective-permute-start | bytes 3932168 | tf_op jit(solution)/shard_map/ppermute | solution.py:396
  10.7 32.6 %collective-permute-start.3 = (bf16[256,2560]{1,0:T(8,128)(2,1)S(1)}, bf16[256,2560]{1,0:T(8,128)(2,1)S(1)}, u32[]{:S(2)}, u32[]{:S(2)}) collective-permute-start(bf16[256,2560]{1,0:T(8,128)(2,1)S(1)} %get-tuple-element.38), channel_id=1, source_target_pairs={{0,3},{1,2},{2,1},{3,0},{4,7},{5,6},{6,5},{7,4},{8,11},{9,10},{10,... | collective-permute-start | bytes 3932168 | tf_op jit(solution)/shard_map/ppermute | solution.py:397
  41.7 23.8 %collective-permute-start.1 = (bf16[2,512,512]{2,1,0:T(8,128)(2,1)S(1)}, bf16[2,512,512]{2,1,0:T(8,128)(2,1)S(1)}, u32[]{:S(2)}, u32[]{:S(2)}) collective-permute-start(bf16[2,512,512]{2,1,0:T(8,128)(2,1)S(1)} %send_a.1), channel_id=1, source_target_pairs={{0,3},{1,2},{2,1},{3,0},{4,7},{5,6},{6,5},{7,4},{8,11},{9,10},{10,... | collective-permute-start | bytes 3145736 | tf_op jit(solution)/shard_map/ppermute | solution.py:408
  44.5 25.9 %collective-permute-start.4 = (bf16[2,512,512]{2,1,0:T(8,128)(2,1)S(1)}, bf16[2,512,512]{2,1,0:T(8,128)(2,1)S(1)}, u32[]{:S(2)}, u32[]{:S(2)}) collective-permute-start(bf16[2,512,512]{2,1,0:T(8,128)(2,1)S(1)} %send_b.1), channel_id=1, source_target_pairs={{0,1},{1,0},{2,3},{3,2},{4,5},{5,4},{6,7},{7,6},{8,9},{9,8},{10,11... | collective-permute-start | bytes 3145736 | tf_op jit(solution)/shard_map/ppermute | solution.py:410
  64.1 26.6 %collective-permute-start.21 = (bf16[2,256,1024]{2,1,0:T(8,128)(2,1)S(1)}, bf16[2,256,1024]{2,1,0:T(8,128)(2,1)S(1)}, u32[]{:S(2)}, u32[]{:S(2)}) collective-permute-start(bf16[2,256,1024]{2,1,0:T(8,128)(2,1)S(1)} %get-tuple-element.52), channel_id=1, source_target_pairs={{0,1},{1,0},{2,3},{3,2},{4,5},{5,4},{6,7},{7,6},{8,9},{9,8},{10,11... | collective-permute-start | bytes 3145736 | tf_op jit(solution)/shard_map/ppermute | solution.py:427
  65.8 14.9 %collective-permute-start.2 = (bf16[512,512]{1,0:T(8,128)(2,1)S(1)}, bf16[512,512]{1,0:T(8,128)(2,1)S(1)}, u32[]{:S(2)}, u32[]{:S(2)}) collective-permute-start(bf16[512,512]{1,0:T(8,128)(2,1)S(1)} %get-tuple-element.74), channel_id=1, source_target_pairs={{0,4},{1,5},{2,6},{3,7},{4,0},{5,1},{6,2},{7,3},{8,12},{9,13},{10,... | collective-permute-start | bytes 1572872 | tf_op jit(solution)/shard_map/ppermute | solution.py:413
  66.7 26.0 %collective-permute-start.23 = (bf16[2,256,1024]{2,1,0:T(8,128)(2,1)S(1)}, bf16[2,256,1024]{2,1,0:T(8,128)(2,1)}, u32[]{:S(2)}, u32[]{:S(2)}) collective-permute-start(bf16[2,256,1024]{2,1,0:T(8,128)(2,1)S(1)} %get-tuple-element.54), channel_id=1, source_target_pairs={{0,3},{1,2},{2,1},{3,0},{4,7},{5,6},{6,5},{7,4},{8,11},{9,10},{10,... | collective-permute-start | bytes 3145736 | tf_op jit(solution)/shard_map/ppermute | solution.py:428
  70.6 18.1 %copy-start.2 = (bf16[1,2,1024,512]{3,2,1,0:T(8,128)(2,1)S(1)}, bf16[1,2,1024,512]{3,2,1,0:T(8,128)(2,1)}, u32[]{:S(2)}) copy-start(bf16[1,2,1024,512]{3,2,1,0:T(8,128)(2,1)} %param.10) | copy-start | bytes 6291460
  70.7 18.1 %collective-permute-start.5 = (bf16[512,512]{1,0:T(8,128)(2,1)S(1)}, bf16[512,512]{1,0:T(8,128)(2,1)S(1)}, u32[]{:S(2)}, u32[]{:S(2)}) collective-permute-start(bf16[512,512]{1,0:T(8,128)(2,1)S(1)} %get-tuple-element.72), channel_id=1, source_target_pairs={{0,4},{1,5},{2,6},{3,7},{4,0},{5,1},{6,2},{7,3},{8,12},{9,13},{10,... | collective-permute-start | bytes 1572872 | tf_op jit(solution)/shard_map/ppermute | solution.py:414
  89.5 6.8 %collective-permute-start.6 = (bf16[16,32,512]{2,1,0:T(8,128)(2,1)S(1)}, bf16[16,32,512]{2,1,0:T(8,128)(2,1)S(1)}, u32[]{:S(2)}, u32[]{:S(2)}) collective-permute-start(bf16[16,32,512]{2,1,0:T(8,128)(2,1)S(1)} %get-tuple-element.40), channel_id=1, source_target_pairs={{0,8},{8,0},{16,24},{24,16},{32,40},{40,32},{48,56},{56,48},{64,72... | collective-permute-start | bytes 1572872 | tf_op jit(solution)/shard_map/ppermute | solution.py:386
  91.0 26.4 %collective-permute-start.22 = (bf16[256,1024]{1,0:T(8,128)(2,1)S(1)}, bf16[256,1024]{1,0:T(8,128)(2,1)S(1)}, u32[]{:S(2)}, u32[]{:S(2)}) collective-permute-start(bf16[256,1024]{1,0:T(8,128)(2,1)S(1)} %get-tuple-element.70), channel_id=1, source_target_pairs={{0,3},{1,2},{2,1},{3,0},{4,7},{5,6},{6,5},{7,4},{8,11},{9,10},{10,... | collective-permute-start | bytes 1572872 | tf_op jit(solution)/shard_map/ppermute | solution.py:435
  94.3 23.2 %collective-permute-start.24 = (bf16[256,1024]{1,0:T(8,128)(2,1)S(1)}, bf16[256,1024]{1,0:T(8,128)(2,1)S(1)}, u32[]{:S(2)}, u32[]{:S(2)}) collective-permute-start(bf16[256,1024]{1,0:T(8,128)(2,1)S(1)} %get-tuple-element.68), channel_id=1, source_target_pairs={{0,1},{1,0},{2,3},{3,2},{4,5},{5,4},{6,7},{7,6},{8,9},{9,8},{10,11... | collective-permute-start | bytes 1572872 | tf_op jit(solution)/shard_map/ppermute | solution.py:436
  96.5 6.7 %collective-permute-start.7 = (bf16[4,32,512]{2,1,0:T(8,128)(2,1)S(1)}, bf16[4,32,512]{2,1,0:T(8,128)(2,1)S(1)}, u32[]{:S(2)}, u32[]{:S(2)}) collective-permute-start(bf16[4,32,512]{2,1,0:T(8,128)(2,1)S(1)} %get-tuple-element.42), channel_id=1, source_target_pairs={{0,64},{8,72},{16,80},{24,88},{32,96},{40,104},{48,112},{56,120},{... | collective-permute-start | bytes 393224 | tf_op jit(solution)/shard_map/ppermute | solution.py:374
  98.1 8.8 %collective-permute-start.8 = (bf16[4,32,512]{2,1,0:T(8,128)(2,1)S(1)}, bf16[4,32,512]{2,1,0:T(8,128)(2,1)S(1)}, u32[]{:S(2)}, u32[]{:S(2)}) collective-permute-start(bf16[4,32,512]{2,1,0:T(8,128)(2,1)S(1)} %get-tuple-element.43), channel_id=1, source_target_pairs={{0,128},{8,136},{16,144},{24,152},{32,160},{40,168},{48,176},{56,1... | collective-permute-start | bytes 393224 | tf_op jit(solution)/shard_map/ppermute | solution.py:374
  100.8 6.1 %collective-permute-start.9 = (bf16[4,32,512]{2,1,0:T(8,128)(2,1)S(1)}, bf16[4,32,512]{2,1,0:T(8,128)(2,1)S(1)}, u32[]{:S(2)}, u32[]{:S(2)}) collective-permute-start(bf16[4,32,512]{2,1,0:T(8,128)(2,1)S(1)} %get-tuple-element.44), channel_id=1, source_target_pairs={{0,192},{8,200},{16,208},{24,216},{32,224},{40,232},{48,240},{56,2... | collective-permute-start | bytes 393224 | tf_op jit(solution)/shard_map/ppermute | solution.py:374
  107.0 12.4 %collective-permute-start.10 = (bf16[32,512]{1,0:T(8,128)(2,1)S(1)}, bf16[32,512]{1,0:T(8,128)(2,1)S(1)}, u32[]{:S(2)}, u32[]{:S(2)}) collective-permute-start(bf16[32,512]{1,0:T(8,128)(2,1)S(1)} %get-tuple-element.46), channel_id=1, source_target_pairs={{0,16},{8,24},{16,32},{24,40},{32,48},{40,56},{48,0},{56,8},{64,80... | collective-permute-start | bytes 98312 | tf_op jit(solution)/shard_map/ppermute | solution.py:378
  110.3 9.0 %collective-permute-start.11 = (bf16[32,512]{1,0:T(8,128)(2,1)S(1)}, bf16[32,512]{1,0:T(8,128)(2,1)S(1)}, u32[]{:S(2)}, u32[]{:S(2)}) collective-permute-start(bf16[32,512]{1,0:T(8,128)(2,1)S(1)} %get-tuple-element.47), channel_id=1, source_target_pairs={{0,32},{8,40},{16,48},{24,56},{32,0},{40,8},{48,16},{56,24},{64,96... | collective-permute-start | bytes 98312 | tf_op jit(solution)/shard_map/ppermute | solution.py:378
  114.8 4.9 %collective-permute-start.12 = (bf16[32,512]{1,0:T(8,128)(2,1)S(1)}, bf16[32,512]{1,0:T(8,128)(2,1)S(1)}, u32[]{:S(2)}, u32[]{:S(2)}) collective-permute-start(bf16[32,512]{1,0:T(8,128)(2,1)S(1)} %get-tuple-element.48), channel_id=1, source_target_pairs={{0,48},{8,56},{16,0},{24,8},{32,16},{40,24},{48,32},{56,40},{64,11... | collective-permute-start | bytes 98312 | tf_op jit(solution)/shard_map/ppermute | solution.py:378
  117.5 2.2 %copy-start.4 = (f32[2,32,512]{2,1,0:T(8,128)S(1)}, f32[2,32,512]{2,1,0:T(8,128)}, u32[]{:S(2)}) copy-start(f32[2,32,512]{2,1,0:T(8,128)} %anchor_ref.3) | copy-start | bytes 393220
  117.5 2.2 %copy-start.5 = (f32[32,512]{1,0:T(8,128)S(1)}, f32[32,512]{1,0:T(8,128)}, u32[]{:S(2)}) copy-start(f32[32,512]{1,0:T(8,128)} %momentum_ref.1) | copy-start | bytes 196612
  119.3 23.5 %collective-permute-start.25 = (bf16[16,32,512]{2,1,0:T(8,128)(2,1)S(1)}, bf16[16,32,512]{2,1,0:T(8,128)(2,1)S(1)}, u32[]{:S(2)}, u32[]{:S(2)}) collective-permute-start(bf16[16,32,512]{2,1,0:T(8,128)(2,1)S(1)} %get-tuple-element.59), channel_id=1, source_target_pairs={{0,8},{8,0},{16,24},{24,16},{32,40},{40,32},{48,56},{56,48},{64,72... | collective-permute-start | bytes 1572872 | tf_op jit(solution)/shard_map/ppermute | solution.py:386
  120.4 6.2 %collective-permute-start.15 = (bf16[32,512]{1,0:T(8,128)(2,1)S(1)}, bf16[32,512]{1,0:T(8,128)(2,1)S(1)}, u32[]{:S(2)}, u32[]{:S(2)}) collective-permute-start(bf16[32,512]{1,0:T(8,128)(2,1)S(1)} %get-tuple-element.49.a), channel_id=1, source_target_pairs={{0,48},{8,56},{16,0},{24,8},{32,16},{40,24},{48,32},{56,40},{64,11... | collective-permute-start | bytes 98312 | tf_op jit(solution)/shard_map/ppermute | solution.py:378
  124.2 7.9 %collective-permute-start.14 = (bf16[32,512]{1,0:T(8,128)(2,1)S(1)}, bf16[32,512]{1,0:T(8,128)(2,1)S(1)}, u32[]{:S(2)}, u32[]{:S(2)}) collective-permute-start(bf16[32,512]{1,0:T(8,128)(2,1)S(1)} %get-tuple-element.49.a), channel_id=1, source_target_pairs={{0,32},{8,40},{16,48},{24,56},{32,0},{40,8},{48,16},{56,24},{64,96... | collective-permute-start | bytes 98312 | tf_op jit(solution)/shard_map/ppermute | solution.py:378
  126.0 6.4 %collective-permute-start.13 = (bf16[32,512]{1,0:T(8,128)(2,1)S(1)}, bf16[32,512]{1,0:T(8,128)(2,1)S(1)}, u32[]{:S(2)}, u32[]{:S(2)}) collective-permute-start(bf16[32,512]{1,0:T(8,128)(2,1)S(1)} %get-tuple-element.49.a), channel_id=1, source_target_pairs={{0,16},{8,24},{16,32},{24,40},{32,48},{40,56},{48,0},{56,8},{64,80... | collective-permute-start | bytes 98312 | tf_op jit(solution)/shard_map/ppermute | solution.py:378
  132.4 5.0 %collective-permute-start.18 = (bf16[4,32,512]{2,1,0:T(8,128)(2,1)S(1)}, bf16[4,32,512]{2,1,0:T(8,128)(2,1)S(1)}, u32[]{:S(2)}, u32[]{:S(2)}) collective-permute-start(bf16[4,32,512]{2,1,0:T(8,128)(2,1)S(1)} %gather_z.1.a), channel_id=1, source_target_pairs={{0,192},{8,200},{16,208},{24,216},{32,224},{40,232},{48,240},{56,2... | collective-permute-start | bytes 393224 | tf_op jit(solution)/shard_map/ppermute | solution.py:374
  134.7 6.5 %collective-permute-start.17 = (bf16[4,32,512]{2,1,0:T(8,128)(2,1)S(1)}, bf16[4,32,512]{2,1,0:T(8,128)(2,1)S(1)}, u32[]{:S(2)}, u32[]{:S(2)}) collective-permute-start(bf16[4,32,512]{2,1,0:T(8,128)(2,1)S(1)} %gather_z.1.a), channel_id=1, source_target_pairs={{0,128},{8,136},{16,144},{24,152},{32,160},{40,168},{48,176},{56,1... | collective-permute-start | bytes 393224 | tf_op jit(solution)/shard_map/ppermute | solution.py:374
  135.9 6.7 %collective-permute-start.16 = (bf16[4,32,512]{2,1,0:T(8,128)(2,1)S(1)}, bf16[4,32,512]{2,1,0:T(8,128)(2,1)S(1)}, u32[]{:S(2)}, u32[]{:S(2)}) collective-permute-start(bf16[4,32,512]{2,1,0:T(8,128)(2,1)S(1)} %gather_z.1.a), channel_id=1, source_target_pairs={{0,64},{8,72},{16,80},{24,88},{32,96},{40,104},{48,112},{56,120},{... | collective-permute-start | bytes 393224 | tf_op jit(solution)/shard_map/ppermute | solution.py:374
  142.7 18.9 %collective-permute-start.19 = (bf16[16,32,512]{2,1,0:T(8,128)(2,1)S(1)}, bf16[16,32,512]{2,1,0:T(8,128)(2,1)S(1)}, u32[]{:S(2)}, u32[]{:S(2)}) collective-permute-start(bf16[16,32,512]{2,1,0:T(8,128)(2,1)S(1)} %gather_x.1.own_ref), channel_id=1, source_target_pairs={{0,8},{8,0},{16,24},{24,16},{32,40},{40,32},{48,56},{56,48},{64,72... | collective-permute-start | bytes 1572872 | tf_op jit(solution)/shard_map/ppermute | solution.py:445
  142.9 10.0 %collective-permute-start.26 = (bf16[4,32,512]{2,1,0:T(8,128)(2,1)S(1)}, bf16[4,32,512]{2,1,0:T(8,128)(2,1)S(1)}, u32[]{:S(2)}, u32[]{:S(2)}) collective-permute-start(bf16[4,32,512]{2,1,0:T(8,128)(2,1)S(1)} %get-tuple-element.61), channel_id=1, source_target_pairs={{0,64},{8,72},{16,80},{24,88},{32,96},{40,104},{48,112},{56,120},{... | collective-permute-start | bytes 393224 | tf_op jit(solution)/shard_map/ppermute | solution.py:374
  143.0 9.9 %collective-permute-start.27 = (bf16[4,32,512]{2,1,0:T(8,128)(2,1)S(1)}, bf16[4,32,512]{2,1,0:T(8,128)(2,1)S(1)}, u32[]{:S(2)}, u32[]{:S(2)}) collective-permute-start(bf16[4,32,512]{2,1,0:T(8,128)(2,1)S(1)} %get-tuple-element.62), channel_id=1, source_target_pairs={{0,128},{8,136},{16,144},{24,152},{32,160},{40,168},{48,176},{56,1... | collective-permute-start | bytes 393224 | tf_op jit(solution)/shard_map/ppermute | solution.py:374
  145.0 8.5 %collective-permute-start.28 = (bf16[4,32,512]{2,1,0:T(8,128)(2,1)S(1)}, bf16[4,32,512]{2,1,0:T(8,128)(2,1)S(1)}, u32[]{:S(2)}, u32[]{:S(2)}) collective-permute-start(bf16[4,32,512]{2,1,0:T(8,128)(2,1)S(1)} %get-tuple-element.63), channel_id=1, source_target_pairs={{0,192},{8,200},{16,208},{24,216},{32,224},{40,232},{48,240},{56,2... | collective-permute-start | bytes 393224 | tf_op jit(solution)/shard_map/ppermute | solution.py:374
  153.6 9.4 %collective-permute-start.29 = (bf16[32,512]{1,0:T(8,128)(2,1)S(1)}, bf16[32,512]{1,0:T(8,128)(2,1)S(1)}, u32[]{:S(2)}, u32[]{:S(2)}) collective-permute-start(bf16[32,512]{1,0:T(8,128)(2,1)S(1)} %get-tuple-element.65), channel_id=1, source_target_pairs={{0,16},{8,24},{16,32},{24,40},{32,48},{40,56},{48,0},{56,8},{64,80... | collective-permute-start | bytes 98312 | tf_op jit(solution)/shard_map/ppermute | solution.py:378
  153.7 9.3 %collective-permute-start.30 = (bf16[32,512]{1,0:T(8,128)(2,1)S(1)}, bf16[32,512]{1,0:T(8,128)(2,1)S(1)}, u32[]{:S(2)}, u32[]{:S(2)}) collective-permute-start(bf16[32,512]{1,0:T(8,128)(2,1)S(1)} %get-tuple-element.66), channel_id=1, source_target_pairs={{0,32},{8,40},{16,48},{24,56},{32,0},{40,8},{48,16},{56,24},{64,96... | collective-permute-start | bytes 98312 | tf_op jit(solution)/shard_map/ppermute | solution.py:378
  157.6 5.6 %collective-permute-start.31 = (bf16[32,512]{1,0:T(8,128)(2,1)S(1)}, bf16[32,512]{1,0:T(8,128)(2,1)S(1)}, u32[]{:S(2)}, u32[]{:S(2)}) collective-permute-start(bf16[32,512]{1,0:T(8,128)(2,1)S(1)} %get-tuple-element.67), channel_id=1, source_target_pairs={{0,48},{8,56},{16,0},{24,8},{32,16},{40,24},{48,32},{56,40},{64,11... | collective-permute-start | bytes 98312 | tf_op jit(solution)/shard_map/ppermute | solution.py:378

commit v2 on v1

v2 whole, which is shorter than its diff:
```python
import jax
import jax.numpy as jnp
from jax import lax
from jax.experimental import pallas as pl
from jax.experimental.pallas import tpu as pltpu
from jax.sharding import PartitionSpec as P

inner_rate = 0.25
decay_rate = 0.1
outer_rate = 0.7
outer_beta = 0.9
mix_weight = 0.5

TOK = 256
KV = 512
ROWS = 1024
HALF = 512
F32 = jnp.float32
BF16 = jnp.bfloat16

HBM = pl.BlockSpec(memory_space=pltpu.HBM)
ANY = pl.BlockSpec(memory_space=pl.ANY)
VM = pl.BlockSpec(memory_space=pltpu.VMEM)
SM = pl.BlockSpec(memory_space=pltpu.SMEM)
MIB = 1024 * 1024
BIG = 24


def place():
    w = lax.axis_index("worker")
    f = lax.axis_index("fsdp")
    return w // 8, (w // 2) % 4, w % 2, f // 4, f % 4


def shape(*dims, dtype=BF16):
    return jax.ShapeDtypeStruct(dims, dtype)


def in_vmem(*dims):
    return pltpu.VMEM(dims, BF16)


def in_hbm(*dims):
    return pltpu.HBM(dims, BF16)


def pinned(value):
    return pltpu.with_memory_space_constraint(value, pltpu.HBM)


class Chain:
    def __init__(self):
        self.token = None


CHAIN = Chain()


def call(kernel, outs, args, specs, out_specs, scratch=(), aliases=None, name=None, vmem=16, hint=0):
    outs, out_specs = list(outs), list(out_specs)
    tokens = [] if CHAIN.token is None else [CHAIN.token]
    count = len(args)

    def chained(*refs):
        rest = refs[count + len(tokens) :]
        kernel(*refs[:count], *rest[: len(outs)], *rest[len(outs) + 1 :])

    *results, CHAIN.token = pl.pallas_call(
        chained,
        out_shape=outs + [in_hbm(8, 128)],
        in_specs=list(specs) + [HBM] * len(tokens),
        out_specs=out_specs + [HBM],
        scratch_shapes=list(scratch),
        compiler_params=pltpu.CompilerParams(vmem_limit_bytes=vmem * MIB),
        cost_estimate=pl.CostEstimate(flops=hint, bytes_accessed=0, transcendentals=0),
        input_output_aliases=aliases or {},
        name=name,
    )(*(pinned(a) if spec is HBM else a for a, spec in zip(args, specs)), *(pinned(t) for t in tokens))
    return results[0] if len(results) == 1 else results


def columns(start, width):
    return pl.ds(pl.multiple_of(start, width), width)


def pack_kernel(plan, tok, x, g, a1, b1, z1, a2, b2, z2, z3, gt_out, gin, gt, sems, gsems):
    _, _, _, z, y = place()
    s = lax.rem(plan[0], 2)
    copies = []

    def send(layer, col, width, dst, at):
        copies.append(
            pltpu.make_async_copy(
                x.at[layer, :, columns(col, width)], dst.at[:, pl.ds(at, width)], sems.at[len(copies)]
            )
        )
        copies[-1].start()

    g_copies = [pltpu.make_async_copy(g.at[layer], gin.at[i], gsems.at[i]) for i, layer in enumerate((s, 1 - s))]
    for c in g_copies:
        c.start()
    for zz, bufs in ((1 - z, (a1, b1)), (z, (a2, b2))):
        for buf, first, offset in ((bufs[0], y ^ 1, 0), (bufs[1], y ^ 3, HALF)):
            for i, yy in enumerate((first, y ^ 2)):
                send(s, (zz * 4 + yy) * ROWS + offset, HALF, buf, i * HALF)
    for j, buf, at in ((1, z1, 0), (2, z1, ROWS), (3, z2, 0), (0, z3, 0)):
        send(1 - s, ((1 - z) * 4 + (y ^ j)) * ROWS, ROWS, buf, at)
    kept = (tok[...] != 0).astype(F32)
    last = []

    def put(src, dst):
        last.append(pltpu.make_async_copy(src, dst, gsems.at[2 + len(last)]))
        last[-1].start()

    for i, bufs, at in ((0, (a1, b1), 2 * HALF), (1, (z1,), 2 * ROWS)):
        g_copies[i].wait()
        gt[i] = (gin[i].astype(F32).T * kept).astype(BF16)
        for buf in bufs:
            for h in range(2):
                put(gt.at[i, pl.ds(h * TOK, TOK)], buf.at[:, pl.ds(at + h * TOK, TOK)])
    put(gt, gt_out)
    for c in copies + last:
        c.wait()


def pack(plan, tok, x, g):
    wide = in_vmem(TOK, 2 * HALF + KV)
    half = in_vmem(TOK, 2 * HALF)
    return call(
        pack_kernel,
        (wide, wide, in_vmem(TOK, 2 * ROWS + KV), half, half, half, half, in_vmem(2, KV, TOK)),
        (plan, tok, x, g),
        [SM, VM, HBM, HBM],
        [VM] * 8,
        [
            pltpu.VMEM((2, TOK, KV), BF16),
            pltpu.VMEM((2, KV, TOK), BF16),
            pltpu.SemaphoreType.DMA((12,)),
            pltpu.SemaphoreType.DMA((9,)),
        ],
        name="pack",
        vmem=BIG,
    )


def product(name, fragment, pieces, width, out_shapes, g_at, plan, x, gt, recvs, hint=0):
    count = len(pieces)
    number = len(recvs)
    total = sum(len(p[3]) for p in pieces)

    def kernel(plan_ref, x_ref, gt_ref, *rest):
        recv_refs = rest[:number]
        outs = rest[number : number + len(out_shapes)]
        stage = rest[number + len(out_shapes) : number + 2 * len(out_shapes)]
        gts, xs, sems, out_sems = rest[number + 2 * len(out_shapes) :]
        _, _, _, z, y = place()
        s = lax.rem(plan_ref[0], 2)
        layer = s if fragment == 0 else 1 - s
        g_copies = [
            pltpu.make_async_copy(gt_ref.at[fragment], gts.at[:, pl.ds(0, TOK)], sems.at[2 * count]),
            *(
                pltpu.make_async_copy(
                    recv_refs[0].at[:, pl.ds(g_at + h * TOK, TOK)],
                    gts.at[pl.ds(h * TOK, TOK), pl.ds(TOK, TOK)],
                    sems.at[2 * count + 1 + h],
                )
                for h in range(2)
            ),
        ]
        copies = []
        for p, (own, source, at, _) in enumerate(pieces):
            copies.append(
                (
                    pltpu.make_async_copy(
                        x_ref.at[layer, :, columns(own(z, y), width)], xs.at[p, pl.ds(0, TOK)], sems.at[2 * p]
                    ),
                    pltpu.make_async_copy(
                        recv_refs[source].at[:, pl.ds(at, width)], xs.at[p, pl.ds(TOK, TOK)], sems.at[2 * p + 1]
                    ),
                )
            )
        for c in g_copies:
            c.start()
        for pair in copies:
            for c in pair:
                c.start()
        for c in g_copies:
            c.wait()
        done = []
        for p, (_, _, _, targets) in enumerate(pieces):
            for c in copies[p]:
                c.wait()
            for out, slot, k0, k1 in targets:
                src = stage[out] if slot is None else stage[out].at[slot]
                dst = outs[out] if slot is None else outs[out].at[slot]
                src[...] = jnp.dot(gts[k0:k1], xs[p], preferred_element_type=F32).astype(BF16)
                c = pltpu.make_async_copy(src, dst, out_sems.at[len(done)])
                c.start()
                done.append(c)
        for c in done:
            c.wait()

    return call(
        kernel,
        tuple(shape(*d) for d in out_shapes),
        (plan, x, gt, *recvs),
        [SM, ANY, ANY] + [ANY] * number,
        [ANY] * len(out_shapes),
        [
            *(pltpu.VMEM(d, BF16) for d in out_shapes),
            pltpu.VMEM((KV, 2 * TOK), BF16),
            pltpu.VMEM((count, 2 * TOK, width), BF16),
            pltpu.SemaphoreType.DMA((2 * count + 3,)),
            pltpu.SemaphoreType.DMA((total,)),
        ],
        name=name,
        vmem=BIG,
        hint=hint,
    )


def flip(*terms):
    return sum(t.astype(F32) for t in terms).T


def stepped(w, gradient):
    return (w.astype(F32) * (1.0 - inner_rate * decay_rate) - inner_rate * gradient).astype(BF16)


WORKERS = (16, 2, 32, KV)


def inner_sync(plan, w, near, across):
    def kernel(plan_ref, w_ref, near_ref, za_ref, zb_ref, inner_ref, send_ref, wv, sem, sem2):
        s = lax.rem(plan_ref[0], 2)
        core = place()[2]
        load = pltpu.make_async_copy(w_ref.at[s], wv, sem)
        load.start()
        load.wait()
        for h, z_ref in enumerate((za_ref, zb_ref)):
            for q in range(4):
                cols = pl.ds(q * 128, 128)
                i = h * 8 + q * 2
                gradient = flip(near_ref[h, :, cols], z_ref[:, cols])
                inner_ref[i : i + 2] = stepped(wv[i : i + 2].reshape(128, KV), gradient).reshape(2, 2, 32, KV)
        out = pltpu.make_async_copy(inner_ref.at[:, 1 - core], send_ref, sem2)
        out.start()
        out.wait()

    return call(
        kernel,
        (shape(*WORKERS), shape(16, 32, KV)),
        (plan, w, near, *across),
        [SM, HBM] + [VM] * 3,
        [VM, ANY],
        [pltpu.VMEM(WORKERS, BF16), pltpu.SemaphoreType.DMA, pltpu.SemaphoreType.DMA],
        name="inner_sync",
    )


def inner_other(plan, w, first, second):
    def kernel(plan_ref, w_ref, *rest):
        k0, r0, l0, k1, r1, l1, inner_ref, send_ref, new_ref, wv, sem, sem2 = rest
        other = 1 - lax.rem(plan_ref[0], 2)
        core = place()[2]
        load = pltpu.make_async_copy(w_ref.at[other], wv, sem)
        load.start()
        load.wait()
        for q in range(8):
            cols = pl.ds(q * 128, 128)
            i = q * 2
            gradient = jnp.concatenate(
                [flip(k[:, cols], r[0, :, cols], l[:, cols]) for k, r, l in ((k0, r0, l0), (k1, r1, l1))], axis=1
            )
            inner_ref[i : i + 2] = stepped(wv[i : i + 2].reshape(128, KV), gradient).reshape(2, 2, 32, KV)
        out = pltpu.make_async_copy(inner_ref.at[:, 1 - core], send_ref, sem2.at[0])
        keep = pltpu.make_async_copy(inner_ref, new_ref.at[other], sem2.at[1])
        out.start()
        keep.start()
        out.wait()
        keep.wait()

    return call(
        kernel,
        (shape(*WORKERS), shape(16, 32, KV), shape(2, *WORKERS)),
        (plan, w, *first, *second),
        [SM, HBM] + [VM] * 6,
        [VM, ANY, ANY],
        [pltpu.VMEM(WORKERS, BF16), pltpu.SemaphoreType.DMA, pltpu.SemaphoreType.DMA((2,))],
        name="inner_other",
    )


def plus(a, b):
    return (a.astype(F32) + b.astype(F32)).astype(BF16)


def to_x(inner_ref, recv_ref, send_ref, keep_ref):
    x, _, core, _, _ = place()
    for ref, at, j in ((send_ref, 0, 1), (send_ref, 1, 2), (keep_ref, 0, 0), (keep_ref, 1, 3)):
        block = pl.ds((x ^ j) * 4, 4)
        ref[at] = plus(inner_ref[block, core], recv_ref[block])


def to_z(keep_ref, recv_ref, send_ref, stay_ref):
    zh = place()[1]
    for ref, at, j in ((send_ref, 0, 1), (send_ref, 1, 2), (stay_ref, 0, 0), (stay_ref, 1, 3)):
        ref[at] = plus(keep_ref[zh ^ j], recv_ref[zh ^ j])


QUAD = (4, 32, KV)


def sums(name, outs, pairs, extra=()):
    def kernel(*refs):
        out_refs = refs[2 * len(pairs) + len(extra) :]
        for i, (_, _, at_a, at_b, out, slot) in enumerate(pairs):
            a, b = refs[2 * i], refs[2 * i + 1]
            total = plus(a[...] if at_a is None else a[at_a], b[...] if at_b is None else b[at_b])
            if slot is None:
                out_refs[out][...] = total
            else:
                out_refs[out][slot] = total

    args = [t for p in pairs for t in p[:2]]
    return call(
        kernel,
        [shape(*d) for d in outs],
        (*args, *extra),
        [VM] * len(args) + [ANY] * len(extra),
        [VM] * len(outs),
        name=name,
    )


def halve(name, dims, keep, recv):
    return sums(name, [dims] * 2, [(keep, recv, 1, 1, 0, None), (keep, recv, 0, 0, 1, None)])


def join(a, b):
    def kernel(a_ref, b_ref, out_ref):
        out_ref[0] = a_ref[...]
        out_ref[1] = b_ref[...]

    return call(kernel, (shape(2, *a.shape),), (a, b), [VM] * 2, [VM], name="join")


def sum_x(inner, recv, name):
    return call(to_x, (shape(2, *QUAD),) * 2, (inner, recv), [VM] * 2, [VM] * 2, name=name)


def sum_z(keep, recv, name):
    return call(to_z, (shape(2, 32, KV),) * 2, (keep, recv), [VM] * 2, [VM] * 2, name=name)


def row_of(own, got):
    def kernel(own_ref, got_ref, out_ref):
        zh = place()[1]
        for ref, at, j in ((own_ref, 0, 0), (own_ref, 1, 1), (got_ref, 0, 3), (got_ref, 1, 2)):
            out_ref[zh ^ j] = ref[at]

    return call(kernel, (shape(*QUAD),), (own, got), [VM] * 2, [VM], name="row")


def block_of(own, got):
    def kernel(own_ref, got_ref, out_ref):
        x = place()[0]
        for ref, at, j in ((own_ref, 0, 0), (own_ref, 1, 3), (got_ref, 0, 1), (got_ref, 1, 2)):
            out_ref[pl.ds((x ^ j) * 4, 4)] = ref[at]

    return call(kernel, (shape(16, 32, KV),), (own, got), [VM] * 2, [VM], name="block")


def outer_sync(plan, anchors, momentum, keep, recv):
    def kernel(plan_ref, anchor_ref, momentum_ref, a, b, new_ref, moment_ref, short_ref):
        s = lax.rem(plan_ref[0], 2)
        mean = (a[...].astype(F32) + b[...].astype(F32)) / 32
        anchor = anchor_ref[s]
        outer_grad = anchor - mean
        moment = outer_beta * momentum_ref[...] + outer_grad
        new = anchor - outer_rate * (outer_grad + outer_beta * moment)
        new_ref[...] = new
        moment_ref[...] = moment
        short_ref[...] = new.astype(BF16)

    return call(
        kernel,
        (shape(32, KV, dtype=F32), shape(32, KV, dtype=F32), shape(32, KV)),
        (plan, anchors, momentum, keep, recv),
        [SM] + [VM] * 4,
        [VM] * 3,
        name="outer_sync",
    )


def outer_other(plan, anchors, keep, recv):
    def kernel(plan_ref, anchor_ref, a, b, out_ref):
        other = 1 - lax.rem(plan_ref[0], 2)
        out_ref[...] = anchor_ref[other] - (a[...].astype(F32) + b[...].astype(F32)) / 32

    return call(
        kernel,
        (shape(32, KV, dtype=F32),),
        (plan, anchors, keep, recv),
        [SM] + [VM] * 3,
        [VM],
        name="outer_other",
    )


def mix(plan, inner, own, recv, new):
    def kernel(plan_ref, inner_ref, own_ref, recv_ref, _, out_ref, stage, sems):
        s = lax.rem(plan_ref[0], 2)
        core = place()[2]
        for t, c in ((own_ref, core), (recv_ref, 1 - core)):
            stage[:, c] = (
                mix_weight * inner_ref[:, c].astype(F32) + (1.0 - mix_weight) * t[...].astype(F32)
            ).astype(BF16)
        out = pltpu.make_async_copy(stage, out_ref.at[s], sems)
        out.start()
        out.wait()

    return call(
        kernel,
        (shape(2, *WORKERS),),
        (plan, inner, own, recv, new),
        [SM, VM, VM, VM, ANY],
        [ANY],
        [pltpu.VMEM(WORKERS, BF16), pltpu.SemaphoreType.DMA],
        aliases={4: 0},
        name="mix",
    )


def along_fsdp(move):
    return [(z * 4 + y, move(z, y)) for z in range(2) for y in range(4)]


def along_worker(move):
    def index(x, z, c):
        return (x * 4 + z) * 2 + c

    return [(index(x, z, c), index(*move(x, z, c))) for x in range(4) for z in range(4) for c in range(2)]


MOVES = {
    "a": ("fsdp", along_fsdp(lambda z, y: z * 4 + (y ^ 1))),
    "b": ("fsdp", along_fsdp(lambda z, y: z * 4 + (y ^ 3))),
    "z": ("fsdp", along_fsdp(lambda z, y: (1 - z) * 4 + y)),
    "core": ("worker", along_worker(lambda x, z, c: (x, z, 1 - c))),
    "x1": ("worker", along_worker(lambda x, z, c: (x ^ 1, z, c))),
    "x3": ("worker", along_worker(lambda x, z, c: (x ^ 3, z, c))),
    "z1": ("worker", along_worker(lambda x, z, c: (x, z ^ 1, c))),
    "z3": ("worker", along_worker(lambda x, z, c: (x, z ^ 3, c))),
}


def swap(value, move):
    return lax.ppermute(value, *MOVES[move])


def body(token_ids, layer_inputs, key_grads, weights, anchors, momentum, plan):
    CHAIN.token = None
    x = layer_inputs
    w = weights.reshape(2, *WORKERS)
    a1, b1, z1, a2, b2, z2, z3, gt = pack(plan, token_ids.reshape(1, TOK), x, key_grads)
    got_a1 = swap(a1, "a")
    got_b1 = swap(b1, "b")
    got_z1 = swap(z1, "z")
    got_a2 = swap(a2, "a")
    got_b2 = swap(b2, "b")
    got_z2 = swap(z2, "z")
    got_z3 = swap(z3, "z")

    def tile(name, far, flip_y, offset, at, recvs):
        piece = (
            lambda z, y: ((1 - z if far else z) * 4 + (y ^ flip_y)) * ROWS + offset,
            len(recvs) - 1,
            at * HALF,
            [(0, None, 0, KV)],
        )
        return product(name, 0, [piece], HALF, [(KV, HALF)], 2 * HALF, plan, x, gt, recvs)

    def dest(j, source, at, targets):
        return (lambda z, y: (z * 4 + (y ^ j)) * ROWS, source, at, targets)

    def other(name, pieces, outs, recvs, hint=0):
        return product(name, 1, pieces, ROWS, outs, 2 * ROWS, plan, x, gt, recvs, hint)

    lo, hi = (0, 256), (256, 512)
    half, pair = (256, ROWS), (2, 256, ROWS)

    far_a = swap(tile("send_a1", True, 3, 0, 1, (got_a1,)), "b")
    far_b = swap(tile("send_b1", True, 1, HALF, 1, (got_b1,)), "a")
    keep_a1 = tile("keep_a1", True, 0, 0, 0, (got_a1,))
    keep_b1 = tile("keep_b1", True, 0, HALF, 0, (got_b1,))
    near_a = swap(tile("send_a2", False, 3, 0, 1, (got_a1, got_a2)), "b")
    near_b = swap(tile("send_b2", False, 1, HALF, 1, (got_b1, got_b2)), "a")
    keep_a2 = tile("keep_a2", False, 0, 0, 0, (got_a1, got_a2))
    keep_b2 = tile("keep_b2", False, 0, HALF, 0, (got_b1, got_b2))
    send_0, stay_1 = other(
        "other_1",
        [dest(2, 0, ROWS, [(0, 1, *lo)]), dest(1, 0, 0, [(0, 0, *lo), (1, None, *hi)])],
        [pair, half],
        (got_z1,),
    )
    got_0 = swap(send_0, "a")
    across = sums(
        "far", [(KV, HALF)] * 2, [(keep_a1, far_a, None, None, 0, None), (keep_b1, far_b, None, None, 1, None)]
    )
    across = [swap(t, "z") for t in across]
    near = sums("near", [(2, KV, HALF)], [(keep_a2, near_a, None, None, 0, 0), (keep_b2, near_b, None, None, 0, 1)])
    send_1, stay_0 = other(
        "other_2",
        [dest(2, 0, ROWS, [(0, 1, *hi)]), dest(3, 1, 0, [(0, 0, *hi), (1, None, *lo)])],
        [pair, half],
        (got_z1, got_z2),
        10**10,
    )
    got_1 = swap(send_1, "b")

    inner_s, send_s = inner_sync(plan, w, near, across)
    send, keep = sum_x(inner_s, swap(send_s, "core"), "sync_x1")
    recv = swap(send, "x1")
    send, keep = halve("sync_x3", QUAD, keep, recv)
    last_0, last_1 = sums(
        "last", [half, half], [(stay_0, got_0, None, 1, 0, None), (stay_1, got_1, None, 1, 1, None)]
    )
    last_0, last_1 = swap(last_0, "b"), swap(last_1, "a")
    send, keep = sum_z(keep, swap(send, "x3"), "sync_z1")
    recv = swap(send, "z1")
    mine_0, mine_1 = other("other_3", [dest(0, 1, 0, [(0, None, *lo), (1, None, *hi)])], [half, half], (got_z1, got_z3))
    send, keep = halve("sync_z3", (32, KV), keep, recv)
    anchor_new, momentum_new, short = outer_sync(plan, anchors, momentum, keep, swap(send, "z3"))
    short_far = swap(short, "z1")

    inner_o, send_o, new = inner_other(plan, w, (mine_0, got_0, last_0), (mine_1, got_1, last_1))
    core_o = swap(send_o, "core")
    own = join(short, short_far)
    send, keep = sum_x(inner_o, core_o, "other_x1")
    recv = swap(send, "x1")
    row = row_of(own, swap(own, "z3"))
    row_far = swap(row, "x3")
    send, keep = halve("other_x3", QUAD, keep, recv)
    recv = swap(send, "x3")
    own = join(row, row_far)
    got = swap(own, "x1")
    send, keep = sum_z(keep, recv, "other_z1")
    recv = swap(send, "z1")
    block = block_of(own, got)
    block_far = swap(block, "core")
    send, keep = halve("other_z3", (32, KV), keep, recv)
    recv = swap(send, "z3")
    new = mix(plan, inner_s, block, block_far, new)
    pending = outer_other(plan, anchors, keep, recv)
    return (new.reshape(1, 2, ROWS, KV), anchor_new, momentum_new, pending)


def solution(mesh):
    return jax.shard_map(
        body,
        mesh=mesh,
        in_specs=(
            P(("worker", "fsdp")),
            P(None, ("worker", "fsdp"), None),
            P(None, ("worker", "fsdp"), None),
            P("worker", None, "fsdp", None),
            P(None, ("fsdp", "worker"), None),
            P(("fsdp", "worker"), None),
            P(),
        ),
        out_specs=(
            P("worker", None, "fsdp", None),
            P(("fsdp", "worker"), None),
            P(("fsdp", "worker"), None),
            P(("fsdp", "worker"), None),
        ),
        check_vma=False,
    )
```

time: 165 us -> 154 us (0.933)
  waiting for transfers between devices: 82.6 us -> 71.9 us
  Pallas kernels: 16.8 us -> 21.4 us
  local copies, waits for them, and re-layouts: 5.11 us -> 0.68 us
  other arithmetic: 2.57 us -> 0 us
  starting transfers between devices: 55.2 us -> 57.3 us
    ppermute x32, waiting for transfers between devices: 82.6 us -> 71.9 us  [swap(): return lax.ppermute(value, *MOVES[move])]
    pallas_call x18 -> x32, Pallas kernels: 16.8 us -> 21.4 us  [call(): pl.pallas_call(chained, out_shape=outs + [in_hbm(8, 128)], in_specs=list(...]
    unnamed x14 -> x8, local copies, waits for them, and re-layouts: 5.11 us -> 0.68 us
    convert_element_type x4 -> x0, other arithmetic: 2.57 us -> none  [add(): return (a.astype(F32) + b.astype(F32)).astype(BF16)]
    ppermute x32, starting transfers between devices: 55.2 us -> 57.3 us  [swap(): return lax.ppermute(value, *MOVES[move])]
  transfers between devices with their start and end apart: 32 -> 32, of which waited for: 18 -> 19; matrix products, arithmetic and copies ran while one was open for 2% -> 0% of each run, Pallas kernels for 9% -> 10%
where the time goes in v2:
time: 154 us; the launch traced here: 153 us
  waiting for transfers between devices  71.9 us (47%)
  starting transfers between devices  57.3 us (37%)
  Pallas kernels  21.4 us (14%)
  between operations  1.55 us (1%)
    ppermute x32, waiting for transfers between devices, swap(): return lax.ppermute(value, *MOVES[move])  71.9 us
    ppermute x32, starting transfers between devices, swap(): return lax.ppermute(value, *MOVES[move])  57.3 us
    pallas_call x32, Pallas kernels, call(): pl.pallas_call(chained, out_shape=outs + [in_hbm(8, 128)], in_specs=list(...  21.4 us
  transfers between devices with their start and end apart: 32, of which 19 were waited for; matrix products, arithmetic and copies ran while one was open for 0% of the time, Pallas kernels for 10%

profile of v2, /device:TPU:8, one launch (start us, length us, event | category | flops | bytes accessed | tf_op | source)
XLA Modules:
  0.0 152.8 jit_solution(1141922679150187198)
XLA Ops:
  1.3 0.7 copy-done.3
  2.0 2.7 %pack.1 = (bf16[256,1536]{1,0:T(8,128)(2,1)S(1)}, bf16[256,1536]{1,0:T(8,128)(2,1)S(1)}, bf16[256,2560]{1,0:T(8,128)(2,1)S(1)}, bf16[256,1024]{1,0:T(8,128)(2,1)...) custom-call(s32[1]{0:T(128)S(6)} %copy.13.refs_0_, ...), custom_call_target="tpu_custom_call" | custom-call | tf_op jit(solution)/shard_map/pack/pallas_call | solution.py:68
  4.7 2.0 %collective-permute-start.8 = (bf16[256,2560]{1,0:T(8,128)(2,1)S(1)}, bf16[256,2560]{1,0:T(8,128)(2,1)S(1)}, u32[]{:S(2)}, u32[]{:S(2)}) collective-permute-start(bf16[256,2560]{1,0:T(8,128)(2,1)S(1)} %get-tuple-element.113), channel_id=1, source_target_pairs={{0,4},{1,5},{2,6},{3,7},{4,0},{5,1},{6,2},{7,3},{8,12},{9,13},{10,... | collective-permute-start | bytes 3932168 | tf_op jit(solution)/shard_map/ppermute | solution.py:459
  7.1 2.4 %collective-permute-start.2 = (bf16[256,1536]{1,0:T(8,128)(2,1)S(1)}, bf16[256,1536]{1,0:T(8,128)(2,1)S(1)}, u32[]{:S(2)}, u32[]{:S(2)}) collective-permute-start(bf16[256,1536]{1,0:T(8,128)(2,1)S(1)} %get-tuple-element.95), channel_id=1, source_target_pairs={{0,3},{1,2},{2,1},{3,0},{4,7},{5,6},{6,5},{7,4},{8,11},{9,10},{10,... | collective-permute-start | bytes 2359304 | tf_op jit(solution)/shard_map/ppermute | solution.py:459
  9.5 1.3 collective-permute-start.1
  11.3 15.8 %collective-permute-done.refs_3_ = bf16[256,1536]{1,0:T(8,128)(2,1)S(1)} collective-permute-done((bf16[256,1536]{1,0:T(8,128)(2,1)S(1)}, bf16[256,1536]{1,0:T(8,128)(2,1)S(1)}, u32[]{:S(2)}, u32[]{:S(2)}) %collective-permute-start) | collective-permute-done | bytes 786464 | tf_op jit(solution)/shard_map/ppermute | solution.py:459
  27.8 1.7 %collective-permute-start.6 = (bf16[512,512]{1,0:T(8,128)(2,1)S(1)}, bf16[512,512]{1,0:T(8,128)(2,1)S(1)}, u32[]{:S(2)}, u32[]{:S(2)}) collective-permute-start(bf16[512,512]{1,0:T(8,128)(2,1)S(1)} %get-tuple-element.110), channel_id=1, source_target_pairs={{0,3},{1,2},{2,1},{3,0},{4,7},{5,6},{6,5},{7,4},{8,11},{9,10},{10,... | collective-permute-start | bytes 1572872 | tf_op jit(solution)/shard_map/ppermute | solution.py:459
  30.1 2.0 %collective-permute-start.7 = (bf16[512,512]{1,0:T(8,128)(2,1)S(1)}, bf16[512,512]{1,0:T(8,128)(2,1)S(1)}, u32[]{:S(2)}, u32[]{:S(2)}) collective-permute-start(bf16[512,512]{1,0:T(8,128)(2,1)S(1)} %get-tuple-element.112), channel_id=1, source_target_pairs={{0,1},{1,0},{2,3},{3,2},{4,5},{5,4},{6,7},{7,6},{8,9},{9,8},{10,11... | collective-permute-start | bytes 1572872 | tf_op jit(solution)/shard_map/ppermute | solution.py:459
  33.3 5.1 %collective-permute-done.1.refs_4_ = bf16[256,1024]{1,0:T(8,128)(2,1)S(1)} collective-permute-done((bf16[256,1024]{1,0:T(8,128)(2,1)S(1)}, bf16[256,1024]{1,0:T(8,128)(2,1)S(1)}, u32[]{:S(2)}, u32[]{:S(2)}) %collective-permute-start.1) | collective-permute-done | bytes 524320 | tf_op jit(solution)/shard_map/ppermute | solution.py:459
  39.8 2.5 %collective-permute-start.5 = (bf16[512,512]{1,0:T(8,128)(2,1)S(1)}, bf16[512,512]{1,0:T(8,128)(2,1)S(1)}, u32[]{:S(2)}, u32[]{:S(2)}) collective-permute-start(bf16[512,512]{1,0:T(8,128)(2,1)S(1)} %get-tuple-element.108), channel_id=1, source_target_pairs={{0,1},{1,0},{2,3},{3,2},{4,5},{5,4},{6,7},{7,6},{8,9},{9,8},{10,11... | collective-permute-start | bytes 1572872 | tf_op jit(solution)/shard_map/ppermute | solution.py:459
  42.4 1.6 %collective-permute-start.4 = (bf16[512,512]{1,0:T(8,128)(2,1)S(1)}, bf16[512,512]{1,0:T(8,128)(2,1)S(1)}, u32[]{:S(2)}, u32[]{:S(2)}) collective-permute-start(bf16[512,512]{1,0:T(8,128)(2,1)S(1)} %get-tuple-element.105), channel_id=1, source_target_pairs={{0,3},{1,2},{2,1},{3,0},{4,7},{5,6},{6,5},{7,4},{8,11},{9,10},{10,... | collective-permute-start | bytes 1572872 | tf_op jit(solution)/shard_map/ppermute | solution.py:459
  45.3 1.8 %other_1.1 = (bf16[2,256,1024]{2,1,0:T(8,128)(2,1)S(1)}, bf16[256,1024]{1,0:T(8,128)(2,1)S(1)}, bf16[8,128]{1,0:T(8,128)(2,1)}) custom-call(s32[1]{0:T(128)S(6)} %copy.13.refs_0_, bf16[2,256,8192]{2,1,0:T(8,128)(2,1)S(1)} %copy-done, bf16[2,512,256]{2,1,0:T(8,128)(2,1)S(1)} %get-tuple-element.92.refs_2_, ...), custom_call_target="tpu_custom_call" | custom-call | tf_op jit(solution)/shard_map/other_1/pallas_call | solution.py:68
  47.1 3.4 %collective-permute-done.6.refs_1_ = bf16[512,512]{1,0:T(8,128)(2,1)S(1)} collective-permute-done((bf16[512,512]{1,0:T(8,128)(2,1)S(1)}, bf16[512,512]{1,0:T(8,128)(2,1)S(1)}, u32[]{:S(2)}, u32[]{:S(2)}) %collective-permute-start.6) | collective-permute-done | bytes 524320 | tf_op jit(solution)/shard_map/ppermute | solution.py:459
  50.7 1.6 %collective-permute-start.9 = (bf16[512,512]{1,0:T(8,128)(2,1)S(1)}, bf16[512,512]{1,0:T(8,128)(2,1)S(1)}, u32[]{:S(2)}, u32[]{:S(2)}) collective-permute-start(bf16[512,512]{1,0:T(8,128)(2,1)S(1)} %get-tuple-element.118), channel_id=1, source_target_pairs={{0,4},{1,5},{2,6},{3,7},{4,0},{5,1},{6,2},{7,3},{8,12},{9,13},{10,... | collective-permute-start | bytes 1572872 | tf_op jit(solution)/shard_map/ppermute | solution.py:459
  52.8 6.6 %collective-permute-done.5.refs_3_ = bf16[512,512]{1,0:T(8,128)(2,1)S(1)} collective-permute-done((bf16[512,512]{1,0:T(8,128)(2,1)S(1)}, bf16[512,512]{1,0:T(8,128)(2,1)S(1)}, u32[]{:S(2)}, u32[]{:S(2)}) %collective-permute-start.5) | collective-permute-done | bytes 524320 | tf_op jit(solution)/shard_map/ppermute | solution.py:459
  59.4 0.8 collective-permute-done.4.refs_1_
  60.5 1.8 %other_2.1 = (bf16[2,256,1024]{2,1,0:T(8,128)(2,1)S(1)}, bf16[256,1024]{1,0:T(8,128)(2,1)S(1)}, bf16[8,128]{1,0:T(8,128)(2,1)}) custom-call(s32[1]{0:T(128)S(6)} %copy.13.refs_0_, bf16[2,256,8192]{2,1,0:T(8,128)(2,1)S(1)} %copy-done, bf16[2,512,256]{2,1,0:T(8,128)(2,1)S(1)} %get-tuple-element.92.refs_2_, ...), custom_call_target="tpu_custom_call" | custom-call | flops 10000000000 | tf_op jit(solution)/shard_map/other_2/pallas_call | solution.py:68
  62.3 1.8 %collective-permute-start.16 = (bf16[2,256,1024]{2,1,0:T(8,128)(2,1)S(1)}, bf16[2,256,1024]{2,1,0:T(8,128)(2,1)S(1)}, u32[]{:S(2)}, u32[]{:S(2)}) collective-permute-start(bf16[2,256,1024]{2,1,0:T(8,128)(2,1)S(1)} %get-tuple-element.134), channel_id=1, source_target_pairs={{0,3},{1,2},{2,1},{3,0},{4,7},{5,6},{6,5},{7,4},{8,11},{9,10},{10,... | collective-permute-start | bytes 3145736 | tf_op jit(solution)/shard_map/ppermute | solution.py:459
  64.1 2.6 %collective-permute-start.15 = (bf16[2,256,1024]{2,1,0:T(8,128)(2,1)S(1)}, bf16[2,256,1024]{2,1,0:T(8,128)(2,1)S(1)}, u32[]{:S(2)}, u32[]{:S(2)}) collective-permute-start(bf16[2,256,1024]{2,1,0:T(8,128)(2,1)S(1)} %get-tuple-element.132), channel_id=1, source_target_pairs={{0,1},{1,0},{2,3},{3,2},{4,5},{5,4},{6,7},{7,6},{8,9},{9,8},{10,11... | collective-permute-start | bytes 3145736 | tf_op jit(solution)/shard_map/ppermute | solution.py:459
  66.6 1.5 collective-permute-done.9.refs_3_
  68.2 8.1 %collective-permute-done.10.refs_4_ = bf16[512,512]{1,0:T(8,128)(2,1)S(1)} collective-permute-done((bf16[512,512]{1,0:T(8,128)(2,1)S(1)}, bf16[512,512]{1,0:T(8,128)(2,1)S(1)}, u32[]{:S(2)}, u32[]{:S(2)}) %collective-permute-start.10) | collective-permute-done | bytes 524320 | tf_op jit(solution)/shard_map/ppermute | solution.py:459
  76.3 1.9 %inner_sync.1 = (bf16[16,2,32,512]{3,2,1,0:T(8,128)(2,1)S(1)}, bf16[16,32,512]{2,1,0:T(8,128)(2,1)S(1)}, bf16[8,128]{1,0:T(8,128)(2,1)}) custom-call(s32[1]{0:T(128)S(6)} %copy.13.refs_0_, bf16[2,16,2,32,512]{4,3,2,1,0:T(8,128)(2,1)} %bitcast.4, bf16[2,512,512]{2,1,0:T(8,128)(2,1)S(1)} %get-tuple-element.117.refs_2_, ...), custom_call_target="tpu_custom_call" | custom-call | tf_op jit(solution)/shard_map/inner_sync/pallas_call | solution.py:68
  78.3 1.9 %collective-permute-done.12.refs_1_ = bf16[16,32,512]{2,1,0:T(8,128)(2,1)S(1)} collective-permute-done((bf16[16,32,512]{2,1,0:T(8,128)(2,1)S(1)}, bf16[16,32,512]{2,1,0:T(8,128)(2,1)S(1)}, u32[]{:S(2)}, u32[]{:S(2)}) %collective-permute-start.12) | collective-permute-done | bytes 524320 | tf_op jit(solution)/shard_map/ppermute | solution.py:459
  80.3 1.6 %collective-permute-start.13 = (bf16[2,4,32,512]{3,2,1,0:T(8,128)(2,1)S(1)}, bf16[2,4,32,512]{3,2,1,0:T(8,128)(2,1)S(1)}, u32[]{:S(2)}, u32[]{:S(2)}) collective-permute-start(bf16[2,4,32,512]{3,2,1,0:T(8,128)(2,1)S(1)} %get-tuple-element.127), channel_id=1, source_target_pairs={{0,64},{8,72},{16,80},{24,88},{32,96},{40,104},{48,112},{56,120},{... | collective-permute-start | bytes 786440 | tf_op jit(solution)/shard_map/ppermute | solution.py:459
  82.5 6.2 %collective-permute-done.13.refs_1_.refs_3_ = bf16[2,4,32,512]{3,2,1,0:T(8,128)(2,1)S(1)} collective-permute-done((bf16[2,4,32,512]{3,2,1,0:T(8,128)(2,1)S(1)}, bf16[2,4,32,512]{3,2,1,0:T(8,128)(2,1)S(1)}, u32[]{:S(2)}, u32[]{:S(2)}) %collective-permute-start.13) | collective-permute-done | bytes 262176 | tf_op jit(solution)/shard_map/ppermute | solution.py:459
  89.6 2.0 %collective-permute-start.22 = (bf16[256,1024]{1,0:T(8,128)(2,1)S(1)}, bf16[256,1024]{1,0:T(8,128)(2,1)S(1)}, u32[]{:S(2)}, u32[]{:S(2)}) collective-permute-start(bf16[256,1024]{1,0:T(8,128)(2,1)S(1)} %get-tuple-element.149), channel_id=1, source_target_pairs={{0,1},{1,0},{2,3},{3,2},{4,5},{5,4},{6,7},{7,6},{8,9},{9,8},{10,11... | collective-permute-start | bytes 1572872 | tf_op jit(solution)/shard_map/ppermute | solution.py:459
  91.6 2.8 %collective-permute-start.14 = (bf16[4,32,512]{2,1,0:T(8,128)(2,1)S(1)}, bf16[4,32,512]{2,1,0:T(8,128)(2,1)S(1)}, u32[]{:S(2)}, u32[]{:S(2)}) collective-permute-start(bf16[4,32,512]{2,1,0:T(8,128)(2,1)S(1)} %get-tuple-element.130), channel_id=1, source_target_pairs={{0,192},{8,200},{16,208},{24,216},{32,224},{40,232},{48,240},{56,2... | collective-permute-start | bytes 393224 | tf_op jit(solution)/shard_map/ppermute | solution.py:459
  94.4 3.4 %collective-permute-done.14.refs_1_ = bf16[4,32,512]{2,1,0:T(8,128)(2,1)S(1)} collective-permute-done((bf16[4,32,512]{2,1,0:T(8,128)(2,1)S(1)}, bf16[4,32,512]{2,1,0:T(8,128)(2,1)S(1)}, u32[]{:S(2)}, u32[]{:S(2)}) %collective-permute-start.14) | collective-permute-done | bytes 131104 | tf_op jit(solution)/shard_map/ppermute | solution.py:459
  97.8 3.4 %collective-permute-start.17 = (bf16[2,32,512]{2,1,0:T(8,128)(2,1)S(1)}, bf16[2,32,512]{2,1,0:T(8,128)(2,1)S(1)}, u32[]{:S(2)}, u32[]{:S(2)}) collective-permute-start(bf16[2,32,512]{2,1,0:T(8,128)(2,1)S(1)} %get-tuple-element.138), channel_id=1, source_target_pairs={{0,16},{8,24},{16,0},{24,8},{32,48},{40,56},{48,32},{56,40},{64,80... | collective-permute-start | bytes 196616 | tf_op jit(solution)/shard_map/ppermute | solution.py:459
  101.2 1.1 other_3.1
  102.4 1.8 %collective-permute-done.17.refs_1_.refs_3_ = bf16[2,32,512]{2,1,0:T(8,128)(2,1)S(1)} collective-permute-done((bf16[2,32,512]{2,1,0:T(8,128)(2,1)S(1)}, bf16[2,32,512]{2,1,0:T(8,128)(2,1)S(1)}, u32[]{:S(2)}, u32[]{:S(2)}) %collective-permute-start.17) | collective-permute-done | bytes 65568 | tf_op jit(solution)/shard_map/ppermute | solution.py:459
  104.2 4.5 %collective-permute-start.19 = (bf16[32,512]{1,0:T(8,128)(2,1)S(1)}, bf16[32,512]{1,0:T(8,128)(2,1)S(1)}, u32[]{:S(2)}, u32[]{:S(2)}) collective-permute-start(bf16[32,512]{1,0:T(8,128)(2,1)S(1)} %get-tuple-element.143), channel_id=1, source_target_pairs={{0,48},{8,56},{16,32},{24,40},{32,16},{40,24},{48,0},{56,8},{64,11... | collective-permute-start | bytes 98312 | tf_op jit(solution)/shard_map/ppermute | solution.py:459
  108.7 1.9 %collective-permute-done.19.refs_4_ = bf16[32,512]{1,0:T(8,128)(2,1)S(1)} collective-permute-done((bf16[32,512]{1,0:T(8,128)(2,1)S(1)}, bf16[32,512]{1,0:T(8,128)(2,1)S(1)}, u32[]{:S(2)}, u32[]{:S(2)}) %collective-permute-start.19) | collective-permute-done | bytes 32800 | tf_op jit(solution)/shard_map/ppermute | solution.py:459
  110.6 0.7 outer_sync.1
  111.3 3.1 %inner_other.1 = (bf16[16,2,32,512]{3,2,1,0:T(8,128)(2,1)S(1)}, bf16[16,32,512]{2,1,0:T(8,128)(2,1)S(1)}, bf16[2,16,2,32,512]{4,3,2,1,0:T(8,128)(2,1)}, bf16[8,128]{1,0:T(8,128)(2,1)}) custom-call(s32[1]{0:T(128)S(6)} %copy.13.refs_0_, bf16[2,16,2,32,512]{4,3,2,1,0:T(8,128)(2,1)} %bitcast.5, bf16[256,1024]{1,0:T(8,128)(2,1)S(1)} %get-tuple-element.146.refs_2_, ...), custom_call_target="tpu_custom_call" | custom-call | tf_op jit(solution)/shard_map/inner_other/pallas_call | solution.py:68
  114.6 2.4 %collective-permute-start.20 = (bf16[32,512]{1,0:T(8,128)(2,1)S(1)}, bf16[32,512]{1,0:T(8,128)(2,1)S(1)}, u32[]{:S(2)}, u32[]{:S(2)}) collective-permute-start(bf16[32,512]{1,0:T(8,128)(2,1)S(1)} %get-tuple-element.145.refs_0_), channel_id=1, source_target_pairs={{0,16},{8,24},{16,0},{24,8},{32,48},{40,56},{48,32},{56,40},{64,80... | collective-permute-start | bytes 98312 | tf_op jit(solution)/shard_map/ppermute | solution.py:459
  117.0 2.5 %collective-permute-done.20.refs_1_ = bf16[32,512]{1,0:T(8,128)(2,1)S(1)} collective-permute-done((bf16[32,512]{1,0:T(8,128)(2,1)S(1)}, bf16[32,512]{1,0:T(8,128)(2,1)S(1)}, u32[]{:S(2)}, u32[]{:S(2)}) %collective-permute-start.20) | collective-permute-done | bytes 32800 | tf_op jit(solution)/shard_map/ppermute | solution.py:459
  120.0 4.1 %collective-permute-start.23 = (bf16[2,32,512]{2,1,0:T(8,128)(2,1)S(1)}, bf16[2,32,512]{2,1,0:T(8,128)(2,1)S(1)}, u32[]{:S(2)}, u32[]{:S(2)}) collective-permute-start(bf16[2,32,512]{2,1,0:T(8,128)(2,1)S(1)} %get-tuple-element.152.refs_0_), channel_id=1, source_target_pairs={{0,48},{8,56},{16,32},{24,40},{32,16},{40,24},{48,0},{56,8},{64,11... | collective-permute-start | bytes 196616 | tf_op jit(solution)/shard_map/ppermute | solution.py:459
  124.2 2.5 %collective-permute-done.23.refs_1_ = bf16[2,32,512]{2,1,0:T(8,128)(2,1)S(1)} collective-permute-done((bf16[2,32,512]{2,1,0:T(8,128)(2,1)S(1)}, bf16[2,32,512]{2,1,0:T(8,128)(2,1)S(1)}, u32[]{:S(2)}, u32[]{:S(2)}) %collective-permute-start.23) | collective-permute-done | bytes 65568 | tf_op jit(solution)/shard_map/ppermute | solution.py:459
  126.7 2.8 %collective-permute-start.25 = (bf16[4,32,512]{2,1,0:T(8,128)(2,1)S(1)}, bf16[4,32,512]{2,1,0:T(8,128)(2,1)S(1)}, u32[]{:S(2)}, u32[]{:S(2)}) collective-permute-start(bf16[4,32,512]{2,1,0:T(8,128)(2,1)S(1)} %get-tuple-element.157.refs_0_), channel_id=1, source_target_pairs={{0,192},{8,200},{16,208},{24,216},{32,224},{40,232},{48,240},{56,2... | collective-permute-start | bytes 393224 | tf_op jit(solution)/shard_map/ppermute | solution.py:459
  129.6 3.4 %collective-permute-done.25.refs_1_ = bf16[4,32,512]{2,1,0:T(8,128)(2,1)S(1)} collective-permute-done((bf16[4,32,512]{2,1,0:T(8,128)(2,1)S(1)}, bf16[4,32,512]{2,1,0:T(8,128)(2,1)S(1)}, u32[]{:S(2)}, u32[]{:S(2)}) %collective-permute-start.25) | collective-permute-done | bytes 131104 | tf_op jit(solution)/shard_map/ppermute | solution.py:459
  133.0 0.7 collective-permute-start.27
  133.7 2.6 %collective-permute-start.28 = (bf16[4,32,512]{2,1,0:T(8,128)(2,1)S(1)}, bf16[4,32,512]{2,1,0:T(8,128)(2,1)S(1)}, u32[]{:S(2)}, u32[]{:S(2)}) collective-permute-start(bf16[4,32,512]{2,1,0:T(8,128)(2,1)S(1)} %get-tuple-element.164), channel_id=1, source_target_pairs={{0,192},{8,200},{16,208},{24,216},{32,224},{40,232},{48,240},{56,2... | collective-permute-start | bytes 393224 | tf_op jit(solution)/shard_map/ppermute | solution.py:459
  136.3 3.6 %collective-permute-done.28.refs_1_ = bf16[4,32,512]{2,1,0:T(8,128)(2,1)S(1)} collective-permute-done((bf16[4,32,512]{2,1,0:T(8,128)(2,1)S(1)}, bf16[4,32,512]{2,1,0:T(8,128)(2,1)S(1)}, u32[]{:S(2)}, u32[]{:S(2)}) %collective-permute-start.28) | collective-permute-done | bytes 131104 | tf_op jit(solution)/shard_map/ppermute | solution.py:459
  140.1 3.1 %collective-permute-start.30 = (bf16[2,32,512]{2,1,0:T(8,128)(2,1)S(1)}, bf16[2,32,512]{2,1,0:T(8,128)(2,1)S(1)}, u32[]{:S(2)}, u32[]{:S(2)}) collective-permute-start(bf16[2,32,512]{2,1,0:T(8,128)(2,1)S(1)} %get-tuple-element.170), channel_id=1, source_target_pairs={{0,16},{8,24},{16,0},{24,8},{32,48},{40,56},{48,32},{56,40},{64,80... | collective-permute-start | bytes 196616 | tf_op jit(solution)/shard_map/ppermute | solution.py:459
  143.2 2.7 %collective-permute-done.30.refs_1_.refs_3_ = bf16[2,32,512]{2,1,0:T(8,128)(2,1)S(1)} collective-permute-done((bf16[2,32,512]{2,1,0:T(8,128)(2,1)S(1)}, bf16[2,32,512]{2,1,0:T(8,128)(2,1)S(1)}, u32[]{:S(2)}, u32[]{:S(2)}) %collective-permute-start.30) | collective-permute-done | bytes 65568 | tf_op jit(solution)/shard_map/ppermute | solution.py:459
  145.9 4.4 %collective-permute-start.31 = (bf16[32,512]{1,0:T(8,128)(2,1)S(1)}, bf16[32,512]{1,0:T(8,128)(2,1)S(1)}, u32[]{:S(2)}, u32[]{:S(2)}) collective-permute-start(bf16[32,512]{1,0:T(8,128)(2,1)S(1)} %get-tuple-element.177), channel_id=1, source_target_pairs={{0,48},{8,56},{16,32},{24,40},{32,16},{40,24},{48,0},{56,8},{64,11... | collective-permute-start | bytes 98312 | tf_op jit(solution)/shard_map/ppermute | solution.py:459
  150.3 1.4 mix.1
  (56 shorter events, 11.2 us)
Async XLA Ops:
  1.3 0.7 copy-start.3
  2.0 25.2 %copy-start = (bf16[2,256,8192]{2,1,0:T(8,128)(2,1)S(1)}, bf16[2,256,8192]{2,1,0:T(8,128)(2,1)}, u32[]{:S(2)}) copy-start(bf16[2,256,8192]{2,1,0:T(8,128)(2,1)} %refs_1_.23) | copy-start | bytes 25165828
  4.7 39.2 %collective-permute-start.8 = (bf16[256,2560]{1,0:T(8,128)(2,1)S(1)}, bf16[256,2560]{1,0:T(8,128)(2,1)S(1)}, u32[]{:S(2)}, u32[]{:S(2)}) collective-permute-start(bf16[256,2560]{1,0:T(8,128)(2,1)S(1)} %get-tuple-element.113), channel_id=1, source_target_pairs={{0,4},{1,5},{2,6},{3,7},{4,0},{5,1},{6,2},{7,3},{8,12},{9,13},{10,... | collective-permute-start | bytes 3932168 | tf_op jit(solution)/shard_map/ppermute | solution.py:459
  6.7 20.5 %collective-permute-start = (bf16[256,1536]{1,0:T(8,128)(2,1)S(1)}, bf16[256,1536]{1,0:T(8,128)(2,1)S(1)}, u32[]{:S(2)}, u32[]{:S(2)}) collective-permute-start(bf16[256,1536]{1,0:T(8,128)(2,1)S(1)} %get-tuple-element.93), channel_id=1, source_target_pairs={{0,1},{1,0},{2,3},{3,2},{4,5},{5,4},{6,7},{7,6},{8,9},{9,8},{10,11... | collective-permute-start | bytes 2359304 | tf_op jit(solution)/shard_map/ppermute | solution.py:459
  7.1 22.3 %collective-permute-start.2 = (bf16[256,1536]{1,0:T(8,128)(2,1)S(1)}, bf16[256,1536]{1,0:T(8,128)(2,1)S(1)}, u32[]{:S(2)}, u32[]{:S(2)}) collective-permute-start(bf16[256,1536]{1,0:T(8,128)(2,1)S(1)} %get-tuple-element.95), channel_id=1, source_target_pairs={{0,3},{1,2},{2,1},{3,0},{4,7},{5,6},{6,5},{7,4},{8,11},{9,10},{10,... | collective-permute-start | bytes 2359304 | tf_op jit(solution)/shard_map/ppermute | solution.py:459
  9.5 28.8 %collective-permute-start.1 = (bf16[256,1024]{1,0:T(8,128)(2,1)S(1)}, bf16[256,1024]{1,0:T(8,128)(2,1)S(1)}, u32[]{:S(2)}, u32[]{:S(2)}) collective-permute-start(bf16[256,1024]{1,0:T(8,128)(2,1)S(1)} %get-tuple-element.94), channel_id=1, source_target_pairs={{0,1},{1,0},{2,3},{3,2},{4,5},{5,4},{6,7},{7,6},{8,9},{9,8},{10,11... | collective-permute-start | bytes 1572872 | tf_op jit(solution)/shard_map/ppermute | solution.py:459
  10.9 28.3 %collective-permute-start.3 = (bf16[256,1024]{1,0:T(8,128)(2,1)S(1)}, bf16[256,1024]{1,0:T(8,128)(2,1)S(1)}, u32[]{:S(2)}, u32[]{:S(2)}) collective-permute-start(bf16[256,1024]{1,0:T(8,128)(2,1)S(1)} %get-tuple-element.96), channel_id=1, source_target_pairs={{0,3},{1,2},{2,1},{3,0},{4,7},{5,6},{6,5},{7,4},{8,11},{9,10},{10,... | collective-permute-start | bytes 1572872 | tf_op jit(solution)/shard_map/ppermute | solution.py:459
  27.8 22.7 %collective-permute-start.6 = (bf16[512,512]{1,0:T(8,128)(2,1)S(1)}, bf16[512,512]{1,0:T(8,128)(2,1)S(1)}, u32[]{:S(2)}, u32[]{:S(2)}) collective-permute-start(bf16[512,512]{1,0:T(8,128)(2,1)S(1)} %get-tuple-element.110), channel_id=1, source_target_pairs={{0,3},{1,2},{2,1},{3,0},{4,7},{5,6},{6,5},{7,4},{8,11},{9,10},{10,... | collective-permute-start | bytes 1572872 | tf_op jit(solution)/shard_map/ppermute | solution.py:459
  30.1 20.4 %collective-permute-start.7 = (bf16[512,512]{1,0:T(8,128)(2,1)S(1)}, bf16[512,512]{1,0:T(8,128)(2,1)S(1)}, u32[]{:S(2)}, u32[]{:S(2)}) collective-permute-start(bf16[512,512]{1,0:T(8,128)(2,1)S(1)} %get-tuple-element.112), channel_id=1, source_target_pairs={{0,1},{1,0},{2,3},{3,2},{4,5},{5,4},{6,7},{7,6},{8,9},{9,8},{10,11... | collective-permute-start | bytes 1572872 | tf_op jit(solution)/shard_map/ppermute | solution.py:459
  39.8 19.5 %collective-permute-start.5 = (bf16[512,512]{1,0:T(8,128)(2,1)S(1)}, bf16[512,512]{1,0:T(8,128)(2,1)S(1)}, u32[]{:S(2)}, u32[]{:S(2)}) collective-permute-start(bf16[512,512]{1,0:T(8,128)(2,1)S(1)} %get-tuple-element.108), channel_id=1, source_target_pairs={{0,1},{1,0},{2,3},{3,2},{4,5},{5,4},{6,7},{7,6},{8,9},{9,8},{10,11... | collective-permute-start | bytes 1572872 | tf_op jit(solution)/shard_map/ppermute | solution.py:459
  42.4 17.9 %collective-permute-start.4 = (bf16[512,512]{1,0:T(8,128)(2,1)S(1)}, bf16[512,512]{1,0:T(8,128)(2,1)S(1)}, u32[]{:S(2)}, u32[]{:S(2)}) collective-permute-start(bf16[512,512]{1,0:T(8,128)(2,1)S(1)} %get-tuple-element.105), channel_id=1, source_target_pairs={{0,3},{1,2},{2,1},{3,0},{4,7},{5,6},{6,5},{7,4},{8,11},{9,10},{10,... | collective-permute-start | bytes 1572872 | tf_op jit(solution)/shard_map/ppermute | solution.py:459
  43.9 16.5 %collective-permute-start.11 = (bf16[256,1024]{1,0:T(8,128)(2,1)S(1)}, bf16[256,1024]{1,0:T(8,128)(2,1)S(1)}, u32[]{:S(2)}, u32[]{:S(2)}) collective-permute-start(bf16[256,1024]{1,0:T(8,128)(2,1)S(1)} %get-tuple-element.120), channel_id=1, source_target_pairs={{0,4},{1,5},{2,6},{3,7},{4,0},{5,1},{6,2},{7,3},{8,12},{9,13},{10,... | collective-permute-start | bytes 1572872 | tf_op jit(solution)/shard_map/ppermute | solution.py:459
  50.7 17.4 %collective-permute-start.9 = (bf16[512,512]{1,0:T(8,128)(2,1)S(1)}, bf16[512,512]{1,0:T(8,128)(2,1)S(1)}, u32[]{:S(2)}, u32[]{:S(2)}) collective-permute-start(bf16[512,512]{1,0:T(8,128)(2,1)S(1)} %get-tuple-element.118), channel_id=1, source_target_pairs={{0,4},{1,5},{2,6},{3,7},{4,0},{5,1},{6,2},{7,3},{8,12},{9,13},{10,... | collective-permute-start | bytes 1572872 | tf_op jit(solution)/shard_map/ppermute | solution.py:459
  52.3 24.0 %collective-permute-start.10 = (bf16[512,512]{1,0:T(8,128)(2,1)S(1)}, bf16[512,512]{1,0:T(8,128)(2,1)S(1)}, u32[]{:S(2)}, u32[]{:S(2)}) collective-permute-start(bf16[512,512]{1,0:T(8,128)(2,1)S(1)} %get-tuple-element.119), channel_id=1, source_target_pairs={{0,4},{1,5},{2,6},{3,7},{4,0},{5,1},{6,2},{7,3},{8,12},{9,13},{10,... | collective-permute-start | bytes 1572872 | tf_op jit(solution)/shard_map/ppermute | solution.py:459
  62.3 26.5 %collective-permute-start.16 = (bf16[2,256,1024]{2,1,0:T(8,128)(2,1)S(1)}, bf16[2,256,1024]{2,1,0:T(8,128)(2,1)S(1)}, u32[]{:S(2)}, u32[]{:S(2)}) collective-permute-start(bf16[2,256,1024]{2,1,0:T(8,128)(2,1)S(1)} %get-tuple-element.134), channel_id=1, source_target_pairs={{0,3},{1,2},{2,1},{3,0},{4,7},{5,6},{6,5},{7,4},{8,11},{9,10},{10,... | collective-permute-start | bytes 3145736 | tf_op jit(solution)/shard_map/ppermute | solution.py:459
  64.1 24.7 %collective-permute-start.15 = (bf16[2,256,1024]{2,1,0:T(8,128)(2,1)S(1)}, bf16[2,256,1024]{2,1,0:T(8,128)(2,1)S(1)}, u32[]{:S(2)}, u32[]{:S(2)}) collective-permute-start(bf16[2,256,1024]{2,1,0:T(8,128)(2,1)S(1)} %get-tuple-element.132), channel_id=1, source_target_pairs={{0,1},{1,0},{2,3},{3,2},{4,5},{5,4},{6,7},{7,6},{8,9},{9,8},{10,11... | collective-permute-start | bytes 3145736 | tf_op jit(solution)/shard_map/ppermute | solution.py:459
  78.2 2.0 %collective-permute-start.12 = (bf16[16,32,512]{2,1,0:T(8,128)(2,1)S(1)}, bf16[16,32,512]{2,1,0:T(8,128)(2,1)S(1)}, u32[]{:S(2)}, u32[]{:S(2)}) collective-permute-start(bf16[16,32,512]{2,1,0:T(8,128)(2,1)S(1)} %get-tuple-element.124), channel_id=1, source_target_pairs={{0,8},{8,0},{16,24},{24,16},{32,40},{40,32},{48,56},{56,48},{64,72... | collective-permute-start | bytes 1572872 | tf_op jit(solution)/shard_map/ppermute | solution.py:459
  80.3 8.4 %collective-permute-start.13 = (bf16[2,4,32,512]{3,2,1,0:T(8,128)(2,1)S(1)}, bf16[2,4,32,512]{3,2,1,0:T(8,128)(2,1)S(1)}, u32[]{:S(2)}, u32[]{:S(2)}) collective-permute-start(bf16[2,4,32,512]{3,2,1,0:T(8,128)(2,1)S(1)} %get-tuple-element.127), channel_id=1, source_target_pairs={{0,64},{8,72},{16,80},{24,88},{32,96},{40,104},{48,112},{56,120},{... | collective-permute-start | bytes 786440 | tf_op jit(solution)/shard_map/ppermute | solution.py:459
  81.9 19.3 %collective-permute-start.18 = (bf16[256,1024]{1,0:T(8,128)(2,1)S(1)}, bf16[256,1024]{1,0:T(8,128)(2,1)S(1)}, u32[]{:S(2)}, u32[]{:S(2)}) collective-permute-start(bf16[256,1024]{1,0:T(8,128)(2,1)S(1)} %get-tuple-element.139), channel_id=1, source_target_pairs={{0,4},{1,5},{2,6},{3,7},{4,0},{5,1},{6,2},{7,3},{8,12},{9,13},{10,... | collective-permute-start | bytes 1572872 | tf_op jit(solution)/shard_map/ppermute | solution.py:459
  89.1 22.2 %collective-permute-start.21 = (bf16[256,1024]{1,0:T(8,128)(2,1)S(1)}, bf16[256,1024]{1,0:T(8,128)(2,1)S(1)}, u32[]{:S(2)}, u32[]{:S(2)}) collective-permute-start(bf16[256,1024]{1,0:T(8,128)(2,1)S(1)} %get-tuple-element.147), channel_id=1, source_target_pairs={{0,3},{1,2},{2,1},{3,0},{4,7},{5,6},{6,5},{7,4},{8,11},{9,10},{10,... | collective-permute-start | bytes 1572872 | tf_op jit(solution)/shard_map/ppermute | solution.py:459
  89.6 21.7 %collective-permute-start.22 = (bf16[256,1024]{1,0:T(8,128)(2,1)S(1)}, bf16[256,1024]{1,0:T(8,128)(2,1)S(1)}, u32[]{:S(2)}, u32[]{:S(2)}) collective-permute-start(bf16[256,1024]{1,0:T(8,128)(2,1)S(1)} %get-tuple-element.149), channel_id=1, source_target_pairs={{0,1},{1,0},{2,3},{3,2},{4,5},{5,4},{6,7},{7,6},{8,9},{9,8},{10,11... | collective-permute-start | bytes 1572872 | tf_op jit(solution)/shard_map/ppermute | solution.py:459
  91.6 6.2 %collective-permute-start.14 = (bf16[4,32,512]{2,1,0:T(8,128)(2,1)S(1)}, bf16[4,32,512]{2,1,0:T(8,128)(2,1)S(1)}, u32[]{:S(2)}, u32[]{:S(2)}) collective-permute-start(bf16[4,32,512]{2,1,0:T(8,128)(2,1)S(1)} %get-tuple-element.130), channel_id=1, source_target_pairs={{0,192},{8,200},{16,208},{24,216},{32,224},{40,232},{48,240},{56,2... | collective-permute-start | bytes 393224 | tf_op jit(solution)/shard_map/ppermute | solution.py:459
  97.8 6.3 %collective-permute-start.17 = (bf16[2,32,512]{2,1,0:T(8,128)(2,1)S(1)}, bf16[2,32,512]{2,1,0:T(8,128)(2,1)S(1)}, u32[]{:S(2)}, u32[]{:S(2)}) collective-permute-start(bf16[2,32,512]{2,1,0:T(8,128)(2,1)S(1)} %get-tuple-element.138), channel_id=1, source_target_pairs={{0,16},{8,24},{16,0},{24,8},{32,48},{40,56},{48,32},{56,40},{64,80... | collective-permute-start | bytes 196616 | tf_op jit(solution)/shard_map/ppermute | solution.py:459
  101.2 9.4 %copy-start.1 = (f32[2,32,512]{2,1,0:T(8,128)S(1)}, f32[2,32,512]{2,1,0:T(8,128)}, u32[]{:S(2)}) copy-start(f32[2,32,512]{2,1,0:T(8,128)} %refs_1_.25) | copy-start | bytes 393220
  101.2 9.4 %copy-start.2 = (f32[32,512]{1,0:T(8,128)S(1)}, f32[32,512]{1,0:T(8,128)}, u32[]{:S(2)}) copy-start(f32[32,512]{1,0:T(8,128)} %refs_2_.3) | copy-start | bytes 196612
  104.2 6.5 %collective-permute-start.19 = (bf16[32,512]{1,0:T(8,128)(2,1)S(1)}, bf16[32,512]{1,0:T(8,128)(2,1)S(1)}, u32[]{:S(2)}, u32[]{:S(2)}) collective-permute-start(bf16[32,512]{1,0:T(8,128)(2,1)S(1)} %get-tuple-element.143), channel_id=1, source_target_pairs={{0,48},{8,56},{16,32},{24,40},{32,16},{40,24},{48,0},{56,8},{64,11... | collective-permute-start | bytes 98312 | tf_op jit(solution)/shard_map/ppermute | solution.py:459
  114.5 5.0 %collective-permute-start.24 = (bf16[16,32,512]{2,1,0:T(8,128)(2,1)S(1)}, bf16[16,32,512]{2,1,0:T(8,128)(2,1)S(1)}, u32[]{:S(2)}, u32[]{:S(2)}) collective-permute-start(bf16[16,32,512]{2,1,0:T(8,128)(2,1)S(1)} %get-tuple-element.154), channel_id=1, source_target_pairs={{0,8},{8,0},{16,24},{24,16},{32,40},{40,32},{48,56},{56,48},{64,72... | collective-permute-start | bytes 1572872 | tf_op jit(solution)/shard_map/ppermute | solution.py:459
  114.6 4.9 %collective-permute-start.20 = (bf16[32,512]{1,0:T(8,128)(2,1)S(1)}, bf16[32,512]{1,0:T(8,128)(2,1)S(1)}, u32[]{:S(2)}, u32[]{:S(2)}) collective-permute-start(bf16[32,512]{1,0:T(8,128)(2,1)S(1)} %get-tuple-element.145.refs_0_), channel_id=1, source_target_pairs={{0,16},{8,24},{16,0},{24,8},{32,48},{40,56},{48,32},{56,40},{64,80... | collective-permute-start | bytes 98312 | tf_op jit(solution)/shard_map/ppermute | solution.py:459
  119.6 9.9 %collective-permute-start.26 = (bf16[2,4,32,512]{3,2,1,0:T(8,128)(2,1)S(1)}, bf16[2,4,32,512]{3,2,1,0:T(8,128)(2,1)S(1)}, u32[]{:S(2)}, u32[]{:S(2)}) collective-permute-start(bf16[2,4,32,512]{3,2,1,0:T(8,128)(2,1)S(1)} %get-tuple-element.159), channel_id=1, source_target_pairs={{0,64},{8,72},{16,80},{24,88},{32,96},{40,104},{48,112},{56,120},{... | collective-permute-start | bytes 786440 | tf_op jit(solution)/shard_map/ppermute | solution.py:459
  120.0 6.7 %collective-permute-start.23 = (bf16[2,32,512]{2,1,0:T(8,128)(2,1)S(1)}, bf16[2,32,512]{2,1,0:T(8,128)(2,1)S(1)}, u32[]{:S(2)}, u32[]{:S(2)}) collective-permute-start(bf16[2,32,512]{2,1,0:T(8,128)(2,1)S(1)} %get-tuple-element.152.refs_0_), channel_id=1, source_target_pairs={{0,48},{8,56},{16,32},{24,40},{32,16},{40,24},{48,0},{56,8},{64,11... | collective-permute-start | bytes 196616 | tf_op jit(solution)/shard_map/ppermute | solution.py:459
  126.7 6.3 %collective-permute-start.25 = (bf16[4,32,512]{2,1,0:T(8,128)(2,1)S(1)}, bf16[4,32,512]{2,1,0:T(8,128)(2,1)S(1)}, u32[]{:S(2)}, u32[]{:S(2)}) collective-permute-start(bf16[4,32,512]{2,1,0:T(8,128)(2,1)S(1)} %get-tuple-element.157.refs_0_), channel_id=1, source_target_pairs={{0,192},{8,200},{16,208},{24,216},{32,224},{40,232},{48,240},{56,2... | collective-permute-start | bytes 393224 | tf_op jit(solution)/shard_map/ppermute | solution.py:459
  133.0 6.9 %collective-permute-start.27 = (bf16[2,4,32,512]{3,2,1,0:T(8,128)(2,1)S(1)}, bf16[2,4,32,512]{3,2,1,0:T(8,128)(2,1)S(1)}, u32[]{:S(2)}, u32[]{:S(2)}) collective-permute-start(bf16[2,4,32,512]{3,2,1,0:T(8,128)(2,1)S(1)} %get-tuple-element.162.refs_0_), channel_id=1, source_target_pairs={{0,64},{8,72},{16,80},{24,88},{32,96},{40,104},{48,112},{56,120},{... | collective-permute-start | bytes 786440 | tf_op jit(solution)/shard_map/ppermute | solution.py:459
  133.7 6.2 %collective-permute-start.28 = (bf16[4,32,512]{2,1,0:T(8,128)(2,1)S(1)}, bf16[4,32,512]{2,1,0:T(8,128)(2,1)S(1)}, u32[]{:S(2)}, u32[]{:S(2)}) collective-permute-start(bf16[4,32,512]{2,1,0:T(8,128)(2,1)S(1)} %get-tuple-element.164), channel_id=1, source_target_pairs={{0,192},{8,200},{16,208},{24,216},{32,224},{40,232},{48,240},{56,2... | collective-permute-start | bytes 393224 | tf_op jit(solution)/shard_map/ppermute | solution.py:459
  140.0 10.3 %collective-permute-start.29 = (bf16[16,32,512]{2,1,0:T(8,128)(2,1)S(1)}, bf16[16,32,512]{2,1,0:T(8,128)(2,1)S(1)}, u32[]{:S(2)}, u32[]{:S(2)}) collective-permute-start(bf16[16,32,512]{2,1,0:T(8,128)(2,1)S(1)} %get-tuple-element.167.refs_2_), channel_id=1, source_target_pairs={{0,8},{8,0},{16,24},{24,16},{32,40},{40,32},{48,56},{56,48},{64,72... | collective-permute-start | bytes 1572872 | tf_op jit(solution)/shard_map/ppermute | solution.py:459
  140.1 5.7 %collective-permute-start.30 = (bf16[2,32,512]{2,1,0:T(8,128)(2,1)S(1)}, bf16[2,32,512]{2,1,0:T(8,128)(2,1)S(1)}, u32[]{:S(2)}, u32[]{:S(2)}) collective-permute-start(bf16[2,32,512]{2,1,0:T(8,128)(2,1)S(1)} %get-tuple-element.170), channel_id=1, source_target_pairs={{0,16},{8,24},{16,0},{24,8},{32,48},{40,56},{48,32},{56,40},{64,80... | collective-permute-start | bytes 196616 | tf_op jit(solution)/shard_map/ppermute | solution.py:459
  145.9 6.3 %collective-permute-start.31 = (bf16[32,512]{1,0:T(8,128)(2,1)S(1)}, bf16[32,512]{1,0:T(8,128)(2,1)S(1)}, u32[]{:S(2)}, u32[]{:S(2)}) collective-permute-start(bf16[32,512]{1,0:T(8,128)(2,1)S(1)} %get-tuple-element.177), channel_id=1, source_target_pairs={{0,48},{8,56},{16,32},{24,40},{32,16},{40,24},{48,0},{56,8},{64,11... | collective-permute-start | bytes 98312 | tf_op jit(solution)/shard_map/ppermute | solution.py:459

commit v3 on v2

--- a/solution.py
+++ b/solution.py
@@ -15,6 +15,8 @@
 KV = 512
 ROWS = 1024
 HALF = 512
+QUARTER = 256
+TAGS = ("s", "o")
 F32 = jnp.float32
 BF16 = jnp.bfloat16
 
@@ -56,7 +58,7 @@
 CHAIN = Chain()
 
 
-def call(kernel, outs, args, specs, out_specs, scratch=(), aliases=None, name=None, vmem=16, hint=0):
+def call(kernel, outs, args, specs, out_specs, scratch=(), aliases=None, name=None, vmem=16):
     outs, out_specs = list(outs), list(out_specs)
     tokens = [] if CHAIN.token is None else [CHAIN.token]
     count = len(args)
@@ -72,7 +74,7 @@
         out_specs=out_specs + [HBM],
         scratch_shapes=list(scratch),
         compiler_params=pltpu.CompilerParams(vmem_limit_bytes=vmem * MIB),
-        cost_estimate=pl.CostEstimate(flops=hint, bytes_accessed=0, transcendentals=0),
+        cost_estimate=pl.CostEstimate(flops=0, bytes_accessed=0, transcendentals=0),
         input_output_aliases=aliases or {},
         name=name,
     )(*(pinned(a) if spec is HBM else a for a, spec in zip(args, specs)), *(pinned(t) for t in tokens))
@@ -83,67 +85,52 @@
     return pl.ds(pl.multiple_of(start, width), width)
 
 
-def pack_kernel(plan, tok, x, g, a1, b1, z1, a2, b2, z2, z3, gt_out, gin, gt, sems, gsems):
-    _, _, _, z, y = place()
-    s = lax.rem(plan[0], 2)
-    copies = []
-
-    def send(layer, col, width, dst, at):
-        copies.append(
-            pltpu.make_async_copy(
-                x.at[layer, :, columns(col, width)], dst.at[:, pl.ds(at, width)], sems.at[len(copies)]
+def pack(fragment, plan, tok, x, g):
+    def kernel(plan_ref, tok_ref, x_ref, g_ref, a, b, c, gt_ref, gin, sems):
+        _, _, _, z, y = place()
+        s = lax.rem(plan_ref[0], 2)
+        layer = s if fragment == 0 else 1 - s
+        g_copy = pltpu.make_async_copy(g_ref.at[layer], gin, sems.at[12])
+        g_copy.start()
+        copies = []
+
+        def send(zz, yy, offset, width, dst, at):
+            col = pl.multiple_of((zz * 4 + yy) * ROWS + offset, QUARTER)
+            copies.append(
+                pltpu.make_async_copy(
+                    x_ref.at[layer, :, pl.ds(col, width)], dst.at[:, pl.ds(at, width)], sems.at[len(copies)]
+                )
             )
-        )
-        copies[-1].start()
-
-    g_copies = [pltpu.make_async_copy(g.at[layer], gin.at[i], gsems.at[i]) for i, layer in enumerate((s, 1 - s))]
-    for c in g_copies:
-        c.start()
-    for zz, bufs in ((1 - z, (a1, b1)), (z, (a2, b2))):
-        for buf, first, offset in ((bufs[0], y ^ 1, 0), (bufs[1], y ^ 3, HALF)):
-            for i, yy in enumerate((first, y ^ 2)):
-                send(s, (zz * 4 + yy) * ROWS + offset, HALF, buf, i * HALF)
-    for j, buf, at in ((1, z1, 0), (2, z1, ROWS), (3, z2, 0), (0, z3, 0)):
-        send(1 - s, ((1 - z) * 4 + (y ^ j)) * ROWS, ROWS, buf, at)
-    kept = (tok[...] != 0).astype(F32)
-    last = []
-
-    def put(src, dst):
-        last.append(pltpu.make_async_copy(src, dst, gsems.at[2 + len(last)]))
-        last[-1].start()
-
-    for i, bufs, at in ((0, (a1, b1), 2 * HALF), (1, (z1,), 2 * ROWS)):
-        g_copies[i].wait()
-        gt[i] = (gin[i].astype(F32).T * kept).astype(BF16)
-        for buf in bufs:
+            copies[-1].start()
+
+        for buf, first, offset in ((a, y ^ 1, HALF), (b, y ^ 3, HALF + QUARTER)):
+            for i, (zz, yy) in enumerate(((1 - z, first), (z, first), (1 - z, y ^ 2), (z, y ^ 2))):
+                send(zz, yy, offset, QUARTER, buf, i * QUARTER)
+        for j in range(4):
+            send(1 - z, y ^ j, 0, HALF, c, j * HALF)
+        kept = (tok_ref[...] != 0).astype(F32)
+        g_copy.wait()
+        gt = (gin[...].astype(F32).T * kept).astype(BF16)
+        gt_ref[...] = gt
+        for buf, at in ((a, ROWS), (b, ROWS), (c, 4 * HALF)):
             for h in range(2):
-                put(gt.at[i, pl.ds(h * TOK, TOK)], buf.at[:, pl.ds(at + h * TOK, TOK)])
-    put(gt, gt_out)
-    for c in copies + last:
-        c.wait()
-
-
-def pack(plan, tok, x, g):
-    wide = in_vmem(TOK, 2 * HALF + KV)
-    half = in_vmem(TOK, 2 * HALF)
-    return call(
-        pack_kernel,
-        (wide, wide, in_vmem(TOK, 2 * ROWS + KV), half, half, half, half, in_vmem(2, KV, TOK)),
+                buf[:, at + h * TOK : at + (h + 1) * TOK] = gt[h * TOK : (h + 1) * TOK]
+        for c in copies:
+            c.wait()
+
+    return call(
+        kernel,
+        (in_vmem(TOK, ROWS + KV), in_vmem(TOK, ROWS + KV), in_vmem(TOK, 4 * HALF + KV), in_vmem(KV, TOK)),
         (plan, tok, x, g),
         [SM, VM, HBM, HBM],
-        [VM] * 8,
-        [
-            pltpu.VMEM((2, TOK, KV), BF16),
-            pltpu.VMEM((2, KV, TOK), BF16),
-            pltpu.SemaphoreType.DMA((12,)),
-            pltpu.SemaphoreType.DMA((9,)),
-        ],
-        name="pack",
+        [VM] * 4,
+        [pltpu.VMEM((TOK, KV), BF16), pltpu.SemaphoreType.DMA((13,))],
+        name="pack_" + TAGS[fragment],
         vmem=BIG,
     )
 
 
-def product(name, fragment, pieces, width, out_shapes, g_at, plan, x, gt, recvs, hint=0):
+def product(name, fragment, pieces, width, out_shapes, g_at, plan, x, gt, recvs):
     count = len(pieces)
     number = len(recvs)
     total = sum(len(p[3]) for p in pieces)
@@ -157,7 +144,7 @@
         s = lax.rem(plan_ref[0], 2)
         layer = s if fragment == 0 else 1 - s
         g_copies = [
-            pltpu.make_async_copy(gt_ref.at[fragment], gts.at[:, pl.ds(0, TOK)], sems.at[2 * count]),
+            pltpu.make_async_copy(gt_ref, gts.at[:, pl.ds(0, TOK)], sems.at[2 * count]),
             *(
                 pltpu.make_async_copy(
                     recv_refs[0].at[:, pl.ds(g_at + h * TOK, TOK)],
@@ -215,7 +202,6 @@
         ],
         name=name,
         vmem=BIG,
-        hint=hint,
     )
 
 
@@ -230,64 +216,43 @@
 WORKERS = (16, 2, 32, KV)
 
 
-def inner_sync(plan, w, near, across):
-    def kernel(plan_ref, w_ref, near_ref, za_ref, zb_ref, inner_ref, send_ref, wv, sem, sem2):
+def inner_step(fragment, plan, w, first, second, third, fourth, across):
+    def kernel(plan_ref, w_ref, *rest):
+        k0, r0, l0, k1, r1, l1, ka, ra, kb, rb, z_ref, inner_ref, send_ref = rest[:13]
+        wv, sems = rest[-2:]
         s = lax.rem(plan_ref[0], 2)
+        layer = s if fragment == 0 else 1 - s
         core = place()[2]
-        load = pltpu.make_async_copy(w_ref.at[s], wv, sem)
+        load = pltpu.make_async_copy(w_ref.at[layer], wv, sems.at[0])
         load.start()
         load.wait()
-        for h, z_ref in enumerate((za_ref, zb_ref)):
-            for q in range(4):
+        for q in range(4):
+            cols = pl.ds(q * 128, 128)
+            halves = [flip(k[:, cols], r[0, :, cols], l[:, cols]) for k, r, l in ((k0, r0, l0), (k1, r1, l1))]
+            put(inner_ref, wv, 2 * q, jnp.concatenate(halves, axis=1))
+        for h, (k, r) in enumerate(((ka, ra), (kb, rb))):
+            for q in range(2):
                 cols = pl.ds(q * 128, 128)
-                i = h * 8 + q * 2
-                gradient = flip(near_ref[h, :, cols], z_ref[:, cols])
-                inner_ref[i : i + 2] = stepped(wv[i : i + 2].reshape(128, KV), gradient).reshape(2, 2, 32, KV)
-        out = pltpu.make_async_copy(inner_ref.at[:, 1 - core], send_ref, sem2)
-        out.start()
-        out.wait()
-
-    return call(
-        kernel,
-        (shape(*WORKERS), shape(16, 32, KV)),
-        (plan, w, near, *across),
-        [SM, HBM] + [VM] * 3,
-        [VM, ANY],
-        [pltpu.VMEM(WORKERS, BF16), pltpu.SemaphoreType.DMA, pltpu.SemaphoreType.DMA],
-        name="inner_sync",
-    )
-
-
-def inner_other(plan, w, first, second):
-    def kernel(plan_ref, w_ref, *rest):
-        k0, r0, l0, k1, r1, l1, inner_ref, send_ref, new_ref, wv, sem, sem2 = rest
-        other = 1 - lax.rem(plan_ref[0], 2)
-        core = place()[2]
-        load = pltpu.make_async_copy(w_ref.at[other], wv, sem)
-        load.start()
-        load.wait()
-        for q in range(8):
-            cols = pl.ds(q * 128, 128)
-            i = q * 2
-            gradient = jnp.concatenate(
-                [flip(k[:, cols], r[0, :, cols], l[:, cols]) for k, r, l in ((k0, r0, l0), (k1, r1, l1))], axis=1
-            )
-            inner_ref[i : i + 2] = stepped(wv[i : i + 2].reshape(128, KV), gradient).reshape(2, 2, 32, KV)
-        out = pltpu.make_async_copy(inner_ref.at[:, 1 - core], send_ref, sem2.at[0])
-        keep = pltpu.make_async_copy(inner_ref, new_ref.at[other], sem2.at[1])
-        out.start()
-        keep.start()
-        out.wait()
-        keep.wait()
-
-    return call(
-        kernel,
-        (shape(*WORKERS), shape(16, 32, KV), shape(2, *WORKERS)),
-        (plan, w, *first, *second),
-        [SM, HBM] + [VM] * 6,
-        [VM, ANY, ANY],
-        [pltpu.VMEM(WORKERS, BF16), pltpu.SemaphoreType.DMA, pltpu.SemaphoreType.DMA((2,))],
-        name="inner_other",
+                put(inner_ref, wv, 8 + 4 * h + 2 * q, flip(k[1, :, cols], r[1, :, cols], z_ref[h, :, cols]))
+        copies = [pltpu.make_async_copy(inner_ref.at[:, 1 - core], send_ref, sems.at[1])]
+        if fragment == 1:
+            copies.append(pltpu.make_async_copy(inner_ref, rest[13].at[layer], sems.at[2]))
+        for c in copies:
+            c.start()
+        for c in copies:
+            c.wait()
+
+    def put(inner_ref, wv, i, gradient):
+        inner_ref[i : i + 2] = stepped(wv[i : i + 2].reshape(128, KV), gradient).reshape(2, 2, 32, KV)
+
+    return call(
+        kernel,
+        (shape(*WORKERS), shape(16, 32, KV), shape(2, *WORKERS))[: 2 + fragment],
+        (plan, w, *first, *second, *third, *fourth, across),
+        [SM, HBM] + [VM] * 11,
+        [VM, ANY, ANY][: 2 + fragment],
+        [pltpu.VMEM(WORKERS, BF16), pltpu.SemaphoreType.DMA((3,))],
+        name="inner_" + TAGS[fragment],
     )
 
 
@@ -459,99 +424,135 @@
     return lax.ppermute(value, *MOVES[move])
 
 
+class Fragment:
+    def __init__(self, index, plan, x, packed):
+        self.index, self.plan, self.x = index, plan, x
+        self.a, self.b, self.c, self.gt = packed
+
+    def start_y(self):
+        self.got_a, self.got_b = swap(self.a, "a"), swap(self.b, "b")
+
+    def start_z(self):
+        self.got_c = swap(self.c, "z")
+
+    def make(self, name, pieces, width, outs, recv):
+        name = name + "_" + TAGS[self.index]
+        g_at = ROWS if width == QUARTER else 4 * HALF
+        return product(name, self.index, pieces, width, outs, g_at, self.plan, self.x, self.gt, (recv,))
+
+    def quarter(self, name, flip_y, offset, at, recv):
+        pieces = [
+            (
+                lambda z, y, far=far: ((1 - z if far else z) * 4 + (y ^ flip_y)) * ROWS + offset,
+                0,
+                (at + i) * QUARTER,
+                [(0, i, 0, KV)],
+            )
+            for i, far in enumerate((True, False))
+        ]
+        return self.make(name, pieces, QUARTER, [(2, KV, QUARTER)], recv)
+
+    def quarters(self):
+        self.next_a = swap(self.quarter("send_a", 3, HALF, 2, self.got_a), "b")
+        self.next_b = swap(self.quarter("send_b", 1, HALF + QUARTER, 2, self.got_b), "a")
+        self.keep_a = self.quarter("keep_a", 0, HALF, 0, self.got_a)
+        self.keep_b = self.quarter("keep_b", 0, HALF + QUARTER, 0, self.got_b)
+
+    def halves(self):
+        lo, hi = (0, 256), (256, 512)
+        one, two = (256, HALF), (2, 256, HALF)
+
+        def dest(j, targets):
+            return (lambda z, y: (z * 4 + (y ^ j)) * ROWS, 0, j * HALF, targets)
+
+        send_0, send_1, self.stay_0, self.stay_1 = self.make(
+            "halves",
+            [
+                dest(2, [(0, 1, *lo), (1, 1, *hi)]),
+                dest(1, [(0, 0, *lo), (3, None, *hi)]),
+                dest(3, [(1, 0, *hi), (2, None, *lo)]),
+            ],
+            HALF,
+            [two, two, one, one],
+            self.got_c,
+        )
+        self.got_0, self.got_1 = swap(send_0, "a"), swap(send_1, "b")
+        self.mine_0, self.mine_1 = self.make(
+            "mine", [dest(0, [(0, None, *lo), (1, None, *hi)])], HALF, [one, one], self.got_c
+        )
+
+    def far(self):
+        pairs = [(self.keep_a, self.next_a, 0, 0, 0, 0), (self.keep_b, self.next_b, 0, 0, 0, 1)]
+        self.across = swap(sums("far_" + TAGS[self.index], [(2, KV, QUARTER)], pairs), "z")
+
+    def last(self, extra=()):
+        pairs = [(self.stay_0, self.got_0, None, 1, 0, None), (self.stay_1, self.got_1, None, 1, 1, None)]
+        last_0, last_1 = sums("last_" + TAGS[self.index], [(256, HALF)] * 2, pairs, extra)
+        self.last_0, self.last_1 = swap(last_0, "b"), swap(last_1, "a")
+
+    def inner(self, w):
+        return inner_step(
+            self.index,
+            self.plan,
+            w,
+            (self.mine_0, self.got_0, self.last_0),
+            (self.mine_1, self.got_1, self.last_1),
+            (self.keep_a, self.next_a),
+            (self.keep_b, self.next_b),
+            self.across,
+        )
+
+
 def body(token_ids, layer_inputs, key_grads, weights, anchors, momentum, plan):
     CHAIN.token = None
     x = layer_inputs
     w = weights.reshape(2, *WORKERS)
-    a1, b1, z1, a2, b2, z2, z3, gt = pack(plan, token_ids.reshape(1, TOK), x, key_grads)
-    got_a1 = swap(a1, "a")
-    got_b1 = swap(b1, "b")
-    got_z1 = swap(z1, "z")
-    got_a2 = swap(a2, "a")
-    got_b2 = swap(b2, "b")
-    got_z2 = swap(z2, "z")
-    got_z3 = swap(z3, "z")
-
-    def tile(name, far, flip_y, offset, at, recvs):
-        piece = (
-            lambda z, y: ((1 - z if far else z) * 4 + (y ^ flip_y)) * ROWS + offset,
-            len(recvs) - 1,
-            at * HALF,
-            [(0, None, 0, KV)],
-        )
-        return product(name, 0, [piece], HALF, [(KV, HALF)], 2 * HALF, plan, x, gt, recvs)
-
-    def dest(j, source, at, targets):
-        return (lambda z, y: (z * 4 + (y ^ j)) * ROWS, source, at, targets)
-
-    def other(name, pieces, outs, recvs, hint=0):
-        return product(name, 1, pieces, ROWS, outs, 2 * ROWS, plan, x, gt, recvs, hint)
-
-    lo, hi = (0, 256), (256, 512)
-    half, pair = (256, ROWS), (2, 256, ROWS)
-
-    far_a = swap(tile("send_a1", True, 3, 0, 1, (got_a1,)), "b")
-    far_b = swap(tile("send_b1", True, 1, HALF, 1, (got_b1,)), "a")
-    keep_a1 = tile("keep_a1", True, 0, 0, 0, (got_a1,))
-    keep_b1 = tile("keep_b1", True, 0, HALF, 0, (got_b1,))
-    near_a = swap(tile("send_a2", False, 3, 0, 1, (got_a1, got_a2)), "b")
-    near_b = swap(tile("send_b2", False, 1, HALF, 1, (got_b1, got_b2)), "a")
-    keep_a2 = tile("keep_a2", False, 0, 0, 0, (got_a1, got_a2))
-    keep_b2 = tile("keep_b2", False, 0, HALF, 0, (got_b1, got_b2))
-    send_0, stay_1 = other(
-        "other_1",
-        [dest(2, 0, ROWS, [(0, 1, *lo)]), dest(1, 0, 0, [(0, 0, *lo), (1, None, *hi)])],
-        [pair, half],
-        (got_z1,),
-    )
-    got_0 = swap(send_0, "a")
-    across = sums(
-        "far", [(KV, HALF)] * 2, [(keep_a1, far_a, None, None, 0, None), (keep_b1, far_b, None, None, 1, None)]
-    )
-    across = [swap(t, "z") for t in across]
-    near = sums("near", [(2, KV, HALF)], [(keep_a2, near_a, None, None, 0, 0), (keep_b2, near_b, None, None, 0, 1)])
-    send_1, stay_0 = other(
-        "other_2",
-        [dest(2, 0, ROWS, [(0, 1, *hi)]), dest(3, 1, 0, [(0, 0, *hi), (1, None, *lo)])],
-        [pair, half],
-        (got_z1, got_z2),
-        10**10,
-    )
-    got_1 = swap(send_1, "b")
-
-    inner_s, send_s = inner_sync(plan, w, near, across)
+    tok = token_ids.reshape(1, TOK)
+    s = Fragment(0, plan, x, pack(0, plan, tok, x, key_grads))
+    s.start_y()
+    s.start_z()
+    o = Fragment(1, plan, x, pack(1, plan, tok, x, key_grads))
+    s.quarters()
+    s.halves()
+    s.far()
+    o.start_z()
+    s.last((s.across,))
+    o.start_y()
+
+    inner_s, send_s = s.inner(w)
     send, keep = sum_x(inner_s, swap(send_s, "core"), "sync_x1")
     recv = swap(send, "x1")
+    o.quarters()
     send, keep = halve("sync_x3", QUAD, keep, recv)
-    last_0, last_1 = sums(
-        "last", [half, half], [(stay_0, got_0, None, 1, 0, None), (stay_1, got_1, None, 1, 1, None)]
-    )
-    last_0, last_1 = swap(last_0, "b"), swap(last_1, "a")
-    send, keep = sum_z(keep, swap(send, "x3"), "sync_z1")
+    recv = swap(send, "x3")
+    send, keep = sum_z(keep, recv, "sync_z1")
     recv = swap(send, "z1")
-    mine_0, mine_1 = other("other_3", [dest(0, 1, 0, [(0, None, *lo), (1, None, *hi)])], [half, half], (got_z1, got_z3))
+    o.halves()
     send, keep = halve("sync_z3", (32, KV), keep, recv)
-    anchor_new, momentum_new, short = outer_sync(plan, anchors, momentum, keep, swap(send, "z3"))
+    recv = swap(send, "z3")
+    o.far()
+    anchor_new, momentum_new, short = outer_sync(plan, anchors, momentum, keep, recv)
     short_far = swap(short, "z1")
-
-    inner_o, send_o, new = inner_other(plan, w, (mine_0, got_0, last_0), (mine_1, got_1, last_1))
+    own = join(short, short_far)
+    got = swap(own, "z3")
+    o.last()
+    row = row_of(own, got)
+    row_far = swap(row, "x3")
+    inner_o, send_o, new = o.inner(w)
     core_o = swap(send_o, "core")
-    own = join(short, short_far)
+    own = join(row, row_far)
+    got = swap(own, "x1")
     send, keep = sum_x(inner_o, core_o, "other_x1")
     recv = swap(send, "x1")
-    row = row_of(own, swap(own, "z3"))
-    row_far = swap(row, "x3")
+    block = block_of(own, got)
+    block_far = swap(block, "core")
     send, keep = halve("other_x3", QUAD, keep, recv)
     recv = swap(send, "x3")
-    own = join(row, row_far)
-    got = swap(own, "x1")
+    new = mix(plan, inner_s, block, block_far, new)
     send, keep = sum_z(keep, recv, "other_z1")
     recv = swap(send, "z1")
-    block = block_of(own, got)
-    block_far = swap(block, "core")
     send, keep = halve("other_z3", (32, KV), keep, recv)
     recv = swap(send, "z3")
-    new = mix(plan, inner_s, block, block_far, new)
     pending = outer_other(plan, anchors, keep, recv)
     return (new.reshape(1, 2, ROWS, KV), anchor_new, momentum_new, pending)
 

time: 154 us -> 178 us (1.16)
  waiting for transfers between devices: 71.9 us -> 101 us
  starting transfers between devices: 57.3 us -> 47.2 us
  Pallas kernels: 21.4 us -> 27.1 us
    ppermute x32 -> x35, waiting for transfers between devices: 71.9 us -> 101 us  [swap(): return lax.ppermute(value, *MOVES[move])]
    ppermute x32 -> x35, starting transfers between devices: 57.3 us -> 47.2 us  [swap(): return lax.ppermute(value, *MOVES[move])]
    pallas_call x32 -> x35, Pallas kernels: 21.4 us -> 27.1 us  [call(): pl.pallas_call(chained, out_shape=outs + [in_hbm(8, 128)], in_specs=list(...]
  transfers between devices with their start and end apart: 32 -> 35, of which waited for: 19 -> 19; matrix products, arithmetic and copies ran while one was open for 0% -> 0% of each run, Pallas kernels for 10% -> 12%
where the time goes in v3:
time: 178 us; the launch traced here: 177 us
  waiting for transfers between devices  101 us (57%)
  starting transfers between devices  47.2 us (27%)
  Pallas kernels  27.1 us (15%)
    ppermute x35, waiting for transfers between devices, swap(): return lax.ppermute(value, *MOVES[move])  101 us
    ppermute x35, starting transfers between devices, swap(): return lax.ppermute(value, *MOVES[move])  47.2 us
    pallas_call x35, Pallas kernels, call(): pl.pallas_call(chained, out_shape=outs + [in_hbm(8, 128)], in_specs=list(...  27.1 us
  transfers between devices with their start and end apart: 35, of which 19 were waited for; matrix products, arithmetic and copies ran while one was open for 0% of the time, Pallas kernels for 12%

profile of v3, /device:TPU:8, one launch (start us, length us, event | category | flops | bytes accessed | tf_op | source)
XLA Modules:
  0.0 177.4 jit_solution(3036184804253979946)
XLA Ops:
  2.0 1.9 %pack_s.1 = (bf16[256,1536]{1,0:T(8,128)(2,1)S(1)}, bf16[256,1536]{1,0:T(8,128)(2,1)S(1)}, bf16[256,2560]{1,0:T(8,128)(2,1)S(1)}, bf16[512,256]{1,0:T(8,128)(2,1)S(1)}, bf16[8,128]{1,0:T(8,128)(2,1)}) custom-call(s32[1]{0:T(128)S(6)} %copy.13.refs_0_, s32[1,256]{1,0:T(1,128)S(1)} %bitcast.5, bf16[2,256,8192]{2,1,0:T(8,128)(2,1)} %refs_1_.25, ...), custom_call_target="tpu_custom_call" | custom-call | tf_op jit(solution)/shard_map/pack_s/pallas_call | solution.py:70
  3.9 2.3 %collective-permute-start.2 = (bf16[256,1536]{1,0:T(8,128)(2,1)S(1)}, bf16[256,1536]{1,0:T(8,128)(2,1)S(1)}, u32[]{:S(2)}, u32[]{:S(2)}) collective-permute-start(bf16[256,1536]{1,0:T(8,128)(2,1)S(1)} %get-tuple-element.105), channel_id=1, source_target_pairs={{0,1},{1,0},{2,3},{3,2},{4,5},{5,4},{6,7},{7,6},{8,9},{9,8},{10,11... | collective-permute-start | bytes 2359304 | tf_op jit(solution)/shard_map/ppermute | solution.py:424
  6.8 1.9 %collective-permute-start = (bf16[256,2560]{1,0:T(8,128)(2,1)S(1)}, bf16[256,2560]{1,0:T(8,128)(2,1)S(1)}, u32[]{:S(2)}, u32[]{:S(2)}) collective-permute-start(bf16[256,2560]{1,0:T(8,128)(2,1)S(1)} %get-tuple-element.103), channel_id=1, source_target_pairs={{0,4},{1,5},{2,6},{3,7},{4,0},{5,1},{6,2},{7,3},{8,12},{9,13},{10,... | collective-permute-start | bytes 3932168 | tf_op jit(solution)/shard_map/ppermute | solution.py:424
  8.7 1.8 pack_o.1
  10.5 12.7 %collective-permute-done.2.refs_3_ = bf16[256,1536]{1,0:T(8,128)(2,1)S(1)} collective-permute-done((bf16[256,1536]{1,0:T(8,128)(2,1)S(1)}, bf16[256,1536]{1,0:T(8,128)(2,1)S(1)}, u32[]{:S(2)}, u32[]{:S(2)}) %collective-permute-start.2) | collective-permute-done | bytes 786464 | tf_op jit(solution)/shard_map/ppermute | solution.py:424
  24.3 1.1 send_b_s.1
  25.4 1.9 %collective-permute-start.6 = (bf16[2,512,256]{2,1,0:T(8,128)(2,1)S(1)}, bf16[2,512,256]{2,1,0:T(8,128)(2,1)S(1)}, u32[]{:S(2)}, u32[]{:S(2)}) collective-permute-start(bf16[2,512,256]{2,1,0:T(8,128)(2,1)S(1)} %get-tuple-element.121), channel_id=1, source_target_pairs={{0,1},{1,0},{2,3},{3,2},{4,5},{5,4},{6,7},{7,6},{8,9},{9,8},{10,11... | collective-permute-start | bytes 1572872 | tf_op jit(solution)/shard_map/ppermute | solution.py:424
  27.4 1.6 collective-permute-start.5
  30.0 1.1 keep_b_s.1
  31.1 5.8 %collective-permute-done.refs_3_ = bf16[256,2560]{1,0:T(8,128)(2,1)S(1)} collective-permute-done((bf16[256,2560]{1,0:T(8,128)(2,1)S(1)}, bf16[256,2560]{1,0:T(8,128)(2,1)S(1)}, u32[]{:S(2)}, u32[]{:S(2)}) %collective-permute-start) | collective-permute-done | bytes 1310752 | tf_op jit(solution)/shard_map/ppermute | solution.py:424
  37.0 2.2 %halves_s.1 = (bf16[2,256,512]{2,1,0:T(8,128)(2,1)S(1)}, bf16[2,256,512]{2,1,0:T(8,128)(2,1)S(1)}, bf16[256,512]{1,0:T(8,128)(2,1)S(1)}, bf16[256,512]{1,0:T(8,128)(2,1)S(1)}, bf16[8,128]{1,0:T(8,128)(2,1)}) custom-call(s32[1]{0:T(128)S(6)} %copy.13.refs_0_, bf16[2,256,8192]{2,1,0:T(8,128)(2,1)S(1)} %bitcast.4, ...), custom_call_target="tpu_custom_call" | custom-call | tf_op jit(solution)/shard_map/halves_s/pallas_call | solution.py:70
  40.2 1.8 %collective-permute-start.7 = (bf16[2,512,256]{2,1,0:T(8,128)(2,1)S(1)}, bf16[2,512,256]{2,1,0:T(8,128)(2,1)S(1)}, u32[]{:S(2)}, u32[]{:S(2)}) collective-permute-start(bf16[2,512,256]{2,1,0:T(8,128)(2,1)S(1)} %get-tuple-element.123), channel_id=1, source_target_pairs={{0,4},{1,5},{2,6},{3,7},{4,0},{5,1},{6,2},{7,3},{8,12},{9,13},{10,... | collective-permute-start | bytes 1572872 | tf_op jit(solution)/shard_map/ppermute | solution.py:424
  42.0 1.4 collective-permute-start.3
  43.4 1.6 collective-permute-start.4
  45.1 10.0 %collective-permute-done.7.refs_4_.refs_12_ = bf16[2,512,256]{2,1,0:T(8,128)(2,1)S(1)} collective-permute-done((bf16[2,512,256]{2,1,0:T(8,128)(2,1)S(1)}, bf16[2,512,256]{2,1,0:T(8,128)(2,1)S(1)}, u32[]{:S(2)}, u32[]{:S(2)}) %collective-permute-start.7) | collective-permute-done | bytes 524320 | tf_op jit(solution)/shard_map/ppermute | solution.py:424
  55.4 1.7 collective-permute-start.8
  57.1 1.7 collective-permute-start.9
  59.7 5.0 %collective-permute-done.8.refs_4_ = bf16[256,512]{1,0:T(8,128)(2,1)S(1)} collective-permute-done((bf16[256,512]{1,0:T(8,128)(2,1)S(1)}, bf16[256,512]{1,0:T(8,128)(2,1)S(1)}, u32[]{:S(2)}, u32[]{:S(2)}) %collective-permute-start.8) | collective-permute-done | bytes 262176 | tf_op jit(solution)/shard_map/ppermute | solution.py:424
  64.7 1.6 collective-permute-done.9.refs_7_
  66.3 2.0 %inner_s.1 = (bf16[16,2,32,512]{3,2,1,0:T(8,128)(2,1)S(1)}, bf16[16,32,512]{2,1,0:T(8,128)(2,1)S(1)}, bf16[8,128]{1,0:T(8,128)(2,1)}) custom-call(s32[1]{0:T(128)S(6)} %copy.13.refs_0_, bf16[2,16,2,32,512]{4,3,2,1,0:T(8,128)(2,1)} %bitcast.7, bf16[256,512]{1,0:T(8,128)(2,1)S(1)} %get-tuple-element.113.refs_2_, ...), custom_call_target="tpu_custom_call" | custom-call | tf_op jit(solution)/shard_map/inner_s/pallas_call | solution.py:70
  68.4 1.9 %collective-permute-done.10.refs_1_ = bf16[16,32,512]{2,1,0:T(8,128)(2,1)S(1)} collective-permute-done((bf16[16,32,512]{2,1,0:T(8,128)(2,1)S(1)}, bf16[16,32,512]{2,1,0:T(8,128)(2,1)S(1)}, u32[]{:S(2)}, u32[]{:S(2)}) %collective-permute-start.10) | collective-permute-done | bytes 524320 | tf_op jit(solution)/shard_map/ppermute | solution.py:424
  70.4 1.6 collective-permute-start.11
  72.0 5.6 %collective-permute-done.13.refs_3_ = bf16[256,1536]{1,0:T(8,128)(2,1)S(1)} collective-permute-done((bf16[256,1536]{1,0:T(8,128)(2,1)S(1)}, bf16[256,1536]{1,0:T(8,128)(2,1)S(1)}, u32[]{:S(2)}, u32[]{:S(2)}) %collective-permute-start.13) | collective-permute-done | bytes 786464 | tf_op jit(solution)/shard_map/ppermute | solution.py:424
  79.8 1.8 %collective-permute-start.19 = (bf16[2,512,256]{2,1,0:T(8,128)(2,1)S(1)}, bf16[2,512,256]{2,1,0:T(8,128)(2,1)S(1)}, u32[]{:S(2)}, u32[]{:S(2)}) collective-permute-start(bf16[2,512,256]{2,1,0:T(8,128)(2,1)S(1)} %get-tuple-element.156), channel_id=1, source_target_pairs={{0,1},{1,0},{2,3},{3,2},{4,5},{5,4},{6,7},{7,6},{8,9},{9,8},{10,11... | collective-permute-start | bytes 1572872 | tf_op jit(solution)/shard_map/ppermute | solution.py:424
  81.6 2.0 %collective-permute-start.18 = (bf16[2,512,256]{2,1,0:T(8,128)(2,1)S(1)}, bf16[2,512,256]{2,1,0:T(8,128)(2,1)S(1)}, u32[]{:S(2)}, u32[]{:S(2)}) collective-permute-start(bf16[2,512,256]{2,1,0:T(8,128)(2,1)S(1)} %get-tuple-element.154), channel_id=1, source_target_pairs={{0,3},{1,2},{2,1},{3,0},{4,7},{5,6},{6,5},{7,4},{8,11},{9,10},{10,... | collective-permute-start | bytes 1572872 | tf_op jit(solution)/shard_map/ppermute | solution.py:424
  84.7 1.1 keep_b_o.1
  85.9 2.8 %collective-permute-start.14 = (bf16[4,32,512]{2,1,0:T(8,128)(2,1)S(1)}, bf16[4,32,512]{2,1,0:T(8,128)(2,1)S(1)}, u32[]{:S(2)}, u32[]{:S(2)}) collective-permute-start(bf16[4,32,512]{2,1,0:T(8,128)(2,1)S(1)} %get-tuple-element.143), channel_id=1, source_target_pairs={{0,192},{8,200},{16,208},{24,216},{32,224},{40,232},{48,240},{56,2... | collective-permute-start | bytes 393224 | tf_op jit(solution)/shard_map/ppermute | solution.py:424
  88.7 3.4 %collective-permute-done.14.refs_1_ = bf16[4,32,512]{2,1,0:T(8,128)(2,1)S(1)} collective-permute-done((bf16[4,32,512]{2,1,0:T(8,128)(2,1)S(1)}, bf16[4,32,512]{2,1,0:T(8,128)(2,1)S(1)}, u32[]{:S(2)}, u32[]{:S(2)}) %collective-permute-start.14) | collective-permute-done | bytes 131104 | tf_op jit(solution)/shard_map/ppermute | solution.py:424
  92.2 2.2 %halves_o.1 = (bf16[2,256,512]{2,1,0:T(8,128)(2,1)S(1)}, bf16[2,256,512]{2,1,0:T(8,128)(2,1)S(1)}, bf16[256,512]{1,0:T(8,128)(2,1)S(1)}, bf16[256,512]{1,0:T(8,128)(2,1)S(1)}, bf16[8,128]{1,0:T(8,128)(2,1)}) custom-call(s32[1]{0:T(128)S(6)} %copy.13.refs_0_, bf16[2,256,8192]{2,1,0:T(8,128)(2,1)S(1)} %bitcast.4, ...), custom_call_target="tpu_custom_call" | custom-call | tf_op jit(solution)/shard_map/halves_o/pallas_call | solution.py:70
  95.5 3.3 %collective-permute-start.15 = (bf16[2,32,512]{2,1,0:T(8,128)(2,1)S(1)}, bf16[2,32,512]{2,1,0:T(8,128)(2,1)S(1)}, u32[]{:S(2)}, u32[]{:S(2)}) collective-permute-start(bf16[2,32,512]{2,1,0:T(8,128)(2,1)S(1)} %get-tuple-element.146), channel_id=1, source_target_pairs={{0,16},{8,24},{16,0},{24,8},{32,48},{40,56},{48,32},{56,40},{64,80... | collective-permute-start | bytes 196616 | tf_op jit(solution)/shard_map/ppermute | solution.py:424
  99.5 1.8 %collective-permute-done.15.refs_1_.refs_3_ = bf16[2,32,512]{2,1,0:T(8,128)(2,1)S(1)} collective-permute-done((bf16[2,32,512]{2,1,0:T(8,128)(2,1)S(1)}, bf16[2,32,512]{2,1,0:T(8,128)(2,1)S(1)}, u32[]{:S(2)}, u32[]{:S(2)}) %collective-permute-start.15) | collective-permute-done | bytes 65568 | tf_op jit(solution)/shard_map/ppermute | solution.py:424
  101.5 1.6 collective-permute-start.27
  103.2 4.3 %collective-permute-start.17 = (bf16[32,512]{1,0:T(8,128)(2,1)S(1)}, bf16[32,512]{1,0:T(8,128)(2,1)S(1)}, u32[]{:S(2)}, u32[]{:S(2)}) collective-permute-start(bf16[32,512]{1,0:T(8,128)(2,1)S(1)} %get-tuple-element.152), channel_id=1, source_target_pairs={{0,48},{8,56},{16,32},{24,40},{32,16},{40,24},{48,0},{56,8},{64,11... | collective-permute-start | bytes 98312 | tf_op jit(solution)/shard_map/ppermute | solution.py:424
  107.5 7.8 %collective-permute-done.17.refs_4_ = bf16[32,512]{1,0:T(8,128)(2,1)S(1)} collective-permute-done((bf16[32,512]{1,0:T(8,128)(2,1)S(1)}, bf16[32,512]{1,0:T(8,128)(2,1)S(1)}, u32[]{:S(2)}, u32[]{:S(2)}) %collective-permute-start.17) | collective-permute-done | bytes 32800 | tf_op jit(solution)/shard_map/ppermute | solution.py:424
  116.0 4.8 %collective-permute-done.20.refs_1_ = bf16[32,512]{1,0:T(8,128)(2,1)S(1)} collective-permute-done((bf16[32,512]{1,0:T(8,128)(2,1)S(1)}, bf16[32,512]{1,0:T(8,128)(2,1)S(1)}, u32[]{:S(2)}, u32[]{:S(2)}) %collective-permute-start.20) | collective-permute-done | bytes 32800 | tf_op jit(solution)/shard_map/ppermute | solution.py:424
  120.9 2.1 %collective-permute-start.25 = (bf16[256,512]{1,0:T(8,128)(2,1)S(1)}, bf16[256,512]{1,0:T(8,128)(2,1)S(1)}, u32[]{:S(2)}, u32[]{:S(2)}) collective-permute-start(bf16[256,512]{1,0:T(8,128)(2,1)S(1)} %get-tuple-element.170), channel_id=1, source_target_pairs={{0,3},{1,2},{2,1},{3,0},{4,7},{5,6},{6,5},{7,4},{8,11},{9,10},{10,... | collective-permute-start | bytes 786440 | tf_op jit(solution)/shard_map/ppermute | solution.py:424
  123.0 2.4 %collective-permute-start.26 = (bf16[256,512]{1,0:T(8,128)(2,1)S(1)}, bf16[256,512]{1,0:T(8,128)(2,1)S(1)}, u32[]{:S(2)}, u32[]{:S(2)}) collective-permute-start(bf16[256,512]{1,0:T(8,128)(2,1)S(1)} %get-tuple-element.172), channel_id=1, source_target_pairs={{0,1},{1,0},{2,3},{3,2},{4,5},{5,4},{6,7},{7,6},{8,9},{9,8},{10,11... | collective-permute-start | bytes 786440 | tf_op jit(solution)/shard_map/ppermute | solution.py:424
  125.4 6.4 %collective-permute-done.21.refs_1_ = bf16[2,32,512]{2,1,0:T(8,128)(2,1)S(1)} collective-permute-done((bf16[2,32,512]{2,1,0:T(8,128)(2,1)S(1)}, bf16[2,32,512]{2,1,0:T(8,128)(2,1)S(1)}, u32[]{:S(2)}, u32[]{:S(2)}) %collective-permute-start.21) | collective-permute-done | bytes 65568 | tf_op jit(solution)/shard_map/ppermute | solution.py:424
  131.8 3.0 %inner_o.1 = (bf16[16,2,32,512]{3,2,1,0:T(8,128)(2,1)S(1)}, bf16[16,32,512]{2,1,0:T(8,128)(2,1)S(1)}, bf16[2,16,2,32,512]{4,3,2,1,0:T(8,128)(2,1)}, bf16[8,128]{1,0:T(8,128)(2,1)}) custom-call(s32[1]{0:T(128)S(6)} %copy.13.refs_0_, bf16[2,16,2,32,512]{4,3,2,1,0:T(8,128)(2,1)} %bitcast.8, bf16[256,512]{1,0:T(8,128)(2,1)S(1)} %get-tuple-element.169.refs_2_, ...), custom_call_target="tpu_custom_call" | custom-call | tf_op jit(solution)/shard_map/inner_o/pallas_call | solution.py:70
  134.9 2.8 %collective-permute-start.24 = (bf16[4,32,512]{2,1,0:T(8,128)(2,1)S(1)}, bf16[4,32,512]{2,1,0:T(8,128)(2,1)S(1)}, u32[]{:S(2)}, u32[]{:S(2)}) collective-permute-start(bf16[4,32,512]{2,1,0:T(8,128)(2,1)S(1)} %get-tuple-element.168.refs_0_), channel_id=1, source_target_pairs={{0,192},{8,200},{16,208},{24,216},{32,224},{40,232},{48,240},{56,2... | collective-permute-start | bytes 393224 | tf_op jit(solution)/shard_map/ppermute | solution.py:424
  137.8 4.3 %collective-permute-done.24.refs_1_ = bf16[4,32,512]{2,1,0:T(8,128)(2,1)S(1)} collective-permute-done((bf16[4,32,512]{2,1,0:T(8,128)(2,1)S(1)}, bf16[4,32,512]{2,1,0:T(8,128)(2,1)S(1)}, u32[]{:S(2)}, u32[]{:S(2)}) %collective-permute-start.24) | collective-permute-done | bytes 131104 | tf_op jit(solution)/shard_map/ppermute | solution.py:424
  142.3 7.7 %collective-permute-done.28.refs_1_ = bf16[2,4,32,512]{3,2,1,0:T(8,128)(2,1)S(1)} collective-permute-done((bf16[2,4,32,512]{3,2,1,0:T(8,128)(2,1)S(1)}, bf16[2,4,32,512]{3,2,1,0:T(8,128)(2,1)S(1)}, u32[]{:S(2)}, u32[]{:S(2)}) %collective-permute-start.28) | collective-permute-done | bytes 262176 | tf_op jit(solution)/shard_map/ppermute | solution.py:424
  150.5 8.4 %collective-permute-done.31.refs_1_.refs_3_ = bf16[2,4,32,512]{3,2,1,0:T(8,128)(2,1)S(1)} collective-permute-done((bf16[2,4,32,512]{3,2,1,0:T(8,128)(2,1)S(1)}, bf16[2,4,32,512]{3,2,1,0:T(8,128)(2,1)S(1)}, u32[]{:S(2)}, u32[]{:S(2)}) %collective-permute-start.31) | collective-permute-done | bytes 262176 | tf_op jit(solution)/shard_map/ppermute | solution.py:424
  158.9 2.8 %collective-permute-start.32 = (bf16[4,32,512]{2,1,0:T(8,128)(2,1)S(1)}, bf16[4,32,512]{2,1,0:T(8,128)(2,1)S(1)}, u32[]{:S(2)}, u32[]{:S(2)}) collective-permute-start(bf16[4,32,512]{2,1,0:T(8,128)(2,1)S(1)} %get-tuple-element.191), channel_id=1, source_target_pairs={{0,192},{8,200},{16,208},{24,216},{32,224},{40,232},{48,240},{56,2... | collective-permute-start | bytes 393224 | tf_op jit(solution)/shard_map/ppermute | solution.py:424
  161.8 1.4 mix.1
  163.2 2.1 %collective-permute-done.32.refs_1_ = bf16[4,32,512]{2,1,0:T(8,128)(2,1)S(1)} collective-permute-done((bf16[4,32,512]{2,1,0:T(8,128)(2,1)S(1)}, bf16[4,32,512]{2,1,0:T(8,128)(2,1)S(1)}, u32[]{:S(2)}, u32[]{:S(2)}) %collective-permute-start.32) | collective-permute-done | bytes 131104 | tf_op jit(solution)/shard_map/ppermute | solution.py:424
  165.4 5.2 %collective-permute-done.33.refs_1_.refs_3_ = bf16[2,32,512]{2,1,0:T(8,128)(2,1)S(1)} collective-permute-done((bf16[2,32,512]{2,1,0:T(8,128)(2,1)S(1)}, bf16[2,32,512]{2,1,0:T(8,128)(2,1)S(1)}, u32[]{:S(2)}, u32[]{:S(2)}) %collective-permute-start.33) | collective-permute-done | bytes 65568 | tf_op jit(solution)/shard_map/ppermute | solution.py:424
  170.7 6.0 %collective-permute-done.34.refs_3_ = bf16[32,512]{1,0:T(8,128)(2,1)S(1)} collective-permute-done((bf16[32,512]{1,0:T(8,128)(2,1)S(1)}, bf16[32,512]{1,0:T(8,128)(2,1)S(1)}, u32[]{:S(2)}, u32[]{:S(2)}) %collective-permute-start.34) | collective-permute-done | bytes 32800 | tf_op jit(solution)/shard_map/ppermute | solution.py:424
  (68 shorter events, 14.0 us)
Async XLA Ops:
  1.3 0.7 copy-start.2
  2.0 21.3 %slice-start = ((s8[8388608]{0:T(1024)(128)(4,1)}), s8[4194304]{0:T(1024)(128)(4,1)S(1)}, s32[]{:S(2)}) async-start(s8[8388608]{0:T(1024)(128)(4,1)} %bitcast.3), calls=%async_computation | async-start | bytes 8388608
  3.9 19.4 %collective-permute-start.2 = (bf16[256,1536]{1,0:T(8,128)(2,1)S(1)}, bf16[256,1536]{1,0:T(8,128)(2,1)S(1)}, u32[]{:S(2)}, u32[]{:S(2)}) collective-permute-start(bf16[256,1536]{1,0:T(8,128)(2,1)S(1)} %get-tuple-element.105), channel_id=1, source_target_pairs={{0,1},{1,0},{2,3},{3,2},{4,5},{5,4},{6,7},{7,6},{8,9},{9,8},{10,11... | collective-permute-start | bytes 2359304 | tf_op jit(solution)/shard_map/ppermute | solution.py:424
  6.2 18.2 %collective-permute-start.1 = (bf16[256,1536]{1,0:T(8,128)(2,1)S(1)}, bf16[256,1536]{1,0:T(8,128)(2,1)S(1)}, u32[]{:S(2)}, u32[]{:S(2)}) collective-permute-start(bf16[256,1536]{1,0:T(8,128)(2,1)S(1)} %get-tuple-element.104), channel_id=1, source_target_pairs={{0,3},{1,2},{2,1},{3,0},{4,7},{5,6},{6,5},{7,4},{8,11},{9,10},{10,... | collective-permute-start | bytes 2359304 | tf_op jit(solution)/shard_map/ppermute | solution.py:424
  6.8 16.4 %slice-start.1 = ((s8[8388608]{0:T(1024)(128)(4,1)}), s8[4194304]{0:T(1024)(128)(4,1)S(1)}, s32[]{:S(2)}) async-start(s8[8388608]{0:T(1024)(128)(4,1)} %bitcast.3), calls=%async_computation.1 | async-start | bytes 8388608
  6.8 30.1 %collective-permute-start = (bf16[256,2560]{1,0:T(8,128)(2,1)S(1)}, bf16[256,2560]{1,0:T(8,128)(2,1)S(1)}, u32[]{:S(2)}, u32[]{:S(2)}) collective-permute-start(bf16[256,2560]{1,0:T(8,128)(2,1)S(1)} %get-tuple-element.103), channel_id=1, source_target_pairs={{0,4},{1,5},{2,6},{3,7},{4,0},{5,1},{6,2},{7,3},{8,12},{9,13},{10,... | collective-permute-start | bytes 3932168 | tf_op jit(solution)/shard_map/ppermute | solution.py:424
  25.4 14.6 %collective-permute-start.6 = (bf16[2,512,256]{2,1,0:T(8,128)(2,1)S(1)}, bf16[2,512,256]{2,1,0:T(8,128)(2,1)S(1)}, u32[]{:S(2)}, u32[]{:S(2)}) collective-permute-start(bf16[2,512,256]{2,1,0:T(8,128)(2,1)S(1)} %get-tuple-element.121), channel_id=1, source_target_pairs={{0,1},{1,0},{2,3},{3,2},{4,5},{5,4},{6,7},{7,6},{8,9},{9,8},{10,11... | collective-permute-start | bytes 1572872 | tf_op jit(solution)/shard_map/ppermute | solution.py:424
  27.4 12.7 %collective-permute-start.5 = (bf16[2,512,256]{2,1,0:T(8,128)(2,1)S(1)}, bf16[2,512,256]{2,1,0:T(8,128)(2,1)S(1)}, u32[]{:S(2)}, u32[]{:S(2)}) collective-permute-start(bf16[2,512,256]{2,1,0:T(8,128)(2,1)S(1)} %get-tuple-element.119), channel_id=1, source_target_pairs={{0,3},{1,2},{2,1},{3,0},{4,7},{5,6},{6,5},{7,4},{8,11},{9,10},{10,... | collective-permute-start | bytes 1572872 | tf_op jit(solution)/shard_map/ppermute | solution.py:424
  40.2 14.9 %collective-permute-start.7 = (bf16[2,512,256]{2,1,0:T(8,128)(2,1)S(1)}, bf16[2,512,256]{2,1,0:T(8,128)(2,1)S(1)}, u32[]{:S(2)}, u32[]{:S(2)}) collective-permute-start(bf16[2,512,256]{2,1,0:T(8,128)(2,1)S(1)} %get-tuple-element.123), channel_id=1, source_target_pairs={{0,4},{1,5},{2,6},{3,7},{4,0},{5,1},{6,2},{7,3},{8,12},{9,13},{10,... | collective-permute-start | bytes 1572872 | tf_op jit(solution)/shard_map/ppermute | solution.py:424
  42.0 13.1 %collective-permute-start.3 = (bf16[2,256,512]{2,1,0:T(8,128)(2,1)S(1)}, bf16[2,256,512]{2,1,0:T(8,128)(2,1)S(1)}, u32[]{:S(2)}, u32[]{:S(2)}) collective-permute-start(bf16[2,256,512]{2,1,0:T(8,128)(2,1)S(1)} %get-tuple-element.114), channel_id=1, source_target_pairs={{0,1},{1,0},{2,3},{3,2},{4,5},{5,4},{6,7},{7,6},{8,9},{9,8},{10,11... | collective-permute-start | bytes 1572872 | tf_op jit(solution)/shard_map/ppermute | solution.py:424
  43.4 11.9 %collective-permute-start.4 = (bf16[2,256,512]{2,1,0:T(8,128)(2,1)S(1)}, bf16[2,256,512]{2,1,0:T(8,128)(2,1)S(1)}, u32[]{:S(2)}, u32[]{:S(2)}) collective-permute-start(bf16[2,256,512]{2,1,0:T(8,128)(2,1)S(1)} %get-tuple-element.117), channel_id=1, source_target_pairs={{0,3},{1,2},{2,1},{3,0},{4,7},{5,6},{6,5},{7,4},{8,11},{9,10},{10,... | collective-permute-start | bytes 1572872 | tf_op jit(solution)/shard_map/ppermute | solution.py:424
  45.0 47.2 %collective-permute-start.16 = (bf16[256,2560]{1,0:T(8,128)(2,1)S(1)}, bf16[256,2560]{1,0:T(8,128)(2,1)S(1)}, u32[]{:S(2)}, u32[]{:S(2)}) collective-permute-start(bf16[256,2560]{1,0:T(8,128)(2,1)S(1)} %get-tuple-element.147), channel_id=1, source_target_pairs={{0,4},{1,5},{2,6},{3,7},{4,0},{5,1},{6,2},{7,3},{8,12},{9,13},{10,... | collective-permute-start | bytes 3932168 | tf_op jit(solution)/shard_map/ppermute | solution.py:424
  55.4 9.3 %collective-permute-start.8 = (bf16[256,512]{1,0:T(8,128)(2,1)S(1)}, bf16[256,512]{1,0:T(8,128)(2,1)S(1)}, u32[]{:S(2)}, u32[]{:S(2)}) collective-permute-start(bf16[256,512]{1,0:T(8,128)(2,1)S(1)} %get-tuple-element.125), channel_id=1, source_target_pairs={{0,3},{1,2},{2,1},{3,0},{4,7},{5,6},{6,5},{7,4},{8,11},{9,10},{10,... | collective-permute-start | bytes 786440 | tf_op jit(solution)/shard_map/ppermute | solution.py:424
  57.1 9.2 %collective-permute-start.9 = (bf16[256,512]{1,0:T(8,128)(2,1)S(1)}, bf16[256,512]{1,0:T(8,128)(2,1)S(1)}, u32[]{:S(2)}, u32[]{:S(2)}) collective-permute-start(bf16[256,512]{1,0:T(8,128)(2,1)S(1)} %get-tuple-element.127), channel_id=1, source_target_pairs={{0,1},{1,0},{2,3},{3,2},{4,5},{5,4},{6,7},{7,6},{8,9},{9,8},{10,11... | collective-permute-start | bytes 786440 | tf_op jit(solution)/shard_map/ppermute | solution.py:424
  58.8 18.9 %collective-permute-start.13 = (bf16[256,1536]{1,0:T(8,128)(2,1)S(1)}, bf16[256,1536]{1,0:T(8,128)(2,1)S(1)}, u32[]{:S(2)}, u32[]{:S(2)}) collective-permute-start(bf16[256,1536]{1,0:T(8,128)(2,1)S(1)} %get-tuple-element.136), channel_id=1, source_target_pairs={{0,1},{1,0},{2,3},{3,2},{4,5},{5,4},{6,7},{7,6},{8,9},{9,8},{10,11... | collective-permute-start | bytes 2359304 | tf_op jit(solution)/shard_map/ppermute | solution.py:424
  59.1 19.6 %collective-permute-start.12 = (bf16[256,1536]{1,0:T(8,128)(2,1)S(1)}, bf16[256,1536]{1,0:T(8,128)(2,1)S(1)}, u32[]{:S(2)}, u32[]{:S(2)}) collective-permute-start(bf16[256,1536]{1,0:T(8,128)(2,1)S(1)} %get-tuple-element.135), channel_id=1, source_target_pairs={{0,3},{1,2},{2,1},{3,0},{4,7},{5,6},{6,5},{7,4},{8,11},{9,10},{10,... | collective-permute-start | bytes 2359304 | tf_op jit(solution)/shard_map/ppermute | solution.py:424
  68.3 2.0 %collective-permute-start.10 = (bf16[16,32,512]{2,1,0:T(8,128)(2,1)S(1)}, bf16[16,32,512]{2,1,0:T(8,128)(2,1)S(1)}, u32[]{:S(2)}, u32[]{:S(2)}) collective-permute-start(bf16[16,32,512]{2,1,0:T(8,128)(2,1)S(1)} %get-tuple-element.130), channel_id=1, source_target_pairs={{0,8},{8,0},{16,24},{24,16},{32,40},{40,32},{48,56},{56,48},{64,72... | collective-permute-start | bytes 1572872 | tf_op jit(solution)/shard_map/ppermute | solution.py:424
  70.4 15.4 %collective-permute-start.11 = (bf16[2,4,32,512]{3,2,1,0:T(8,128)(2,1)S(1)}, bf16[2,4,32,512]{3,2,1,0:T(8,128)(2,1)S(1)}, u32[]{:S(2)}, u32[]{:S(2)}) collective-permute-start(bf16[2,4,32,512]{3,2,1,0:T(8,128)(2,1)S(1)} %get-tuple-element.133), channel_id=1, source_target_pairs={{0,64},{8,72},{16,80},{24,88},{32,96},{40,104},{48,112},{56,120},{... | collective-permute-start | bytes 786440 | tf_op jit(solution)/shard_map/ppermute | solution.py:424
  79.8 21.6 %collective-permute-start.19 = (bf16[2,512,256]{2,1,0:T(8,128)(2,1)S(1)}, bf16[2,512,256]{2,1,0:T(8,128)(2,1)S(1)}, u32[]{:S(2)}, u32[]{:S(2)}) collective-permute-start(bf16[2,512,256]{2,1,0:T(8,128)(2,1)S(1)} %get-tuple-element.156), channel_id=1, source_target_pairs={{0,1},{1,0},{2,3},{3,2},{4,5},{5,4},{6,7},{7,6},{8,9},{9,8},{10,11... | collective-permute-start | bytes 1572872 | tf_op jit(solution)/shard_map/ppermute | solution.py:424
  81.6 19.8 %collective-permute-start.18 = (bf16[2,512,256]{2,1,0:T(8,128)(2,1)S(1)}, bf16[2,512,256]{2,1,0:T(8,128)(2,1)S(1)}, u32[]{:S(2)}, u32[]{:S(2)}) collective-permute-start(bf16[2,512,256]{2,1,0:T(8,128)(2,1)S(1)} %get-tuple-element.154), channel_id=1, source_target_pairs={{0,3},{1,2},{2,1},{3,0},{4,7},{5,6},{6,5},{7,4},{8,11},{9,10},{10,... | collective-permute-start | bytes 1572872 | tf_op jit(solution)/shard_map/ppermute | solution.py:424
  85.9 6.3 %collective-permute-start.14 = (bf16[4,32,512]{2,1,0:T(8,128)(2,1)S(1)}, bf16[4,32,512]{2,1,0:T(8,128)(2,1)S(1)}, u32[]{:S(2)}, u32[]{:S(2)}) collective-permute-start(bf16[4,32,512]{2,1,0:T(8,128)(2,1)S(1)} %get-tuple-element.143), channel_id=1, source_target_pairs={{0,192},{8,200},{16,208},{24,216},{32,224},{40,232},{48,240},{56,2... | collective-permute-start | bytes 393224 | tf_op jit(solution)/shard_map/ppermute | solution.py:424
  94.4 26.3 %collective-permute-start.22 = (bf16[2,256,512]{2,1,0:T(8,128)(2,1)S(1)}, bf16[2,256,512]{2,1,0:T(8,128)(2,1)S(1)}, u32[]{:S(2)}, u32[]{:S(2)}) collective-permute-start(bf16[2,256,512]{2,1,0:T(8,128)(2,1)S(1)} %get-tuple-element.163), channel_id=1, source_target_pairs={{0,1},{1,0},{2,3},{3,2},{4,5},{5,4},{6,7},{7,6},{8,9},{9,8},{10,11... | collective-permute-start | bytes 1572872 | tf_op jit(solution)/shard_map/ppermute | solution.py:424
  95.4 25.4 %collective-permute-start.23 = (bf16[2,256,512]{2,1,0:T(8,128)(2,1)S(1)}, bf16[2,256,512]{2,1,0:T(8,128)(2,1)S(1)}, u32[]{:S(2)}, u32[]{:S(2)}) collective-permute-start(bf16[2,256,512]{2,1,0:T(8,128)(2,1)S(1)} %get-tuple-element.165), channel_id=1, source_target_pairs={{0,3},{1,2},{2,1},{3,0},{4,7},{5,6},{6,5},{7,4},{8,11},{9,10},{10,... | collective-permute-start | bytes 1572872 | tf_op jit(solution)/shard_map/ppermute | solution.py:424
  95.5 5.9 %collective-permute-start.15 = (bf16[2,32,512]{2,1,0:T(8,128)(2,1)S(1)}, bf16[2,32,512]{2,1,0:T(8,128)(2,1)S(1)}, u32[]{:S(2)}, u32[]{:S(2)}) collective-permute-start(bf16[2,32,512]{2,1,0:T(8,128)(2,1)S(1)} %get-tuple-element.146), channel_id=1, source_target_pairs={{0,16},{8,24},{16,0},{24,8},{32,48},{40,56},{48,32},{56,40},{64,80... | collective-permute-start | bytes 196616 | tf_op jit(solution)/shard_map/ppermute | solution.py:424
  99.5 15.8 %copy-start = (f32[2,32,512]{2,1,0:T(8,128)S(1)}, f32[2,32,512]{2,1,0:T(8,128)}, u32[]{:S(2)}) copy-start(f32[2,32,512]{2,1,0:T(8,128)} %refs_1_.27) | copy-start | bytes 393220
  99.5 15.7 %copy-start.1 = (f32[32,512]{1,0:T(8,128)S(1)}, f32[32,512]{1,0:T(8,128)}, u32[]{:S(2)}) copy-start(f32[32,512]{1,0:T(8,128)} %refs_2_.5) | copy-start | bytes 196612
  101.5 30.3 %collective-permute-start.27 = (bf16[2,512,256]{2,1,0:T(8,128)(2,1)S(1)}, bf16[2,512,256]{2,1,0:T(8,128)(2,1)S(1)}, u32[]{:S(2)}, u32[]{:S(2)}) collective-permute-start(bf16[2,512,256]{2,1,0:T(8,128)(2,1)S(1)} %get-tuple-element.173), channel_id=1, source_target_pairs={{0,4},{1,5},{2,6},{3,7},{4,0},{5,1},{6,2},{7,3},{8,12},{9,13},{10,... | collective-permute-start | bytes 1572872 | tf_op jit(solution)/shard_map/ppermute | solution.py:424
  103.2 12.1 %collective-permute-start.17 = (bf16[32,512]{1,0:T(8,128)(2,1)S(1)}, bf16[32,512]{1,0:T(8,128)(2,1)S(1)}, u32[]{:S(2)}, u32[]{:S(2)}) collective-permute-start(bf16[32,512]{1,0:T(8,128)(2,1)S(1)} %get-tuple-element.152), channel_id=1, source_target_pairs={{0,48},{8,56},{16,32},{24,40},{32,16},{40,24},{48,0},{56,8},{64,11... | collective-permute-start | bytes 98312 | tf_op jit(solution)/shard_map/ppermute | solution.py:424
  116.0 4.8 %collective-permute-start.20 = (bf16[32,512]{1,0:T(8,128)(2,1)S(1)}, bf16[32,512]{1,0:T(8,128)(2,1)S(1)}, u32[]{:S(2)}, u32[]{:S(2)}) collective-permute-start(bf16[32,512]{1,0:T(8,128)(2,1)S(1)} %get-tuple-element.159.refs_0_), channel_id=1, source_target_pairs={{0,16},{8,24},{16,0},{24,8},{32,48},{40,56},{48,32},{56,40},{64,80... | collective-permute-start | bytes 98312 | tf_op jit(solution)/shard_map/ppermute | solution.py:424
  120.9 10.9 %collective-permute-start.25 = (bf16[256,512]{1,0:T(8,128)(2,1)S(1)}, bf16[256,512]{1,0:T(8,128)(2,1)S(1)}, u32[]{:S(2)}, u32[]{:S(2)}) collective-permute-start(bf16[256,512]{1,0:T(8,128)(2,1)S(1)} %get-tuple-element.170), channel_id=1, source_target_pairs={{0,3},{1,2},{2,1},{3,0},{4,7},{5,6},{6,5},{7,4},{8,11},{9,10},{10,... | collective-permute-start | bytes 786440 | tf_op jit(solution)/shard_map/ppermute | solution.py:424
  123.0 8.8 %collective-permute-start.26 = (bf16[256,512]{1,0:T(8,128)(2,1)S(1)}, bf16[256,512]{1,0:T(8,128)(2,1)S(1)}, u32[]{:S(2)}, u32[]{:S(2)}) collective-permute-start(bf16[256,512]{1,0:T(8,128)(2,1)S(1)} %get-tuple-element.172), channel_id=1, source_target_pairs={{0,1},{1,0},{2,3},{3,2},{4,5},{5,4},{6,7},{7,6},{8,9},{9,8},{10,11... | collective-permute-start | bytes 786440 | tf_op jit(solution)/shard_map/ppermute | solution.py:424
  125.4 6.4 %collective-permute-start.21 = (bf16[2,32,512]{2,1,0:T(8,128)(2,1)S(1)}, bf16[2,32,512]{2,1,0:T(8,128)(2,1)S(1)}, u32[]{:S(2)}, u32[]{:S(2)}) collective-permute-start(bf16[2,32,512]{2,1,0:T(8,128)(2,1)S(1)} %get-tuple-element.161.refs_0_), channel_id=1, source_target_pairs={{0,48},{8,56},{16,32},{24,40},{32,16},{40,24},{48,0},{56,8},{64,11... | collective-permute-start | bytes 196616 | tf_op jit(solution)/shard_map/ppermute | solution.py:424
  134.8 7.4 %collective-permute-start.29 = (bf16[16,32,512]{2,1,0:T(8,128)(2,1)S(1)}, bf16[16,32,512]{2,1,0:T(8,128)(2,1)S(1)}, u32[]{:S(2)}, u32[]{:S(2)}) collective-permute-start(bf16[16,32,512]{2,1,0:T(8,128)(2,1)S(1)} %get-tuple-element.178), channel_id=1, source_target_pairs={{0,8},{8,0},{16,24},{24,16},{32,40},{40,32},{48,56},{56,48},{64,72... | collective-permute-start | bytes 1572872 | tf_op jit(solution)/shard_map/ppermute | solution.py:424
  134.9 7.1 %collective-permute-start.24 = (bf16[4,32,512]{2,1,0:T(8,128)(2,1)S(1)}, bf16[4,32,512]{2,1,0:T(8,128)(2,1)S(1)}, u32[]{:S(2)}, u32[]{:S(2)}) collective-permute-start(bf16[4,32,512]{2,1,0:T(8,128)(2,1)S(1)} %get-tuple-element.168.refs_0_), channel_id=1, source_target_pairs={{0,192},{8,200},{16,208},{24,216},{32,224},{40,232},{48,240},{56,2... | collective-permute-start | bytes 393224 | tf_op jit(solution)/shard_map/ppermute | solution.py:424
  142.1 7.9 %collective-permute-start.28 = (bf16[2,4,32,512]{3,2,1,0:T(8,128)(2,1)S(1)}, bf16[2,4,32,512]{3,2,1,0:T(8,128)(2,1)S(1)}, u32[]{:S(2)}, u32[]{:S(2)}) collective-permute-start(bf16[2,4,32,512]{3,2,1,0:T(8,128)(2,1)S(1)} %get-tuple-element.176.refs_0_), channel_id=1, source_target_pairs={{0,64},{8,72},{16,80},{24,88},{32,96},{40,104},{48,112},{56,120},{... | collective-permute-start | bytes 786440 | tf_op jit(solution)/shard_map/ppermute | solution.py:424
  150.1 11.7 %collective-permute-start.30 = (bf16[16,32,512]{2,1,0:T(8,128)(2,1)S(1)}, bf16[16,32,512]{2,1,0:T(8,128)(2,1)S(1)}, u32[]{:S(2)}, u32[]{:S(2)}) collective-permute-start(bf16[16,32,512]{2,1,0:T(8,128)(2,1)S(1)} %get-tuple-element.181.refs_2_), channel_id=1, source_target_pairs={{0,8},{8,0},{16,24},{24,16},{32,40},{40,32},{48,56},{56,48},{64,72... | collective-permute-start | bytes 1572872 | tf_op jit(solution)/shard_map/ppermute | solution.py:424
  150.2 8.7 %collective-permute-start.31 = (bf16[2,4,32,512]{3,2,1,0:T(8,128)(2,1)S(1)}, bf16[2,4,32,512]{3,2,1,0:T(8,128)(2,1)S(1)}, u32[]{:S(2)}, u32[]{:S(2)}) collective-permute-start(bf16[2,4,32,512]{3,2,1,0:T(8,128)(2,1)S(1)} %get-tuple-element.184), channel_id=1, source_target_pairs={{0,64},{8,72},{16,80},{24,88},{32,96},{40,104},{48,112},{56,120},{... | collective-permute-start | bytes 786440 | tf_op jit(solution)/shard_map/ppermute | solution.py:424
  158.9 6.3 %collective-permute-start.32 = (bf16[4,32,512]{2,1,0:T(8,128)(2,1)S(1)}, bf16[4,32,512]{2,1,0:T(8,128)(2,1)S(1)}, u32[]{:S(2)}, u32[]{:S(2)}) collective-permute-start(bf16[4,32,512]{2,1,0:T(8,128)(2,1)S(1)} %get-tuple-element.191), channel_id=1, source_target_pairs={{0,192},{8,200},{16,208},{24,216},{32,224},{40,232},{48,240},{56,2... | collective-permute-start | bytes 393224 | tf_op jit(solution)/shard_map/ppermute | solution.py:424
  165.3 5.3 %collective-permute-start.33 = (bf16[2,32,512]{2,1,0:T(8,128)(2,1)S(1)}, bf16[2,32,512]{2,1,0:T(8,128)(2,1)S(1)}, u32[]{:S(2)}, u32[]{:S(2)}) collective-permute-start(bf16[2,32,512]{2,1,0:T(8,128)(2,1)S(1)} %get-tuple-element.194), channel_id=1, source_target_pairs={{0,16},{8,24},{16,0},{24,8},{32,48},{40,56},{48,32},{56,40},{64,80... | collective-permute-start | bytes 196616 | tf_op jit(solution)/shard_map/ppermute | solution.py:424
  170.6 6.1 %collective-permute-start.34 = (bf16[32,512]{1,0:T(8,128)(2,1)S(1)}, bf16[32,512]{1,0:T(8,128)(2,1)S(1)}, u32[]{:S(2)}, u32[]{:S(2)}) collective-permute-start(bf16[32,512]{1,0:T(8,128)(2,1)S(1)} %get-tuple-element.197), channel_id=1, source_target_pairs={{0,48},{8,56},{16,32},{24,40},{32,16},{40,24},{48,0},{56,8},{64,11... | collective-permute-start | bytes 98312 | tf_op jit(solution)/shard_map/ppermute | solution.py:424

commit v4 on v2

--- a/solution.py
+++ b/solution.py
@@ -83,7 +83,7 @@
     return pl.ds(pl.multiple_of(start, width), width)
 
 
-def pack_kernel(plan, tok, x, g, a1, b1, z1, a2, b2, z2, z3, gt_out, gin, gt, sems, gsems):
+def pack_kernel(plan, ids, x, g, a1, b1, z1, a2, b2, z3, gt_out, gin, gt, tok, sems, gsems):
     _, _, _, z, y = place()
     s = lax.rem(plan[0], 2)
     copies = []
@@ -97,14 +97,16 @@
         copies[-1].start()
 
     g_copies = [pltpu.make_async_copy(g.at[layer], gin.at[i], gsems.at[i]) for i, layer in enumerate((s, 1 - s))]
-    for c in g_copies:
+    ids_copy = pltpu.make_async_copy(ids, tok, gsems.at[9])
+    for c in (*g_copies, ids_copy):
         c.start()
     for zz, bufs in ((1 - z, (a1, b1)), (z, (a2, b2))):
         for buf, first, offset in ((bufs[0], y ^ 1, 0), (bufs[1], y ^ 3, HALF)):
             for i, yy in enumerate((first, y ^ 2)):
                 send(s, (zz * 4 + yy) * ROWS + offset, HALF, buf, i * HALF)
-    for j, buf, at in ((1, z1, 0), (2, z1, ROWS), (3, z2, 0), (0, z3, 0)):
+    for j, buf, at in ((1, z1, 0), (2, z1, ROWS), (3, z1, 2 * ROWS), (0, z3, 0)):
         send(1 - s, ((1 - z) * 4 + (y ^ j)) * ROWS, ROWS, buf, at)
+    ids_copy.wait()
     kept = (tok[...] != 0).astype(F32)
     last = []
 
@@ -112,7 +114,7 @@
         last.append(pltpu.make_async_copy(src, dst, gsems.at[2 + len(last)]))
         last[-1].start()
 
-    for i, bufs, at in ((0, (a1, b1), 2 * HALF), (1, (z1,), 2 * ROWS)):
+    for i, bufs, at in ((0, (a1, b1), 2 * HALF), (1, (z1,), 3 * ROWS)):
         g_copies[i].wait()
         gt[i] = (gin[i].astype(F32).T * kept).astype(BF16)
         for buf in bufs:
@@ -128,15 +130,16 @@
     half = in_vmem(TOK, 2 * HALF)
     return call(
         pack_kernel,
-        (wide, wide, in_vmem(TOK, 2 * ROWS + KV), half, half, half, half, in_vmem(2, KV, TOK)),
+        (wide, wide, in_vmem(TOK, 3 * ROWS + KV), half, half, half, in_vmem(2, KV, TOK)),
         (plan, tok, x, g),
-        [SM, VM, HBM, HBM],
-        [VM] * 8,
+        [SM, HBM, HBM, HBM],
+        [VM] * 7,
         [
             pltpu.VMEM((2, TOK, KV), BF16),
             pltpu.VMEM((2, KV, TOK), BF16),
+            pltpu.VMEM((1, TOK), jnp.int32),
             pltpu.SemaphoreType.DMA((12,)),
-            pltpu.SemaphoreType.DMA((9,)),
+            pltpu.SemaphoreType.DMA((10,)),
         ],
         name="pack",
         vmem=BIG,
@@ -231,17 +234,17 @@
 
 
 def inner_sync(plan, w, near, across):
-    def kernel(plan_ref, w_ref, near_ref, za_ref, zb_ref, inner_ref, send_ref, wv, sem, sem2):
+    def kernel(plan_ref, w_ref, near_ref, z_ref, inner_ref, send_ref, wv, sem, sem2):
         s = lax.rem(plan_ref[0], 2)
         core = place()[2]
         load = pltpu.make_async_copy(w_ref.at[s], wv, sem)
         load.start()
         load.wait()
-        for h, z_ref in enumerate((za_ref, zb_ref)):
+        for h in range(2):
             for q in range(4):
                 cols = pl.ds(q * 128, 128)
                 i = h * 8 + q * 2
-                gradient = flip(near_ref[h, :, cols], z_ref[:, cols])
+                gradient = flip(near_ref[h, :, cols], z_ref[h, :, cols])
                 inner_ref[i : i + 2] = stepped(wv[i : i + 2].reshape(128, KV), gradient).reshape(2, 2, 32, KV)
         out = pltpu.make_async_copy(inner_ref.at[:, 1 - core], send_ref, sem2)
         out.start()
@@ -250,8 +253,8 @@
     return call(
         kernel,
         (shape(*WORKERS), shape(16, 32, KV)),
-        (plan, w, near, *across),
-        [SM, HBM] + [VM] * 3,
+        (plan, w, near, across),
+        [SM, HBM] + [VM] * 2,
         [VM, ANY],
         [pltpu.VMEM(WORKERS, BF16), pltpu.SemaphoreType.DMA, pltpu.SemaphoreType.DMA],
         name="inner_sync",
@@ -371,24 +374,41 @@
     return call(kernel, (shape(16, 32, KV),), (own, got), [VM] * 2, [VM], name="block")
 
 
+def ahead(plan, anchors, momentum):
+    def kernel(plan_ref, anchor_ref, momentum_ref, out_ref):
+        anchor = anchor_ref[lax.rem(plan_ref[0], 2)]
+        out_ref[...] = (
+            (1.0 - outer_rate * (1.0 + outer_beta)) * anchor - outer_rate * outer_beta**2 * momentum_ref[...]
+        ).astype(BF16)
+
+    return call(kernel, (shape(32, KV),), (plan, anchors, momentum), [SM] + [VM] * 2, [VM], name="ahead")
+
+
+def new_rows(known, keep, recv):
+    def kernel(known_ref, a, b, out_ref):
+        mean = (a[...].astype(F32) + b[...].astype(F32)) / 32
+        out_ref[...] = (known_ref[...].astype(F32) + outer_rate * (1.0 + outer_beta) * mean).astype(BF16)
+
+    return call(kernel, (shape(*QUAD),), (known, keep, recv), [VM] * 3, [VM], name="new_rows")
+
+
 def outer_sync(plan, anchors, momentum, keep, recv):
-    def kernel(plan_ref, anchor_ref, momentum_ref, a, b, new_ref, moment_ref, short_ref):
+    def kernel(plan_ref, anchor_ref, momentum_ref, a, b, new_ref, moment_ref):
         s = lax.rem(plan_ref[0], 2)
-        mean = (a[...].astype(F32) + b[...].astype(F32)) / 32
+        zh = place()[1]
+        mean = (a[zh].astype(F32) + b[zh].astype(F32)) / 32
         anchor = anchor_ref[s]
         outer_grad = anchor - mean
         moment = outer_beta * momentum_ref[...] + outer_grad
-        new = anchor - outer_rate * (outer_grad + outer_beta * moment)
-        new_ref[...] = new
+        new_ref[...] = anchor - outer_rate * (outer_grad + outer_beta * moment)
         moment_ref[...] = moment
-        short_ref[...] = new.astype(BF16)
-
-    return call(
-        kernel,
-        (shape(32, KV, dtype=F32), shape(32, KV, dtype=F32), shape(32, KV)),
+
+    return call(
+        kernel,
+        (shape(32, KV, dtype=F32), shape(32, KV, dtype=F32)),
         (plan, anchors, momentum, keep, recv),
         [SM] + [VM] * 4,
-        [VM] * 3,
+        [VM] * 2,
         name="outer_sync",
     )
 
@@ -463,13 +483,12 @@
     CHAIN.token = None
     x = layer_inputs
     w = weights.reshape(2, *WORKERS)
-    a1, b1, z1, a2, b2, z2, z3, gt = pack(plan, token_ids.reshape(1, TOK), x, key_grads)
+    a1, b1, z1, a2, b2, z3, gt = pack(plan, token_ids.reshape(1, TOK), x, key_grads)
     got_a1 = swap(a1, "a")
     got_b1 = swap(b1, "b")
     got_z1 = swap(z1, "z")
     got_a2 = swap(a2, "a")
     got_b2 = swap(b2, "b")
-    got_z2 = swap(z2, "z")
     got_z3 = swap(z3, "z")
 
     def tile(name, far, flip_y, offset, at, recvs):
@@ -485,7 +504,7 @@
         return (lambda z, y: (z * 4 + (y ^ j)) * ROWS, source, at, targets)
 
     def other(name, pieces, outs, recvs, hint=0):
-        return product(name, 1, pieces, ROWS, outs, 2 * ROWS, plan, x, gt, recvs, hint)
+        return product(name, 1, pieces, ROWS, outs, 3 * ROWS, plan, x, gt, recvs, hint)
 
     lo, hi = (0, 256), (256, 512)
     half, pair = (256, ROWS), (2, 256, ROWS)
@@ -498,26 +517,25 @@
     near_b = swap(tile("send_b2", False, 1, HALF, 1, (got_b1, got_b2)), "a")
     keep_a2 = tile("keep_a2", False, 0, 0, 0, (got_a1, got_a2))
     keep_b2 = tile("keep_b2", False, 0, HALF, 0, (got_b1, got_b2))
-    send_0, stay_1 = other(
+    across = swap(
+        sums("far", [(2, KV, HALF)], [(keep_a1, far_a, None, None, 0, 0), (keep_b1, far_b, None, None, 0, 1)]), "z"
+    )
+    send_0, send_1, stay_0, stay_1 = other(
         "other_1",
-        [dest(2, 0, ROWS, [(0, 1, *lo)]), dest(1, 0, 0, [(0, 0, *lo), (1, None, *hi)])],
-        [pair, half],
+        [
+            dest(2, 0, ROWS, [(0, 1, *lo), (1, 1, *hi)]),
+            dest(1, 0, 0, [(0, 0, *lo), (3, None, *hi)]),
+            dest(3, 0, 2 * ROWS, [(1, 0, *hi), (2, None, *lo)]),
+        ],
+        [pair, pair, half, half],
         (got_z1,),
-    )
-    got_0 = swap(send_0, "a")
-    across = sums(
-        "far", [(KV, HALF)] * 2, [(keep_a1, far_a, None, None, 0, None), (keep_b1, far_b, None, None, 1, None)]
-    )
-    across = [swap(t, "z") for t in across]
+        10**10,
+    )
+    got_0, got_1 = swap(send_0, "a"), swap(send_1, "b")
     near = sums("near", [(2, KV, HALF)], [(keep_a2, near_a, None, None, 0, 0), (keep_b2, near_b, None, None, 0, 1)])
-    send_1, stay_0 = other(
-        "other_2",
-        [dest(2, 0, ROWS, [(0, 1, *hi)]), dest(3, 1, 0, [(0, 0, *hi), (1, None, *lo)])],
-        [pair, half],
-        (got_z1, got_z2),
-        10**10,
-    )
-    got_1 = swap(send_1, "b")
+    known = ahead(plan, anchors, momentum)
+    known = join(known, swap(known, "z1"))
+    known = row_of(known, swap(known, "z3"))
 
     inner_s, send_s = inner_sync(plan, w, near, across)
     send, keep = sum_x(inner_s, swap(send_s, "core"), "sync_x1")
@@ -527,31 +545,30 @@
         "last", [half, half], [(stay_0, got_0, None, 1, 0, None), (stay_1, got_1, None, 1, 1, None)]
     )
     last_0, last_1 = swap(last_0, "b"), swap(last_1, "a")
-    send, keep = sum_z(keep, swap(send, "x3"), "sync_z1")
-    recv = swap(send, "z1")
+    keep = sums("sync_z1", [QUAD], [(keep, swap(send, "x3"), None, None, 0, None)])
+    recv = swap(keep, "z1")
     mine_0, mine_1 = other("other_3", [dest(0, 1, 0, [(0, None, *lo), (1, None, *hi)])], [half, half], (got_z1, got_z3))
-    send, keep = halve("sync_z3", (32, KV), keep, recv)
-    anchor_new, momentum_new, short = outer_sync(plan, anchors, momentum, keep, swap(send, "z3"))
-    short_far = swap(short, "z1")
-
+    keep = sums("sync_z3", [QUAD], [(keep, recv, None, None, 0, None)])
+    recv = swap(keep, "z3")
+    row = new_rows(known, keep, recv)
+    row_far = swap(row, "x3")
+    anchor_new, momentum_new = outer_sync(plan, anchors, momentum, keep, recv)
+
+    own = join(row, row_far)
+    got = swap(own, "x1")
     inner_o, send_o, new = inner_other(plan, w, (mine_0, got_0, last_0), (mine_1, got_1, last_1))
     core_o = swap(send_o, "core")
-    own = join(short, short_far)
     send, keep = sum_x(inner_o, core_o, "other_x1")
     recv = swap(send, "x1")
-    row = row_of(own, swap(own, "z3"))
-    row_far = swap(row, "x3")
+    block = block_of(own, got)
+    block_far = swap(block, "core")
     send, keep = halve("other_x3", QUAD, keep, recv)
     recv = swap(send, "x3")
-    own = join(row, row_far)
-    got = swap(own, "x1")
+    new = mix(plan, inner_s, block, block_far, new)
     send, keep = sum_z(keep, recv, "other_z1")
     recv = swap(send, "z1")
-    block = block_of(own, got)
-    block_far = swap(block, "core")
     send, keep = halve("other_z3", (32, KV), keep, recv)
     recv = swap(send, "z3")
-    new = mix(plan, inner_s, block, block_far, new)
     pending = outer_other(plan, anchors, keep, recv)
     return (new.reshape(1, 2, ROWS, KV), anchor_new, momentum_new, pending)
 

time: 154 us -> 162 us (1.052)
  waiting for transfers between devices: 71.9 us -> 88.4 us
  starting transfers between devices: 57.3 us -> 50.7 us
    ppermute x32 -> x30, waiting for transfers between devices: 71.9 us -> 88.4 us  [swap(): return lax.ppermute(value, *MOVES[move])]
    ppermute x32 -> x30, starting transfers between devices: 57.3 us -> 50.7 us  [swap(): return lax.ppermute(value, *MOVES[move])]
    pallas_call x32 -> x33, Pallas kernels: 21.4 us -> 21.3 us  [call(): pl.pallas_call(chained, out_shape=outs + [in_hbm(8, 128)], in_specs=list(...]
  transfers between devices with their start and end apart: 32 -> 30, of which waited for: 19 -> 19; matrix products, arithmetic and copies ran while one was open for 0% -> 0% of each run, Pallas kernels for 10% -> 9%
where the time goes in v4:
time: 162 us
  waiting for transfers between devices  88.4 us (55%)
  starting transfers between devices  50.7 us (31%)
  Pallas kernels  21.3 us (13%)
    ppermute x30, waiting for transfers between devices, swap(): return lax.ppermute(value, *MOVES[move])  88.4 us
    ppermute x30, starting transfers between devices, swap(): return lax.ppermute(value, *MOVES[move])  50.7 us
    pallas_call x33, Pallas kernels, call(): pl.pallas_call(chained, out_shape=outs + [in_hbm(8, 128)], in_specs=list(...  21.3 us
  transfers between devices with their start and end apart: 30, of which 19 were waited for; matrix products, arithmetic and copies ran while one was open for 0% of the time, Pallas kernels for 9%

profile of v4, /device:TPU:8, one launch (start us, length us, event | category | flops | bytes accessed | tf_op | source)
XLA Modules:
  0.0 161.9 jit_solution(4447629237777290963)
XLA Ops:
  1.3 2.7 %pack.1 = (bf16[256,1536]{1,0:T(8,128)(2,1)S(1)}, bf16[256,1536]{1,0:T(8,128)(2,1)S(1)}, bf16[256,3584]{1,0:T(8,128)(2,1)S(1)}, bf16[256,1024]{1,0:T(8,128)(2,1)...) custom-call(s32[1]{0:T(128)S(6)} %copy.13.refs_0_, ...), custom_call_target="tpu_custom_call" | custom-call | tf_op jit(solution)/shard_map/pack/pallas_call | solution.py:68
  4.0 2.0 %collective-permute-start.6 = (bf16[256,3584]{1,0:T(8,128)(2,1)S(1)}, bf16[256,3584]{1,0:T(8,128)(2,1)S(1)}, u32[]{:S(2)}, u32[]{:S(2)}) collective-permute-start(bf16[256,3584]{1,0:T(8,128)(2,1)S(1)} %get-tuple-element.107), channel_id=1, source_target_pairs={{0,4},{1,5},{2,6},{3,7},{4,0},{5,1},{6,2},{7,3},{8,12},{9,13},{10,... | collective-permute-start | bytes 5505032 | tf_op jit(solution)/shard_map/ppermute | solution.py:479
  6.5 2.4 %collective-permute-start.2 = (bf16[256,1536]{1,0:T(8,128)(2,1)S(1)}, bf16[256,1536]{1,0:T(8,128)(2,1)S(1)}, u32[]{:S(2)}, u32[]{:S(2)}) collective-permute-start(bf16[256,1536]{1,0:T(8,128)(2,1)S(1)} %get-tuple-element.93), channel_id=1, source_target_pairs={{0,3},{1,2},{2,1},{3,0},{4,7},{5,6},{6,5},{7,4},{8,11},{9,10},{10,... | collective-permute-start | bytes 2359304 | tf_op jit(solution)/shard_map/ppermute | solution.py:479
  8.9 1.3 collective-permute-start.1
  10.7 15.8 %collective-permute-done.refs_3_ = bf16[256,1536]{1,0:T(8,128)(2,1)S(1)} collective-permute-done((bf16[256,1536]{1,0:T(8,128)(2,1)S(1)}, bf16[256,1536]{1,0:T(8,128)(2,1)S(1)}, u32[]{:S(2)}, u32[]{:S(2)}) %collective-permute-start) | collective-permute-done | bytes 786464 | tf_op jit(solution)/shard_map/ppermute | solution.py:479
  27.1 1.7 %collective-permute-start.7 = (bf16[512,512]{1,0:T(8,128)(2,1)S(1)}, bf16[512,512]{1,0:T(8,128)(2,1)S(1)}, u32[]{:S(2)}, u32[]{:S(2)}) collective-permute-start(bf16[512,512]{1,0:T(8,128)(2,1)S(1)} %get-tuple-element.109), channel_id=1, source_target_pairs={{0,3},{1,2},{2,1},{3,0},{4,7},{5,6},{6,5},{7,4},{8,11},{9,10},{10,... | collective-permute-start | bytes 1572872 | tf_op jit(solution)/shard_map/ppermute | solution.py:479
  29.4 2.0 %collective-permute-start.8 = (bf16[512,512]{1,0:T(8,128)(2,1)S(1)}, bf16[512,512]{1,0:T(8,128)(2,1)S(1)}, u32[]{:S(2)}, u32[]{:S(2)}) collective-permute-start(bf16[512,512]{1,0:T(8,128)(2,1)S(1)} %get-tuple-element.111), channel_id=1, source_target_pairs={{0,1},{1,0},{2,3},{3,2},{4,5},{5,4},{6,7},{7,6},{8,9},{9,8},{10,11... | collective-permute-start | bytes 1572872 | tf_op jit(solution)/shard_map/ppermute | solution.py:479
  32.0 0.6 keep_b1.1
  32.7 5.1 %collective-permute-done.1.refs_4_ = bf16[256,1024]{1,0:T(8,128)(2,1)S(1)} collective-permute-done((bf16[256,1024]{1,0:T(8,128)(2,1)S(1)}, bf16[256,1024]{1,0:T(8,128)(2,1)S(1)}, u32[]{:S(2)}, u32[]{:S(2)}) %collective-permute-start.1) | collective-permute-done | bytes 524320 | tf_op jit(solution)/shard_map/ppermute | solution.py:479
  39.2 2.5 %collective-permute-start.5 = (bf16[512,512]{1,0:T(8,128)(2,1)S(1)}, bf16[512,512]{1,0:T(8,128)(2,1)S(1)}, u32[]{:S(2)}, u32[]{:S(2)}) collective-permute-start(bf16[512,512]{1,0:T(8,128)(2,1)S(1)} %get-tuple-element.106), channel_id=1, source_target_pairs={{0,1},{1,0},{2,3},{3,2},{4,5},{5,4},{6,7},{7,6},{8,9},{9,8},{10,11... | collective-permute-start | bytes 1572872 | tf_op jit(solution)/shard_map/ppermute | solution.py:479
  41.7 1.6 collective-permute-start.4
  43.9 0.6 keep_b2.1
  44.5 5.3 %collective-permute-done.7.refs_1_ = bf16[512,512]{1,0:T(8,128)(2,1)S(1)} collective-permute-done((bf16[512,512]{1,0:T(8,128)(2,1)S(1)}, bf16[512,512]{1,0:T(8,128)(2,1)S(1)}, u32[]{:S(2)}, u32[]{:S(2)}) %collective-permute-start.7) | collective-permute-done | bytes 524320 | tf_op jit(solution)/shard_map/ppermute | solution.py:479
  50.1 1.6 collective-permute-start.9
  51.6 3.3 %other_1.1 = (bf16[2,256,1024]{2,1,0:T(8,128)(2,1)S(1)}, bf16[2,256,1024]{2,1,0:T(8,128)(2,1)S(1)}, bf16[256,1024]{1,0:T(8,128)(2,1)S(1)}, bf16[256,1024]{1,0:T(8,128)(2,1)S(1)}, bf16[8,128]{1,0:T(8,128)(2,1)}) custom-call(s32[1]{0:T(128)S(6)} %copy.13.refs_0_, bf16[2,256,8192]{2,1,0:T(8,128)(2,1)S(1)} %copy-done, ...), custom_call_target="tpu_custom_call" | custom-call | flops 10000000000 | tf_op jit(solution)/shard_map/other_1/pallas_call | solution.py:68
  55.0 1.3 collective-permute-start.15
  56.3 1.4 collective-permute-start.16
  57.7 2.5 %collective-permute-done.5.refs_3_ = bf16[512,512]{1,0:T(8,128)(2,1)S(1)} collective-permute-done((bf16[512,512]{1,0:T(8,128)(2,1)S(1)}, bf16[512,512]{1,0:T(8,128)(2,1)S(1)}, u32[]{:S(2)}, u32[]{:S(2)}) %collective-permute-start.5) | collective-permute-done | bytes 524320 | tf_op jit(solution)/shard_map/ppermute | solution.py:479
  60.2 0.8 collective-permute-done.4.refs_1_
  61.3 3.4 %collective-permute-start.10 = (bf16[32,512]{1,0:T(8,128)(2,1)S(1)}, bf16[32,512]{1,0:T(8,128)(2,1)S(1)}, u32[]{:S(2)}, u32[]{:S(2)}) collective-permute-start(bf16[32,512]{1,0:T(8,128)(2,1)S(1)} %get-tuple-element.118.refs_0_), channel_id=1, source_target_pairs={{0,16},{8,24},{16,0},{24,8},{32,48},{40,56},{48,32},{56,40},{64,80... | collective-permute-start | bytes 98312 | tf_op jit(solution)/shard_map/ppermute | solution.py:479
  64.7 6.2 %collective-permute-done.10.refs_1_ = bf16[32,512]{1,0:T(8,128)(2,1)S(1)} collective-permute-done((bf16[32,512]{1,0:T(8,128)(2,1)S(1)}, bf16[32,512]{1,0:T(8,128)(2,1)S(1)}, u32[]{:S(2)}, u32[]{:S(2)}) %collective-permute-start.10) | collective-permute-done | bytes 32800 | tf_op jit(solution)/shard_map/ppermute | solution.py:479
  70.9 8.0 %collective-permute-start.11 = (bf16[2,32,512]{2,1,0:T(8,128)(2,1)S(1)}, bf16[2,32,512]{2,1,0:T(8,128)(2,1)S(1)}, u32[]{:S(2)}, u32[]{:S(2)}) collective-permute-start(bf16[2,32,512]{2,1,0:T(8,128)(2,1)S(1)} %get-tuple-element.120.refs_0_), channel_id=1, source_target_pairs={{0,48},{8,56},{16,32},{24,40},{32,16},{40,24},{48,0},{56,8},{64,11... | collective-permute-start | bytes 196616 | tf_op jit(solution)/shard_map/ppermute | solution.py:479
  78.9 2.2 %collective-permute-done.11.refs_1_ = bf16[2,32,512]{2,1,0:T(8,128)(2,1)S(1)} collective-permute-done((bf16[2,32,512]{2,1,0:T(8,128)(2,1)S(1)}, bf16[2,32,512]{2,1,0:T(8,128)(2,1)S(1)}, u32[]{:S(2)}, u32[]{:S(2)}) %collective-permute-start.11) | collective-permute-done | bytes 65568 | tf_op jit(solution)/shard_map/ppermute | solution.py:479
  81.2 1.9 %inner_sync.1 = (bf16[16,2,32,512]{3,2,1,0:T(8,128)(2,1)S(1)}, bf16[16,32,512]{2,1,0:T(8,128)(2,1)S(1)}, bf16[8,128]{1,0:T(8,128)(2,1)}) custom-call(s32[1]{0:T(128)S(6)} %copy.13.refs_0_, bf16[2,16,2,32,512]{4,3,2,1,0:T(8,128)(2,1)} %bitcast.3, bf16[2,512,512]{2,1,0:T(8,128)(2,1)S(1)} %get-tuple-element.115.refs_2_, ...), custom_call_target="tpu_custom_call" | custom-call | tf_op jit(solution)/shard_map/inner_sync/pallas_call | solution.py:68
  83.2 1.9 %collective-permute-done.12.refs_1_ = bf16[16,32,512]{2,1,0:T(8,128)(2,1)S(1)} collective-permute-done((bf16[16,32,512]{2,1,0:T(8,128)(2,1)S(1)}, bf16[16,32,512]{2,1,0:T(8,128)(2,1)S(1)}, u32[]{:S(2)}, u32[]{:S(2)}) %collective-permute-start.12) | collective-permute-done | bytes 524320 | tf_op jit(solution)/shard_map/ppermute | solution.py:479
  85.2 1.6 collective-permute-start.13
  86.8 2.3 %collective-permute-start.18 = (bf16[256,1024]{1,0:T(8,128)(2,1)S(1)}, bf16[256,1024]{1,0:T(8,128)(2,1)S(1)}, u32[]{:S(2)}, u32[]{:S(2)}) collective-permute-start(bf16[256,1024]{1,0:T(8,128)(2,1)S(1)} %get-tuple-element.139), channel_id=1, source_target_pairs={{0,4},{1,5},{2,6},{3,7},{4,0},{5,1},{6,2},{7,3},{8,12},{9,13},{10,... | collective-permute-start | bytes 1572872 | tf_op jit(solution)/shard_map/ppermute | solution.py:479
  89.1 4.6 %collective-permute-done.13.refs_1_.refs_3_ = bf16[2,4,32,512]{3,2,1,0:T(8,128)(2,1)S(1)} collective-permute-done((bf16[2,4,32,512]{3,2,1,0:T(8,128)(2,1)S(1)}, bf16[2,4,32,512]{3,2,1,0:T(8,128)(2,1)S(1)}, u32[]{:S(2)}, u32[]{:S(2)}) %collective-permute-start.13) | collective-permute-done | bytes 262176 | tf_op jit(solution)/shard_map/ppermute | solution.py:479
  93.7 2.8 %collective-permute-start.14 = (bf16[4,32,512]{2,1,0:T(8,128)(2,1)S(1)}, bf16[4,32,512]{2,1,0:T(8,128)(2,1)S(1)}, u32[]{:S(2)}, u32[]{:S(2)}) collective-permute-start(bf16[4,32,512]{2,1,0:T(8,128)(2,1)S(1)} %get-tuple-element.131), channel_id=1, source_target_pairs={{0,192},{8,200},{16,208},{24,216},{32,224},{40,232},{48,240},{56,2... | collective-permute-start | bytes 393224 | tf_op jit(solution)/shard_map/ppermute | solution.py:479
  96.8 1.5 collective-permute-start.22
  98.4 2.6 %collective-permute-start.23 = (bf16[256,1024]{1,0:T(8,128)(2,1)S(1)}, bf16[256,1024]{1,0:T(8,128)(2,1)S(1)}, u32[]{:S(2)}, u32[]{:S(2)}) collective-permute-start(bf16[256,1024]{1,0:T(8,128)(2,1)S(1)} %get-tuple-element.151), channel_id=1, source_target_pairs={{0,1},{1,0},{2,3},{3,2},{4,5},{5,4},{6,7},{7,6},{8,9},{9,8},{10,11... | collective-permute-start | bytes 1572872 | tf_op jit(solution)/shard_map/ppermute | solution.py:479
  101.1 1.2 other_3.1
  102.3 6.7 %collective-permute-done.17.refs_1_ = bf16[4,32,512]{2,1,0:T(8,128)(2,1)S(1)} collective-permute-done((bf16[4,32,512]{2,1,0:T(8,128)(2,1)S(1)}, bf16[4,32,512]{2,1,0:T(8,128)(2,1)S(1)}, u32[]{:S(2)}, u32[]{:S(2)}) %collective-permute-start.17) | collective-permute-done | bytes 131104 | tf_op jit(solution)/shard_map/ppermute | solution.py:479
  109.0 2.3 %collective-permute-start.19 = (bf16[4,32,512]{2,1,0:T(8,128)(2,1)S(1)}, bf16[4,32,512]{2,1,0:T(8,128)(2,1)S(1)}, u32[]{:S(2)}, u32[]{:S(2)}) collective-permute-start(bf16[4,32,512]{2,1,0:T(8,128)(2,1)S(1)} %get-tuple-element.142.refs_1_.refs_3_), channel_id=1, source_target_pairs={{0,48},{8,56},{16,32},{24,40},{32,16},{40,24},{48,0},{56,8},{64,11... | collective-permute-start | bytes 393224 | tf_op jit(solution)/shard_map/ppermute | solution.py:479
  111.3 5.0 %collective-permute-done.19.refs_2_.refs_4_ = bf16[4,32,512]{2,1,0:T(8,128)(2,1)S(1)} collective-permute-done((bf16[4,32,512]{2,1,0:T(8,128)(2,1)S(1)}, bf16[4,32,512]{2,1,0:T(8,128)(2,1)S(1)}, u32[]{:S(2)}, u32[]{:S(2)}) %collective-permute-start.19) | collective-permute-done | bytes 131104 | tf_op jit(solution)/shard_map/ppermute | solution.py:479
  116.5 0.7 outer_sync.1
  117.2 5.3 %collective-permute-done.20.refs_1_ = bf16[4,32,512]{2,1,0:T(8,128)(2,1)S(1)} collective-permute-done((bf16[4,32,512]{2,1,0:T(8,128)(2,1)S(1)}, bf16[4,32,512]{2,1,0:T(8,128)(2,1)S(1)}, u32[]{:S(2)}, u32[]{:S(2)}) %collective-permute-start.20) | collective-permute-done | bytes 131104 | tf_op jit(solution)/shard_map/ppermute | solution.py:479
  122.6 3.1 %inner_other.1 = (bf16[16,2,32,512]{3,2,1,0:T(8,128)(2,1)S(1)}, bf16[16,32,512]{2,1,0:T(8,128)(2,1)S(1)}, bf16[2,16,2,32,512]{4,3,2,1,0:T(8,128)(2,1)}, bf16[8,128]{1,0:T(8,128)(2,1)}) custom-call(s32[1]{0:T(128)S(6)} %copy.13.refs_0_, bf16[2,16,2,32,512]{4,3,2,1,0:T(8,128)(2,1)} %bitcast.4, bf16[256,1024]{1,0:T(8,128)(2,1)S(1)} %get-tuple-element.148.refs_2_, ...), custom_call_target="tpu_custom_call" | custom-call | tf_op jit(solution)/shard_map/inner_other/pallas_call | solution.py:68
  125.9 1.8 %collective-permute-done.24.refs_1_ = bf16[16,32,512]{2,1,0:T(8,128)(2,1)S(1)} collective-permute-done((bf16[16,32,512]{2,1,0:T(8,128)(2,1)S(1)}, bf16[16,32,512]{2,1,0:T(8,128)(2,1)S(1)}, u32[]{:S(2)}, u32[]{:S(2)}) %collective-permute-start.24) | collective-permute-done | bytes 524320 | tf_op jit(solution)/shard_map/ppermute | solution.py:479
  127.9 6.7 %collective-permute-done.21.refs_1_ = bf16[2,4,32,512]{3,2,1,0:T(8,128)(2,1)S(1)} collective-permute-done((bf16[2,4,32,512]{3,2,1,0:T(8,128)(2,1)S(1)}, bf16[2,4,32,512]{3,2,1,0:T(8,128)(2,1)S(1)}, u32[]{:S(2)}, u32[]{:S(2)}) %collective-permute-start.21) | collective-permute-done | bytes 262176 | tf_op jit(solution)/shard_map/ppermute | solution.py:479
  135.1 8.4 %collective-permute-done.26.refs_1_.refs_3_ = bf16[2,4,32,512]{3,2,1,0:T(8,128)(2,1)S(1)} collective-permute-done((bf16[2,4,32,512]{3,2,1,0:T(8,128)(2,1)S(1)}, bf16[2,4,32,512]{3,2,1,0:T(8,128)(2,1)S(1)}, u32[]{:S(2)}, u32[]{:S(2)}) %collective-permute-start.26) | collective-permute-done | bytes 262176 | tf_op jit(solution)/shard_map/ppermute | solution.py:479
  143.8 1.4 mix.1
  145.1 4.7 %collective-permute-done.27.refs_1_ = bf16[4,32,512]{2,1,0:T(8,128)(2,1)S(1)} collective-permute-done((bf16[4,32,512]{2,1,0:T(8,128)(2,1)S(1)}, bf16[4,32,512]{2,1,0:T(8,128)(2,1)S(1)}, u32[]{:S(2)}, u32[]{:S(2)}) %collective-permute-start.27) | collective-permute-done | bytes 131104 | tf_op jit(solution)/shard_map/ppermute | solution.py:479
  149.9 2.7 %collective-permute-start.28 = (bf16[2,32,512]{2,1,0:T(8,128)(2,1)S(1)}, bf16[2,32,512]{2,1,0:T(8,128)(2,1)S(1)}, u32[]{:S(2)}, u32[]{:S(2)}) collective-permute-start(bf16[2,32,512]{2,1,0:T(8,128)(2,1)S(1)} %get-tuple-element.170), channel_id=1, source_target_pairs={{0,16},{8,24},{16,0},{24,8},{32,48},{40,56},{48,32},{56,40},{64,80... | collective-permute-start | bytes 196616 | tf_op jit(solution)/shard_map/ppermute | solution.py:479
  152.6 2.6 %collective-permute-done.28.refs_1_.refs_3_ = bf16[2,32,512]{2,1,0:T(8,128)(2,1)S(1)} collective-permute-done((bf16[2,32,512]{2,1,0:T(8,128)(2,1)S(1)}, bf16[2,32,512]{2,1,0:T(8,128)(2,1)S(1)}, u32[]{:S(2)}, u32[]{:S(2)}) %collective-permute-start.28) | collective-permute-done | bytes 65568 | tf_op jit(solution)/shard_map/ppermute | solution.py:479
  155.2 3.6 %collective-permute-start.29 = (bf16[32,512]{1,0:T(8,128)(2,1)S(1)}, bf16[32,512]{1,0:T(8,128)(2,1)S(1)}, u32[]{:S(2)}, u32[]{:S(2)}) collective-permute-start(bf16[32,512]{1,0:T(8,128)(2,1)S(1)} %get-tuple-element.173), channel_id=1, source_target_pairs={{0,48},{8,56},{16,32},{24,40},{32,16},{40,24},{48,0},{56,8},{64,11... | collective-permute-start | bytes 98312 | tf_op jit(solution)/shard_map/ppermute | solution.py:479
  158.8 2.5 %collective-permute-done.29.refs_3_ = bf16[32,512]{1,0:T(8,128)(2,1)S(1)} collective-permute-done((bf16[32,512]{1,0:T(8,128)(2,1)S(1)}, bf16[32,512]{1,0:T(8,128)(2,1)S(1)}, u32[]{:S(2)}, u32[]{:S(2)}) %collective-permute-start.29) | collective-permute-done | bytes 32800 | tf_op jit(solution)/shard_map/ppermute | solution.py:479
  161.3 0.6 outer_other.1
  (51 shorter events, 7.5 us)
Async XLA Ops:
  1.3 25.2 %copy-start = (bf16[2,256,8192]{2,1,0:T(8,128)(2,1)S(1)}, bf16[2,256,8192]{2,1,0:T(8,128)(2,1)}, u32[]{:S(2)}) copy-start(bf16[2,256,8192]{2,1,0:T(8,128)(2,1)} %refs_1_.23) | copy-start | bytes 25165828
  4.0 47.6 %collective-permute-start.6 = (bf16[256,3584]{1,0:T(8,128)(2,1)S(1)}, bf16[256,3584]{1,0:T(8,128)(2,1)S(1)}, u32[]{:S(2)}, u32[]{:S(2)}) collective-permute-start(bf16[256,3584]{1,0:T(8,128)(2,1)S(1)} %get-tuple-element.107), channel_id=1, source_target_pairs={{0,4},{1,5},{2,6},{3,7},{4,0},{5,1},{6,2},{7,3},{8,12},{9,13},{10,... | collective-permute-start | bytes 5505032 | tf_op jit(solution)/shard_map/ppermute | solution.py:479
  6.0 20.5 %collective-permute-start = (bf16[256,1536]{1,0:T(8,128)(2,1)S(1)}, bf16[256,1536]{1,0:T(8,128)(2,1)S(1)}, u32[]{:S(2)}, u32[]{:S(2)}) collective-permute-start(bf16[256,1536]{1,0:T(8,128)(2,1)S(1)} %get-tuple-element.91), channel_id=1, source_target_pairs={{0,1},{1,0},{2,3},{3,2},{4,5},{5,4},{6,7},{7,6},{8,9},{9,8},{10,11... | collective-permute-start | bytes 2359304 | tf_op jit(solution)/shard_map/ppermute | solution.py:479
  6.5 22.3 %collective-permute-start.2 = (bf16[256,1536]{1,0:T(8,128)(2,1)S(1)}, bf16[256,1536]{1,0:T(8,128)(2,1)S(1)}, u32[]{:S(2)}, u32[]{:S(2)}) collective-permute-start(bf16[256,1536]{1,0:T(8,128)(2,1)S(1)} %get-tuple-element.93), channel_id=1, source_target_pairs={{0,3},{1,2},{2,1},{3,0},{4,7},{5,6},{6,5},{7,4},{8,11},{9,10},{10,... | collective-permute-start | bytes 2359304 | tf_op jit(solution)/shard_map/ppermute | solution.py:479
  8.9 28.8 %collective-permute-start.1 = (bf16[256,1024]{1,0:T(8,128)(2,1)S(1)}, bf16[256,1024]{1,0:T(8,128)(2,1)S(1)}, u32[]{:S(2)}, u32[]{:S(2)}) collective-permute-start(bf16[256,1024]{1,0:T(8,128)(2,1)S(1)} %get-tuple-element.92), channel_id=1, source_target_pairs={{0,1},{1,0},{2,3},{3,2},{4,5},{5,4},{6,7},{7,6},{8,9},{9,8},{10,11... | collective-permute-start | bytes 1572872 | tf_op jit(solution)/shard_map/ppermute | solution.py:479
  10.2 28.3 %collective-permute-start.3 = (bf16[256,1024]{1,0:T(8,128)(2,1)S(1)}, bf16[256,1024]{1,0:T(8,128)(2,1)S(1)}, u32[]{:S(2)}, u32[]{:S(2)}) collective-permute-start(bf16[256,1024]{1,0:T(8,128)(2,1)S(1)} %get-tuple-element.94), channel_id=1, source_target_pairs={{0,3},{1,2},{2,1},{3,0},{4,7},{5,6},{6,5},{7,4},{8,11},{9,10},{10,... | collective-permute-start | bytes 1572872 | tf_op jit(solution)/shard_map/ppermute | solution.py:479
  27.1 22.7 %collective-permute-start.7 = (bf16[512,512]{1,0:T(8,128)(2,1)S(1)}, bf16[512,512]{1,0:T(8,128)(2,1)S(1)}, u32[]{:S(2)}, u32[]{:S(2)}) collective-permute-start(bf16[512,512]{1,0:T(8,128)(2,1)S(1)} %get-tuple-element.109), channel_id=1, source_target_pairs={{0,3},{1,2},{2,1},{3,0},{4,7},{5,6},{6,5},{7,4},{8,11},{9,10},{10,... | collective-permute-start | bytes 1572872 | tf_op jit(solution)/shard_map/ppermute | solution.py:479
  29.4 20.4 %collective-permute-start.8 = (bf16[512,512]{1,0:T(8,128)(2,1)S(1)}, bf16[512,512]{1,0:T(8,128)(2,1)S(1)}, u32[]{:S(2)}, u32[]{:S(2)}) collective-permute-start(bf16[512,512]{1,0:T(8,128)(2,1)S(1)} %get-tuple-element.111), channel_id=1, source_target_pairs={{0,1},{1,0},{2,3},{3,2},{4,5},{5,4},{6,7},{7,6},{8,9},{9,8},{10,11... | collective-permute-start | bytes 1572872 | tf_op jit(solution)/shard_map/ppermute | solution.py:479
  39.2 21.0 %collective-permute-start.5 = (bf16[512,512]{1,0:T(8,128)(2,1)S(1)}, bf16[512,512]{1,0:T(8,128)(2,1)S(1)}, u32[]{:S(2)}, u32[]{:S(2)}) collective-permute-start(bf16[512,512]{1,0:T(8,128)(2,1)S(1)} %get-tuple-element.106), channel_id=1, source_target_pairs={{0,1},{1,0},{2,3},{3,2},{4,5},{5,4},{6,7},{7,6},{8,9},{9,8},{10,11... | collective-permute-start | bytes 1572872 | tf_op jit(solution)/shard_map/ppermute | solution.py:479
  41.7 19.3 %collective-permute-start.4 = (bf16[512,512]{1,0:T(8,128)(2,1)S(1)}, bf16[512,512]{1,0:T(8,128)(2,1)S(1)}, u32[]{:S(2)}, u32[]{:S(2)}) collective-permute-start(bf16[512,512]{1,0:T(8,128)(2,1)S(1)} %get-tuple-element.103), channel_id=1, source_target_pairs={{0,3},{1,2},{2,1},{3,0},{4,7},{5,6},{6,5},{7,4},{8,11},{9,10},{10,... | collective-permute-start | bytes 1572872 | tf_op jit(solution)/shard_map/ppermute | solution.py:479
  50.1 31.1 %collective-permute-start.9 = (bf16[2,512,512]{2,1,0:T(8,128)(2,1)S(1)}, bf16[2,512,512]{2,1,0:T(8,128)(2,1)S(1)}, u32[]{:S(2)}, u32[]{:S(2)}) collective-permute-start(bf16[2,512,512]{2,1,0:T(8,128)(2,1)S(1)} %get-tuple-element.116), channel_id=1, source_target_pairs={{0,4},{1,5},{2,6},{3,7},{4,0},{5,1},{6,2},{7,3},{8,12},{9,13},{10,... | collective-permute-start | bytes 3145736 | tf_op jit(solution)/shard_map/ppermute | solution.py:479
  54.9 6.4 %copy-start.1 = (f32[2,32,512]{2,1,0:T(8,128)S(1)}, f32[2,32,512]{2,1,0:T(8,128)}, u32[]{:S(2)}) copy-start(f32[2,32,512]{2,1,0:T(8,128)} %refs_1_.25) | copy-start | bytes 393220
  55.0 6.3 %copy-start.2 = (f32[32,512]{1,0:T(8,128)S(1)}, f32[32,512]{1,0:T(8,128)}, u32[]{:S(2)}) copy-start(f32[32,512]{1,0:T(8,128)} %refs_2_.5) | copy-start | bytes 196612
  55.0 41.6 %collective-permute-start.15 = (bf16[2,256,1024]{2,1,0:T(8,128)(2,1)S(1)}, bf16[2,256,1024]{2,1,0:T(8,128)(2,1)S(1)}, u32[]{:S(2)}, u32[]{:S(2)}) collective-permute-start(bf16[2,256,1024]{2,1,0:T(8,128)(2,1)S(1)} %get-tuple-element.133), channel_id=1, source_target_pairs={{0,1},{1,0},{2,3},{3,2},{4,5},{5,4},{6,7},{7,6},{8,9},{9,8},{10,11... | collective-permute-start | bytes 3145736 | tf_op jit(solution)/shard_map/ppermute | solution.py:479
  56.3 40.3 %collective-permute-start.16 = (bf16[2,256,1024]{2,1,0:T(8,128)(2,1)S(1)}, bf16[2,256,1024]{2,1,0:T(8,128)(2,1)S(1)}, u32[]{:S(2)}, u32[]{:S(2)}) collective-permute-start(bf16[2,256,1024]{2,1,0:T(8,128)(2,1)S(1)} %get-tuple-element.135), channel_id=1, source_target_pairs={{0,3},{1,2},{2,1},{3,0},{4,7},{5,6},{6,5},{7,4},{8,11},{9,10},{10,... | collective-permute-start | bytes 3145736 | tf_op jit(solution)/shard_map/ppermute | solution.py:479
  61.3 9.6 %collective-permute-start.10 = (bf16[32,512]{1,0:T(8,128)(2,1)S(1)}, bf16[32,512]{1,0:T(8,128)(2,1)S(1)}, u32[]{:S(2)}, u32[]{:S(2)}) collective-permute-start(bf16[32,512]{1,0:T(8,128)(2,1)S(1)} %get-tuple-element.118.refs_0_), channel_id=1, source_target_pairs={{0,16},{8,24},{16,0},{24,8},{32,48},{40,56},{48,32},{56,40},{64,80... | collective-permute-start | bytes 98312 | tf_op jit(solution)/shard_map/ppermute | solution.py:479
  70.9 10.3 %collective-permute-start.11 = (bf16[2,32,512]{2,1,0:T(8,128)(2,1)S(1)}, bf16[2,32,512]{2,1,0:T(8,128)(2,1)S(1)}, u32[]{:S(2)}, u32[]{:S(2)}) collective-permute-start(bf16[2,32,512]{2,1,0:T(8,128)(2,1)S(1)} %get-tuple-element.120.refs_0_), channel_id=1, source_target_pairs={{0,48},{8,56},{16,32},{24,40},{32,16},{40,24},{48,0},{56,8},{64,11... | collective-permute-start | bytes 196616 | tf_op jit(solution)/shard_map/ppermute | solution.py:479
  83.1 2.0 %collective-permute-start.12 = (bf16[16,32,512]{2,1,0:T(8,128)(2,1)S(1)}, bf16[16,32,512]{2,1,0:T(8,128)(2,1)S(1)}, u32[]{:S(2)}, u32[]{:S(2)}) collective-permute-start(bf16[16,32,512]{2,1,0:T(8,128)(2,1)S(1)} %get-tuple-element.125), channel_id=1, source_target_pairs={{0,8},{8,0},{16,24},{24,16},{32,40},{40,32},{48,56},{56,48},{64,72... | collective-permute-start | bytes 1572872 | tf_op jit(solution)/shard_map/ppermute | solution.py:479
  85.2 8.4 %collective-permute-start.13 = (bf16[2,4,32,512]{3,2,1,0:T(8,128)(2,1)S(1)}, bf16[2,4,32,512]{3,2,1,0:T(8,128)(2,1)S(1)}, u32[]{:S(2)}, u32[]{:S(2)}) collective-permute-start(bf16[2,4,32,512]{3,2,1,0:T(8,128)(2,1)S(1)} %get-tuple-element.128), channel_id=1, source_target_pairs={{0,64},{8,72},{16,80},{24,88},{32,96},{40,104},{48,112},{56,120},{... | collective-permute-start | bytes 786440 | tf_op jit(solution)/shard_map/ppermute | solution.py:479
  86.8 14.3 %collective-permute-start.18 = (bf16[256,1024]{1,0:T(8,128)(2,1)S(1)}, bf16[256,1024]{1,0:T(8,128)(2,1)S(1)}, u32[]{:S(2)}, u32[]{:S(2)}) collective-permute-start(bf16[256,1024]{1,0:T(8,128)(2,1)S(1)} %get-tuple-element.139), channel_id=1, source_target_pairs={{0,4},{1,5},{2,6},{3,7},{4,0},{5,1},{6,2},{7,3},{8,12},{9,13},{10,... | collective-permute-start | bytes 1572872 | tf_op jit(solution)/shard_map/ppermute | solution.py:479
  93.7 7.2 %collective-permute-start.14 = (bf16[4,32,512]{2,1,0:T(8,128)(2,1)S(1)}, bf16[4,32,512]{2,1,0:T(8,128)(2,1)S(1)}, u32[]{:S(2)}, u32[]{:S(2)}) collective-permute-start(bf16[4,32,512]{2,1,0:T(8,128)(2,1)S(1)} %get-tuple-element.131), channel_id=1, source_target_pairs={{0,192},{8,200},{16,208},{24,216},{32,224},{40,232},{48,240},{56,2... | collective-permute-start | bytes 393224 | tf_op jit(solution)/shard_map/ppermute | solution.py:479
  96.8 25.8 %collective-permute-start.22 = (bf16[256,1024]{1,0:T(8,128)(2,1)S(1)}, bf16[256,1024]{1,0:T(8,128)(2,1)S(1)}, u32[]{:S(2)}, u32[]{:S(2)}) collective-permute-start(bf16[256,1024]{1,0:T(8,128)(2,1)S(1)} %get-tuple-element.149), channel_id=1, source_target_pairs={{0,3},{1,2},{2,1},{3,0},{4,7},{5,6},{6,5},{7,4},{8,11},{9,10},{10,... | collective-permute-start | bytes 1572872 | tf_op jit(solution)/shard_map/ppermute | solution.py:479
  98.4 24.2 %collective-permute-start.23 = (bf16[256,1024]{1,0:T(8,128)(2,1)S(1)}, bf16[256,1024]{1,0:T(8,128)(2,1)S(1)}, u32[]{:S(2)}, u32[]{:S(2)}) collective-permute-start(bf16[256,1024]{1,0:T(8,128)(2,1)S(1)} %get-tuple-element.151), channel_id=1, source_target_pairs={{0,1},{1,0},{2,3},{3,2},{4,5},{5,4},{6,7},{7,6},{8,9},{9,8},{10,11... | collective-permute-start | bytes 1572872 | tf_op jit(solution)/shard_map/ppermute | solution.py:479
  101.0 8.0 %collective-permute-start.17 = (bf16[4,32,512]{2,1,0:T(8,128)(2,1)S(1)}, bf16[4,32,512]{2,1,0:T(8,128)(2,1)S(1)}, u32[]{:S(2)}, u32[]{:S(2)}) collective-permute-start(bf16[4,32,512]{2,1,0:T(8,128)(2,1)S(1)} %get-tuple-element.138.refs_0_), channel_id=1, source_target_pairs={{0,16},{8,24},{16,0},{24,8},{32,48},{40,56},{48,32},{56,40},{64,80... | collective-permute-start | bytes 393224 | tf_op jit(solution)/shard_map/ppermute | solution.py:479
  109.0 7.3 %collective-permute-start.19 = (bf16[4,32,512]{2,1,0:T(8,128)(2,1)S(1)}, bf16[4,32,512]{2,1,0:T(8,128)(2,1)S(1)}, u32[]{:S(2)}, u32[]{:S(2)}) collective-permute-start(bf16[4,32,512]{2,1,0:T(8,128)(2,1)S(1)} %get-tuple-element.142.refs_1_.refs_3_), channel_id=1, source_target_pairs={{0,48},{8,56},{16,32},{24,40},{32,16},{40,24},{48,0},{56,8},{64,11... | collective-permute-start | bytes 393224 | tf_op jit(solution)/shard_map/ppermute | solution.py:479
  116.3 6.3 %collective-permute-start.20 = (bf16[4,32,512]{2,1,0:T(8,128)(2,1)S(1)}, bf16[4,32,512]{2,1,0:T(8,128)(2,1)S(1)}, u32[]{:S(2)}, u32[]{:S(2)}) collective-permute-start(bf16[4,32,512]{2,1,0:T(8,128)(2,1)S(1)} %get-tuple-element.144.refs_0_), channel_id=1, source_target_pairs={{0,192},{8,200},{16,208},{24,216},{32,224},{40,232},{48,240},{56,2... | collective-permute-start | bytes 393224 | tf_op jit(solution)/shard_map/ppermute | solution.py:479
  125.7 2.0 %collective-permute-start.24 = (bf16[16,32,512]{2,1,0:T(8,128)(2,1)S(1)}, bf16[16,32,512]{2,1,0:T(8,128)(2,1)S(1)}, u32[]{:S(2)}, u32[]{:S(2)}) collective-permute-start(bf16[16,32,512]{2,1,0:T(8,128)(2,1)S(1)} %get-tuple-element.154), channel_id=1, source_target_pairs={{0,8},{8,0},{16,24},{24,16},{32,40},{40,32},{48,56},{56,48},{64,72... | collective-permute-start | bytes 1572872 | tf_op jit(solution)/shard_map/ppermute | solution.py:479
  125.8 8.7 %collective-permute-start.21 = (bf16[2,4,32,512]{3,2,1,0:T(8,128)(2,1)S(1)}, bf16[2,4,32,512]{3,2,1,0:T(8,128)(2,1)S(1)}, u32[]{:S(2)}, u32[]{:S(2)}) collective-permute-start(bf16[2,4,32,512]{3,2,1,0:T(8,128)(2,1)S(1)} %get-tuple-element.147.refs_0_), channel_id=1, source_target_pairs={{0,64},{8,72},{16,80},{24,88},{32,96},{40,104},{48,112},{56,120},{... | collective-permute-start | bytes 786440 | tf_op jit(solution)/shard_map/ppermute | solution.py:479
  134.6 9.1 %collective-permute-start.25 = (bf16[16,32,512]{2,1,0:T(8,128)(2,1)S(1)}, bf16[16,32,512]{2,1,0:T(8,128)(2,1)S(1)}, u32[]{:S(2)}, u32[]{:S(2)}) collective-permute-start(bf16[16,32,512]{2,1,0:T(8,128)(2,1)S(1)} %get-tuple-element.157.refs_2_), channel_id=1, source_target_pairs={{0,8},{8,0},{16,24},{24,16},{32,40},{40,32},{48,56},{56,48},{64,72... | collective-permute-start | bytes 1572872 | tf_op jit(solution)/shard_map/ppermute | solution.py:479
  134.7 8.7 %collective-permute-start.26 = (bf16[2,4,32,512]{3,2,1,0:T(8,128)(2,1)S(1)}, bf16[2,4,32,512]{3,2,1,0:T(8,128)(2,1)S(1)}, u32[]{:S(2)}, u32[]{:S(2)}) collective-permute-start(bf16[2,4,32,512]{3,2,1,0:T(8,128)(2,1)S(1)} %get-tuple-element.160), channel_id=1, source_target_pairs={{0,64},{8,72},{16,80},{24,88},{32,96},{40,104},{48,112},{56,120},{... | collective-permute-start | bytes 786440 | tf_op jit(solution)/shard_map/ppermute | solution.py:479
  143.5 6.3 %collective-permute-start.27 = (bf16[4,32,512]{2,1,0:T(8,128)(2,1)S(1)}, bf16[4,32,512]{2,1,0:T(8,128)(2,1)S(1)}, u32[]{:S(2)}, u32[]{:S(2)}) collective-permute-start(bf16[4,32,512]{2,1,0:T(8,128)(2,1)S(1)} %get-tuple-element.167), channel_id=1, source_target_pairs={{0,192},{8,200},{16,208},{24,216},{32,224},{40,232},{48,240},{56,2... | collective-permute-start | bytes 393224 | tf_op jit(solution)/shard_map/ppermute | solution.py:479
  149.9 5.3 %collective-permute-start.28 = (bf16[2,32,512]{2,1,0:T(8,128)(2,1)S(1)}, bf16[2,32,512]{2,1,0:T(8,128)(2,1)S(1)}, u32[]{:S(2)}, u32[]{:S(2)}) collective-permute-start(bf16[2,32,512]{2,1,0:T(8,128)(2,1)S(1)} %get-tuple-element.170), channel_id=1, source_target_pairs={{0,16},{8,24},{16,0},{24,8},{32,48},{40,56},{48,32},{56,40},{64,80... | collective-permute-start | bytes 196616 | tf_op jit(solution)/shard_map/ppermute | solution.py:479
  155.2 6.1 %collective-permute-start.29 = (bf16[32,512]{1,0:T(8,128)(2,1)S(1)}, bf16[32,512]{1,0:T(8,128)(2,1)S(1)}, u32[]{:S(2)}, u32[]{:S(2)}) collective-permute-start(bf16[32,512]{1,0:T(8,128)(2,1)S(1)} %get-tuple-element.173), channel_id=1, source_target_pairs={{0,48},{8,56},{16,32},{24,40},{32,16},{40,24},{48,0},{56,8},{64,11... | collective-permute-start | bytes 98312 | tf_op jit(solution)/shard_map/ppermute | solution.py:479

commit v5 on v4

--- a/solution.py
+++ b/solution.py
@@ -305,12 +305,6 @@
         ref[at] = plus(inner_ref[block, core], recv_ref[block])
 
 
-def to_z(keep_ref, recv_ref, send_ref, stay_ref):
-    zh = place()[1]
-    for ref, at, j in ((send_ref, 0, 1), (send_ref, 1, 2), (stay_ref, 0, 0), (stay_ref, 1, 3)):
-        ref[at] = plus(keep_ref[zh ^ j], recv_ref[zh ^ j])
-
-
 QUAD = (4, 32, KV)
 
 
@@ -340,89 +334,84 @@
     return sums(name, [dims] * 2, [(keep, recv, 1, 1, 0, None), (keep, recv, 0, 0, 1, None)])
 
 
-def join(a, b):
-    def kernel(a_ref, b_ref, out_ref):
-        out_ref[0] = a_ref[...]
-        out_ref[1] = b_ref[...]
-
-    return call(kernel, (shape(2, *a.shape),), (a, b), [VM] * 2, [VM], name="join")
-
-
 def sum_x(inner, recv, name):
     return call(to_x, (shape(2, *QUAD),) * 2, (inner, recv), [VM] * 2, [VM] * 2, name=name)
 
 
-def sum_z(keep, recv, name):
-    return call(to_z, (shape(2, 32, KV),) * 2, (keep, recv), [VM] * 2, [VM] * 2, name=name)
-
-
-def row_of(own, got):
-    def kernel(own_ref, got_ref, out_ref):
+def spread_x(inner, recv, name):
+    def kernel(inner_ref, recv_ref, *outs):
+        x, _, core, _, _ = place()
+        for j in range(4):
+            block = pl.ds((x ^ j) * 4, 4)
+            outs[j][...] = plus(inner_ref[block, core], recv_ref[block])
+
+    return call(kernel, (shape(*QUAD),) * 4, (inner, recv), [VM] * 2, [VM] * 4, name=name)
+
+
+def spread_z(parts, name):
+    def kernel(*refs):
         zh = place()[1]
-        for ref, at, j in ((own_ref, 0, 0), (own_ref, 1, 1), (got_ref, 0, 3), (got_ref, 1, 2)):
-            out_ref[zh ^ j] = ref[at]
-
-    return call(kernel, (shape(*QUAD),), (own, got), [VM] * 2, [VM], name="row")
-
-
-def block_of(own, got):
-    def kernel(own_ref, got_ref, out_ref):
+        terms, outs = refs[: len(parts)], refs[len(parts) :]
+        for j in range(4):
+            outs[j][...] = sum(t[zh ^ j].astype(F32) for t in terms).astype(BF16)
+
+    return call(kernel, (shape(32, KV),) * 4, parts, [VM] * len(parts), [VM] * 4, name=name)
+
+
+def row_of(parts):
+    def kernel(*refs):
+        zh = place()[1]
+        for j in range(4):
+            refs[4][zh ^ j] = refs[j][...]
+
+    return call(kernel, (shape(*QUAD),), parts, [VM] * 4, [VM], name="row")
+
+
+def block_of(parts):
+    def kernel(*refs):
         x = place()[0]
-        for ref, at, j in ((own_ref, 0, 0), (own_ref, 1, 3), (got_ref, 0, 1), (got_ref, 1, 2)):
-            out_ref[pl.ds((x ^ j) * 4, 4)] = ref[at]
-
-    return call(kernel, (shape(16, 32, KV),), (own, got), [VM] * 2, [VM], name="block")
-
-
-def ahead(plan, anchors, momentum):
-    def kernel(plan_ref, anchor_ref, momentum_ref, out_ref):
-        anchor = anchor_ref[lax.rem(plan_ref[0], 2)]
-        out_ref[...] = (
-            (1.0 - outer_rate * (1.0 + outer_beta)) * anchor - outer_rate * outer_beta**2 * momentum_ref[...]
-        ).astype(BF16)
-
-    return call(kernel, (shape(32, KV),), (plan, anchors, momentum), [SM] + [VM] * 2, [VM], name="ahead")
-
-
-def new_rows(known, keep, recv):
-    def kernel(known_ref, a, b, out_ref):
-        mean = (a[...].astype(F32) + b[...].astype(F32)) / 32
-        out_ref[...] = (known_ref[...].astype(F32) + outer_rate * (1.0 + outer_beta) * mean).astype(BF16)
-
-    return call(kernel, (shape(*QUAD),), (known, keep, recv), [VM] * 3, [VM], name="new_rows")
-
-
-def outer_sync(plan, anchors, momentum, keep, recv):
-    def kernel(plan_ref, anchor_ref, momentum_ref, a, b, new_ref, moment_ref):
+        for j in range(4):
+            refs[4][pl.ds((x ^ j) * 4, 4)] = refs[j][...]
+
+    return call(kernel, (shape(16, 32, KV),), parts, [VM] * 4, [VM], name="block")
+
+
+def total(*refs):
+    return sum(r[...].astype(F32) for r in refs)
+
+
+def outer_sync(plan, anchors, momentum, parts):
+    def kernel(plan_ref, anchor_ref, momentum_ref, a, b, c, d, new_ref, moment_ref, short_ref):
         s = lax.rem(plan_ref[0], 2)
-        zh = place()[1]
-        mean = (a[zh].astype(F32) + b[zh].astype(F32)) / 32
+        mean = total(a, b, c, d) / 32
         anchor = anchor_ref[s]
         outer_grad = anchor - mean
         moment = outer_beta * momentum_ref[...] + outer_grad
-        new_ref[...] = anchor - outer_rate * (outer_grad + outer_beta * moment)
+        new = anchor - outer_rate * (outer_grad + outer_beta * moment)
+        new_ref[...] = new
         moment_ref[...] = moment
-
-    return call(
-        kernel,
-        (shape(32, KV, dtype=F32), shape(32, KV, dtype=F32)),
-        (plan, anchors, momentum, keep, recv),
-        [SM] + [VM] * 4,
-        [VM] * 2,
+        short_ref[...] = new.astype(BF16)
+
+    return call(
+        kernel,
+        (shape(32, KV, dtype=F32), shape(32, KV, dtype=F32), shape(32, KV)),
+        (plan, anchors, momentum, *parts),
+        [SM] + [VM] * 6,
+        [VM] * 3,
         name="outer_sync",
     )
 
 
-def outer_other(plan, anchors, keep, recv):
-    def kernel(plan_ref, anchor_ref, a, b, out_ref):
+def outer_other(plan, anchors, parts):
+    def kernel(plan_ref, anchor_ref, a, b, c, d, out_ref):
         other = 1 - lax.rem(plan_ref[0], 2)
-        out_ref[...] = anchor_ref[other] - (a[...].astype(F32) + b[...].astype(F32)) / 32
+        out_ref[...] = anchor_ref[other] - total(a, b, c, d) / 32
 
     return call(
         kernel,
         (shape(32, KV, dtype=F32),),
-        (plan, anchors, keep, recv),
-        [SM] + [VM] * 3,
+        (plan, anchors, *parts),
+        [SM] + [VM] * 5,
         [VM],
         name="outer_other",
     )
@@ -469,14 +458,24 @@
     "z": ("fsdp", along_fsdp(lambda z, y: (1 - z) * 4 + y)),
     "core": ("worker", along_worker(lambda x, z, c: (x, z, 1 - c))),
     "x1": ("worker", along_worker(lambda x, z, c: (x ^ 1, z, c))),
+    "x2": ("worker", along_worker(lambda x, z, c: (x ^ 2, z, c))),
     "x3": ("worker", along_worker(lambda x, z, c: (x ^ 3, z, c))),
     "z1": ("worker", along_worker(lambda x, z, c: (x, z ^ 1, c))),
+    "z2": ("worker", along_worker(lambda x, z, c: (x, z ^ 2, c))),
     "z3": ("worker", along_worker(lambda x, z, c: (x, z ^ 3, c))),
 }
 
 
 def swap(value, move):
     return lax.ppermute(value, *MOVES[move])
+
+
+def shared(value, axis):
+    return (value, *(swap(value, axis + j) for j in "123"))
+
+
+def dealt(parts, axis):
+    return (parts[0], *(swap(parts[j], axis + str(j)) for j in (1, 2, 3)))
 
 
 def body(token_ids, layer_inputs, key_grads, weights, anchors, momentum, plan):
@@ -533,43 +532,30 @@
     )
     got_0, got_1 = swap(send_0, "a"), swap(send_1, "b")
     near = sums("near", [(2, KV, HALF)], [(keep_a2, near_a, None, None, 0, 0), (keep_b2, near_b, None, None, 0, 1)])
-    known = ahead(plan, anchors, momentum)
-    known = join(known, swap(known, "z1"))
-    known = row_of(known, swap(known, "z3"))
 
     inner_s, send_s = inner_sync(plan, w, near, across)
     send, keep = sum_x(inner_s, swap(send_s, "core"), "sync_x1")
     recv = swap(send, "x1")
     send, keep = halve("sync_x3", QUAD, keep, recv)
+    recv = swap(send, "x3")
     last_0, last_1 = sums(
         "last", [half, half], [(stay_0, got_0, None, 1, 0, None), (stay_1, got_1, None, 1, 1, None)]
     )
     last_0, last_1 = swap(last_0, "b"), swap(last_1, "a")
-    keep = sums("sync_z1", [QUAD], [(keep, swap(send, "x3"), None, None, 0, None)])
-    recv = swap(keep, "z1")
+    parts = dealt(spread_z((keep, recv), "sync_z"), "z")
     mine_0, mine_1 = other("other_3", [dest(0, 1, 0, [(0, None, *lo), (1, None, *hi)])], [half, half], (got_z1, got_z3))
-    keep = sums("sync_z3", [QUAD], [(keep, recv, None, None, 0, None)])
-    recv = swap(keep, "z3")
-    row = new_rows(known, keep, recv)
-    row_far = swap(row, "x3")
-    anchor_new, momentum_new = outer_sync(plan, anchors, momentum, keep, recv)
-
-    own = join(row, row_far)
-    got = swap(own, "x1")
+    anchor_new, momentum_new, short = outer_sync(plan, anchors, momentum, parts)
+    parts = shared(short, "z")
+
     inner_o, send_o, new = inner_other(plan, w, (mine_0, got_0, last_0), (mine_1, got_1, last_1))
     core_o = swap(send_o, "core")
-    send, keep = sum_x(inner_o, core_o, "other_x1")
-    recv = swap(send, "x1")
-    block = block_of(own, got)
+    blocks = shared(row_of(parts), "x")
+    parts = dealt(spread_x(inner_o, core_o, "other_x"), "x")
+    block = block_of(blocks)
     block_far = swap(block, "core")
-    send, keep = halve("other_x3", QUAD, keep, recv)
-    recv = swap(send, "x3")
+    parts = dealt(spread_z(parts, "other_z"), "z")
     new = mix(plan, inner_s, block, block_far, new)
-    send, keep = sum_z(keep, recv, "other_z1")
-    recv = swap(send, "z1")
-    send, keep = halve("other_z3", (32, KV), keep, recv)
-    recv = swap(send, "z3")
-    pending = outer_other(plan, anchors, keep, recv)
+    pending = outer_other(plan, anchors, parts)
     return (new.reshape(1, 2, ROWS, KV), anchor_new, momentum_new, pending)
 
 

time: 162 us -> 157 us (0.969)
  waiting for transfers between devices: 88.4 us -> 76.7 us
  starting transfers between devices: 50.7 us -> 58 us
    ppermute x30 -> x35, waiting for transfers between devices: 88.4 us -> 76.7 us  [swap(): return lax.ppermute(value, *MOVES[move])]
    ppermute x30 -> x35, starting transfers between devices: 50.7 us -> 58 us  [swap(): return lax.ppermute(value, *MOVES[move])]
    pallas_call x33 -> x26, Pallas kernels: 21.3 us -> 21.1 us  [call(): pl.pallas_call(chained, out_shape=outs + [in_hbm(8, 128)], in_specs=list(...]
  transfers between devices with their start and end apart: 30 -> 35, of which waited for: 19 -> 21; matrix products, arithmetic and copies ran while one was open for 0% -> 0% of each run, Pallas kernels for 9% -> 9%
where the time goes in v5:
time: 157 us
  waiting for transfers between devices  76.7 us (49%)
  starting transfers between devices  58 us (37%)
  Pallas kernels  21.1 us (13%)
    ppermute x35, waiting for transfers between devices, swap(): return lax.ppermute(value, *MOVES[move])  76.7 us
    ppermute x35, starting transfers between devices, swap(): return lax.ppermute(value, *MOVES[move])  58 us
    pallas_call x26, Pallas kernels, call(): pl.pallas_call(chained, out_shape=outs + [in_hbm(8, 128)], in_specs=list(...  21.1 us
  transfers between devices with their start and end apart: 35, of which 21 were waited for; matrix products, arithmetic and copies ran while one was open for 0% of the time, Pallas kernels for 9%

profile of v5, /device:TPU:8, one launch (start us, length us, event | category | flops | bytes accessed | tf_op | source)
XLA Modules:
  0.0 157.3 jit_solution(14070021722083008646)
XLA Ops:
  1.3 2.7 %pack.1 = (bf16[256,1536]{1,0:T(8,128)(2,1)S(1)}, bf16[256,1536]{1,0:T(8,128)(2,1)S(1)}, bf16[256,3584]{1,0:T(8,128)(2,1)S(1)}, bf16[256,1024]{1,0:T(8,128)(2,1)...) custom-call(s32[1]{0:T(128)S(6)} %copy.13.refs_0_, ...), custom_call_target="tpu_custom_call" | custom-call | tf_op jit(solution)/shard_map/pack/pallas_call | solution.py:68
  4.0 2.0 %collective-permute-start.6 = (bf16[256,3584]{1,0:T(8,128)(2,1)S(1)}, bf16[256,3584]{1,0:T(8,128)(2,1)S(1)}, u32[]{:S(2)}, u32[]{:S(2)}) collective-permute-start(bf16[256,3584]{1,0:T(8,128)(2,1)S(1)} %get-tuple-element.99), channel_id=1, source_target_pairs={{0,4},{1,5},{2,6},{3,7},{4,0},{5,1},{6,2},{7,3},{8,12},{9,13},{10,... | collective-permute-start | bytes 5505032 | tf_op jit(solution)/shard_map/ppermute | solution.py:470
  6.5 2.4 %collective-permute-start.2 = (bf16[256,1536]{1,0:T(8,128)(2,1)S(1)}, bf16[256,1536]{1,0:T(8,128)(2,1)S(1)}, u32[]{:S(2)}, u32[]{:S(2)}) collective-permute-start(bf16[256,1536]{1,0:T(8,128)(2,1)S(1)} %get-tuple-element.85), channel_id=1, source_target_pairs={{0,3},{1,2},{2,1},{3,0},{4,7},{5,6},{6,5},{7,4},{8,11},{9,10},{10,... | collective-permute-start | bytes 2359304 | tf_op jit(solution)/shard_map/ppermute | solution.py:470
  8.9 1.3 collective-permute-start.1
  10.7 15.8 %collective-permute-done.refs_3_ = bf16[256,1536]{1,0:T(8,128)(2,1)S(1)} collective-permute-done((bf16[256,1536]{1,0:T(8,128)(2,1)S(1)}, bf16[256,1536]{1,0:T(8,128)(2,1)S(1)}, u32[]{:S(2)}, u32[]{:S(2)}) %collective-permute-start) | collective-permute-done | bytes 786464 | tf_op jit(solution)/shard_map/ppermute | solution.py:470
  27.1 1.7 %collective-permute-start.7 = (bf16[512,512]{1,0:T(8,128)(2,1)S(1)}, bf16[512,512]{1,0:T(8,128)(2,1)S(1)}, u32[]{:S(2)}, u32[]{:S(2)}) collective-permute-start(bf16[512,512]{1,0:T(8,128)(2,1)S(1)} %get-tuple-element.101), channel_id=1, source_target_pairs={{0,3},{1,2},{2,1},{3,0},{4,7},{5,6},{6,5},{7,4},{8,11},{9,10},{10,... | collective-permute-start | bytes 1572872 | tf_op jit(solution)/shard_map/ppermute | solution.py:470
  29.4 2.0 %collective-permute-start.8 = (bf16[512,512]{1,0:T(8,128)(2,1)S(1)}, bf16[512,512]{1,0:T(8,128)(2,1)S(1)}, u32[]{:S(2)}, u32[]{:S(2)}) collective-permute-start(bf16[512,512]{1,0:T(8,128)(2,1)S(1)} %get-tuple-element.103), channel_id=1, source_target_pairs={{0,1},{1,0},{2,3},{3,2},{4,5},{5,4},{6,7},{7,6},{8,9},{9,8},{10,11... | collective-permute-start | bytes 1572872 | tf_op jit(solution)/shard_map/ppermute | solution.py:470
  32.7 5.1 %collective-permute-done.1.refs_4_ = bf16[256,1024]{1,0:T(8,128)(2,1)S(1)} collective-permute-done((bf16[256,1024]{1,0:T(8,128)(2,1)S(1)}, bf16[256,1024]{1,0:T(8,128)(2,1)S(1)}, u32[]{:S(2)}, u32[]{:S(2)}) %collective-permute-start.1) | collective-permute-done | bytes 524320 | tf_op jit(solution)/shard_map/ppermute | solution.py:470
  39.2 2.5 %collective-permute-start.5 = (bf16[512,512]{1,0:T(8,128)(2,1)S(1)}, bf16[512,512]{1,0:T(8,128)(2,1)S(1)}, u32[]{:S(2)}, u32[]{:S(2)}) collective-permute-start(bf16[512,512]{1,0:T(8,128)(2,1)S(1)} %get-tuple-element.98), channel_id=1, source_target_pairs={{0,1},{1,0},{2,3},{3,2},{4,5},{5,4},{6,7},{7,6},{8,9},{9,8},{10,11... | collective-permute-start | bytes 1572872 | tf_op jit(solution)/shard_map/ppermute | solution.py:470
  41.7 1.6 %collective-permute-start.4 = (bf16[512,512]{1,0:T(8,128)(2,1)S(1)}, bf16[512,512]{1,0:T(8,128)(2,1)S(1)}, u32[]{:S(2)}, u32[]{:S(2)}) collective-permute-start(bf16[512,512]{1,0:T(8,128)(2,1)S(1)} %get-tuple-element.95), channel_id=1, source_target_pairs={{0,3},{1,2},{2,1},{3,0},{4,7},{5,6},{6,5},{7,4},{8,11},{9,10},{10,... | collective-permute-start | bytes 1572872 | tf_op jit(solution)/shard_map/ppermute | solution.py:470
  44.5 5.3 %collective-permute-done.7.refs_1_ = bf16[512,512]{1,0:T(8,128)(2,1)S(1)} collective-permute-done((bf16[512,512]{1,0:T(8,128)(2,1)S(1)}, bf16[512,512]{1,0:T(8,128)(2,1)S(1)}, u32[]{:S(2)}, u32[]{:S(2)}) %collective-permute-start.7) | collective-permute-done | bytes 524320 | tf_op jit(solution)/shard_map/ppermute | solution.py:470
  50.1 1.6 collective-permute-start.9
  51.6 3.3 %other_1.1 = (bf16[2,256,1024]{2,1,0:T(8,128)(2,1)S(1)}, bf16[2,256,1024]{2,1,0:T(8,128)(2,1)S(1)}, bf16[256,1024]{1,0:T(8,128)(2,1)S(1)}, bf16[256,1024]{1,0:T(8,128)(2,1)S(1)}, bf16[8,128]{1,0:T(8,128)(2,1)}) custom-call(s32[1]{0:T(128)S(6)} %copy.13.refs_0_, bf16[2,256,8192]{2,1,0:T(8,128)(2,1)S(1)} %copy-done, ...), custom_call_target="tpu_custom_call" | custom-call | flops 10000000000 | tf_op jit(solution)/shard_map/other_1/pallas_call | solution.py:68
  54.9 1.3 collective-permute-start.13
  56.2 1.4 collective-permute-start.14
  57.6 2.6 %collective-permute-done.5.refs_3_ = bf16[512,512]{1,0:T(8,128)(2,1)S(1)} collective-permute-done((bf16[512,512]{1,0:T(8,128)(2,1)S(1)}, bf16[512,512]{1,0:T(8,128)(2,1)S(1)}, u32[]{:S(2)}, u32[]{:S(2)}) %collective-permute-start.5) | collective-permute-done | bytes 524320 | tf_op jit(solution)/shard_map/ppermute | solution.py:470
  61.3 11.1 %collective-permute-done.9.refs_3_ = bf16[2,512,512]{2,1,0:T(8,128)(2,1)S(1)} collective-permute-done((bf16[2,512,512]{2,1,0:T(8,128)(2,1)S(1)}, bf16[2,512,512]{2,1,0:T(8,128)(2,1)S(1)}, u32[]{:S(2)}, u32[]{:S(2)}) %collective-permute-start.9) | collective-permute-done | bytes 1048608 | tf_op jit(solution)/shard_map/ppermute | solution.py:470
  72.4 1.9 %inner_sync.1 = (bf16[16,2,32,512]{3,2,1,0:T(8,128)(2,1)S(1)}, bf16[16,32,512]{2,1,0:T(8,128)(2,1)S(1)}, bf16[8,128]{1,0:T(8,128)(2,1)}) custom-call(s32[1]{0:T(128)S(6)} %copy.13.refs_0_, bf16[2,16,2,32,512]{4,3,2,1,0:T(8,128)(2,1)} %bitcast.3, bf16[2,512,512]{2,1,0:T(8,128)(2,1)S(1)} %get-tuple-element.107.refs_2_, ...), custom_call_target="tpu_custom_call" | custom-call | tf_op jit(solution)/shard_map/inner_sync/pallas_call | solution.py:68
  74.4 1.9 %collective-permute-done.10.refs_1_ = bf16[16,32,512]{2,1,0:T(8,128)(2,1)S(1)} collective-permute-done((bf16[16,32,512]{2,1,0:T(8,128)(2,1)S(1)}, bf16[16,32,512]{2,1,0:T(8,128)(2,1)S(1)}, u32[]{:S(2)}, u32[]{:S(2)}) %collective-permute-start.10) | collective-permute-done | bytes 524320 | tf_op jit(solution)/shard_map/ppermute | solution.py:470
  76.4 1.6 %collective-permute-start.11 = (bf16[2,4,32,512]{3,2,1,0:T(8,128)(2,1)S(1)}, bf16[2,4,32,512]{3,2,1,0:T(8,128)(2,1)S(1)}, u32[]{:S(2)}, u32[]{:S(2)}) collective-permute-start(bf16[2,4,32,512]{3,2,1,0:T(8,128)(2,1)S(1)} %get-tuple-element.114), channel_id=1, source_target_pairs={{0,64},{8,72},{16,80},{24,88},{32,96},{40,104},{48,112},{56,120},{... | collective-permute-start | bytes 786440 | tf_op jit(solution)/shard_map/ppermute | solution.py:470
  78.7 6.2 %collective-permute-done.11.refs_1_.refs_3_ = bf16[2,4,32,512]{3,2,1,0:T(8,128)(2,1)S(1)} collective-permute-done((bf16[2,4,32,512]{3,2,1,0:T(8,128)(2,1)S(1)}, bf16[2,4,32,512]{3,2,1,0:T(8,128)(2,1)S(1)}, u32[]{:S(2)}, u32[]{:S(2)}) %collective-permute-start.11) | collective-permute-done | bytes 262176 | tf_op jit(solution)/shard_map/ppermute | solution.py:470
  85.2 1.5 collective-permute-start.22
  86.7 2.6 %collective-permute-start.23 = (bf16[256,1024]{1,0:T(8,128)(2,1)S(1)}, bf16[256,1024]{1,0:T(8,128)(2,1)S(1)}, u32[]{:S(2)}, u32[]{:S(2)}) collective-permute-start(bf16[256,1024]{1,0:T(8,128)(2,1)S(1)} %get-tuple-element.135), channel_id=1, source_target_pairs={{0,1},{1,0},{2,3},{3,2},{4,5},{5,4},{6,7},{7,6},{8,9},{9,8},{10,11... | collective-permute-start | bytes 1572872 | tf_op jit(solution)/shard_map/ppermute | solution.py:470
  89.3 2.8 %collective-permute-start.12 = (bf16[4,32,512]{2,1,0:T(8,128)(2,1)S(1)}, bf16[4,32,512]{2,1,0:T(8,128)(2,1)S(1)}, u32[]{:S(2)}, u32[]{:S(2)}) collective-permute-start(bf16[4,32,512]{2,1,0:T(8,128)(2,1)S(1)} %get-tuple-element.117), channel_id=1, source_target_pairs={{0,192},{8,200},{16,208},{24,216},{32,224},{40,232},{48,240},{56,2... | collective-permute-start | bytes 393224 | tf_op jit(solution)/shard_map/ppermute | solution.py:470
  92.0 3.4 %collective-permute-done.12.refs_1_ = bf16[4,32,512]{2,1,0:T(8,128)(2,1)S(1)} collective-permute-done((bf16[4,32,512]{2,1,0:T(8,128)(2,1)S(1)}, bf16[4,32,512]{2,1,0:T(8,128)(2,1)S(1)}, u32[]{:S(2)}, u32[]{:S(2)}) %collective-permute-start.12) | collective-permute-done | bytes 131104 | tf_op jit(solution)/shard_map/ppermute | solution.py:470
  95.5 3.4 %collective-permute-start.15 = (bf16[32,512]{1,0:T(8,128)(2,1)S(1)}, bf16[32,512]{1,0:T(8,128)(2,1)S(1)}, u32[]{:S(2)}, u32[]{:S(2)}) collective-permute-start(bf16[32,512]{1,0:T(8,128)(2,1)S(1)} %get-tuple-element.125), channel_id=1, source_target_pairs={{0,16},{8,24},{16,0},{24,8},{32,48},{40,56},{48,32},{56,40},{64,80... | collective-permute-start | bytes 98312 | tf_op jit(solution)/shard_map/ppermute | solution.py:470
  98.8 4.5 %collective-permute-start.16 = (bf16[32,512]{1,0:T(8,128)(2,1)S(1)}, bf16[32,512]{1,0:T(8,128)(2,1)S(1)}, u32[]{:S(2)}, u32[]{:S(2)}) collective-permute-start(bf16[32,512]{1,0:T(8,128)(2,1)S(1)} %get-tuple-element.126), channel_id=1, source_target_pairs={{0,32},{8,40},{16,48},{24,56},{32,0},{40,8},{48,16},{56,24},{64,96... | collective-permute-start | bytes 98312 | tf_op jit(solution)/shard_map/ppermute | solution.py:470
  103.4 1.2 other_3.1
  104.5 2.1 %collective-permute-done.16.refs_5_ = bf16[32,512]{1,0:T(8,128)(2,1)S(1)} collective-permute-done((bf16[32,512]{1,0:T(8,128)(2,1)S(1)}, bf16[32,512]{1,0:T(8,128)(2,1)S(1)}, u32[]{:S(2)}, u32[]{:S(2)}) %collective-permute-start.16) | collective-permute-done | bytes 32800 | tf_op jit(solution)/shard_map/ppermute | solution.py:470
  106.7 2.7 %collective-permute-done.17.refs_6_ = bf16[32,512]{1,0:T(8,128)(2,1)S(1)} collective-permute-done((bf16[32,512]{1,0:T(8,128)(2,1)S(1)}, bf16[32,512]{1,0:T(8,128)(2,1)S(1)}, u32[]{:S(2)}, u32[]{:S(2)}) %collective-permute-start.17) | collective-permute-done | bytes 32800 | tf_op jit(solution)/shard_map/ppermute | solution.py:470
  110.1 3.1 %inner_other.1 = (bf16[16,2,32,512]{3,2,1,0:T(8,128)(2,1)S(1)}, bf16[16,32,512]{2,1,0:T(8,128)(2,1)S(1)}, bf16[2,16,2,32,512]{4,3,2,1,0:T(8,128)(2,1)}, bf16[8,128]{1,0:T(8,128)(2,1)}) custom-call(s32[1]{0:T(128)S(6)} %copy.13.refs_0_, bf16[2,16,2,32,512]{4,3,2,1,0:T(8,128)(2,1)} %bitcast.4, bf16[256,1024]{1,0:T(8,128)(2,1)S(1)} %get-tuple-element.132.refs_2_, ...), custom_call_target="tpu_custom_call" | custom-call | tf_op jit(solution)/shard_map/inner_other/pallas_call | solution.py:68
  113.3 1.1 collective-permute-start.21
  114.4 4.0 %collective-permute-start.20 = (bf16[32,512]{1,0:T(8,128)(2,1)S(1)}, bf16[32,512]{1,0:T(8,128)(2,1)S(1)}, u32[]{:S(2)}, u32[]{:S(2)}) collective-permute-start(bf16[32,512]{1,0:T(8,128)(2,1)S(1)} %get-tuple-element.131.refs_0_), channel_id=1, source_target_pairs={{0,32},{8,40},{16,48},{24,56},{32,0},{40,8},{48,16},{56,24},{64,96... | collective-permute-start | bytes 98312 | tf_op jit(solution)/shard_map/ppermute | solution.py:470
  118.4 1.5 collective-permute-start.19
  119.9 2.5 %collective-permute-done.20.refs_2_ = bf16[32,512]{1,0:T(8,128)(2,1)S(1)} collective-permute-done((bf16[32,512]{1,0:T(8,128)(2,1)S(1)}, bf16[32,512]{1,0:T(8,128)(2,1)S(1)}, u32[]{:S(2)}, u32[]{:S(2)}) %collective-permute-start.20) | collective-permute-done | bytes 32800 | tf_op jit(solution)/shard_map/ppermute | solution.py:470
  122.4 1.7 %collective-permute-done.19.refs_1_ = bf16[32,512]{1,0:T(8,128)(2,1)S(1)} collective-permute-done((bf16[32,512]{1,0:T(8,128)(2,1)S(1)}, bf16[32,512]{1,0:T(8,128)(2,1)S(1)}, u32[]{:S(2)}, u32[]{:S(2)}) %collective-permute-start.19) | collective-permute-done | bytes 32800 | tf_op jit(solution)/shard_map/ppermute | solution.py:470
  124.1 2.8 %collective-permute-start.26 = (bf16[4,32,512]{2,1,0:T(8,128)(2,1)S(1)}, bf16[4,32,512]{2,1,0:T(8,128)(2,1)S(1)}, u32[]{:S(2)}, u32[]{:S(2)}) collective-permute-start(bf16[4,32,512]{2,1,0:T(8,128)(2,1)S(1)} %get-tuple-element.138.refs_0_), channel_id=1, source_target_pairs={{0,192},{8,200},{16,208},{24,216},{32,224},{40,232},{48,240},{56,2... | collective-permute-start | bytes 393224 | tf_op jit(solution)/shard_map/ppermute | solution.py:470
  126.9 1.3 collective-permute-start.24
  128.4 4.3 %collective-permute-done.26.refs_3_ = bf16[4,32,512]{2,1,0:T(8,128)(2,1)S(1)} collective-permute-done((bf16[4,32,512]{2,1,0:T(8,128)(2,1)S(1)}, bf16[4,32,512]{2,1,0:T(8,128)(2,1)S(1)}, u32[]{:S(2)}, u32[]{:S(2)}) %collective-permute-start.26) | collective-permute-done | bytes 131104 | tf_op jit(solution)/shard_map/ppermute | solution.py:470
  132.7 2.1 %collective-permute-done.25.refs_2_ = bf16[4,32,512]{2,1,0:T(8,128)(2,1)S(1)} collective-permute-done((bf16[4,32,512]{2,1,0:T(8,128)(2,1)S(1)}, bf16[4,32,512]{2,1,0:T(8,128)(2,1)S(1)}, u32[]{:S(2)}, u32[]{:S(2)}) %collective-permute-start.25) | collective-permute-done | bytes 131104 | tf_op jit(solution)/shard_map/ppermute | solution.py:470
  135.4 3.2 %collective-permute-start.30 = (bf16[4,32,512]{2,1,0:T(8,128)(2,1)S(1)}, bf16[4,32,512]{2,1,0:T(8,128)(2,1)S(1)}, u32[]{:S(2)}, u32[]{:S(2)}) collective-permute-start(bf16[4,32,512]{2,1,0:T(8,128)(2,1)S(1)} %get-tuple-element.147), channel_id=1, source_target_pairs={{0,128},{8,136},{16,144},{24,152},{32,160},{40,168},{48,176},{56,1... | collective-permute-start | bytes 393224 | tf_op jit(solution)/shard_map/ppermute | solution.py:470
  138.6 1.1 collective-permute-start.31
  139.8 1.6 %collective-permute-done.29.refs_1_ = bf16[4,32,512]{2,1,0:T(8,128)(2,1)S(1)} collective-permute-done((bf16[4,32,512]{2,1,0:T(8,128)(2,1)S(1)}, bf16[4,32,512]{2,1,0:T(8,128)(2,1)S(1)}, u32[]{:S(2)}, u32[]{:S(2)}) %collective-permute-start.29) | collective-permute-done | bytes 131104 | tf_op jit(solution)/shard_map/ppermute | solution.py:470
  141.4 4.0 %collective-permute-done.30.refs_2_ = bf16[4,32,512]{2,1,0:T(8,128)(2,1)S(1)} collective-permute-done((bf16[4,32,512]{2,1,0:T(8,128)(2,1)S(1)}, bf16[4,32,512]{2,1,0:T(8,128)(2,1)S(1)}, u32[]{:S(2)}, u32[]{:S(2)}) %collective-permute-start.30) | collective-permute-done | bytes 131104 | tf_op jit(solution)/shard_map/ppermute | solution.py:470
  145.4 2.4 %collective-permute-done.31.refs_3_ = bf16[4,32,512]{2,1,0:T(8,128)(2,1)S(1)} collective-permute-done((bf16[4,32,512]{2,1,0:T(8,128)(2,1)S(1)}, bf16[4,32,512]{2,1,0:T(8,128)(2,1)S(1)}, u32[]{:S(2)}, u32[]{:S(2)}) %collective-permute-start.31) | collective-permute-done | bytes 131104 | tf_op jit(solution)/shard_map/ppermute | solution.py:470
  147.9 2.7 %collective-permute-start.33 = (bf16[32,512]{1,0:T(8,128)(2,1)S(1)}, bf16[32,512]{1,0:T(8,128)(2,1)S(1)}, u32[]{:S(2)}, u32[]{:S(2)}) collective-permute-start(bf16[32,512]{1,0:T(8,128)(2,1)S(1)} %get-tuple-element.156), channel_id=1, source_target_pairs={{0,32},{8,40},{16,48},{24,56},{32,0},{40,8},{48,16},{56,24},{64,96... | collective-permute-start | bytes 98312 | tf_op jit(solution)/shard_map/ppermute | solution.py:470
  150.6 3.8 %collective-permute-start.34 = (bf16[32,512]{1,0:T(8,128)(2,1)S(1)}, bf16[32,512]{1,0:T(8,128)(2,1)S(1)}, u32[]{:S(2)}, u32[]{:S(2)}) collective-permute-start(bf16[32,512]{1,0:T(8,128)(2,1)S(1)} %get-tuple-element.157), channel_id=1, source_target_pairs={{0,48},{8,56},{16,32},{24,40},{32,16},{40,24},{48,0},{56,8},{64,11... | collective-permute-start | bytes 98312 | tf_op jit(solution)/shard_map/ppermute | solution.py:470
  154.4 1.4 mix.1
  (54 shorter events, 11.9 us)
Async XLA Ops:
  1.3 25.2 %copy-start = (bf16[2,256,8192]{2,1,0:T(8,128)(2,1)S(1)}, bf16[2,256,8192]{2,1,0:T(8,128)(2,1)}, u32[]{:S(2)}) copy-start(bf16[2,256,8192]{2,1,0:T(8,128)(2,1)} %refs_1_.21) | copy-start | bytes 25165828
  4.0 47.6 %collective-permute-start.6 = (bf16[256,3584]{1,0:T(8,128)(2,1)S(1)}, bf16[256,3584]{1,0:T(8,128)(2,1)S(1)}, u32[]{:S(2)}, u32[]{:S(2)}) collective-permute-start(bf16[256,3584]{1,0:T(8,128)(2,1)S(1)} %get-tuple-element.99), channel_id=1, source_target_pairs={{0,4},{1,5},{2,6},{3,7},{4,0},{5,1},{6,2},{7,3},{8,12},{9,13},{10,... | collective-permute-start | bytes 5505032 | tf_op jit(solution)/shard_map/ppermute | solution.py:470
  6.0 20.5 %collective-permute-start = (bf16[256,1536]{1,0:T(8,128)(2,1)S(1)}, bf16[256,1536]{1,0:T(8,128)(2,1)S(1)}, u32[]{:S(2)}, u32[]{:S(2)}) collective-permute-start(bf16[256,1536]{1,0:T(8,128)(2,1)S(1)} %get-tuple-element.83), channel_id=1, source_target_pairs={{0,1},{1,0},{2,3},{3,2},{4,5},{5,4},{6,7},{7,6},{8,9},{9,8},{10,11... | collective-permute-start | bytes 2359304 | tf_op jit(solution)/shard_map/ppermute | solution.py:470
  6.5 22.3 %collective-permute-start.2 = (bf16[256,1536]{1,0:T(8,128)(2,1)S(1)}, bf16[256,1536]{1,0:T(8,128)(2,1)S(1)}, u32[]{:S(2)}, u32[]{:S(2)}) collective-permute-start(bf16[256,1536]{1,0:T(8,128)(2,1)S(1)} %get-tuple-element.85), channel_id=1, source_target_pairs={{0,3},{1,2},{2,1},{3,0},{4,7},{5,6},{6,5},{7,4},{8,11},{9,10},{10,... | collective-permute-start | bytes 2359304 | tf_op jit(solution)/shard_map/ppermute | solution.py:470
  8.9 28.8 %collective-permute-start.1 = (bf16[256,1024]{1,0:T(8,128)(2,1)S(1)}, bf16[256,1024]{1,0:T(8,128)(2,1)S(1)}, u32[]{:S(2)}, u32[]{:S(2)}) collective-permute-start(bf16[256,1024]{1,0:T(8,128)(2,1)S(1)} %get-tuple-element.84), channel_id=1, source_target_pairs={{0,1},{1,0},{2,3},{3,2},{4,5},{5,4},{6,7},{7,6},{8,9},{9,8},{10,11... | collective-permute-start | bytes 1572872 | tf_op jit(solution)/shard_map/ppermute | solution.py:470
  10.2 28.3 %collective-permute-start.3 = (bf16[256,1024]{1,0:T(8,128)(2,1)S(1)}, bf16[256,1024]{1,0:T(8,128)(2,1)S(1)}, u32[]{:S(2)}, u32[]{:S(2)}) collective-permute-start(bf16[256,1024]{1,0:T(8,128)(2,1)S(1)} %get-tuple-element.86), channel_id=1, source_target_pairs={{0,3},{1,2},{2,1},{3,0},{4,7},{5,6},{6,5},{7,4},{8,11},{9,10},{10,... | collective-permute-start | bytes 1572872 | tf_op jit(solution)/shard_map/ppermute | solution.py:470
  27.1 22.7 %collective-permute-start.7 = (bf16[512,512]{1,0:T(8,128)(2,1)S(1)}, bf16[512,512]{1,0:T(8,128)(2,1)S(1)}, u32[]{:S(2)}, u32[]{:S(2)}) collective-permute-start(bf16[512,512]{1,0:T(8,128)(2,1)S(1)} %get-tuple-element.101), channel_id=1, source_target_pairs={{0,3},{1,2},{2,1},{3,0},{4,7},{5,6},{6,5},{7,4},{8,11},{9,10},{10,... | collective-permute-start | bytes 1572872 | tf_op jit(solution)/shard_map/ppermute | solution.py:470
  29.4 20.4 %collective-permute-start.8 = (bf16[512,512]{1,0:T(8,128)(2,1)S(1)}, bf16[512,512]{1,0:T(8,128)(2,1)S(1)}, u32[]{:S(2)}, u32[]{:S(2)}) collective-permute-start(bf16[512,512]{1,0:T(8,128)(2,1)S(1)} %get-tuple-element.103), channel_id=1, source_target_pairs={{0,1},{1,0},{2,3},{3,2},{4,5},{5,4},{6,7},{7,6},{8,9},{9,8},{10,11... | collective-permute-start | bytes 1572872 | tf_op jit(solution)/shard_map/ppermute | solution.py:470
  39.2 21.0 %collective-permute-start.5 = (bf16[512,512]{1,0:T(8,128)(2,1)S(1)}, bf16[512,512]{1,0:T(8,128)(2,1)S(1)}, u32[]{:S(2)}, u32[]{:S(2)}) collective-permute-start(bf16[512,512]{1,0:T(8,128)(2,1)S(1)} %get-tuple-element.98), channel_id=1, source_target_pairs={{0,1},{1,0},{2,3},{3,2},{4,5},{5,4},{6,7},{7,6},{8,9},{9,8},{10,11... | collective-permute-start | bytes 1572872 | tf_op jit(solution)/shard_map/ppermute | solution.py:470
  41.7 19.3 %collective-permute-start.4 = (bf16[512,512]{1,0:T(8,128)(2,1)S(1)}, bf16[512,512]{1,0:T(8,128)(2,1)S(1)}, u32[]{:S(2)}, u32[]{:S(2)}) collective-permute-start(bf16[512,512]{1,0:T(8,128)(2,1)S(1)} %get-tuple-element.95), channel_id=1, source_target_pairs={{0,3},{1,2},{2,1},{3,0},{4,7},{5,6},{6,5},{7,4},{8,11},{9,10},{10,... | collective-permute-start | bytes 1572872 | tf_op jit(solution)/shard_map/ppermute | solution.py:470
  50.1 22.3 %collective-permute-start.9 = (bf16[2,512,512]{2,1,0:T(8,128)(2,1)S(1)}, bf16[2,512,512]{2,1,0:T(8,128)(2,1)S(1)}, u32[]{:S(2)}, u32[]{:S(2)}) collective-permute-start(bf16[2,512,512]{2,1,0:T(8,128)(2,1)S(1)} %get-tuple-element.108), channel_id=1, source_target_pairs={{0,4},{1,5},{2,6},{3,7},{4,0},{5,1},{6,2},{7,3},{8,12},{9,13},{10,... | collective-permute-start | bytes 3145736 | tf_op jit(solution)/shard_map/ppermute | solution.py:470
  54.9 30.0 %collective-permute-start.13 = (bf16[2,256,1024]{2,1,0:T(8,128)(2,1)S(1)}, bf16[2,256,1024]{2,1,0:T(8,128)(2,1)S(1)}, u32[]{:S(2)}, u32[]{:S(2)}) collective-permute-start(bf16[2,256,1024]{2,1,0:T(8,128)(2,1)S(1)} %get-tuple-element.119), channel_id=1, source_target_pairs={{0,1},{1,0},{2,3},{3,2},{4,5},{5,4},{6,7},{7,6},{8,9},{9,8},{10,11... | collective-permute-start | bytes 3145736 | tf_op jit(solution)/shard_map/ppermute | solution.py:470
  56.2 28.7 %collective-permute-start.14 = (bf16[2,256,1024]{2,1,0:T(8,128)(2,1)S(1)}, bf16[2,256,1024]{2,1,0:T(8,128)(2,1)S(1)}, u32[]{:S(2)}, u32[]{:S(2)}) collective-permute-start(bf16[2,256,1024]{2,1,0:T(8,128)(2,1)S(1)} %get-tuple-element.121), channel_id=1, source_target_pairs={{0,3},{1,2},{2,1},{3,0},{4,7},{5,6},{6,5},{7,4},{8,11},{9,10},{10,... | collective-permute-start | bytes 3145736 | tf_op jit(solution)/shard_map/ppermute | solution.py:470
  74.3 2.0 %collective-permute-start.10 = (bf16[16,32,512]{2,1,0:T(8,128)(2,1)S(1)}, bf16[16,32,512]{2,1,0:T(8,128)(2,1)S(1)}, u32[]{:S(2)}, u32[]{:S(2)}) collective-permute-start(bf16[16,32,512]{2,1,0:T(8,128)(2,1)S(1)} %get-tuple-element.111), channel_id=1, source_target_pairs={{0,8},{8,0},{16,24},{24,16},{32,40},{40,32},{48,56},{56,48},{64,72... | collective-permute-start | bytes 1572872 | tf_op jit(solution)/shard_map/ppermute | solution.py:470
  76.4 8.4 %collective-permute-start.11 = (bf16[2,4,32,512]{3,2,1,0:T(8,128)(2,1)S(1)}, bf16[2,4,32,512]{3,2,1,0:T(8,128)(2,1)S(1)}, u32[]{:S(2)}, u32[]{:S(2)}) collective-permute-start(bf16[2,4,32,512]{3,2,1,0:T(8,128)(2,1)S(1)} %get-tuple-element.114), channel_id=1, source_target_pairs={{0,64},{8,72},{16,80},{24,88},{32,96},{40,104},{48,112},{56,120},{... | collective-permute-start | bytes 786440 | tf_op jit(solution)/shard_map/ppermute | solution.py:470
  78.0 25.4 %collective-permute-start.18 = (bf16[256,1024]{1,0:T(8,128)(2,1)S(1)}, bf16[256,1024]{1,0:T(8,128)(2,1)S(1)}, u32[]{:S(2)}, u32[]{:S(2)}) collective-permute-start(bf16[256,1024]{1,0:T(8,128)(2,1)S(1)} %get-tuple-element.128), channel_id=1, source_target_pairs={{0,4},{1,5},{2,6},{3,7},{4,0},{5,1},{6,2},{7,3},{8,12},{9,13},{10,... | collective-permute-start | bytes 1572872 | tf_op jit(solution)/shard_map/ppermute | solution.py:470
  85.2 24.9 %collective-permute-start.22 = (bf16[256,1024]{1,0:T(8,128)(2,1)S(1)}, bf16[256,1024]{1,0:T(8,128)(2,1)S(1)}, u32[]{:S(2)}, u32[]{:S(2)}) collective-permute-start(bf16[256,1024]{1,0:T(8,128)(2,1)S(1)} %get-tuple-element.133), channel_id=1, source_target_pairs={{0,3},{1,2},{2,1},{3,0},{4,7},{5,6},{6,5},{7,4},{8,11},{9,10},{10,... | collective-permute-start | bytes 1572872 | tf_op jit(solution)/shard_map/ppermute | solution.py:470
  86.7 23.4 %collective-permute-start.23 = (bf16[256,1024]{1,0:T(8,128)(2,1)S(1)}, bf16[256,1024]{1,0:T(8,128)(2,1)S(1)}, u32[]{:S(2)}, u32[]{:S(2)}) collective-permute-start(bf16[256,1024]{1,0:T(8,128)(2,1)S(1)} %get-tuple-element.135), channel_id=1, source_target_pairs={{0,1},{1,0},{2,3},{3,2},{4,5},{5,4},{6,7},{7,6},{8,9},{9,8},{10,11... | collective-permute-start | bytes 1572872 | tf_op jit(solution)/shard_map/ppermute | solution.py:470
  89.3 6.2 %collective-permute-start.12 = (bf16[4,32,512]{2,1,0:T(8,128)(2,1)S(1)}, bf16[4,32,512]{2,1,0:T(8,128)(2,1)S(1)}, u32[]{:S(2)}, u32[]{:S(2)}) collective-permute-start(bf16[4,32,512]{2,1,0:T(8,128)(2,1)S(1)} %get-tuple-element.117), channel_id=1, source_target_pairs={{0,192},{8,200},{16,208},{24,216},{32,224},{40,232},{48,240},{56,2... | collective-permute-start | bytes 393224 | tf_op jit(solution)/shard_map/ppermute | solution.py:470
  95.5 9.1 %collective-permute-start.15 = (bf16[32,512]{1,0:T(8,128)(2,1)S(1)}, bf16[32,512]{1,0:T(8,128)(2,1)S(1)}, u32[]{:S(2)}, u32[]{:S(2)}) collective-permute-start(bf16[32,512]{1,0:T(8,128)(2,1)S(1)} %get-tuple-element.125), channel_id=1, source_target_pairs={{0,16},{8,24},{16,0},{24,8},{32,48},{40,56},{48,32},{56,40},{64,80... | collective-permute-start | bytes 98312 | tf_op jit(solution)/shard_map/ppermute | solution.py:470
  98.8 7.8 %collective-permute-start.16 = (bf16[32,512]{1,0:T(8,128)(2,1)S(1)}, bf16[32,512]{1,0:T(8,128)(2,1)S(1)}, u32[]{:S(2)}, u32[]{:S(2)}) collective-permute-start(bf16[32,512]{1,0:T(8,128)(2,1)S(1)} %get-tuple-element.126), channel_id=1, source_target_pairs={{0,32},{8,40},{16,48},{24,56},{32,0},{40,8},{48,16},{56,24},{64,96... | collective-permute-start | bytes 98312 | tf_op jit(solution)/shard_map/ppermute | solution.py:470
  103.3 6.0 %collective-permute-start.17 = (bf16[32,512]{1,0:T(8,128)(2,1)S(1)}, bf16[32,512]{1,0:T(8,128)(2,1)S(1)}, u32[]{:S(2)}, u32[]{:S(2)}) collective-permute-start(bf16[32,512]{1,0:T(8,128)(2,1)S(1)} %get-tuple-element.127), channel_id=1, source_target_pairs={{0,48},{8,56},{16,32},{24,40},{32,16},{40,24},{48,0},{56,8},{64,11... | collective-permute-start | bytes 98312 | tf_op jit(solution)/shard_map/ppermute | solution.py:470
  103.3 6.0 %copy-start.1 = (f32[2,32,512]{2,1,0:T(8,128)S(1)}, f32[2,32,512]{2,1,0:T(8,128)}, u32[]{:S(2)}) copy-start(f32[2,32,512]{2,1,0:T(8,128)} %refs_1_.23) | copy-start | bytes 393220
  103.4 6.0 %copy-start.2 = (f32[32,512]{1,0:T(8,128)S(1)}, f32[32,512]{1,0:T(8,128)}, u32[]{:S(2)}) copy-start(f32[32,512]{1,0:T(8,128)} %refs_2_.3) | copy-start | bytes 196612
  113.2 15.1 %collective-permute-start.27 = (bf16[16,32,512]{2,1,0:T(8,128)(2,1)S(1)}, bf16[16,32,512]{2,1,0:T(8,128)(2,1)S(1)}, u32[]{:S(2)}, u32[]{:S(2)}) collective-permute-start(bf16[16,32,512]{2,1,0:T(8,128)(2,1)S(1)} %get-tuple-element.140), channel_id=1, source_target_pairs={{0,8},{8,0},{16,24},{24,16},{32,40},{40,32},{48,56},{56,48},{64,72... | collective-permute-start | bytes 1572872 | tf_op jit(solution)/shard_map/ppermute | solution.py:470
  113.3 6.6 %collective-permute-start.21 = (bf16[32,512]{1,0:T(8,128)(2,1)S(1)}, bf16[32,512]{1,0:T(8,128)(2,1)S(1)}, u32[]{:S(2)}, u32[]{:S(2)}) collective-permute-start(bf16[32,512]{1,0:T(8,128)(2,1)S(1)} %get-tuple-element.131.refs_0_), channel_id=1, source_target_pairs={{0,48},{8,56},{16,32},{24,40},{32,16},{40,24},{48,0},{56,8},{64,11... | collective-permute-start | bytes 98312 | tf_op jit(solution)/shard_map/ppermute | solution.py:470
  114.4 8.0 %collective-permute-start.20 = (bf16[32,512]{1,0:T(8,128)(2,1)S(1)}, bf16[32,512]{1,0:T(8,128)(2,1)S(1)}, u32[]{:S(2)}, u32[]{:S(2)}) collective-permute-start(bf16[32,512]{1,0:T(8,128)(2,1)S(1)} %get-tuple-element.131.refs_0_), channel_id=1, source_target_pairs={{0,32},{8,40},{16,48},{24,56},{32,0},{40,8},{48,16},{56,24},{64,96... | collective-permute-start | bytes 98312 | tf_op jit(solution)/shard_map/ppermute | solution.py:470
  118.4 5.6 %collective-permute-start.19 = (bf16[32,512]{1,0:T(8,128)(2,1)S(1)}, bf16[32,512]{1,0:T(8,128)(2,1)S(1)}, u32[]{:S(2)}, u32[]{:S(2)}) collective-permute-start(bf16[32,512]{1,0:T(8,128)(2,1)S(1)} %get-tuple-element.131.refs_0_), channel_id=1, source_target_pairs={{0,16},{8,24},{16,0},{24,8},{32,48},{40,56},{48,32},{56,40},{64,80... | collective-permute-start | bytes 98312 | tf_op jit(solution)/shard_map/ppermute | solution.py:470
  124.1 8.6 %collective-permute-start.26 = (bf16[4,32,512]{2,1,0:T(8,128)(2,1)S(1)}, bf16[4,32,512]{2,1,0:T(8,128)(2,1)S(1)}, u32[]{:S(2)}, u32[]{:S(2)}) collective-permute-start(bf16[4,32,512]{2,1,0:T(8,128)(2,1)S(1)} %get-tuple-element.138.refs_0_), channel_id=1, source_target_pairs={{0,192},{8,200},{16,208},{24,216},{32,224},{40,232},{48,240},{56,2... | collective-permute-start | bytes 393224 | tf_op jit(solution)/shard_map/ppermute | solution.py:470
  126.9 7.9 %collective-permute-start.25 = (bf16[4,32,512]{2,1,0:T(8,128)(2,1)S(1)}, bf16[4,32,512]{2,1,0:T(8,128)(2,1)S(1)}, u32[]{:S(2)}, u32[]{:S(2)}) collective-permute-start(bf16[4,32,512]{2,1,0:T(8,128)(2,1)S(1)} %get-tuple-element.138.refs_0_), channel_id=1, source_target_pairs={{0,128},{8,136},{16,144},{24,152},{32,160},{40,168},{48,176},{56,1... | collective-permute-start | bytes 393224 | tf_op jit(solution)/shard_map/ppermute | solution.py:470
  126.9 7.9 %collective-permute-start.24 = (bf16[4,32,512]{2,1,0:T(8,128)(2,1)S(1)}, bf16[4,32,512]{2,1,0:T(8,128)(2,1)S(1)}, u32[]{:S(2)}, u32[]{:S(2)}) collective-permute-start(bf16[4,32,512]{2,1,0:T(8,128)(2,1)S(1)} %get-tuple-element.138.refs_0_), channel_id=1, source_target_pairs={{0,64},{8,72},{16,80},{24,88},{32,96},{40,104},{48,112},{56,120},{... | collective-permute-start | bytes 393224 | tf_op jit(solution)/shard_map/ppermute | solution.py:470
  134.9 19.5 %collective-permute-start.28 = (bf16[16,32,512]{2,1,0:T(8,128)(2,1)S(1)}, bf16[16,32,512]{2,1,0:T(8,128)(2,1)S(1)}, u32[]{:S(2)}, u32[]{:S(2)}) collective-permute-start(bf16[16,32,512]{2,1,0:T(8,128)(2,1)S(1)} %get-tuple-element.143.refs_2_), channel_id=1, source_target_pairs={{0,8},{8,0},{16,24},{24,16},{32,40},{40,32},{48,56},{56,48},{64,72... | collective-permute-start | bytes 1572872 | tf_op jit(solution)/shard_map/ppermute | solution.py:470
  135.0 6.4 %collective-permute-start.29 = (bf16[4,32,512]{2,1,0:T(8,128)(2,1)S(1)}, bf16[4,32,512]{2,1,0:T(8,128)(2,1)S(1)}, u32[]{:S(2)}, u32[]{:S(2)}) collective-permute-start(bf16[4,32,512]{2,1,0:T(8,128)(2,1)S(1)} %get-tuple-element.146), channel_id=1, source_target_pairs={{0,64},{8,72},{16,80},{24,88},{32,96},{40,104},{48,112},{56,120},{... | collective-permute-start | bytes 393224 | tf_op jit(solution)/shard_map/ppermute | solution.py:470
  135.4 9.9 %collective-permute-start.30 = (bf16[4,32,512]{2,1,0:T(8,128)(2,1)S(1)}, bf16[4,32,512]{2,1,0:T(8,128)(2,1)S(1)}, u32[]{:S(2)}, u32[]{:S(2)}) collective-permute-start(bf16[4,32,512]{2,1,0:T(8,128)(2,1)S(1)} %get-tuple-element.147), channel_id=1, source_target_pairs={{0,128},{8,136},{16,144},{24,152},{32,160},{40,168},{48,176},{56,1... | collective-permute-start | bytes 393224 | tf_op jit(solution)/shard_map/ppermute | solution.py:470
  138.6 9.1 %collective-permute-start.31 = (bf16[4,32,512]{2,1,0:T(8,128)(2,1)S(1)}, bf16[4,32,512]{2,1,0:T(8,128)(2,1)S(1)}, u32[]{:S(2)}, u32[]{:S(2)}) collective-permute-start(bf16[4,32,512]{2,1,0:T(8,128)(2,1)S(1)} %get-tuple-element.148), channel_id=1, source_target_pairs={{0,192},{8,200},{16,208},{24,216},{32,224},{40,232},{48,240},{56,2... | collective-permute-start | bytes 393224 | tf_op jit(solution)/shard_map/ppermute | solution.py:470
  147.8 8.0 %collective-permute-start.32 = (bf16[32,512]{1,0:T(8,128)(2,1)S(1)}, bf16[32,512]{1,0:T(8,128)(2,1)S(1)}, u32[]{:S(2)}, u32[]{:S(2)}) collective-permute-start(bf16[32,512]{1,0:T(8,128)(2,1)S(1)} %get-tuple-element.155), channel_id=1, source_target_pairs={{0,16},{8,24},{16,0},{24,8},{32,48},{40,56},{48,32},{56,40},{64,80... | collective-permute-start | bytes 98312 | tf_op jit(solution)/shard_map/ppermute | solution.py:470
  147.9 7.9 %collective-permute-start.33 = (bf16[32,512]{1,0:T(8,128)(2,1)S(1)}, bf16[32,512]{1,0:T(8,128)(2,1)S(1)}, u32[]{:S(2)}, u32[]{:S(2)}) collective-permute-start(bf16[32,512]{1,0:T(8,128)(2,1)S(1)} %get-tuple-element.156), channel_id=1, source_target_pairs={{0,32},{8,40},{16,48},{24,56},{32,0},{40,8},{48,16},{56,24},{64,96... | collective-permute-start | bytes 98312 | tf_op jit(solution)/shard_map/ppermute | solution.py:470
  150.6 6.0 %collective-permute-start.34 = (bf16[32,512]{1,0:T(8,128)(2,1)S(1)}, bf16[32,512]{1,0:T(8,128)(2,1)S(1)}, u32[]{:S(2)}, u32[]{:S(2)}) collective-permute-start(bf16[32,512]{1,0:T(8,128)(2,1)S(1)} %get-tuple-element.157), channel_id=1, source_target_pairs={{0,48},{8,56},{16,32},{24,40},{32,16},{40,24},{48,0},{56,8},{64,11... | collective-permute-start | bytes 98312 | tf_op jit(solution)/shard_map/ppermute | solution.py:470

commit v6 on v4

--- a/solution.py
+++ b/solution.py
@@ -83,67 +83,84 @@
     return pl.ds(pl.multiple_of(start, width), width)
 
 
-def pack_kernel(plan, ids, x, g, a1, b1, z1, a2, b2, z3, gt_out, gin, gt, tok, sems, gsems):
-    _, _, _, z, y = place()
-    s = lax.rem(plan[0], 2)
-    copies = []
-
-    def send(layer, col, width, dst, at):
-        copies.append(
-            pltpu.make_async_copy(
-                x.at[layer, :, columns(col, width)], dst.at[:, pl.ds(at, width)], sems.at[len(copies)]
+def pack(name, fragment, plan, ids, x, g, outs, pieces, g_to):
+    def kernel(plan_ref, ids_ref, x_ref, g_ref, *rest):
+        bufs, gt_ref = rest[: len(outs)], rest[len(outs)]
+        gin, tok, sems = rest[len(outs) + 1 :]
+        _, _, _, z, y = place()
+        s = lax.rem(plan_ref[0], 2)
+        layers = (s, 1 - s)
+        first = [
+            pltpu.make_async_copy(ids_ref, tok, sems.at[0]),
+            pltpu.make_async_copy(g_ref.at[layers[fragment]], gin, sems.at[1]),
+        ]
+        copies = []
+        for layer, start, width, out, at in pieces:
+            col = pl.multiple_of(start(z, y), HALF)
+            copies.append(
+                pltpu.make_async_copy(
+                    x_ref.at[layers[layer], :, pl.ds(col, width)],
+                    bufs[out].at[:, pl.ds(at, width)],
+                    sems.at[2 + len(copies)],
+                )
             )
-        )
-        copies[-1].start()
-
-    g_copies = [pltpu.make_async_copy(g.at[layer], gin.at[i], gsems.at[i]) for i, layer in enumerate((s, 1 - s))]
-    ids_copy = pltpu.make_async_copy(ids, tok, gsems.at[9])
-    for c in (*g_copies, ids_copy):
-        c.start()
-    for zz, bufs in ((1 - z, (a1, b1)), (z, (a2, b2))):
-        for buf, first, offset in ((bufs[0], y ^ 1, 0), (bufs[1], y ^ 3, HALF)):
-            for i, yy in enumerate((first, y ^ 2)):
-                send(s, (zz * 4 + yy) * ROWS + offset, HALF, buf, i * HALF)
-    for j, buf, at in ((1, z1, 0), (2, z1, ROWS), (3, z1, 2 * ROWS), (0, z3, 0)):
-        send(1 - s, ((1 - z) * 4 + (y ^ j)) * ROWS, ROWS, buf, at)
-    ids_copy.wait()
-    kept = (tok[...] != 0).astype(F32)
-    last = []
-
-    def put(src, dst):
-        last.append(pltpu.make_async_copy(src, dst, gsems.at[2 + len(last)]))
-        last[-1].start()
-
-    for i, bufs, at in ((0, (a1, b1), 2 * HALF), (1, (z1,), 3 * ROWS)):
-        g_copies[i].wait()
-        gt[i] = (gin[i].astype(F32).T * kept).astype(BF16)
-        for buf in bufs:
+        for c in first + copies:
+            c.start()
+        for c in first:
+            c.wait()
+        gt = (gin[...].astype(F32).T * (tok[...] != 0).astype(F32)).astype(BF16)
+        gt_ref[...] = gt
+        for out, at in g_to:
             for h in range(2):
-                put(gt.at[i, pl.ds(h * TOK, TOK)], buf.at[:, pl.ds(at + h * TOK, TOK)])
-    put(gt, gt_out)
-    for c in copies + last:
-        c.wait()
-
-
-def pack(plan, tok, x, g):
-    wide = in_vmem(TOK, 2 * HALF + KV)
-    half = in_vmem(TOK, 2 * HALF)
-    return call(
-        pack_kernel,
-        (wide, wide, in_vmem(TOK, 3 * ROWS + KV), half, half, half, in_vmem(2, KV, TOK)),
-        (plan, tok, x, g),
+                bufs[out][:, at + h * TOK : at + (h + 1) * TOK] = gt[h * TOK : (h + 1) * TOK]
+        for c in copies:
+            c.wait()
+
+    return call(
+        kernel,
+        [in_vmem(TOK, n) for n in outs] + [in_vmem(KV, TOK)],
+        (plan, ids, x, g),
         [SM, HBM, HBM, HBM],
-        [VM] * 7,
+        [VM] * (len(outs) + 1),
         [
-            pltpu.VMEM((2, TOK, KV), BF16),
-            pltpu.VMEM((2, KV, TOK), BF16),
+            pltpu.VMEM((TOK, KV), BF16),
             pltpu.VMEM((1, TOK), jnp.int32),
-            pltpu.SemaphoreType.DMA((12,)),
-            pltpu.SemaphoreType.DMA((10,)),
+            pltpu.SemaphoreType.DMA((2 + len(pieces),)),
         ],
-        name="pack",
+        name=name,
         vmem=BIG,
     )
+
+
+def pack_all(plan, ids, x, g):
+    def sync(far, flip_y, offset, out, at):
+        return (0, lambda z, y: ((1 - z if far else z) * 4 + (y ^ flip_y)) * ROWS + offset, HALF, out, at * HALF)
+
+    def other(j, out, at):
+        return (1, lambda z, y: ((1 - z) * 4 + (y ^ j)) * ROWS, ROWS, out, at * ROWS)
+
+    def pair(far, out):
+        return [
+            sync(far, 1, 0, out, 0),
+            sync(far, 2, 0, out, 1),
+            sync(far, 3, HALF, out + 1, 0),
+            sync(far, 2, HALF, out + 1, 1),
+        ]
+
+    wide, half = 2 * HALF + KV, 2 * HALF
+    a1, b1, gt_s = pack("pack_1", 0, plan, ids, x, g, [wide, wide], pair(True, 0), [(0, half), (1, half)])
+    z1, a2, b2, z3, gt_o = pack(
+        "pack_2",
+        1,
+        plan,
+        ids,
+        x,
+        g,
+        [3 * ROWS + KV, half, half, ROWS],
+        [other(1, 0, 0), other(2, 0, 1), other(3, 0, 2), *pair(False, 1), other(0, 3, 0)],
+        [(0, 3 * ROWS)],
+    )
+    return a1, b1, z1, a2, b2, z3, gt_s, gt_o
 
 
 def product(name, fragment, pieces, width, out_shapes, g_at, plan, x, gt, recvs, hint=0):
@@ -160,7 +177,7 @@
         s = lax.rem(plan_ref[0], 2)
         layer = s if fragment == 0 else 1 - s
         g_copies = [
-            pltpu.make_async_copy(gt_ref.at[fragment], gts.at[:, pl.ds(0, TOK)], sems.at[2 * count]),
+            pltpu.make_async_copy(gt_ref, gts.at[:, pl.ds(0, TOK)], sems.at[2 * count]),
             *(
                 pltpu.make_async_copy(
                     recv_refs[0].at[:, pl.ds(g_at + h * TOK, TOK)],
@@ -340,29 +357,57 @@
     return sums(name, [dims] * 2, [(keep, recv, 1, 1, 0, None), (keep, recv, 0, 0, 1, None)])
 
 
-def join(a, b):
+def sum_x(inner, recv, name):
+    return call(to_x, (shape(2, *QUAD),) * 2, (inner, recv), [VM] * 2, [VM] * 2, name=name)
+
+
+def sum_z(keep, recv, name):
+    return call(to_z, (shape(2, 32, KV),) * 2, (keep, recv), [VM] * 2, [VM] * 2, name=name)
+
+
+def sync_z1(plan, anchors, momentum, keep, recv):
+    def kernel(plan_ref, anchor_ref, momentum_ref, keep_ref, recv_ref, out_ref):
+        out_ref[:4] = plus(keep_ref[...], recv_ref[...])
+        anchor = anchor_ref[lax.rem(plan_ref[0], 2)]
+        q = (1.0 - outer_rate * (1.0 + outer_beta)) * anchor - outer_rate * outer_beta**2 * momentum_ref[...]
+        out_ref[4] = q.astype(BF16)
+
+    return call(
+        kernel,
+        (shape(5, 32, KV),),
+        (plan, anchors, momentum, keep, recv),
+        [SM] + [VM] * 4,
+        [VM],
+        name="sync_z1",
+    )
+
+
+def sync_z3(sent, recv):
+    def kernel(sent_ref, recv_ref, out_ref):
+        out_ref[:4] = plus(sent_ref[:4], recv_ref[:4])
+        out_ref[4] = sent_ref[4]
+        out_ref[5] = recv_ref[4]
+
+    return call(kernel, (shape(6, 32, KV),), (sent, recv), [VM] * 2, [VM], name="sync_z3")
+
+
+def new_rows(sent, recv):
+    def kernel(sent_ref, recv_ref, out_ref):
+        zh = place()[1]
+        for ref, at, j in ((sent_ref, 4, 0), (sent_ref, 5, 1), (recv_ref, 4, 3), (recv_ref, 5, 2)):
+            i = zh ^ j
+            mean = (sent_ref[i].astype(F32) + recv_ref[i].astype(F32)) / 32
+            out_ref[i] = (ref[at].astype(F32) + outer_rate * (1.0 + outer_beta) * mean).astype(BF16)
+
+    return call(kernel, (shape(*QUAD),), (sent, recv), [VM] * 2, [VM], name="new_rows")
+
+
+def join(a, b, hint=0):
     def kernel(a_ref, b_ref, out_ref):
         out_ref[0] = a_ref[...]
         out_ref[1] = b_ref[...]
 
-    return call(kernel, (shape(2, *a.shape),), (a, b), [VM] * 2, [VM], name="join")
-
-
-def sum_x(inner, recv, name):
-    return call(to_x, (shape(2, *QUAD),) * 2, (inner, recv), [VM] * 2, [VM] * 2, name=name)
-
-
-def sum_z(keep, recv, name):
-    return call(to_z, (shape(2, 32, KV),) * 2, (keep, recv), [VM] * 2, [VM] * 2, name=name)
-
-
-def row_of(own, got):
-    def kernel(own_ref, got_ref, out_ref):
-        zh = place()[1]
-        for ref, at, j in ((own_ref, 0, 0), (own_ref, 1, 1), (got_ref, 0, 3), (got_ref, 1, 2)):
-            out_ref[zh ^ j] = ref[at]
-
-    return call(kernel, (shape(*QUAD),), (own, got), [VM] * 2, [VM], name="row")
+    return call(kernel, (shape(2, *a.shape),), (a, b), [VM] * 2, [VM], name="join", hint=hint)
 
 
 def block_of(own, got):
@@ -372,24 +417,6 @@
             out_ref[pl.ds((x ^ j) * 4, 4)] = ref[at]
 
     return call(kernel, (shape(16, 32, KV),), (own, got), [VM] * 2, [VM], name="block")
-
-
-def ahead(plan, anchors, momentum):
-    def kernel(plan_ref, anchor_ref, momentum_ref, out_ref):
-        anchor = anchor_ref[lax.rem(plan_ref[0], 2)]
-        out_ref[...] = (
-            (1.0 - outer_rate * (1.0 + outer_beta)) * anchor - outer_rate * outer_beta**2 * momentum_ref[...]
-        ).astype(BF16)
-
-    return call(kernel, (shape(32, KV),), (plan, anchors, momentum), [SM] + [VM] * 2, [VM], name="ahead")
-
-
-def new_rows(known, keep, recv):
-    def kernel(known_ref, a, b, out_ref):
-        mean = (a[...].astype(F32) + b[...].astype(F32)) / 32
-        out_ref[...] = (known_ref[...].astype(F32) + outer_rate * (1.0 + outer_beta) * mean).astype(BF16)
-
-    return call(kernel, (shape(*QUAD),), (known, keep, recv), [VM] * 3, [VM], name="new_rows")
 
 
 def outer_sync(plan, anchors, momentum, keep, recv):
@@ -483,7 +510,7 @@
     CHAIN.token = None
     x = layer_inputs
     w = weights.reshape(2, *WORKERS)
-    a1, b1, z1, a2, b2, z3, gt = pack(plan, token_ids.reshape(1, TOK), x, key_grads)
+    a1, b1, z1, a2, b2, z3, gt_s, gt_o = pack_all(plan, token_ids.reshape(1, TOK), x, key_grads)
     got_a1 = swap(a1, "a")
     got_b1 = swap(b1, "b")
     got_z1 = swap(z1, "z")
@@ -491,20 +518,20 @@
     got_b2 = swap(b2, "b")
     got_z3 = swap(z3, "z")
 
-    def tile(name, far, flip_y, offset, at, recvs):
+    def tile(name, far, flip_y, offset, at, recvs, hint=0):
         piece = (
             lambda z, y: ((1 - z if far else z) * 4 + (y ^ flip_y)) * ROWS + offset,
             len(recvs) - 1,
             at * HALF,
             [(0, None, 0, KV)],
         )
-        return product(name, 0, [piece], HALF, [(KV, HALF)], 2 * HALF, plan, x, gt, recvs)
+        return product(name, 0, [piece], HALF, [(KV, HALF)], 2 * HALF, plan, x, gt_s, recvs, hint)
 
     def dest(j, source, at, targets):
         return (lambda z, y: (z * 4 + (y ^ j)) * ROWS, source, at, targets)
 
     def other(name, pieces, outs, recvs, hint=0):
-        return product(name, 1, pieces, ROWS, outs, 3 * ROWS, plan, x, gt, recvs, hint)
+        return product(name, 1, pieces, ROWS, outs, 3 * ROWS, plan, x, gt_o, recvs, hint)
 
     lo, hi = (0, 256), (256, 512)
     half, pair = (256, ROWS), (2, 256, ROWS)
@@ -516,7 +543,7 @@
     near_a = swap(tile("send_a2", False, 3, 0, 1, (got_a1, got_a2)), "b")
     near_b = swap(tile("send_b2", False, 1, HALF, 1, (got_b1, got_b2)), "a")
     keep_a2 = tile("keep_a2", False, 0, 0, 0, (got_a1, got_a2))
-    keep_b2 = tile("keep_b2", False, 0, HALF, 0, (got_b1, got_b2))
+    keep_b2 = tile("keep_b2", False, 0, HALF, 0, (got_b1, got_b2), 4 * 10**10)
     across = swap(
         sums("far", [(2, KV, HALF)], [(keep_a1, far_a, None, None, 0, 0), (keep_b1, far_b, None, None, 0, 1)]), "z"
     )
@@ -533,31 +560,28 @@
     )
     got_0, got_1 = swap(send_0, "a"), swap(send_1, "b")
     near = sums("near", [(2, KV, HALF)], [(keep_a2, near_a, None, None, 0, 0), (keep_b2, near_b, None, None, 0, 1)])
-    known = ahead(plan, anchors, momentum)
-    known = join(known, swap(known, "z1"))
-    known = row_of(known, swap(known, "z3"))
 
     inner_s, send_s = inner_sync(plan, w, near, across)
     send, keep = sum_x(inner_s, swap(send_s, "core"), "sync_x1")
     recv = swap(send, "x1")
-    send, keep = halve("sync_x3", QUAD, keep, recv)
     last_0, last_1 = sums(
         "last", [half, half], [(stay_0, got_0, None, 1, 0, None), (stay_1, got_1, None, 1, 1, None)]
     )
     last_0, last_1 = swap(last_0, "b"), swap(last_1, "a")
-    keep = sums("sync_z1", [QUAD], [(keep, swap(send, "x3"), None, None, 0, None)])
-    recv = swap(keep, "z1")
+    send, keep = halve("sync_x3", QUAD, keep, recv)
+    sent = sync_z1(plan, anchors, momentum, keep, swap(send, "x3"))
+    recv = swap(sent, "z1")
     mine_0, mine_1 = other("other_3", [dest(0, 1, 0, [(0, None, *lo), (1, None, *hi)])], [half, half], (got_z1, got_z3))
-    keep = sums("sync_z3", [QUAD], [(keep, recv, None, None, 0, None)])
-    recv = swap(keep, "z3")
-    row = new_rows(known, keep, recv)
+    sent = sync_z3(sent, recv)
+    recv = swap(sent, "z3")
+    row = new_rows(sent, recv)
     row_far = swap(row, "x3")
-    anchor_new, momentum_new = outer_sync(plan, anchors, momentum, keep, recv)
-
-    own = join(row, row_far)
-    got = swap(own, "x1")
+    anchor_new, momentum_new = outer_sync(plan, anchors, momentum, sent, recv)
+
     inner_o, send_o, new = inner_other(plan, w, (mine_0, got_0, last_0), (mine_1, got_1, last_1))
     core_o = swap(send_o, "core")
+    own = join(row, row_far, 10**11)
+    got = swap(own, "x1")
     send, keep = sum_x(inner_o, core_o, "other_x1")
     recv = swap(send, "x1")
     block = block_of(own, got)

time: 162 us -> 158 us (0.975)
  starting transfers between devices: 50.7 us -> 44.7 us
    ppermute x30 -> x28, starting transfers between devices: 50.7 us -> 44.7 us  [swap(): return lax.ppermute(value, *MOVES[move])]
    pallas_call x33 -> x31, Pallas kernels: 21.3 us -> 22.2 us  [call(): pl.pallas_call(chained, out_shape=outs + [in_hbm(8, 128)], in_specs=list(...]
    ppermute x30 -> x28, waiting for transfers between devices: 88.4 us -> 88.4 us  [swap(): return lax.ppermute(value, *MOVES[move])]
  transfers between devices with their start and end apart: 30 -> 28, of which waited for: 19 -> 18; matrix products, arithmetic and copies ran while one was open for 0% -> 0% of each run, Pallas kernels for 9% -> 13%
where the time goes in v6:
time: 158 us; the launch traced here: 157 us
  waiting for transfers between devices  88.4 us (56%)
  starting transfers between devices  44.7 us (28%)
  Pallas kernels  22.2 us (14%)
    ppermute x28, waiting for transfers between devices, swap(): return lax.ppermute(value, *MOVES[move])  88.4 us
    ppermute x28, starting transfers between devices, swap(): return lax.ppermute(value, *MOVES[move])  44.7 us
    pallas_call x31, Pallas kernels, call(): pl.pallas_call(chained, out_shape=outs + [in_hbm(8, 128)], in_specs=list(...  22.2 us
  transfers between devices with their start and end apart: 28, of which 18 were waited for; matrix products, arithmetic and copies ran while one was open for 0% of the time, Pallas kernels for 13%

profile of v6, /device:TPU:8, one launch (start us, length us, event | category | flops | bytes accessed | tf_op | source)
XLA Modules:
  0.0 156.8 jit_solution(12392359076471076676)
XLA Ops:
  1.3 1.5 pack_1.1
  2.8 2.3 %collective-permute-start = (bf16[256,1536]{1,0:T(8,128)(2,1)S(1)}, bf16[256,1536]{1,0:T(8,128)(2,1)S(1)}, u32[]{:S(2)}, u32[]{:S(2)}) collective-permute-start(bf16[256,1536]{1,0:T(8,128)(2,1)S(1)} %get-tuple-element.87), channel_id=1, source_target_pairs={{0,1},{1,0},{2,3},{3,2},{4,5},{5,4},{6,7},{7,6},{8,9},{9,8},{10,11... | collective-permute-start | bytes 2359304 | tf_op jit(solution)/shard_map/ppermute | solution.py:506
  5.1 0.7 collective-permute-start.2
  5.7 2.2 %pack_2.1 = (bf16[256,3584]{1,0:T(8,128)(2,1)S(1)}, bf16[256,1024]{1,0:T(8,128)(2,1)S(1)}, bf16[256,1024]{1,0:T(8,128)(2,1)S(1)}, bf16[256,1024]{1,0:T(8,128)(2,...) custom-call(s32[1]{0:T(128)S(6)} %copy.13.refs_0_, s32[1,256]{1,0:T(1,128)} %bitcast.9, ...), custom_call_target="tpu_custom_call" | custom-call | tf_op jit(solution)/shard_map/pack_2/pallas_call | solution.py:68
  7.9 1.4 collective-permute-start.1
  9.4 0.7 collective-permute-start.3
  10.1 1.7 %collective-permute-start.6 = (bf16[256,3584]{1,0:T(8,128)(2,1)S(1)}, bf16[256,3584]{1,0:T(8,128)(2,1)S(1)}, u32[]{:S(2)}, u32[]{:S(2)}) collective-permute-start(bf16[256,3584]{1,0:T(8,128)(2,1)S(1)} %get-tuple-element.105), channel_id=1, source_target_pairs={{0,4},{1,5},{2,6},{3,7},{4,0},{5,1},{6,2},{7,3},{8,12},{9,13},{10,... | collective-permute-start | bytes 5505032 | tf_op jit(solution)/shard_map/ppermute | solution.py:506
  11.7 11.8 %collective-permute-done.refs_3_ = bf16[256,1536]{1,0:T(8,128)(2,1)S(1)} collective-permute-done((bf16[256,1536]{1,0:T(8,128)(2,1)S(1)}, bf16[256,1536]{1,0:T(8,128)(2,1)S(1)}, u32[]{:S(2)}, u32[]{:S(2)}) %collective-permute-start) | collective-permute-done | bytes 786464 | tf_op jit(solution)/shard_map/ppermute | solution.py:506
  24.1 1.4 collective-permute-done.2.refs_3_
  26.2 1.4 collective-permute-start.8
  27.6 1.3 collective-permute-start.7
  30.1 4.6 %collective-permute-done.1.refs_4_ = bf16[256,1024]{1,0:T(8,128)(2,1)S(1)} collective-permute-done((bf16[256,1024]{1,0:T(8,128)(2,1)S(1)}, bf16[256,1024]{1,0:T(8,128)(2,1)S(1)}, u32[]{:S(2)}, u32[]{:S(2)}) %collective-permute-start.1) | collective-permute-done | bytes 524320 | tf_op jit(solution)/shard_map/ppermute | solution.py:506
  35.4 1.5 collective-permute-start.4
  37.5 2.0 %collective-permute-start.5 = (bf16[512,512]{1,0:T(8,128)(2,1)S(1)}, bf16[512,512]{1,0:T(8,128)(2,1)S(1)}, u32[]{:S(2)}, u32[]{:S(2)}) collective-permute-start(bf16[512,512]{1,0:T(8,128)(2,1)S(1)} %get-tuple-element.103), channel_id=1, source_target_pairs={{0,1},{1,0},{2,3},{3,2},{4,5},{5,4},{6,7},{7,6},{8,9},{9,8},{10,11... | collective-permute-start | bytes 1572872 | tf_op jit(solution)/shard_map/ppermute | solution.py:506
  40.7 5.3 %collective-permute-done.8.refs_3_ = bf16[512,512]{1,0:T(8,128)(2,1)S(1)} collective-permute-done((bf16[512,512]{1,0:T(8,128)(2,1)S(1)}, bf16[512,512]{1,0:T(8,128)(2,1)S(1)}, u32[]{:S(2)}, u32[]{:S(2)}) %collective-permute-start.8) | collective-permute-done | bytes 524320 | tf_op jit(solution)/shard_map/ppermute | solution.py:506
  46.0 2.0 %collective-permute-done.7.refs_1_ = bf16[512,512]{1,0:T(8,128)(2,1)S(1)} collective-permute-done((bf16[512,512]{1,0:T(8,128)(2,1)S(1)}, bf16[512,512]{1,0:T(8,128)(2,1)S(1)}, u32[]{:S(2)}, u32[]{:S(2)}) %collective-permute-start.7) | collective-permute-done | bytes 524320 | tf_op jit(solution)/shard_map/ppermute | solution.py:506
  48.9 4.2 %collective-permute-done.6.refs_3_ = bf16[256,3584]{1,0:T(8,128)(2,1)S(1)} collective-permute-done((bf16[256,3584]{1,0:T(8,128)(2,1)S(1)}, bf16[256,3584]{1,0:T(8,128)(2,1)S(1)}, u32[]{:S(2)}, u32[]{:S(2)}) %collective-permute-start.6) | collective-permute-done | bytes 1835040 | tf_op jit(solution)/shard_map/ppermute | solution.py:506
  53.0 3.3 %other_1.1 = (bf16[2,256,1024]{2,1,0:T(8,128)(2,1)S(1)}, bf16[2,256,1024]{2,1,0:T(8,128)(2,1)S(1)}, bf16[256,1024]{1,0:T(8,128)(2,1)S(1)}, bf16[256,1024]{1,0:T(8,128)(2,1)S(1)}, bf16[8,128]{1,0:T(8,128)(2,1)}) custom-call(s32[1]{0:T(128)S(6)} %copy.13.refs_0_, bf16[2,256,8192]{2,1,0:T(8,128)(2,1)S(1)} %bitcast.4, ...), custom_call_target="tpu_custom_call" | custom-call | flops 10000000000 | tf_op jit(solution)/shard_map/other_1/pallas_call | solution.py:68
  56.3 1.1 collective-permute-start.12
  57.5 1.6 collective-permute-start.13
  59.3 13.8 %collective-permute-done.9.refs_3_ = bf16[2,512,512]{2,1,0:T(8,128)(2,1)S(1)} collective-permute-done((bf16[2,512,512]{2,1,0:T(8,128)(2,1)S(1)}, bf16[2,512,512]{2,1,0:T(8,128)(2,1)S(1)}, u32[]{:S(2)}, u32[]{:S(2)}) %collective-permute-start.9) | collective-permute-done | bytes 1048608 | tf_op jit(solution)/shard_map/ppermute | solution.py:506
  73.1 1.9 %inner_sync.1 = (bf16[16,2,32,512]{3,2,1,0:T(8,128)(2,1)S(1)}, bf16[16,32,512]{2,1,0:T(8,128)(2,1)S(1)}, bf16[8,128]{1,0:T(8,128)(2,1)}) custom-call(s32[1]{0:T(128)S(6)} %copy.13.refs_0_, bf16[2,16,2,32,512]{4,3,2,1,0:T(8,128)(2,1)} %bitcast.5, bf16[2,512,512]{2,1,0:T(8,128)(2,1)S(1)} %get-tuple-element.113.refs_2_, ...), custom_call_target="tpu_custom_call" | custom-call | tf_op jit(solution)/shard_map/inner_sync/pallas_call | solution.py:68
  75.1 1.9 %collective-permute-done.10.refs_1_ = bf16[16,32,512]{2,1,0:T(8,128)(2,1)S(1)} collective-permute-done((bf16[16,32,512]{2,1,0:T(8,128)(2,1)S(1)}, bf16[16,32,512]{2,1,0:T(8,128)(2,1)S(1)}, u32[]{:S(2)}, u32[]{:S(2)}) %collective-permute-start.10) | collective-permute-done | bytes 524320 | tf_op jit(solution)/shard_map/ppermute | solution.py:506
  77.1 1.6 %collective-permute-start.11 = (bf16[2,4,32,512]{3,2,1,0:T(8,128)(2,1)S(1)}, bf16[2,4,32,512]{3,2,1,0:T(8,128)(2,1)S(1)}, u32[]{:S(2)}, u32[]{:S(2)}) collective-permute-start(bf16[2,4,32,512]{3,2,1,0:T(8,128)(2,1)S(1)} %get-tuple-element.120), channel_id=1, source_target_pairs={{0,64},{8,72},{16,80},{24,88},{32,96},{40,104},{48,112},{56,120},{... | collective-permute-start | bytes 786440 | tf_op jit(solution)/shard_map/ppermute | solution.py:506
  78.7 1.7 %collective-permute-start.16 = (bf16[256,1024]{1,0:T(8,128)(2,1)S(1)}, bf16[256,1024]{1,0:T(8,128)(2,1)S(1)}, u32[]{:S(2)}, u32[]{:S(2)}) collective-permute-start(bf16[256,1024]{1,0:T(8,128)(2,1)S(1)} %get-tuple-element.131), channel_id=1, source_target_pairs={{0,4},{1,5},{2,6},{3,7},{4,0},{5,1},{6,2},{7,3},{8,12},{9,13},{10,... | collective-permute-start | bytes 1572872 | tf_op jit(solution)/shard_map/ppermute | solution.py:506
  80.7 4.8 %collective-permute-done.11.refs_1_.refs_3_ = bf16[2,4,32,512]{3,2,1,0:T(8,128)(2,1)S(1)} collective-permute-done((bf16[2,4,32,512]{3,2,1,0:T(8,128)(2,1)S(1)}, bf16[2,4,32,512]{3,2,1,0:T(8,128)(2,1)S(1)}, u32[]{:S(2)}, u32[]{:S(2)}) %collective-permute-start.11) | collective-permute-done | bytes 262176 | tf_op jit(solution)/shard_map/ppermute | solution.py:506
  85.6 2.8 %collective-permute-start.14 = (bf16[4,32,512]{2,1,0:T(8,128)(2,1)S(1)}, bf16[4,32,512]{2,1,0:T(8,128)(2,1)S(1)}, u32[]{:S(2)}, u32[]{:S(2)}) collective-permute-start(bf16[4,32,512]{2,1,0:T(8,128)(2,1)S(1)} %get-tuple-element.128), channel_id=1, source_target_pairs={{0,192},{8,200},{16,208},{24,216},{32,224},{40,232},{48,240},{56,2... | collective-permute-start | bytes 393224 | tf_op jit(solution)/shard_map/ppermute | solution.py:506
  88.5 1.6 %collective-permute-start.19 = (bf16[256,1024]{1,0:T(8,128)(2,1)S(1)}, bf16[256,1024]{1,0:T(8,128)(2,1)S(1)}, u32[]{:S(2)}, u32[]{:S(2)}) collective-permute-start(bf16[256,1024]{1,0:T(8,128)(2,1)S(1)} %get-tuple-element.138), channel_id=1, source_target_pairs={{0,3},{1,2},{2,1},{3,0},{4,7},{5,6},{6,5},{7,4},{8,11},{9,10},{10,... | collective-permute-start | bytes 1572872 | tf_op jit(solution)/shard_map/ppermute | solution.py:506
  90.0 1.9 %collective-permute-start.20 = (bf16[256,1024]{1,0:T(8,128)(2,1)S(1)}, bf16[256,1024]{1,0:T(8,128)(2,1)S(1)}, u32[]{:S(2)}, u32[]{:S(2)}) collective-permute-start(bf16[256,1024]{1,0:T(8,128)(2,1)S(1)} %get-tuple-element.140), channel_id=1, source_target_pairs={{0,1},{1,0},{2,3},{3,2},{4,5},{5,4},{6,7},{7,6},{8,9},{9,8},{10,11... | collective-permute-start | bytes 1572872 | tf_op jit(solution)/shard_map/ppermute | solution.py:506
  92.0 3.4 %collective-permute-start.15 = (bf16[5,32,512]{2,1,0:T(8,128)(2,1)S(1)}, bf16[5,32,512]{2,1,0:T(8,128)(2,1)S(1)}, u32[]{:S(2)}, u32[]{:S(2)}) collective-permute-start(bf16[5,32,512]{2,1,0:T(8,128)(2,1)S(1)} %get-tuple-element.130.refs_0_), channel_id=1, source_target_pairs={{0,16},{8,24},{16,0},{24,8},{32,48},{40,56},{48,32},{56,40},{64,80... | collective-permute-start | bytes 491528 | tf_op jit(solution)/shard_map/ppermute | solution.py:506
  95.3 1.1 other_3.1
  96.5 5.2 %collective-permute-done.15.refs_1_ = bf16[5,32,512]{2,1,0:T(8,128)(2,1)S(1)} collective-permute-done((bf16[5,32,512]{2,1,0:T(8,128)(2,1)S(1)}, bf16[5,32,512]{2,1,0:T(8,128)(2,1)S(1)}, u32[]{:S(2)}, u32[]{:S(2)}) %collective-permute-start.15) | collective-permute-done | bytes 163872 | tf_op jit(solution)/shard_map/ppermute | solution.py:506
  101.7 3.7 %collective-permute-start.17 = (bf16[6,32,512]{2,1,0:T(8,128)(2,1)S(1)}, bf16[6,32,512]{2,1,0:T(8,128)(2,1)S(1)}, u32[]{:S(2)}, u32[]{:S(2)}) collective-permute-start(bf16[6,32,512]{2,1,0:T(8,128)(2,1)S(1)} %get-tuple-element.134.refs_0_.refs_3_), channel_id=1, source_target_pairs={{0,48},{8,56},{16,32},{24,40},{32,16},{40,24},{48,0},{56,8},{64,11... | collective-permute-start | bytes 589832 | tf_op jit(solution)/shard_map/ppermute | solution.py:506
  105.4 7.8 %collective-permute-done.17.refs_1_.refs_4_ = bf16[6,32,512]{2,1,0:T(8,128)(2,1)S(1)} collective-permute-done((bf16[6,32,512]{2,1,0:T(8,128)(2,1)S(1)}, bf16[6,32,512]{2,1,0:T(8,128)(2,1)S(1)}, u32[]{:S(2)}, u32[]{:S(2)}) %collective-permute-start.17) | collective-permute-done | bytes 196640 | tf_op jit(solution)/shard_map/ppermute | solution.py:506
  113.3 2.0 %collective-permute-start.18 = (bf16[4,32,512]{2,1,0:T(8,128)(2,1)S(1)}, bf16[4,32,512]{2,1,0:T(8,128)(2,1)S(1)}, u32[]{:S(2)}, u32[]{:S(2)}) collective-permute-start(bf16[4,32,512]{2,1,0:T(8,128)(2,1)S(1)} %get-tuple-element.136.refs_0_), channel_id=1, source_target_pairs={{0,192},{8,200},{16,208},{24,216},{32,224},{40,232},{48,240},{56,2... | collective-permute-start | bytes 393224 | tf_op jit(solution)/shard_map/ppermute | solution.py:506
  115.3 0.7 outer_sync.1
  116.0 3.1 %inner_other.1 = (bf16[16,2,32,512]{3,2,1,0:T(8,128)(2,1)S(1)}, bf16[16,32,512]{2,1,0:T(8,128)(2,1)S(1)}, bf16[2,16,2,32,512]{4,3,2,1,0:T(8,128)(2,1)}, bf16[8,128]{1,0:T(8,128)(2,1)}) custom-call(s32[1]{0:T(128)S(6)} %copy.13.refs_0_, bf16[2,16,2,32,512]{4,3,2,1,0:T(8,128)(2,1)} %bitcast.6, bf16[256,1024]{1,0:T(8,128)(2,1)S(1)} %get-tuple-element.137.refs_2_, ...), custom_call_target="tpu_custom_call" | custom-call | tf_op jit(solution)/shard_map/inner_other/pallas_call | solution.py:68
  119.7 1.5 collective-permute-done.22.refs_1_
  121.3 6.8 %collective-permute-done.21.refs_1_ = bf16[2,4,32,512]{3,2,1,0:T(8,128)(2,1)S(1)} collective-permute-done((bf16[2,4,32,512]{3,2,1,0:T(8,128)(2,1)S(1)}, bf16[2,4,32,512]{3,2,1,0:T(8,128)(2,1)S(1)}, u32[]{:S(2)}, u32[]{:S(2)}) %collective-permute-start.21) | collective-permute-done | bytes 262176 | tf_op jit(solution)/shard_map/ppermute | solution.py:506
  128.6 8.4 %collective-permute-done.24.refs_1_.refs_3_ = bf16[2,4,32,512]{3,2,1,0:T(8,128)(2,1)S(1)} collective-permute-done((bf16[2,4,32,512]{3,2,1,0:T(8,128)(2,1)S(1)}, bf16[2,4,32,512]{3,2,1,0:T(8,128)(2,1)S(1)}, u32[]{:S(2)}, u32[]{:S(2)}) %collective-permute-start.24) | collective-permute-done | bytes 262176 | tf_op jit(solution)/shard_map/ppermute | solution.py:506
  137.0 1.4 collective-permute-start.25
  138.4 1.4 mix.1
  139.8 3.6 %collective-permute-done.25.refs_1_ = bf16[4,32,512]{2,1,0:T(8,128)(2,1)S(1)} collective-permute-done((bf16[4,32,512]{2,1,0:T(8,128)(2,1)S(1)}, bf16[4,32,512]{2,1,0:T(8,128)(2,1)S(1)}, u32[]{:S(2)}, u32[]{:S(2)}) %collective-permute-start.25) | collective-permute-done | bytes 131104 | tf_op jit(solution)/shard_map/ppermute | solution.py:506
  143.4 4.3 %collective-permute-start.26 = (bf16[2,32,512]{2,1,0:T(8,128)(2,1)S(1)}, bf16[2,32,512]{2,1,0:T(8,128)(2,1)S(1)}, u32[]{:S(2)}, u32[]{:S(2)}) collective-permute-start(bf16[2,32,512]{2,1,0:T(8,128)(2,1)S(1)} %get-tuple-element.162), channel_id=1, source_target_pairs={{0,16},{8,24},{16,0},{24,8},{32,48},{40,56},{48,32},{56,40},{64,80... | collective-permute-start | bytes 196616 | tf_op jit(solution)/shard_map/ppermute | solution.py:506
  147.8 2.2 %collective-permute-done.26.refs_1_.refs_3_ = bf16[2,32,512]{2,1,0:T(8,128)(2,1)S(1)} collective-permute-done((bf16[2,32,512]{2,1,0:T(8,128)(2,1)S(1)}, bf16[2,32,512]{2,1,0:T(8,128)(2,1)S(1)}, u32[]{:S(2)}, u32[]{:S(2)}) %collective-permute-start.26) | collective-permute-done | bytes 65568 | tf_op jit(solution)/shard_map/ppermute | solution.py:506
  150.0 3.3 %collective-permute-start.27 = (bf16[32,512]{1,0:T(8,128)(2,1)S(1)}, bf16[32,512]{1,0:T(8,128)(2,1)S(1)}, u32[]{:S(2)}, u32[]{:S(2)}) collective-permute-start(bf16[32,512]{1,0:T(8,128)(2,1)S(1)} %get-tuple-element.165), channel_id=1, source_target_pairs={{0,48},{8,56},{16,32},{24,40},{32,16},{40,24},{48,0},{56,8},{64,11... | collective-permute-start | bytes 98312 | tf_op jit(solution)/shard_map/ppermute | solution.py:506
  153.4 2.8 %collective-permute-done.27.refs_3_ = bf16[32,512]{1,0:T(8,128)(2,1)S(1)} collective-permute-done((bf16[32,512]{1,0:T(8,128)(2,1)S(1)}, bf16[32,512]{1,0:T(8,128)(2,1)S(1)}, u32[]{:S(2)}, u32[]{:S(2)}) %collective-permute-start.27) | collective-permute-done | bytes 32800 | tf_op jit(solution)/shard_map/ppermute | solution.py:506
  156.1 0.6 outer_other.1
  (48 shorter events, 8.0 us)
Async XLA Ops:
  1.3 22.2 %slice-start = ((s8[8388608]{0:T(1024)(128)(4,1)}), s8[4194304]{0:T(1024)(128)(4,1)S(1)}, s32[]{:S(2)}) async-start(s8[8388608]{0:T(1024)(128)(4,1)} %bitcast.3), calls=%async_computation | async-start | bytes 8388608
  2.8 20.7 %collective-permute-start = (bf16[256,1536]{1,0:T(8,128)(2,1)S(1)}, bf16[256,1536]{1,0:T(8,128)(2,1)S(1)}, u32[]{:S(2)}, u32[]{:S(2)}) collective-permute-start(bf16[256,1536]{1,0:T(8,128)(2,1)S(1)} %get-tuple-element.87), channel_id=1, source_target_pairs={{0,1},{1,0},{2,3},{3,2},{4,5},{5,4},{6,7},{7,6},{8,9},{9,8},{10,11... | collective-permute-start | bytes 2359304 | tf_op jit(solution)/shard_map/ppermute | solution.py:506
  5.1 20.5 %collective-permute-start.2 = (bf16[256,1536]{1,0:T(8,128)(2,1)S(1)}, bf16[256,1536]{1,0:T(8,128)(2,1)S(1)}, u32[]{:S(2)}, u32[]{:S(2)}) collective-permute-start(bf16[256,1536]{1,0:T(8,128)(2,1)S(1)} %get-tuple-element.90), channel_id=1, source_target_pairs={{0,3},{1,2},{2,1},{3,0},{4,7},{5,6},{6,5},{7,4},{8,11},{9,10},{10,... | collective-permute-start | bytes 2359304 | tf_op jit(solution)/shard_map/ppermute | solution.py:506
  5.7 17.8 %slice-start.1 = ((s8[8388608]{0:T(1024)(128)(4,1)}), s8[4194304]{0:T(1024)(128)(4,1)S(1)}, s32[]{:S(2)}) async-start(s8[8388608]{0:T(1024)(128)(4,1)} %bitcast.3), calls=%async_computation.1 | async-start | bytes 8388608
  7.9 26.8 %collective-permute-start.1 = (bf16[256,1024]{1,0:T(8,128)(2,1)S(1)}, bf16[256,1024]{1,0:T(8,128)(2,1)S(1)}, u32[]{:S(2)}, u32[]{:S(2)}) collective-permute-start(bf16[256,1024]{1,0:T(8,128)(2,1)S(1)} %get-tuple-element.89), channel_id=1, source_target_pairs={{0,1},{1,0},{2,3},{3,2},{4,5},{5,4},{6,7},{7,6},{8,9},{9,8},{10,11... | collective-permute-start | bytes 1572872 | tf_op jit(solution)/shard_map/ppermute | solution.py:506
  9.4 27.5 %collective-permute-start.3 = (bf16[256,1024]{1,0:T(8,128)(2,1)S(1)}, bf16[256,1024]{1,0:T(8,128)(2,1)S(1)}, u32[]{:S(2)}, u32[]{:S(2)}) collective-permute-start(bf16[256,1024]{1,0:T(8,128)(2,1)S(1)} %get-tuple-element.91), channel_id=1, source_target_pairs={{0,3},{1,2},{2,1},{3,0},{4,7},{5,6},{6,5},{7,4},{8,11},{9,10},{10,... | collective-permute-start | bytes 1572872 | tf_op jit(solution)/shard_map/ppermute | solution.py:506
  10.1 42.9 %collective-permute-start.6 = (bf16[256,3584]{1,0:T(8,128)(2,1)S(1)}, bf16[256,3584]{1,0:T(8,128)(2,1)S(1)}, u32[]{:S(2)}, u32[]{:S(2)}) collective-permute-start(bf16[256,3584]{1,0:T(8,128)(2,1)S(1)} %get-tuple-element.105), channel_id=1, source_target_pairs={{0,4},{1,5},{2,6},{3,7},{4,0},{5,1},{6,2},{7,3},{8,12},{9,13},{10,... | collective-permute-start | bytes 5505032 | tf_op jit(solution)/shard_map/ppermute | solution.py:506
  26.2 19.8 %collective-permute-start.8 = (bf16[512,512]{1,0:T(8,128)(2,1)S(1)}, bf16[512,512]{1,0:T(8,128)(2,1)S(1)}, u32[]{:S(2)}, u32[]{:S(2)}) collective-permute-start(bf16[512,512]{1,0:T(8,128)(2,1)S(1)} %get-tuple-element.109), channel_id=1, source_target_pairs={{0,1},{1,0},{2,3},{3,2},{4,5},{5,4},{6,7},{7,6},{8,9},{9,8},{10,11... | collective-permute-start | bytes 1572872 | tf_op jit(solution)/shard_map/ppermute | solution.py:506
  27.6 20.4 %collective-permute-start.7 = (bf16[512,512]{1,0:T(8,128)(2,1)S(1)}, bf16[512,512]{1,0:T(8,128)(2,1)S(1)}, u32[]{:S(2)}, u32[]{:S(2)}) collective-permute-start(bf16[512,512]{1,0:T(8,128)(2,1)S(1)} %get-tuple-element.107), channel_id=1, source_target_pairs={{0,3},{1,2},{2,1},{3,0},{4,7},{5,6},{6,5},{7,4},{8,11},{9,10},{10,... | collective-permute-start | bytes 1572872 | tf_op jit(solution)/shard_map/ppermute | solution.py:506
  35.4 23.7 %collective-permute-start.4 = (bf16[512,512]{1,0:T(8,128)(2,1)S(1)}, bf16[512,512]{1,0:T(8,128)(2,1)S(1)}, u32[]{:S(2)}, u32[]{:S(2)}) collective-permute-start(bf16[512,512]{1,0:T(8,128)(2,1)S(1)} %get-tuple-element.100), channel_id=1, source_target_pairs={{0,3},{1,2},{2,1},{3,0},{4,7},{5,6},{6,5},{7,4},{8,11},{9,10},{10,... | collective-permute-start | bytes 1572872 | tf_op jit(solution)/shard_map/ppermute | solution.py:506
  37.5 21.6 %collective-permute-start.5 = (bf16[512,512]{1,0:T(8,128)(2,1)S(1)}, bf16[512,512]{1,0:T(8,128)(2,1)S(1)}, u32[]{:S(2)}, u32[]{:S(2)}) collective-permute-start(bf16[512,512]{1,0:T(8,128)(2,1)S(1)} %get-tuple-element.103), channel_id=1, source_target_pairs={{0,1},{1,0},{2,3},{3,2},{4,5},{5,4},{6,7},{7,6},{8,9},{9,8},{10,11... | collective-permute-start | bytes 1572872 | tf_op jit(solution)/shard_map/ppermute | solution.py:506
  48.3 24.8 %collective-permute-start.9 = (bf16[2,512,512]{2,1,0:T(8,128)(2,1)S(1)}, bf16[2,512,512]{2,1,0:T(8,128)(2,1)S(1)}, u32[]{:S(2)}, u32[]{:S(2)}) collective-permute-start(bf16[2,512,512]{2,1,0:T(8,128)(2,1)S(1)} %get-tuple-element.114), channel_id=1, source_target_pairs={{0,4},{1,5},{2,6},{3,7},{4,0},{5,1},{6,2},{7,3},{8,12},{9,13},{10,... | collective-permute-start | bytes 3145736 | tf_op jit(solution)/shard_map/ppermute | solution.py:506
  56.3 24.1 %collective-permute-start.12 = (bf16[2,256,1024]{2,1,0:T(8,128)(2,1)S(1)}, bf16[2,256,1024]{2,1,0:T(8,128)(2,1)S(1)}, u32[]{:S(2)}, u32[]{:S(2)}) collective-permute-start(bf16[2,256,1024]{2,1,0:T(8,128)(2,1)S(1)} %get-tuple-element.122), channel_id=1, source_target_pairs={{0,1},{1,0},{2,3},{3,2},{4,5},{5,4},{6,7},{7,6},{8,9},{9,8},{10,11... | collective-permute-start | bytes 3145736 | tf_op jit(solution)/shard_map/ppermute | solution.py:506
  57.5 23.0 %collective-permute-start.13 = (bf16[2,256,1024]{2,1,0:T(8,128)(2,1)S(1)}, bf16[2,256,1024]{2,1,0:T(8,128)(2,1)S(1)}, u32[]{:S(2)}, u32[]{:S(2)}) collective-permute-start(bf16[2,256,1024]{2,1,0:T(8,128)(2,1)S(1)} %get-tuple-element.124), channel_id=1, source_target_pairs={{0,3},{1,2},{2,1},{3,0},{4,7},{5,6},{6,5},{7,4},{8,11},{9,10},{10,... | collective-permute-start | bytes 3145736 | tf_op jit(solution)/shard_map/ppermute | solution.py:506
  75.0 2.0 %collective-permute-start.10 = (bf16[16,32,512]{2,1,0:T(8,128)(2,1)S(1)}, bf16[16,32,512]{2,1,0:T(8,128)(2,1)S(1)}, u32[]{:S(2)}, u32[]{:S(2)}) collective-permute-start(bf16[16,32,512]{2,1,0:T(8,128)(2,1)S(1)} %get-tuple-element.117), channel_id=1, source_target_pairs={{0,8},{8,0},{16,24},{24,16},{32,40},{40,32},{48,56},{56,48},{64,72... | collective-permute-start | bytes 1572872 | tf_op jit(solution)/shard_map/ppermute | solution.py:506
  77.1 8.4 %collective-permute-start.11 = (bf16[2,4,32,512]{3,2,1,0:T(8,128)(2,1)S(1)}, bf16[2,4,32,512]{3,2,1,0:T(8,128)(2,1)S(1)}, u32[]{:S(2)}, u32[]{:S(2)}) collective-permute-start(bf16[2,4,32,512]{3,2,1,0:T(8,128)(2,1)S(1)} %get-tuple-element.120), channel_id=1, source_target_pairs={{0,64},{8,72},{16,80},{24,88},{32,96},{40,104},{48,112},{56,120},{... | collective-permute-start | bytes 786440 | tf_op jit(solution)/shard_map/ppermute | solution.py:506
  78.7 16.7 %collective-permute-start.16 = (bf16[256,1024]{1,0:T(8,128)(2,1)S(1)}, bf16[256,1024]{1,0:T(8,128)(2,1)S(1)}, u32[]{:S(2)}, u32[]{:S(2)}) collective-permute-start(bf16[256,1024]{1,0:T(8,128)(2,1)S(1)} %get-tuple-element.131), channel_id=1, source_target_pairs={{0,4},{1,5},{2,6},{3,7},{4,0},{5,1},{6,2},{7,3},{8,12},{9,13},{10,... | collective-permute-start | bytes 1572872 | tf_op jit(solution)/shard_map/ppermute | solution.py:506
  80.4 11.5 %copy-start = (f32[2,32,512]{2,1,0:T(8,128)S(1)}, f32[2,32,512]{2,1,0:T(8,128)}, u32[]{:S(2)}) copy-start(f32[2,32,512]{2,1,0:T(8,128)} %refs_1_.25) | copy-start | bytes 393220
  80.4 11.5 %copy-start.1 = (f32[32,512]{1,0:T(8,128)S(1)}, f32[32,512]{1,0:T(8,128)}, u32[]{:S(2)}) copy-start(f32[32,512]{1,0:T(8,128)} %refs_2_.7) | copy-start | bytes 196612
  85.6 6.3 %collective-permute-start.14 = (bf16[4,32,512]{2,1,0:T(8,128)(2,1)S(1)}, bf16[4,32,512]{2,1,0:T(8,128)(2,1)S(1)}, u32[]{:S(2)}, u32[]{:S(2)}) collective-permute-start(bf16[4,32,512]{2,1,0:T(8,128)(2,1)S(1)} %get-tuple-element.128), channel_id=1, source_target_pairs={{0,192},{8,200},{16,208},{24,216},{32,224},{40,232},{48,240},{56,2... | collective-permute-start | bytes 393224 | tf_op jit(solution)/shard_map/ppermute | solution.py:506
  88.5 27.6 %collective-permute-start.19 = (bf16[256,1024]{1,0:T(8,128)(2,1)S(1)}, bf16[256,1024]{1,0:T(8,128)(2,1)S(1)}, u32[]{:S(2)}, u32[]{:S(2)}) collective-permute-start(bf16[256,1024]{1,0:T(8,128)(2,1)S(1)} %get-tuple-element.138), channel_id=1, source_target_pairs={{0,3},{1,2},{2,1},{3,0},{4,7},{5,6},{6,5},{7,4},{8,11},{9,10},{10,... | collective-permute-start | bytes 1572872 | tf_op jit(solution)/shard_map/ppermute | solution.py:506
  90.0 26.0 %collective-permute-start.20 = (bf16[256,1024]{1,0:T(8,128)(2,1)S(1)}, bf16[256,1024]{1,0:T(8,128)(2,1)S(1)}, u32[]{:S(2)}, u32[]{:S(2)}) collective-permute-start(bf16[256,1024]{1,0:T(8,128)(2,1)S(1)} %get-tuple-element.140), channel_id=1, source_target_pairs={{0,1},{1,0},{2,3},{3,2},{4,5},{5,4},{6,7},{7,6},{8,9},{9,8},{10,11... | collective-permute-start | bytes 1572872 | tf_op jit(solution)/shard_map/ppermute | solution.py:506
  92.0 9.7 %collective-permute-start.15 = (bf16[5,32,512]{2,1,0:T(8,128)(2,1)S(1)}, bf16[5,32,512]{2,1,0:T(8,128)(2,1)S(1)}, u32[]{:S(2)}, u32[]{:S(2)}) collective-permute-start(bf16[5,32,512]{2,1,0:T(8,128)(2,1)S(1)} %get-tuple-element.130.refs_0_), channel_id=1, source_target_pairs={{0,16},{8,24},{16,0},{24,8},{32,48},{40,56},{48,32},{56,40},{64,80... | collective-permute-start | bytes 491528 | tf_op jit(solution)/shard_map/ppermute | solution.py:506
  101.7 11.5 %collective-permute-start.17 = (bf16[6,32,512]{2,1,0:T(8,128)(2,1)S(1)}, bf16[6,32,512]{2,1,0:T(8,128)(2,1)S(1)}, u32[]{:S(2)}, u32[]{:S(2)}) collective-permute-start(bf16[6,32,512]{2,1,0:T(8,128)(2,1)S(1)} %get-tuple-element.134.refs_0_.refs_3_), channel_id=1, source_target_pairs={{0,48},{8,56},{16,32},{24,40},{32,16},{40,24},{48,0},{56,8},{64,11... | collective-permute-start | bytes 589832 | tf_op jit(solution)/shard_map/ppermute | solution.py:506
  113.3 6.3 %collective-permute-start.18 = (bf16[4,32,512]{2,1,0:T(8,128)(2,1)S(1)}, bf16[4,32,512]{2,1,0:T(8,128)(2,1)S(1)}, u32[]{:S(2)}, u32[]{:S(2)}) collective-permute-start(bf16[4,32,512]{2,1,0:T(8,128)(2,1)S(1)} %get-tuple-element.136.refs_0_), channel_id=1, source_target_pairs={{0,192},{8,200},{16,208},{24,216},{32,224},{40,232},{48,240},{56,2... | collective-permute-start | bytes 393224 | tf_op jit(solution)/shard_map/ppermute | solution.py:506
  119.2 2.0 %collective-permute-start.22 = (bf16[16,32,512]{2,1,0:T(8,128)(2,1)S(1)}, bf16[16,32,512]{2,1,0:T(8,128)(2,1)S(1)}, u32[]{:S(2)}, u32[]{:S(2)}) collective-permute-start(bf16[16,32,512]{2,1,0:T(8,128)(2,1)S(1)} %get-tuple-element.146), channel_id=1, source_target_pairs={{0,8},{8,0},{16,24},{24,16},{32,40},{40,32},{48,56},{56,48},{64,72... | collective-permute-start | bytes 1572872 | tf_op jit(solution)/shard_map/ppermute | solution.py:506
  119.6 8.5 %collective-permute-start.21 = (bf16[2,4,32,512]{3,2,1,0:T(8,128)(2,1)S(1)}, bf16[2,4,32,512]{3,2,1,0:T(8,128)(2,1)S(1)}, u32[]{:S(2)}, u32[]{:S(2)}) collective-permute-start(bf16[2,4,32,512]{3,2,1,0:T(8,128)(2,1)S(1)} %get-tuple-element.144.refs_0_), channel_id=1, source_target_pairs={{0,64},{8,72},{16,80},{24,88},{32,96},{40,104},{48,112},{56,120},{... | collective-permute-start | bytes 786440 | tf_op jit(solution)/shard_map/ppermute | solution.py:506
  128.1 10.3 %collective-permute-start.23 = (bf16[16,32,512]{2,1,0:T(8,128)(2,1)S(1)}, bf16[16,32,512]{2,1,0:T(8,128)(2,1)S(1)}, u32[]{:S(2)}, u32[]{:S(2)}) collective-permute-start(bf16[16,32,512]{2,1,0:T(8,128)(2,1)S(1)} %get-tuple-element.149.refs_2_), channel_id=1, source_target_pairs={{0,8},{8,0},{16,24},{24,16},{32,40},{40,32},{48,56},{56,48},{64,72... | collective-permute-start | bytes 1572872 | tf_op jit(solution)/shard_map/ppermute | solution.py:506
  128.2 8.7 %collective-permute-start.24 = (bf16[2,4,32,512]{3,2,1,0:T(8,128)(2,1)S(1)}, bf16[2,4,32,512]{3,2,1,0:T(8,128)(2,1)S(1)}, u32[]{:S(2)}, u32[]{:S(2)}) collective-permute-start(bf16[2,4,32,512]{3,2,1,0:T(8,128)(2,1)S(1)} %get-tuple-element.152), channel_id=1, source_target_pairs={{0,64},{8,72},{16,80},{24,88},{32,96},{40,104},{48,112},{56,120},{... | collective-permute-start | bytes 786440 | tf_op jit(solution)/shard_map/ppermute | solution.py:506
  137.0 6.3 %collective-permute-start.25 = (bf16[4,32,512]{2,1,0:T(8,128)(2,1)S(1)}, bf16[4,32,512]{2,1,0:T(8,128)(2,1)S(1)}, u32[]{:S(2)}, u32[]{:S(2)}) collective-permute-start(bf16[4,32,512]{2,1,0:T(8,128)(2,1)S(1)} %get-tuple-element.159), channel_id=1, source_target_pairs={{0,192},{8,200},{16,208},{24,216},{32,224},{40,232},{48,240},{56,2... | collective-permute-start | bytes 393224 | tf_op jit(solution)/shard_map/ppermute | solution.py:506
  143.4 6.6 %collective-permute-start.26 = (bf16[2,32,512]{2,1,0:T(8,128)(2,1)S(1)}, bf16[2,32,512]{2,1,0:T(8,128)(2,1)S(1)}, u32[]{:S(2)}, u32[]{:S(2)}) collective-permute-start(bf16[2,32,512]{2,1,0:T(8,128)(2,1)S(1)} %get-tuple-element.162), channel_id=1, source_target_pairs={{0,16},{8,24},{16,0},{24,8},{32,48},{40,56},{48,32},{56,40},{64,80... | collective-permute-start | bytes 196616 | tf_op jit(solution)/shard_map/ppermute | solution.py:506
  150.0 6.1 %collective-permute-start.27 = (bf16[32,512]{1,0:T(8,128)(2,1)S(1)}, bf16[32,512]{1,0:T(8,128)(2,1)S(1)}, u32[]{:S(2)}, u32[]{:S(2)}) collective-permute-start(bf16[32,512]{1,0:T(8,128)(2,1)S(1)} %get-tuple-element.165), channel_id=1, source_target_pairs={{0,48},{8,56},{16,32},{24,40},{32,16},{40,24},{48,0},{56,8},{64,11... | collective-permute-start | bytes 98312 | tf_op jit(solution)/shard_map/ppermute | solution.py:506

commit v7 on v6

--- a/solution.py
+++ b/solution.py
@@ -24,6 +24,8 @@
 SM = pl.BlockSpec(memory_space=pltpu.SMEM)
 MIB = 1024 * 1024
 BIG = 24
+LONG = 2 * 10**10
+SHORT = 3 * 10**9
 
 
 def place():
@@ -331,9 +333,9 @@
 QUAD = (4, 32, KV)
 
 
-def sums(name, outs, pairs, extra=()):
+def sums(name, outs, pairs, hint=0):
     def kernel(*refs):
-        out_refs = refs[2 * len(pairs) + len(extra) :]
+        out_refs = refs[2 * len(pairs) :]
         for i, (_, _, at_a, at_b, out, slot) in enumerate(pairs):
             a, b = refs[2 * i], refs[2 * i + 1]
             total = plus(a[...] if at_a is None else a[at_a], b[...] if at_b is None else b[at_b])
@@ -346,15 +348,16 @@
     return call(
         kernel,
         [shape(*d) for d in outs],
-        (*args, *extra),
-        [VM] * len(args) + [ANY] * len(extra),
+        args,
+        [VM] * len(args),
         [VM] * len(outs),
         name=name,
-    )
-
-
-def halve(name, dims, keep, recv):
-    return sums(name, [dims] * 2, [(keep, recv, 1, 1, 0, None), (keep, recv, 0, 0, 1, None)])
+        hint=hint,
+    )
+
+
+def halve(name, dims, keep, recv, hint=0):
+    return sums(name, [dims] * 2, [(keep, recv, 1, 1, 0, None), (keep, recv, 0, 0, 1, None)], hint)
 
 
 def sum_x(inner, recv, name):
@@ -365,41 +368,40 @@
     return call(to_z, (shape(2, 32, KV),) * 2, (keep, recv), [VM] * 2, [VM] * 2, name=name)
 
 
-def sync_z1(plan, anchors, momentum, keep, recv):
-    def kernel(plan_ref, anchor_ref, momentum_ref, keep_ref, recv_ref, out_ref):
-        out_ref[:4] = plus(keep_ref[...], recv_ref[...])
-        anchor = anchor_ref[lax.rem(plan_ref[0], 2)]
-        q = (1.0 - outer_rate * (1.0 + outer_beta)) * anchor - outer_rate * outer_beta**2 * momentum_ref[...]
-        out_ref[4] = q.astype(BF16)
-
-    return call(
-        kernel,
-        (shape(5, 32, KV),),
-        (plan, anchors, momentum, keep, recv),
-        [SM] + [VM] * 4,
-        [VM],
-        name="sync_z1",
-    )
-
-
-def sync_z3(sent, recv):
-    def kernel(sent_ref, recv_ref, out_ref):
-        out_ref[:4] = plus(sent_ref[:4], recv_ref[:4])
-        out_ref[4] = sent_ref[4]
-        out_ref[5] = recv_ref[4]
-
-    return call(kernel, (shape(6, 32, KV),), (sent, recv), [VM] * 2, [VM], name="sync_z3")
-
-
-def new_rows(sent, recv):
+def both_z1(keep, recv, short):
+    def kernel(keep_ref, recv_ref, short_ref, send_ref, stay_ref):
+        to_z(keep_ref, recv_ref, send_ref, stay_ref)
+        send_ref[2] = short_ref[...]
+
+    return call(
+        kernel,
+        (shape(3, 32, KV), shape(2, 32, KV)),
+        (keep, recv, short),
+        [VM] * 3,
+        [VM] * 2,
+        name="both_z1",
+    )
+
+
+def both_z3(stay, sent, recv):
+    def kernel(stay_ref, sent_ref, recv_ref, send_ref, keep_ref):
+        send_ref[0] = plus(stay_ref[1], recv_ref[1])
+        send_ref[1] = sent_ref[2]
+        send_ref[2] = recv_ref[2]
+        keep_ref[...] = plus(stay_ref[0], recv_ref[0])
+
+    return call(
+        kernel, (shape(3, 32, KV), shape(32, KV)), (stay, sent, recv), [VM] * 3, [VM] * 2, name="both_z3"
+    )
+
+
+def row_of(sent, recv):
     def kernel(sent_ref, recv_ref, out_ref):
         zh = place()[1]
-        for ref, at, j in ((sent_ref, 4, 0), (sent_ref, 5, 1), (recv_ref, 4, 3), (recv_ref, 5, 2)):
-            i = zh ^ j
-            mean = (sent_ref[i].astype(F32) + recv_ref[i].astype(F32)) / 32
-            out_ref[i] = (ref[at].astype(F32) + outer_rate * (1.0 + outer_beta) * mean).astype(BF16)
-
-    return call(kernel, (shape(*QUAD),), (sent, recv), [VM] * 2, [VM], name="new_rows")
+        for ref, at, j in ((sent_ref, 1, 0), (sent_ref, 2, 1), (recv_ref, 1, 3), (recv_ref, 2, 2)):
+            out_ref[zh ^ j] = ref[at]
+
+    return call(kernel, (shape(*QUAD),), (sent, recv), [VM] * 2, [VM], name="row")
 
 
 def join(a, b, hint=0):
@@ -420,30 +422,32 @@
 
 
 def outer_sync(plan, anchors, momentum, keep, recv):
-    def kernel(plan_ref, anchor_ref, momentum_ref, a, b, new_ref, moment_ref):
+    def kernel(plan_ref, anchor_ref, momentum_ref, a, b, new_ref, moment_ref, short_ref):
         s = lax.rem(plan_ref[0], 2)
-        zh = place()[1]
-        mean = (a[zh].astype(F32) + b[zh].astype(F32)) / 32
+        mean = (a[...].astype(F32) + b[...].astype(F32)) / 32
         anchor = anchor_ref[s]
         outer_grad = anchor - mean
         moment = outer_beta * momentum_ref[...] + outer_grad
-        new_ref[...] = anchor - outer_rate * (outer_grad + outer_beta * moment)
+        new = anchor - outer_rate * (outer_grad + outer_beta * moment)
+        new_ref[...] = new
         moment_ref[...] = moment
-
-    return call(
-        kernel,
-        (shape(32, KV, dtype=F32), shape(32, KV, dtype=F32)),
+        short_ref[...] = new.astype(BF16)
+
+    return call(
+        kernel,
+        (shape(32, KV, dtype=F32), shape(32, KV, dtype=F32), shape(32, KV)),
         (plan, anchors, momentum, keep, recv),
         [SM] + [VM] * 4,
-        [VM] * 2,
+        [VM] * 3,
         name="outer_sync",
+        hint=LONG,
     )
 
 
 def outer_other(plan, anchors, keep, recv):
     def kernel(plan_ref, anchor_ref, a, b, out_ref):
         other = 1 - lax.rem(plan_ref[0], 2)
-        out_ref[...] = anchor_ref[other] - (a[...].astype(F32) + b[...].astype(F32)) / 32
+        out_ref[...] = anchor_ref[other] - (a[...].astype(F32) + b[0].astype(F32)) / 32
 
     return call(
         kernel,
@@ -543,7 +547,7 @@
     near_a = swap(tile("send_a2", False, 3, 0, 1, (got_a1, got_a2)), "b")
     near_b = swap(tile("send_b2", False, 1, HALF, 1, (got_b1, got_b2)), "a")
     keep_a2 = tile("keep_a2", False, 0, 0, 0, (got_a1, got_a2))
-    keep_b2 = tile("keep_b2", False, 0, HALF, 0, (got_b1, got_b2), 4 * 10**10)
+    keep_b2 = tile("keep_b2", False, 0, HALF, 0, (got_b1, got_b2), 2 * LONG)
     across = swap(
         sums("far", [(2, KV, HALF)], [(keep_a1, far_a, None, None, 0, 0), (keep_b1, far_b, None, None, 0, 1)]), "z"
     )
@@ -556,7 +560,7 @@
         ],
         [pair, pair, half, half],
         (got_z1,),
-        10**10,
+        LONG,
     )
     got_0, got_1 = swap(send_0, "a"), swap(send_1, "b")
     near = sums("near", [(2, KV, HALF)], [(keep_a2, near_a, None, None, 0, 0), (keep_b2, near_b, None, None, 0, 1)])
@@ -569,31 +573,28 @@
     )
     last_0, last_1 = swap(last_0, "b"), swap(last_1, "a")
     send, keep = halve("sync_x3", QUAD, keep, recv)
-    sent = sync_z1(plan, anchors, momentum, keep, swap(send, "x3"))
-    recv = swap(sent, "z1")
-    mine_0, mine_1 = other("other_3", [dest(0, 1, 0, [(0, None, *lo), (1, None, *hi)])], [half, half], (got_z1, got_z3))
-    sent = sync_z3(sent, recv)
-    recv = swap(sent, "z3")
-    row = new_rows(sent, recv)
-    row_far = swap(row, "x3")
-    anchor_new, momentum_new = outer_sync(plan, anchors, momentum, sent, recv)
-
+    send, keep = sum_z(keep, swap(send, "x3"), "sync_z1")
+    recv = swap(send, "z1")
+    mine_0, mine_1 = other("other_3", [dest(0, 1, 0, [(0, None, *lo), (1, None, *hi)])], [half, half], (got_z1, got_z3), SHORT)
     inner_o, send_o, new = inner_other(plan, w, (mine_0, got_0, last_0), (mine_1, got_1, last_1))
     core_o = swap(send_o, "core")
-    own = join(row, row_far, 10**11)
-    got = swap(own, "x1")
-    send, keep = sum_x(inner_o, core_o, "other_x1")
-    recv = swap(send, "x1")
-    block = block_of(own, got)
-    block_far = swap(block, "core")
-    send, keep = halve("other_x3", QUAD, keep, recv)
-    recv = swap(send, "x3")
-    new = mix(plan, inner_s, block, block_far, new)
-    send, keep = sum_z(keep, recv, "other_z1")
-    recv = swap(send, "z1")
-    send, keep = halve("other_z3", (32, KV), keep, recv)
+    send, keep = halve("sync_z3", (32, KV), keep, recv, LONG)
     recv = swap(send, "z3")
+    send_o, keep_o = sum_x(inner_o, core_o, "other_x1")
+    recv_o = swap(send_o, "x1")
+    anchor_new, momentum_new, short = outer_sync(plan, anchors, momentum, keep, recv)
+    send_o, keep_o = halve("other_x3", QUAD, keep_o, recv_o)
+    recv_o = swap(send_o, "x3")
+    sent, keep = both_z1(keep_o, recv_o, short)
+    recv = swap(sent, "z1")
+    sent, keep = both_z3(keep, sent, recv)
+    recv = swap(sent, "z3")
+    row = row_of(sent, recv)
+    row_far = swap(row, "x3")
     pending = outer_other(plan, anchors, keep, recv)
+    own = join(row, row_far)
+    block = block_of(own, swap(own, "x1"))
+    new = mix(plan, inner_s, block, swap(block, "core"), new)
     return (new.reshape(1, 2, ROWS, KV), anchor_new, momentum_new, pending)
 
 

time: 158 us -> 151 us (0.956)
  waiting for transfers between devices: 88.4 us -> 81.8 us
    ppermute x28, waiting for transfers between devices: 88.4 us -> 81.8 us  [swap(): return lax.ppermute(value, *MOVES[move])]
  transfers between devices with their start and end apart: 28 -> 28, of which waited for: 18 -> 19; matrix products, arithmetic and copies ran while one was open for 0% -> 0% of each run, Pallas kernels for 13% -> 13%
where the time goes in v7:
time: 151 us; the launch traced here: 149 us
  waiting for transfers between devices  81.8 us (54%)
  starting transfers between devices  43.4 us (29%)
  Pallas kernels  22.1 us (15%)
  between operations  1.7 us (1%)
    ppermute x28, waiting for transfers between devices, swap(): return lax.ppermute(value, *MOVES[move])  81.8 us
    ppermute x28, starting transfers between devices, swap(): return lax.ppermute(value, *MOVES[move])  43.4 us
    pallas_call x31, Pallas kernels, call(): pl.pallas_call(chained, out_shape=outs + [in_hbm(8, 128)], in_specs=list(...  22.1 us
  transfers between devices with their start and end apart: 28, of which 19 were waited for; matrix products, arithmetic and copies ran while one was open for 0% of the time, Pallas kernels for 13%

profile of v7, /device:TPU:8, one launch (start us, length us, event | category | flops | bytes accessed | tf_op | source)
XLA Modules:
  0.0 148.9 jit_solution(2335479069645328648)
XLA Ops:
  1.3 1.5 %pack_1.1 = (bf16[256,1536]{1,0:T(8,128)(2,1)S(1)}, bf16[256,1536]{1,0:T(8,128)(2,1)S(1)}, bf16[512,256]{1,0:T(8,128)(2,1)S(1)}, bf16[8,128]{1,0:T(8,128)(2,1)}) custom-call(s32[1]{0:T(128)S(6)} %copy.13.refs_0_, s32[1,256]{1,0:T(1,128)} %bitcast.8, bf16[2,256,8192]{2,1,0:T(8,128)(2,1)} %refs_1_.21, bf16[2,256,512]{2,1,0:T(8,128)(2,1)} %refs_3_.3), custom_call_target="tpu_custom_call" | custom-call | tf_op jit(solution)/shard_map/pack_1/pallas_call | solution.py:70
  2.8 2.3 %collective-permute-start = (bf16[256,1536]{1,0:T(8,128)(2,1)S(1)}, bf16[256,1536]{1,0:T(8,128)(2,1)S(1)}, u32[]{:S(2)}, u32[]{:S(2)}) collective-permute-start(bf16[256,1536]{1,0:T(8,128)(2,1)S(1)} %get-tuple-element.90), channel_id=1, source_target_pairs={{0,1},{1,0},{2,3},{3,2},{4,5},{5,4},{6,7},{7,6},{8,9},{9,8},{10,11... | collective-permute-start | bytes 2359304 | tf_op jit(solution)/shard_map/ppermute | solution.py:510
  5.1 0.7 collective-permute-start.2
  5.7 2.2 %pack_2.1 = (bf16[256,3584]{1,0:T(8,128)(2,1)S(1)}, bf16[256,1024]{1,0:T(8,128)(2,1)S(1)}, bf16[256,1024]{1,0:T(8,128)(2,1)S(1)}, bf16[256,1024]{1,0:T(8,128)(2,...) custom-call(s32[1]{0:T(128)S(6)} %copy.13.refs_0_, s32[1,256]{1,0:T(1,128)} %bitcast.9, ...), custom_call_target="tpu_custom_call" | custom-call | tf_op jit(solution)/shard_map/pack_2/pallas_call | solution.py:70
  7.9 1.4 collective-permute-start.1
  9.4 0.7 collective-permute-start.3
  10.1 1.7 %collective-permute-start.6 = (bf16[256,3584]{1,0:T(8,128)(2,1)S(1)}, bf16[256,3584]{1,0:T(8,128)(2,1)S(1)}, u32[]{:S(2)}, u32[]{:S(2)}) collective-permute-start(bf16[256,3584]{1,0:T(8,128)(2,1)S(1)} %get-tuple-element.108), channel_id=1, source_target_pairs={{0,4},{1,5},{2,6},{3,7},{4,0},{5,1},{6,2},{7,3},{8,12},{9,13},{10,... | collective-permute-start | bytes 5505032 | tf_op jit(solution)/shard_map/ppermute | solution.py:510
  11.7 11.8 %collective-permute-done.refs_3_ = bf16[256,1536]{1,0:T(8,128)(2,1)S(1)} collective-permute-done((bf16[256,1536]{1,0:T(8,128)(2,1)S(1)}, bf16[256,1536]{1,0:T(8,128)(2,1)S(1)}, u32[]{:S(2)}, u32[]{:S(2)}) %collective-permute-start) | collective-permute-done | bytes 786464 | tf_op jit(solution)/shard_map/ppermute | solution.py:510
  24.1 1.4 collective-permute-done.2.refs_3_
  26.2 1.4 collective-permute-start.8
  27.6 1.3 collective-permute-start.7
  30.1 4.6 %collective-permute-done.1.refs_4_ = bf16[256,1024]{1,0:T(8,128)(2,1)S(1)} collective-permute-done((bf16[256,1024]{1,0:T(8,128)(2,1)S(1)}, bf16[256,1024]{1,0:T(8,128)(2,1)S(1)}, u32[]{:S(2)}, u32[]{:S(2)}) %collective-permute-start.1) | collective-permute-done | bytes 524320 | tf_op jit(solution)/shard_map/ppermute | solution.py:510
  35.4 1.5 collective-permute-start.4
  37.5 2.0 %collective-permute-start.5 = (bf16[512,512]{1,0:T(8,128)(2,1)S(1)}, bf16[512,512]{1,0:T(8,128)(2,1)S(1)}, u32[]{:S(2)}, u32[]{:S(2)}) collective-permute-start(bf16[512,512]{1,0:T(8,128)(2,1)S(1)} %get-tuple-element.106), channel_id=1, source_target_pairs={{0,1},{1,0},{2,3},{3,2},{4,5},{5,4},{6,7},{7,6},{8,9},{9,8},{10,11... | collective-permute-start | bytes 1572872 | tf_op jit(solution)/shard_map/ppermute | solution.py:510
  40.7 5.3 %collective-permute-done.8.refs_3_ = bf16[512,512]{1,0:T(8,128)(2,1)S(1)} collective-permute-done((bf16[512,512]{1,0:T(8,128)(2,1)S(1)}, bf16[512,512]{1,0:T(8,128)(2,1)S(1)}, u32[]{:S(2)}, u32[]{:S(2)}) %collective-permute-start.8) | collective-permute-done | bytes 524320 | tf_op jit(solution)/shard_map/ppermute | solution.py:510
  46.0 2.0 %collective-permute-done.7.refs_1_ = bf16[512,512]{1,0:T(8,128)(2,1)S(1)} collective-permute-done((bf16[512,512]{1,0:T(8,128)(2,1)S(1)}, bf16[512,512]{1,0:T(8,128)(2,1)S(1)}, u32[]{:S(2)}, u32[]{:S(2)}) %collective-permute-start.7) | collective-permute-done | bytes 524320 | tf_op jit(solution)/shard_map/ppermute | solution.py:510
  48.9 4.2 %collective-permute-done.6.refs_3_ = bf16[256,3584]{1,0:T(8,128)(2,1)S(1)} collective-permute-done((bf16[256,3584]{1,0:T(8,128)(2,1)S(1)}, bf16[256,3584]{1,0:T(8,128)(2,1)S(1)}, u32[]{:S(2)}, u32[]{:S(2)}) %collective-permute-start.6) | collective-permute-done | bytes 1835040 | tf_op jit(solution)/shard_map/ppermute | solution.py:510
  53.0 3.3 %other_1.1 = (bf16[2,256,1024]{2,1,0:T(8,128)(2,1)S(1)}, bf16[2,256,1024]{2,1,0:T(8,128)(2,1)S(1)}, bf16[256,1024]{1,0:T(8,128)(2,1)S(1)}, bf16[256,1024]{1,0:T(8,128)(2,1)S(1)}, bf16[8,128]{1,0:T(8,128)(2,1)}) custom-call(s32[1]{0:T(128)S(6)} %copy.13.refs_0_, bf16[2,256,8192]{2,1,0:T(8,128)(2,1)S(1)} %bitcast.4, ...), custom_call_target="tpu_custom_call" | custom-call | flops 20000000000 | tf_op jit(solution)/shard_map/other_1/pallas_call | solution.py:70
  56.3 1.1 collective-permute-start.13
  57.5 1.6 %collective-permute-start.14 = (bf16[2,256,1024]{2,1,0:T(8,128)(2,1)S(1)}, bf16[2,256,1024]{2,1,0:T(8,128)(2,1)S(1)}, u32[]{:S(2)}, u32[]{:S(2)}) collective-permute-start(bf16[2,256,1024]{2,1,0:T(8,128)(2,1)S(1)} %get-tuple-element.128), channel_id=1, source_target_pairs={{0,3},{1,2},{2,1},{3,0},{4,7},{5,6},{6,5},{7,4},{8,11},{9,10},{10,... | collective-permute-start | bytes 3145736 | tf_op jit(solution)/shard_map/ppermute | solution.py:510
  59.3 13.8 %collective-permute-done.9.refs_3_ = bf16[2,512,512]{2,1,0:T(8,128)(2,1)S(1)} collective-permute-done((bf16[2,512,512]{2,1,0:T(8,128)(2,1)S(1)}, bf16[2,512,512]{2,1,0:T(8,128)(2,1)S(1)}, u32[]{:S(2)}, u32[]{:S(2)}) %collective-permute-start.9) | collective-permute-done | bytes 1048608 | tf_op jit(solution)/shard_map/ppermute | solution.py:510
  73.1 1.9 %inner_sync.1 = (bf16[16,2,32,512]{3,2,1,0:T(8,128)(2,1)S(1)}, bf16[16,32,512]{2,1,0:T(8,128)(2,1)S(1)}, bf16[8,128]{1,0:T(8,128)(2,1)}) custom-call(s32[1]{0:T(128)S(6)} %copy.13.refs_0_, bf16[2,16,2,32,512]{4,3,2,1,0:T(8,128)(2,1)} %bitcast.5, bf16[2,512,512]{2,1,0:T(8,128)(2,1)S(1)} %get-tuple-element.116.refs_2_, ...), custom_call_target="tpu_custom_call" | custom-call | tf_op jit(solution)/shard_map/inner_sync/pallas_call | solution.py:70
  75.1 1.8 %collective-permute-start.10 = (bf16[256,1024]{1,0:T(8,128)(2,1)S(1)}, bf16[256,1024]{1,0:T(8,128)(2,1)S(1)}, u32[]{:S(2)}, u32[]{:S(2)}) collective-permute-start(bf16[256,1024]{1,0:T(8,128)(2,1)S(1)} %get-tuple-element.120), channel_id=1, source_target_pairs={{0,4},{1,5},{2,6},{3,7},{4,0},{5,1},{6,2},{7,3},{8,12},{9,13},{10,... | collective-permute-start | bytes 1572872 | tf_op jit(solution)/shard_map/ppermute | solution.py:510
  77.1 1.6 %collective-permute-start.12 = (bf16[2,4,32,512]{3,2,1,0:T(8,128)(2,1)S(1)}, bf16[2,4,32,512]{3,2,1,0:T(8,128)(2,1)S(1)}, u32[]{:S(2)}, u32[]{:S(2)}) collective-permute-start(bf16[2,4,32,512]{3,2,1,0:T(8,128)(2,1)S(1)} %get-tuple-element.124), channel_id=1, source_target_pairs={{0,64},{8,72},{16,80},{24,88},{32,96},{40,104},{48,112},{56,120},{... | collective-permute-start | bytes 786440 | tf_op jit(solution)/shard_map/ppermute | solution.py:510
  79.4 1.8 %collective-permute-start.16 = (bf16[256,1024]{1,0:T(8,128)(2,1)S(1)}, bf16[256,1024]{1,0:T(8,128)(2,1)S(1)}, u32[]{:S(2)}, u32[]{:S(2)}) collective-permute-start(bf16[256,1024]{1,0:T(8,128)(2,1)S(1)} %get-tuple-element.136), channel_id=1, source_target_pairs={{0,3},{1,2},{2,1},{3,0},{4,7},{5,6},{6,5},{7,4},{8,11},{9,10},{10,... | collective-permute-start | bytes 1572872 | tf_op jit(solution)/shard_map/ppermute | solution.py:510
  81.2 2.6 %collective-permute-start.17 = (bf16[256,1024]{1,0:T(8,128)(2,1)S(1)}, bf16[256,1024]{1,0:T(8,128)(2,1)S(1)}, u32[]{:S(2)}, u32[]{:S(2)}) collective-permute-start(bf16[256,1024]{1,0:T(8,128)(2,1)S(1)} %get-tuple-element.138), channel_id=1, source_target_pairs={{0,1},{1,0},{2,3},{3,2},{4,5},{5,4},{6,7},{7,6},{8,9},{9,8},{10,11... | collective-permute-start | bytes 1572872 | tf_op jit(solution)/shard_map/ppermute | solution.py:510
  83.8 1.7 %collective-permute-done.12.refs_1_.refs_3_ = bf16[2,4,32,512]{3,2,1,0:T(8,128)(2,1)S(1)} collective-permute-done((bf16[2,4,32,512]{3,2,1,0:T(8,128)(2,1)S(1)}, bf16[2,4,32,512]{3,2,1,0:T(8,128)(2,1)S(1)}, u32[]{:S(2)}, u32[]{:S(2)}) %collective-permute-start.12) | collective-permute-done | bytes 262176 | tf_op jit(solution)/shard_map/ppermute | solution.py:510
  85.6 2.8 %collective-permute-start.15 = (bf16[4,32,512]{2,1,0:T(8,128)(2,1)S(1)}, bf16[4,32,512]{2,1,0:T(8,128)(2,1)S(1)}, u32[]{:S(2)}, u32[]{:S(2)}) collective-permute-start(bf16[4,32,512]{2,1,0:T(8,128)(2,1)S(1)} %get-tuple-element.132), channel_id=1, source_target_pairs={{0,192},{8,200},{16,208},{24,216},{32,224},{40,232},{48,240},{56,2... | collective-permute-start | bytes 393224 | tf_op jit(solution)/shard_map/ppermute | solution.py:510
  88.5 3.4 %collective-permute-done.15.refs_1_ = bf16[4,32,512]{2,1,0:T(8,128)(2,1)S(1)} collective-permute-done((bf16[4,32,512]{2,1,0:T(8,128)(2,1)S(1)}, bf16[4,32,512]{2,1,0:T(8,128)(2,1)S(1)}, u32[]{:S(2)}, u32[]{:S(2)}) %collective-permute-start.15) | collective-permute-done | bytes 131104 | tf_op jit(solution)/shard_map/ppermute | solution.py:510
  91.9 3.4 %collective-permute-start.19 = (bf16[2,32,512]{2,1,0:T(8,128)(2,1)S(1)}, bf16[2,32,512]{2,1,0:T(8,128)(2,1)S(1)}, u32[]{:S(2)}, u32[]{:S(2)}) collective-permute-start(bf16[2,32,512]{2,1,0:T(8,128)(2,1)S(1)} %get-tuple-element.143), channel_id=1, source_target_pairs={{0,16},{8,24},{16,0},{24,8},{32,48},{40,56},{48,32},{56,40},{64,80... | collective-permute-start | bytes 196616 | tf_op jit(solution)/shard_map/ppermute | solution.py:510
  95.3 1.1 other_3.1
  96.4 3.1 %inner_other.1 = (bf16[16,2,32,512]{3,2,1,0:T(8,128)(2,1)S(1)}, bf16[16,32,512]{2,1,0:T(8,128)(2,1)S(1)}, bf16[2,16,2,32,512]{4,3,2,1,0:T(8,128)(2,1)}, bf16[8,128]{1,0:T(8,128)(2,1)}) custom-call(s32[1]{0:T(128)S(6)} %copy.13.refs_0_, bf16[2,16,2,32,512]{4,3,2,1,0:T(8,128)(2,1)} %bitcast.6, bf16[256,1024]{1,0:T(8,128)(2,1)S(1)} %get-tuple-element.135.refs_2_, ...), custom_call_target="tpu_custom_call" | custom-call | tf_op jit(solution)/shard_map/inner_other/pallas_call | solution.py:70
  99.7 4.4 %collective-permute-start.21 = (bf16[32,512]{1,0:T(8,128)(2,1)S(1)}, bf16[32,512]{1,0:T(8,128)(2,1)S(1)}, u32[]{:S(2)}, u32[]{:S(2)}) collective-permute-start(bf16[32,512]{1,0:T(8,128)(2,1)S(1)} %get-tuple-element.149), channel_id=1, source_target_pairs={{0,48},{8,56},{16,32},{24,40},{32,16},{40,24},{48,0},{56,8},{64,11... | collective-permute-start | bytes 98312 | tf_op jit(solution)/shard_map/ppermute | solution.py:510
  104.6 1.6 %collective-permute-done.21.refs_4_ = bf16[32,512]{1,0:T(8,128)(2,1)S(1)} collective-permute-done((bf16[32,512]{1,0:T(8,128)(2,1)S(1)}, bf16[32,512]{1,0:T(8,128)(2,1)S(1)}, u32[]{:S(2)}, u32[]{:S(2)}) %collective-permute-start.21) | collective-permute-done | bytes 32800 | tf_op jit(solution)/shard_map/ppermute | solution.py:510
  106.3 0.7 outer_sync.1
  106.9 5.8 %collective-permute-done.20.refs_1_.refs_3_ = bf16[2,4,32,512]{3,2,1,0:T(8,128)(2,1)S(1)} collective-permute-done((bf16[2,4,32,512]{3,2,1,0:T(8,128)(2,1)S(1)}, bf16[2,4,32,512]{3,2,1,0:T(8,128)(2,1)S(1)}, u32[]{:S(2)}, u32[]{:S(2)}) %collective-permute-start.20) | collective-permute-done | bytes 262176 | tf_op jit(solution)/shard_map/ppermute | solution.py:510
  112.8 2.8 %collective-permute-start.22 = (bf16[4,32,512]{2,1,0:T(8,128)(2,1)S(1)}, bf16[4,32,512]{2,1,0:T(8,128)(2,1)S(1)}, u32[]{:S(2)}, u32[]{:S(2)}) collective-permute-start(bf16[4,32,512]{2,1,0:T(8,128)(2,1)S(1)} %get-tuple-element.153), channel_id=1, source_target_pairs={{0,192},{8,200},{16,208},{24,216},{32,224},{40,232},{48,240},{56,2... | collective-permute-start | bytes 393224 | tf_op jit(solution)/shard_map/ppermute | solution.py:510
  115.7 3.4 %collective-permute-done.22.refs_1_ = bf16[4,32,512]{2,1,0:T(8,128)(2,1)S(1)} collective-permute-done((bf16[4,32,512]{2,1,0:T(8,128)(2,1)S(1)}, bf16[4,32,512]{2,1,0:T(8,128)(2,1)S(1)}, u32[]{:S(2)}, u32[]{:S(2)}) %collective-permute-start.22) | collective-permute-done | bytes 131104 | tf_op jit(solution)/shard_map/ppermute | solution.py:510
  119.1 1.6 %collective-permute-start.23 = (bf16[3,32,512]{2,1,0:T(8,128)(2,1)S(1)}, bf16[3,32,512]{2,1,0:T(8,128)(2,1)S(1)}, u32[]{:S(2)}, u32[]{:S(2)}) collective-permute-start(bf16[3,32,512]{2,1,0:T(8,128)(2,1)S(1)} %get-tuple-element.157.refs_1_), channel_id=1, source_target_pairs={{0,16},{8,24},{16,0},{24,8},{32,48},{40,56},{48,32},{56,40},{64,80... | collective-permute-start | bytes 294920 | tf_op jit(solution)/shard_map/ppermute | solution.py:510
  120.7 5.1 %collective-permute-done.23.refs_2_ = bf16[3,32,512]{2,1,0:T(8,128)(2,1)S(1)} collective-permute-done((bf16[3,32,512]{2,1,0:T(8,128)(2,1)S(1)}, bf16[3,32,512]{2,1,0:T(8,128)(2,1)S(1)}, u32[]{:S(2)}, u32[]{:S(2)}) %collective-permute-start.23) | collective-permute-done | bytes 98336 | tf_op jit(solution)/shard_map/ppermute | solution.py:510
  125.8 0.8 collective-permute-start.24
  126.6 6.0 %collective-permute-done.24.refs_1_.refs_3_ = bf16[3,32,512]{2,1,0:T(8,128)(2,1)S(1)} collective-permute-done((bf16[3,32,512]{2,1,0:T(8,128)(2,1)S(1)}, bf16[3,32,512]{2,1,0:T(8,128)(2,1)S(1)}, u32[]{:S(2)}, u32[]{:S(2)}) %collective-permute-start.24) | collective-permute-done | bytes 98336 | tf_op jit(solution)/shard_map/ppermute | solution.py:510
  132.6 2.8 %collective-permute-start.25 = (bf16[4,32,512]{2,1,0:T(8,128)(2,1)S(1)}, bf16[4,32,512]{2,1,0:T(8,128)(2,1)S(1)}, u32[]{:S(2)}, u32[]{:S(2)}) collective-permute-start(bf16[4,32,512]{2,1,0:T(8,128)(2,1)S(1)} %get-tuple-element.161.refs_0_), channel_id=1, source_target_pairs={{0,192},{8,200},{16,208},{24,216},{32,224},{40,232},{48,240},{56,2... | collective-permute-start | bytes 393224 | tf_op jit(solution)/shard_map/ppermute | solution.py:510
  135.5 0.6 outer_other.1
  136.1 2.8 %collective-permute-done.25.refs_1_ = bf16[4,32,512]{2,1,0:T(8,128)(2,1)S(1)} collective-permute-done((bf16[4,32,512]{2,1,0:T(8,128)(2,1)S(1)}, bf16[4,32,512]{2,1,0:T(8,128)(2,1)S(1)}, u32[]{:S(2)}, u32[]{:S(2)}) %collective-permute-start.25) | collective-permute-done | bytes 131104 | tf_op jit(solution)/shard_map/ppermute | solution.py:510
  139.0 6.4 %collective-permute-done.26.refs_1_ = bf16[2,4,32,512]{3,2,1,0:T(8,128)(2,1)S(1)} collective-permute-done((bf16[2,4,32,512]{3,2,1,0:T(8,128)(2,1)S(1)}, bf16[2,4,32,512]{3,2,1,0:T(8,128)(2,1)S(1)}, u32[]{:S(2)}, u32[]{:S(2)}) %collective-permute-start.26) | collective-permute-done | bytes 262176 | tf_op jit(solution)/shard_map/ppermute | solution.py:510
  145.5 1.9 %collective-permute-done.27.refs_3_ = bf16[16,32,512]{2,1,0:T(8,128)(2,1)S(1)} collective-permute-done((bf16[16,32,512]{2,1,0:T(8,128)(2,1)S(1)}, bf16[16,32,512]{2,1,0:T(8,128)(2,1)S(1)}, u32[]{:S(2)}, u32[]{:S(2)}) %collective-permute-start.27) | collective-permute-done | bytes 524320 | tf_op jit(solution)/shard_map/ppermute | solution.py:510
  147.4 1.4 mix.1
  (48 shorter events, 8.2 us)
Async XLA Ops:
  1.3 22.2 %slice-start = ((s8[8388608]{0:T(1024)(128)(4,1)}), s8[4194304]{0:T(1024)(128)(4,1)S(1)}, s32[]{:S(2)}) async-start(s8[8388608]{0:T(1024)(128)(4,1)} %bitcast.3), calls=%async_computation | async-start | bytes 8388608
  2.8 20.7 %collective-permute-start = (bf16[256,1536]{1,0:T(8,128)(2,1)S(1)}, bf16[256,1536]{1,0:T(8,128)(2,1)S(1)}, u32[]{:S(2)}, u32[]{:S(2)}) collective-permute-start(bf16[256,1536]{1,0:T(8,128)(2,1)S(1)} %get-tuple-element.90), channel_id=1, source_target_pairs={{0,1},{1,0},{2,3},{3,2},{4,5},{5,4},{6,7},{7,6},{8,9},{9,8},{10,11... | collective-permute-start | bytes 2359304 | tf_op jit(solution)/shard_map/ppermute | solution.py:510
  5.1 20.5 %collective-permute-start.2 = (bf16[256,1536]{1,0:T(8,128)(2,1)S(1)}, bf16[256,1536]{1,0:T(8,128)(2,1)S(1)}, u32[]{:S(2)}, u32[]{:S(2)}) collective-permute-start(bf16[256,1536]{1,0:T(8,128)(2,1)S(1)} %get-tuple-element.93), channel_id=1, source_target_pairs={{0,3},{1,2},{2,1},{3,0},{4,7},{5,6},{6,5},{7,4},{8,11},{9,10},{10,... | collective-permute-start | bytes 2359304 | tf_op jit(solution)/shard_map/ppermute | solution.py:510
  5.7 17.8 %slice-start.1 = ((s8[8388608]{0:T(1024)(128)(4,1)}), s8[4194304]{0:T(1024)(128)(4,1)S(1)}, s32[]{:S(2)}) async-start(s8[8388608]{0:T(1024)(128)(4,1)} %bitcast.3), calls=%async_computation.1 | async-start | bytes 8388608
  7.9 26.8 %collective-permute-start.1 = (bf16[256,1024]{1,0:T(8,128)(2,1)S(1)}, bf16[256,1024]{1,0:T(8,128)(2,1)S(1)}, u32[]{:S(2)}, u32[]{:S(2)}) collective-permute-start(bf16[256,1024]{1,0:T(8,128)(2,1)S(1)} %get-tuple-element.92), channel_id=1, source_target_pairs={{0,1},{1,0},{2,3},{3,2},{4,5},{5,4},{6,7},{7,6},{8,9},{9,8},{10,11... | collective-permute-start | bytes 1572872 | tf_op jit(solution)/shard_map/ppermute | solution.py:510
  9.4 27.5 %collective-permute-start.3 = (bf16[256,1024]{1,0:T(8,128)(2,1)S(1)}, bf16[256,1024]{1,0:T(8,128)(2,1)S(1)}, u32[]{:S(2)}, u32[]{:S(2)}) collective-permute-start(bf16[256,1024]{1,0:T(8,128)(2,1)S(1)} %get-tuple-element.94), channel_id=1, source_target_pairs={{0,3},{1,2},{2,1},{3,0},{4,7},{5,6},{6,5},{7,4},{8,11},{9,10},{10,... | collective-permute-start | bytes 1572872 | tf_op jit(solution)/shard_map/ppermute | solution.py:510
  10.1 42.9 %collective-permute-start.6 = (bf16[256,3584]{1,0:T(8,128)(2,1)S(1)}, bf16[256,3584]{1,0:T(8,128)(2,1)S(1)}, u32[]{:S(2)}, u32[]{:S(2)}) collective-permute-start(bf16[256,3584]{1,0:T(8,128)(2,1)S(1)} %get-tuple-element.108), channel_id=1, source_target_pairs={{0,4},{1,5},{2,6},{3,7},{4,0},{5,1},{6,2},{7,3},{8,12},{9,13},{10,... | collective-permute-start | bytes 5505032 | tf_op jit(solution)/shard_map/ppermute | solution.py:510
  26.2 19.8 %collective-permute-start.8 = (bf16[512,512]{1,0:T(8,128)(2,1)S(1)}, bf16[512,512]{1,0:T(8,128)(2,1)S(1)}, u32[]{:S(2)}, u32[]{:S(2)}) collective-permute-start(bf16[512,512]{1,0:T(8,128)(2,1)S(1)} %get-tuple-element.112), channel_id=1, source_target_pairs={{0,1},{1,0},{2,3},{3,2},{4,5},{5,4},{6,7},{7,6},{8,9},{9,8},{10,11... | collective-permute-start | bytes 1572872 | tf_op jit(solution)/shard_map/ppermute | solution.py:510
  27.6 20.4 %collective-permute-start.7 = (bf16[512,512]{1,0:T(8,128)(2,1)S(1)}, bf16[512,512]{1,0:T(8,128)(2,1)S(1)}, u32[]{:S(2)}, u32[]{:S(2)}) collective-permute-start(bf16[512,512]{1,0:T(8,128)(2,1)S(1)} %get-tuple-element.110), channel_id=1, source_target_pairs={{0,3},{1,2},{2,1},{3,0},{4,7},{5,6},{6,5},{7,4},{8,11},{9,10},{10,... | collective-permute-start | bytes 1572872 | tf_op jit(solution)/shard_map/ppermute | solution.py:510
  35.4 23.7 %collective-permute-start.4 = (bf16[512,512]{1,0:T(8,128)(2,1)S(1)}, bf16[512,512]{1,0:T(8,128)(2,1)S(1)}, u32[]{:S(2)}, u32[]{:S(2)}) collective-permute-start(bf16[512,512]{1,0:T(8,128)(2,1)S(1)} %get-tuple-element.103), channel_id=1, source_target_pairs={{0,3},{1,2},{2,1},{3,0},{4,7},{5,6},{6,5},{7,4},{8,11},{9,10},{10,... | collective-permute-start | bytes 1572872 | tf_op jit(solution)/shard_map/ppermute | solution.py:510
  37.5 21.6 %collective-permute-start.5 = (bf16[512,512]{1,0:T(8,128)(2,1)S(1)}, bf16[512,512]{1,0:T(8,128)(2,1)S(1)}, u32[]{:S(2)}, u32[]{:S(2)}) collective-permute-start(bf16[512,512]{1,0:T(8,128)(2,1)S(1)} %get-tuple-element.106), channel_id=1, source_target_pairs={{0,1},{1,0},{2,3},{3,2},{4,5},{5,4},{6,7},{7,6},{8,9},{9,8},{10,11... | collective-permute-start | bytes 1572872 | tf_op jit(solution)/shard_map/ppermute | solution.py:510
  48.3 24.8 %collective-permute-start.9 = (bf16[2,512,512]{2,1,0:T(8,128)(2,1)S(1)}, bf16[2,512,512]{2,1,0:T(8,128)(2,1)S(1)}, u32[]{:S(2)}, u32[]{:S(2)}) collective-permute-start(bf16[2,512,512]{2,1,0:T(8,128)(2,1)S(1)} %get-tuple-element.117), channel_id=1, source_target_pairs={{0,4},{1,5},{2,6},{3,7},{4,0},{5,1},{6,2},{7,3},{8,12},{9,13},{10,... | collective-permute-start | bytes 3145736 | tf_op jit(solution)/shard_map/ppermute | solution.py:510
  56.3 22.4 %collective-permute-start.13 = (bf16[2,256,1024]{2,1,0:T(8,128)(2,1)S(1)}, bf16[2,256,1024]{2,1,0:T(8,128)(2,1)S(1)}, u32[]{:S(2)}, u32[]{:S(2)}) collective-permute-start(bf16[2,256,1024]{2,1,0:T(8,128)(2,1)S(1)} %get-tuple-element.126), channel_id=1, source_target_pairs={{0,1},{1,0},{2,3},{3,2},{4,5},{5,4},{6,7},{7,6},{8,9},{9,8},{10,11... | collective-permute-start | bytes 3145736 | tf_op jit(solution)/shard_map/ppermute | solution.py:510
  57.5 21.7 %collective-permute-start.14 = (bf16[2,256,1024]{2,1,0:T(8,128)(2,1)S(1)}, bf16[2,256,1024]{2,1,0:T(8,128)(2,1)S(1)}, u32[]{:S(2)}, u32[]{:S(2)}) collective-permute-start(bf16[2,256,1024]{2,1,0:T(8,128)(2,1)S(1)} %get-tuple-element.128), channel_id=1, source_target_pairs={{0,3},{1,2},{2,1},{3,0},{4,7},{5,6},{6,5},{7,4},{8,11},{9,10},{10,... | collective-permute-start | bytes 3145736 | tf_op jit(solution)/shard_map/ppermute | solution.py:510
  75.0 2.0 %collective-permute-start.11 = (bf16[16,32,512]{2,1,0:T(8,128)(2,1)S(1)}, bf16[16,32,512]{2,1,0:T(8,128)(2,1)S(1)}, u32[]{:S(2)}, u32[]{:S(2)}) collective-permute-start(bf16[16,32,512]{2,1,0:T(8,128)(2,1)S(1)} %get-tuple-element.121), channel_id=1, source_target_pairs={{0,8},{8,0},{16,24},{24,16},{32,40},{40,32},{48,56},{56,48},{64,72... | collective-permute-start | bytes 1572872 | tf_op jit(solution)/shard_map/ppermute | solution.py:510
  75.1 20.2 %collective-permute-start.10 = (bf16[256,1024]{1,0:T(8,128)(2,1)S(1)}, bf16[256,1024]{1,0:T(8,128)(2,1)S(1)}, u32[]{:S(2)}, u32[]{:S(2)}) collective-permute-start(bf16[256,1024]{1,0:T(8,128)(2,1)S(1)} %get-tuple-element.120), channel_id=1, source_target_pairs={{0,4},{1,5},{2,6},{3,7},{4,0},{5,1},{6,2},{7,3},{8,12},{9,13},{10,... | collective-permute-start | bytes 1572872 | tf_op jit(solution)/shard_map/ppermute | solution.py:510
  77.1 8.4 %collective-permute-start.12 = (bf16[2,4,32,512]{3,2,1,0:T(8,128)(2,1)S(1)}, bf16[2,4,32,512]{3,2,1,0:T(8,128)(2,1)S(1)}, u32[]{:S(2)}, u32[]{:S(2)}) collective-permute-start(bf16[2,4,32,512]{3,2,1,0:T(8,128)(2,1)S(1)} %get-tuple-element.124), channel_id=1, source_target_pairs={{0,64},{8,72},{16,80},{24,88},{32,96},{40,104},{48,112},{56,120},{... | collective-permute-start | bytes 786440 | tf_op jit(solution)/shard_map/ppermute | solution.py:510
  79.4 17.0 %collective-permute-start.16 = (bf16[256,1024]{1,0:T(8,128)(2,1)S(1)}, bf16[256,1024]{1,0:T(8,128)(2,1)S(1)}, u32[]{:S(2)}, u32[]{:S(2)}) collective-permute-start(bf16[256,1024]{1,0:T(8,128)(2,1)S(1)} %get-tuple-element.136), channel_id=1, source_target_pairs={{0,3},{1,2},{2,1},{3,0},{4,7},{5,6},{6,5},{7,4},{8,11},{9,10},{10,... | collective-permute-start | bytes 1572872 | tf_op jit(solution)/shard_map/ppermute | solution.py:510
  81.2 15.2 %collective-permute-start.17 = (bf16[256,1024]{1,0:T(8,128)(2,1)S(1)}, bf16[256,1024]{1,0:T(8,128)(2,1)S(1)}, u32[]{:S(2)}, u32[]{:S(2)}) collective-permute-start(bf16[256,1024]{1,0:T(8,128)(2,1)S(1)} %get-tuple-element.138), channel_id=1, source_target_pairs={{0,1},{1,0},{2,3},{3,2},{4,5},{5,4},{6,7},{7,6},{8,9},{9,8},{10,11... | collective-permute-start | bytes 1572872 | tf_op jit(solution)/shard_map/ppermute | solution.py:510
  85.6 6.3 %collective-permute-start.15 = (bf16[4,32,512]{2,1,0:T(8,128)(2,1)S(1)}, bf16[4,32,512]{2,1,0:T(8,128)(2,1)S(1)}, u32[]{:S(2)}, u32[]{:S(2)}) collective-permute-start(bf16[4,32,512]{2,1,0:T(8,128)(2,1)S(1)} %get-tuple-element.132), channel_id=1, source_target_pairs={{0,192},{8,200},{16,208},{24,216},{32,224},{40,232},{48,240},{56,2... | collective-permute-start | bytes 393224 | tf_op jit(solution)/shard_map/ppermute | solution.py:510
  91.9 7.8 %collective-permute-start.19 = (bf16[2,32,512]{2,1,0:T(8,128)(2,1)S(1)}, bf16[2,32,512]{2,1,0:T(8,128)(2,1)S(1)}, u32[]{:S(2)}, u32[]{:S(2)}) collective-permute-start(bf16[2,32,512]{2,1,0:T(8,128)(2,1)S(1)} %get-tuple-element.143), channel_id=1, source_target_pairs={{0,16},{8,24},{16,0},{24,8},{32,48},{40,56},{48,32},{56,40},{64,80... | collective-permute-start | bytes 196616 | tf_op jit(solution)/shard_map/ppermute | solution.py:510
  99.6 4.6 %collective-permute-start.18 = (bf16[16,32,512]{2,1,0:T(8,128)(2,1)S(1)}, bf16[16,32,512]{2,1,0:T(8,128)(2,1)S(1)}, u32[]{:S(2)}, u32[]{:S(2)}) collective-permute-start(bf16[16,32,512]{2,1,0:T(8,128)(2,1)S(1)} %get-tuple-element.141), channel_id=1, source_target_pairs={{0,8},{8,0},{16,24},{24,16},{32,40},{40,32},{48,56},{56,48},{64,72... | collective-permute-start | bytes 1572872 | tf_op jit(solution)/shard_map/ppermute | solution.py:510
  99.7 6.6 %copy-start = (f32[2,32,512]{2,1,0:T(8,128)S(1)}, f32[2,32,512]{2,1,0:T(8,128)}, u32[]{:S(2)}) copy-start(f32[2,32,512]{2,1,0:T(8,128)} %refs_1_.23) | copy-start | bytes 393220
  99.7 6.6 %copy-start.1 = (f32[32,512]{1,0:T(8,128)S(1)}, f32[32,512]{1,0:T(8,128)}, u32[]{:S(2)}) copy-start(f32[32,512]{1,0:T(8,128)} %refs_2_.5) | copy-start | bytes 196612
  99.7 6.5 %collective-permute-start.21 = (bf16[32,512]{1,0:T(8,128)(2,1)S(1)}, bf16[32,512]{1,0:T(8,128)(2,1)S(1)}, u32[]{:S(2)}, u32[]{:S(2)}) collective-permute-start(bf16[32,512]{1,0:T(8,128)(2,1)S(1)} %get-tuple-element.149), channel_id=1, source_target_pairs={{0,48},{8,56},{16,32},{24,40},{32,16},{40,24},{48,0},{56,8},{64,11... | collective-permute-start | bytes 98312 | tf_op jit(solution)/shard_map/ppermute | solution.py:510
  104.3 8.5 %collective-permute-start.20 = (bf16[2,4,32,512]{3,2,1,0:T(8,128)(2,1)S(1)}, bf16[2,4,32,512]{3,2,1,0:T(8,128)(2,1)S(1)}, u32[]{:S(2)}, u32[]{:S(2)}) collective-permute-start(bf16[2,4,32,512]{3,2,1,0:T(8,128)(2,1)S(1)} %get-tuple-element.147), channel_id=1, source_target_pairs={{0,64},{8,72},{16,80},{24,88},{32,96},{40,104},{48,112},{56,120},{... | collective-permute-start | bytes 786440 | tf_op jit(solution)/shard_map/ppermute | solution.py:510
  112.8 6.3 %collective-permute-start.22 = (bf16[4,32,512]{2,1,0:T(8,128)(2,1)S(1)}, bf16[4,32,512]{2,1,0:T(8,128)(2,1)S(1)}, u32[]{:S(2)}, u32[]{:S(2)}) collective-permute-start(bf16[4,32,512]{2,1,0:T(8,128)(2,1)S(1)} %get-tuple-element.153), channel_id=1, source_target_pairs={{0,192},{8,200},{16,208},{24,216},{32,224},{40,232},{48,240},{56,2... | collective-permute-start | bytes 393224 | tf_op jit(solution)/shard_map/ppermute | solution.py:510
  119.1 6.7 %collective-permute-start.23 = (bf16[3,32,512]{2,1,0:T(8,128)(2,1)S(1)}, bf16[3,32,512]{2,1,0:T(8,128)(2,1)S(1)}, u32[]{:S(2)}, u32[]{:S(2)}) collective-permute-start(bf16[3,32,512]{2,1,0:T(8,128)(2,1)S(1)} %get-tuple-element.157.refs_1_), channel_id=1, source_target_pairs={{0,16},{8,24},{16,0},{24,8},{32,48},{40,56},{48,32},{56,40},{64,80... | collective-permute-start | bytes 294920 | tf_op jit(solution)/shard_map/ppermute | solution.py:510
  125.8 6.8 %collective-permute-start.24 = (bf16[3,32,512]{2,1,0:T(8,128)(2,1)S(1)}, bf16[3,32,512]{2,1,0:T(8,128)(2,1)S(1)}, u32[]{:S(2)}, u32[]{:S(2)}) collective-permute-start(bf16[3,32,512]{2,1,0:T(8,128)(2,1)S(1)} %get-tuple-element.159.refs_0_), channel_id=1, source_target_pairs={{0,48},{8,56},{16,32},{24,40},{32,16},{40,24},{48,0},{56,8},{64,11... | collective-permute-start | bytes 294920 | tf_op jit(solution)/shard_map/ppermute | solution.py:510
  132.6 6.3 %collective-permute-start.25 = (bf16[4,32,512]{2,1,0:T(8,128)(2,1)S(1)}, bf16[4,32,512]{2,1,0:T(8,128)(2,1)S(1)}, u32[]{:S(2)}, u32[]{:S(2)}) collective-permute-start(bf16[4,32,512]{2,1,0:T(8,128)(2,1)S(1)} %get-tuple-element.161.refs_0_), channel_id=1, source_target_pairs={{0,192},{8,200},{16,208},{24,216},{32,224},{40,232},{48,240},{56,2... | collective-permute-start | bytes 393224 | tf_op jit(solution)/shard_map/ppermute | solution.py:510
  138.9 6.5 %collective-permute-start.26 = (bf16[2,4,32,512]{3,2,1,0:T(8,128)(2,1)S(1)}, bf16[2,4,32,512]{3,2,1,0:T(8,128)(2,1)S(1)}, u32[]{:S(2)}, u32[]{:S(2)}) collective-permute-start(bf16[2,4,32,512]{3,2,1,0:T(8,128)(2,1)S(1)} %get-tuple-element.165.refs_0_), channel_id=1, source_target_pairs={{0,64},{8,72},{16,80},{24,88},{32,96},{40,104},{48,112},{56,120},{... | collective-permute-start | bytes 786440 | tf_op jit(solution)/shard_map/ppermute | solution.py:510
  145.4 2.0 %collective-permute-start.27 = (bf16[16,32,512]{2,1,0:T(8,128)(2,1)S(1)}, bf16[16,32,512]{2,1,0:T(8,128)(2,1)S(1)}, u32[]{:S(2)}, u32[]{:S(2)}) collective-permute-start(bf16[16,32,512]{2,1,0:T(8,128)(2,1)S(1)} %get-tuple-element.167.refs_2_), channel_id=1, source_target_pairs={{0,8},{8,0},{16,24},{24,16},{32,40},{40,32},{48,56},{56,48},{64,72... | collective-permute-start | bytes 1572872 | tf_op jit(solution)/shard_map/ppermute | solution.py:510

commit v8 on v7

--- a/solution.py
+++ b/solution.py
@@ -368,57 +368,11 @@
     return call(to_z, (shape(2, 32, KV),) * 2, (keep, recv), [VM] * 2, [VM] * 2, name=name)
 
 
-def both_z1(keep, recv, short):
-    def kernel(keep_ref, recv_ref, short_ref, send_ref, stay_ref):
-        to_z(keep_ref, recv_ref, send_ref, stay_ref)
-        send_ref[2] = short_ref[...]
-
-    return call(
-        kernel,
-        (shape(3, 32, KV), shape(2, 32, KV)),
-        (keep, recv, short),
-        [VM] * 3,
-        [VM] * 2,
-        name="both_z1",
-    )
-
-
-def both_z3(stay, sent, recv):
-    def kernel(stay_ref, sent_ref, recv_ref, send_ref, keep_ref):
-        send_ref[0] = plus(stay_ref[1], recv_ref[1])
-        send_ref[1] = sent_ref[2]
-        send_ref[2] = recv_ref[2]
-        keep_ref[...] = plus(stay_ref[0], recv_ref[0])
-
-    return call(
-        kernel, (shape(3, 32, KV), shape(32, KV)), (stay, sent, recv), [VM] * 3, [VM] * 2, name="both_z3"
-    )
-
-
-def row_of(sent, recv):
-    def kernel(sent_ref, recv_ref, out_ref):
-        zh = place()[1]
-        for ref, at, j in ((sent_ref, 1, 0), (sent_ref, 2, 1), (recv_ref, 1, 3), (recv_ref, 2, 2)):
-            out_ref[zh ^ j] = ref[at]
-
-    return call(kernel, (shape(*QUAD),), (sent, recv), [VM] * 2, [VM], name="row")
-
-
-def join(a, b, hint=0):
-    def kernel(a_ref, b_ref, out_ref):
-        out_ref[0] = a_ref[...]
-        out_ref[1] = b_ref[...]
-
-    return call(kernel, (shape(2, *a.shape),), (a, b), [VM] * 2, [VM], name="join", hint=hint)
-
-
-def block_of(own, got):
-    def kernel(own_ref, got_ref, out_ref):
-        x = place()[0]
-        for ref, at, j in ((own_ref, 0, 0), (own_ref, 1, 3), (got_ref, 0, 1), (got_ref, 1, 2)):
-            out_ref[pl.ds((x ^ j) * 4, 4)] = ref[at]
-
-    return call(kernel, (shape(16, 32, KV),), (own, got), [VM] * 2, [VM], name="block")
+def plane_sums(inner, recv, after):
+    def kernel(inner_ref, recv_ref, _, out_ref):
+        out_ref[...] = plus(inner_ref[:, place()[2]], recv_ref[...])
+
+    return call(kernel, (shape(16, 32, KV),), (inner, recv, after), [VM, VM, ANY], [VM], name="plane_sums")
 
 
 def outer_sync(plan, anchors, momentum, keep, recv):
@@ -431,11 +385,12 @@
         new = anchor - outer_rate * (outer_grad + outer_beta * moment)
         new_ref[...] = new
         moment_ref[...] = moment
-        short_ref[...] = new.astype(BF16)
-
-    return call(
-        kernel,
-        (shape(32, KV, dtype=F32), shape(32, KV, dtype=F32), shape(32, KV)),
+        for i in range(16):
+            short_ref[i] = new.astype(BF16)
+
+    return call(
+        kernel,
+        (shape(32, KV, dtype=F32), shape(32, KV, dtype=F32), shape(16, 32, KV)),
         (plan, anchors, momentum, keep, recv),
         [SM] + [VM] * 4,
         [VM] * 3,
@@ -444,16 +399,16 @@
     )
 
 
-def outer_other(plan, anchors, keep, recv):
-    def kernel(plan_ref, anchor_ref, a, b, out_ref):
+def outer_other(plan, anchors, parts):
+    def kernel(plan_ref, anchor_ref, parts_ref, out_ref):
         other = 1 - lax.rem(plan_ref[0], 2)
-        out_ref[...] = anchor_ref[other] - (a[...].astype(F32) + b[0].astype(F32)) / 32
+        out_ref[...] = anchor_ref[other] - sum(parts_ref[i].astype(F32) for i in range(16)) / 32
 
     return call(
         kernel,
         (shape(32, KV, dtype=F32),),
-        (plan, anchors, keep, recv),
-        [SM] + [VM] * 3,
+        (plan, anchors, parts),
+        [SM] + [VM] * 2,
         [VM],
         name="outer_other",
     )
@@ -506,6 +461,13 @@
 }
 
 
+PLANES = [[i * 2 + c for i in range(16)] for c in range(2)]
+
+
+def exchange(value):
+    return lax.all_to_all(value, "worker", 0, 0, axis_index_groups=PLANES, tiled=True)
+
+
 def swap(value, move):
     return lax.ppermute(value, *MOVES[move])
 
@@ -580,21 +542,12 @@
     core_o = swap(send_o, "core")
     send, keep = halve("sync_z3", (32, KV), keep, recv, LONG)
     recv = swap(send, "z3")
-    send_o, keep_o = sum_x(inner_o, core_o, "other_x1")
-    recv_o = swap(send_o, "x1")
     anchor_new, momentum_new, short = outer_sync(plan, anchors, momentum, keep, recv)
-    send_o, keep_o = halve("other_x3", QUAD, keep_o, recv_o)
-    recv_o = swap(send_o, "x3")
-    sent, keep = both_z1(keep_o, recv_o, short)
-    recv = swap(sent, "z1")
-    sent, keep = both_z3(keep, sent, recv)
-    recv = swap(sent, "z3")
-    row = row_of(sent, recv)
-    row_far = swap(row, "x3")
-    pending = outer_other(plan, anchors, keep, recv)
-    own = join(row, row_far)
-    block = block_of(own, swap(own, "x1"))
-    new = mix(plan, inner_s, block, swap(block, "core"), new)
+    block = exchange(short)
+    block_far = swap(block, "core")
+    parts = exchange(plane_sums(inner_o, core_o, block))
+    new = mix(plan, inner_s, block, block_far, new)
+    pending = outer_other(plan, anchors, parts)
     return (new.reshape(1, 2, ROWS, KV), anchor_new, momentum_new, pending)
 
 

time: 151 us -> 154 us (1.020)
  starting transfers between devices: 43.4 us -> 47 us
  local copies, waits for them, and re-layouts: 0.02 us -> 1.62 us
    ppermute x28 -> x22, waiting for transfers between devices: 81.8 us -> 54.7 us  [swap(): return lax.ppermute(value, *MOVES[move])]
    all_to_all x0 -> x2, waiting for transfers between devices: none -> 25.8 us  [exchange(): lax.all_to_all(value, 'worker', 0, 0, axis_index_groups=PLANES, tiled=True)]
    all_to_all x0 -> x2, starting transfers between devices: none -> 12.2 us  [exchange(): lax.all_to_all(value, 'worker', 0, 0, axis_index_groups=PLANES, tiled=True)]
    ppermute x28 -> x22, starting transfers between devices: 43.4 us -> 34.9 us  [swap(): return lax.ppermute(value, *MOVES[move])]
    unnamed x8 -> x12, local copies, waits for them, and re-layouts: 0.02 us -> 1.62 us
    pallas_call x31 -> x25, Pallas kernels: 22.1 us -> 22.2 us  [call(): pl.pallas_call(chained, out_shape=outs + [in_hbm(8, 128)], in_specs=list(...]
  transfers between devices with their start and end apart: 28 -> 24, of which waited for: 19 -> 16; matrix products, arithmetic and copies ran while one was open for 0% -> 0% of each run, Pallas kernels for 13% -> 12%
where the time goes in v8:
time: 154 us; the launch traced here: 153 us
  waiting for transfers between devices  80.6 us (52%)
  starting transfers between devices  47 us (31%)
  Pallas kernels  22.2 us (14%)
  local copies, waits for them, and re-layouts  1.62 us (1%)
    ppermute x22, waiting for transfers between devices, swap(): return lax.ppermute(value, *MOVES[move])  54.7 us
    ppermute x22, starting transfers between devices, swap(): return lax.ppermute(value, *MOVES[move])  34.9 us
    all_to_all x2, waiting for transfers between devices, exchange(): lax.all_to_all(value, 'worker', 0, 0, axis_index_groups=PLANES, tiled=True)  25.8 us
    pallas_call x25, Pallas kernels, call(): pl.pallas_call(chained, out_shape=outs + [in_hbm(8, 128)], in_specs=list(...  22.2 us
    all_to_all x2, starting transfers between devices, exchange(): lax.all_to_all(value, 'worker', 0, 0, axis_index_groups=PLANES, tiled=True)  12.2 us
  transfers between devices with their start and end apart: 24, of which 16 were waited for; matrix products, arithmetic and copies ran while one was open for 0% of the time, Pallas kernels for 12%

profile of v8, /device:TPU:8, one launch (start us, length us, event | category | flops | bytes accessed | tf_op | source)
XLA Modules:
  0.0 152.9 jit_solution(15553671116701436722)
XLA Ops:
  1.3 1.5 pack_1.1
  2.8 2.3 %collective-permute-start = (bf16[256,1536]{1,0:T(8,128)(2,1)S(1)}, bf16[256,1536]{1,0:T(8,128)(2,1)S(1)}, u32[]{:S(2)}, u32[]{:S(2)}) collective-permute-start(bf16[256,1536]{1,0:T(8,128)(2,1)S(1)} %get-tuple-element.74), channel_id=1, source_target_pairs={{0,1},{1,0},{2,3},{3,2},{4,5},{5,4},{6,7},{7,6},{8,9},{9,8},{10,11... | collective-permute-start | bytes 2359304 | tf_op jit(solution)/shard_map/ppermute | solution.py:472
  5.1 0.7 collective-permute-start.2
  5.7 2.2 %pack_2.1 = (bf16[256,3584]{1,0:T(8,128)(2,1)S(1)}, bf16[256,1024]{1,0:T(8,128)(2,1)S(1)}, bf16[256,1024]{1,0:T(8,128)(2,1)S(1)}, bf16[256,1024]{1,0:T(8,128)(2,...) custom-call(s32[1]{0:T(128)S(6)} %copy.13.refs_0_, s32[1,256]{1,0:T(1,128)} %bitcast.9, ...), custom_call_target="tpu_custom_call" | custom-call | tf_op jit(solution)/shard_map/pack_2/pallas_call | solution.py:70
  7.9 1.4 collective-permute-start.1
  9.4 0.7 collective-permute-start.3
  10.1 1.7 %collective-permute-start.6 = (bf16[256,3584]{1,0:T(8,128)(2,1)S(1)}, bf16[256,3584]{1,0:T(8,128)(2,1)S(1)}, u32[]{:S(2)}, u32[]{:S(2)}) collective-permute-start(bf16[256,3584]{1,0:T(8,128)(2,1)S(1)} %get-tuple-element.92), channel_id=1, source_target_pairs={{0,4},{1,5},{2,6},{3,7},{4,0},{5,1},{6,2},{7,3},{8,12},{9,13},{10,... | collective-permute-start | bytes 5505032 | tf_op jit(solution)/shard_map/ppermute | solution.py:472
  11.7 11.8 %collective-permute-done.refs_3_ = bf16[256,1536]{1,0:T(8,128)(2,1)S(1)} collective-permute-done((bf16[256,1536]{1,0:T(8,128)(2,1)S(1)}, bf16[256,1536]{1,0:T(8,128)(2,1)S(1)}, u32[]{:S(2)}, u32[]{:S(2)}) %collective-permute-start) | collective-permute-done | bytes 786464 | tf_op jit(solution)/shard_map/ppermute | solution.py:472
  23.5 0.6 send_a1.1
  24.1 1.4 collective-permute-done.2.refs_3_
  26.2 1.4 collective-permute-start.8
  27.6 1.3 collective-permute-start.7
  29.5 0.6 keep_b1.1
  30.1 4.6 %collective-permute-done.1.refs_4_ = bf16[256,1024]{1,0:T(8,128)(2,1)S(1)} collective-permute-done((bf16[256,1024]{1,0:T(8,128)(2,1)S(1)}, bf16[256,1024]{1,0:T(8,128)(2,1)S(1)}, u32[]{:S(2)}, u32[]{:S(2)}) %collective-permute-start.1) | collective-permute-done | bytes 524320 | tf_op jit(solution)/shard_map/ppermute | solution.py:472
  35.4 1.5 collective-permute-start.4
  37.5 2.0 %collective-permute-start.5 = (bf16[512,512]{1,0:T(8,128)(2,1)S(1)}, bf16[512,512]{1,0:T(8,128)(2,1)S(1)}, u32[]{:S(2)}, u32[]{:S(2)}) collective-permute-start(bf16[512,512]{1,0:T(8,128)(2,1)S(1)} %get-tuple-element.90), channel_id=1, source_target_pairs={{0,1},{1,0},{2,3},{3,2},{4,5},{5,4},{6,7},{7,6},{8,9},{9,8},{10,11... | collective-permute-start | bytes 1572872 | tf_op jit(solution)/shard_map/ppermute | solution.py:472
  40.1 0.6 keep_b2.1
  40.7 5.3 %collective-permute-done.8.refs_3_ = bf16[512,512]{1,0:T(8,128)(2,1)S(1)} collective-permute-done((bf16[512,512]{1,0:T(8,128)(2,1)S(1)}, bf16[512,512]{1,0:T(8,128)(2,1)S(1)}, u32[]{:S(2)}, u32[]{:S(2)}) %collective-permute-start.8) | collective-permute-done | bytes 524320 | tf_op jit(solution)/shard_map/ppermute | solution.py:472
  46.0 2.0 %collective-permute-done.7.refs_1_ = bf16[512,512]{1,0:T(8,128)(2,1)S(1)} collective-permute-done((bf16[512,512]{1,0:T(8,128)(2,1)S(1)}, bf16[512,512]{1,0:T(8,128)(2,1)S(1)}, u32[]{:S(2)}, u32[]{:S(2)}) %collective-permute-start.7) | collective-permute-done | bytes 524320 | tf_op jit(solution)/shard_map/ppermute | solution.py:472
  48.9 4.2 %collective-permute-done.6.refs_3_ = bf16[256,3584]{1,0:T(8,128)(2,1)S(1)} collective-permute-done((bf16[256,3584]{1,0:T(8,128)(2,1)S(1)}, bf16[256,3584]{1,0:T(8,128)(2,1)S(1)}, u32[]{:S(2)}, u32[]{:S(2)}) %collective-permute-start.6) | collective-permute-done | bytes 1835040 | tf_op jit(solution)/shard_map/ppermute | solution.py:472
  53.0 3.3 %other_1.1 = (bf16[2,256,1024]{2,1,0:T(8,128)(2,1)S(1)}, bf16[2,256,1024]{2,1,0:T(8,128)(2,1)S(1)}, bf16[256,1024]{1,0:T(8,128)(2,1)S(1)}, bf16[256,1024]{1,0:T(8,128)(2,1)S(1)}, bf16[8,128]{1,0:T(8,128)(2,1)}) custom-call(s32[1]{0:T(128)S(6)} %copy.13.refs_0_, bf16[2,256,8192]{2,1,0:T(8,128)(2,1)S(1)} %bitcast.4, ...), custom_call_target="tpu_custom_call" | custom-call | flops 20000000000 | tf_op jit(solution)/shard_map/other_1/pallas_call | solution.py:70
  56.3 1.1 collective-permute-start.12
  57.5 1.6 %collective-permute-start.13 = (bf16[2,256,1024]{2,1,0:T(8,128)(2,1)S(1)}, bf16[2,256,1024]{2,1,0:T(8,128)(2,1)S(1)}, u32[]{:S(2)}, u32[]{:S(2)}) collective-permute-start(bf16[2,256,1024]{2,1,0:T(8,128)(2,1)S(1)} %get-tuple-element.111), channel_id=1, source_target_pairs={{0,3},{1,2},{2,1},{3,0},{4,7},{5,6},{6,5},{7,4},{8,11},{9,10},{10,... | collective-permute-start | bytes 3145736 | tf_op jit(solution)/shard_map/ppermute | solution.py:472
  59.3 13.8 %collective-permute-done.9.refs_3_ = bf16[2,512,512]{2,1,0:T(8,128)(2,1)S(1)} collective-permute-done((bf16[2,512,512]{2,1,0:T(8,128)(2,1)S(1)}, bf16[2,512,512]{2,1,0:T(8,128)(2,1)S(1)}, u32[]{:S(2)}, u32[]{:S(2)}) %collective-permute-start.9) | collective-permute-done | bytes 1048608 | tf_op jit(solution)/shard_map/ppermute | solution.py:472
  73.1 1.9 %inner_sync.1 = (bf16[16,2,32,512]{3,2,1,0:T(8,128)(2,1)S(1)}, bf16[16,32,512]{2,1,0:T(8,128)(2,1)S(1)}, bf16[8,128]{1,0:T(8,128)(2,1)}) custom-call(s32[1]{0:T(128)S(6)} %copy.13.refs_0_, bf16[2,16,2,32,512]{4,3,2,1,0:T(8,128)(2,1)} %bitcast.5, bf16[2,512,512]{2,1,0:T(8,128)(2,1)S(1)} %get-tuple-element.100.refs_2_, ...), custom_call_target="tpu_custom_call" | custom-call | tf_op jit(solution)/shard_map/inner_sync/pallas_call | solution.py:70
  75.1 1.8 %collective-permute-start.16 = (bf16[256,1024]{1,0:T(8,128)(2,1)S(1)}, bf16[256,1024]{1,0:T(8,128)(2,1)S(1)}, u32[]{:S(2)}, u32[]{:S(2)}) collective-permute-start(bf16[256,1024]{1,0:T(8,128)(2,1)S(1)} %get-tuple-element.119), channel_id=1, source_target_pairs={{0,4},{1,5},{2,6},{3,7},{4,0},{5,1},{6,2},{7,3},{8,12},{9,13},{10,... | collective-permute-start | bytes 1572872 | tf_op jit(solution)/shard_map/ppermute | solution.py:472
  77.1 1.6 %collective-permute-start.11 = (bf16[2,4,32,512]{3,2,1,0:T(8,128)(2,1)S(1)}, bf16[2,4,32,512]{3,2,1,0:T(8,128)(2,1)S(1)}, u32[]{:S(2)}, u32[]{:S(2)}) collective-permute-start(bf16[2,4,32,512]{3,2,1,0:T(8,128)(2,1)S(1)} %get-tuple-element.107), channel_id=1, source_target_pairs={{0,64},{8,72},{16,80},{24,88},{32,96},{40,104},{48,112},{56,120},{... | collective-permute-start | bytes 786440 | tf_op jit(solution)/shard_map/ppermute | solution.py:472
  79.4 1.8 %collective-permute-start.17 = (bf16[256,1024]{1,0:T(8,128)(2,1)S(1)}, bf16[256,1024]{1,0:T(8,128)(2,1)S(1)}, u32[]{:S(2)}, u32[]{:S(2)}) collective-permute-start(bf16[256,1024]{1,0:T(8,128)(2,1)S(1)} %get-tuple-element.122), channel_id=1, source_target_pairs={{0,3},{1,2},{2,1},{3,0},{4,7},{5,6},{6,5},{7,4},{8,11},{9,10},{10,... | collective-permute-start | bytes 1572872 | tf_op jit(solution)/shard_map/ppermute | solution.py:472
  81.2 2.6 %collective-permute-start.18 = (bf16[256,1024]{1,0:T(8,128)(2,1)S(1)}, bf16[256,1024]{1,0:T(8,128)(2,1)S(1)}, u32[]{:S(2)}, u32[]{:S(2)}) collective-permute-start(bf16[256,1024]{1,0:T(8,128)(2,1)S(1)} %get-tuple-element.124), channel_id=1, source_target_pairs={{0,1},{1,0},{2,3},{3,2},{4,5},{5,4},{6,7},{7,6},{8,9},{9,8},{10,11... | collective-permute-start | bytes 1572872 | tf_op jit(solution)/shard_map/ppermute | solution.py:472
  83.8 1.7 %collective-permute-done.11.refs_1_.refs_3_ = bf16[2,4,32,512]{3,2,1,0:T(8,128)(2,1)S(1)} collective-permute-done((bf16[2,4,32,512]{3,2,1,0:T(8,128)(2,1)S(1)}, bf16[2,4,32,512]{3,2,1,0:T(8,128)(2,1)S(1)}, u32[]{:S(2)}, u32[]{:S(2)}) %collective-permute-start.11) | collective-permute-done | bytes 262176 | tf_op jit(solution)/shard_map/ppermute | solution.py:472
  85.6 2.8 %collective-permute-start.14 = (bf16[4,32,512]{2,1,0:T(8,128)(2,1)S(1)}, bf16[4,32,512]{2,1,0:T(8,128)(2,1)S(1)}, u32[]{:S(2)}, u32[]{:S(2)}) collective-permute-start(bf16[4,32,512]{2,1,0:T(8,128)(2,1)S(1)} %get-tuple-element.115), channel_id=1, source_target_pairs={{0,192},{8,200},{16,208},{24,216},{32,224},{40,232},{48,240},{56,2... | collective-permute-start | bytes 393224 | tf_op jit(solution)/shard_map/ppermute | solution.py:472
  88.5 3.4 %collective-permute-done.14.refs_1_ = bf16[4,32,512]{2,1,0:T(8,128)(2,1)S(1)} collective-permute-done((bf16[4,32,512]{2,1,0:T(8,128)(2,1)S(1)}, bf16[4,32,512]{2,1,0:T(8,128)(2,1)S(1)}, u32[]{:S(2)}, u32[]{:S(2)}) %collective-permute-start.14) | collective-permute-done | bytes 131104 | tf_op jit(solution)/shard_map/ppermute | solution.py:472
  91.9 3.4 %collective-permute-start.15 = (bf16[2,32,512]{2,1,0:T(8,128)(2,1)S(1)}, bf16[2,32,512]{2,1,0:T(8,128)(2,1)S(1)}, u32[]{:S(2)}, u32[]{:S(2)}) collective-permute-start(bf16[2,32,512]{2,1,0:T(8,128)(2,1)S(1)} %get-tuple-element.118), channel_id=1, source_target_pairs={{0,16},{8,24},{16,0},{24,8},{32,48},{40,56},{48,32},{56,40},{64,80... | collective-permute-start | bytes 196616 | tf_op jit(solution)/shard_map/ppermute | solution.py:472
  95.3 1.1 other_3.1
  96.4 3.1 %inner_other.1 = (bf16[16,2,32,512]{3,2,1,0:T(8,128)(2,1)S(1)}, bf16[16,32,512]{2,1,0:T(8,128)(2,1)S(1)}, bf16[2,16,2,32,512]{4,3,2,1,0:T(8,128)(2,1)}, bf16[8,128]{1,0:T(8,128)(2,1)}) custom-call(s32[1]{0:T(128)S(6)} %copy.13.refs_0_, bf16[2,16,2,32,512]{4,3,2,1,0:T(8,128)(2,1)} %bitcast.6, bf16[256,1024]{1,0:T(8,128)(2,1)S(1)} %get-tuple-element.121.refs_2_, ...), custom_call_target="tpu_custom_call" | custom-call | tf_op jit(solution)/shard_map/inner_other/pallas_call | solution.py:70
  99.6 0.8 copy-done.2
  100.4 4.4 %collective-permute-start.19 = (bf16[32,512]{1,0:T(8,128)(2,1)S(1)}, bf16[32,512]{1,0:T(8,128)(2,1)S(1)}, u32[]{:S(2)}, u32[]{:S(2)}) collective-permute-start(bf16[32,512]{1,0:T(8,128)(2,1)S(1)} %get-tuple-element.128), channel_id=1, source_target_pairs={{0,48},{8,56},{16,32},{24,40},{32,16},{40,24},{48,0},{56,8},{64,11... | collective-permute-start | bytes 98312 | tf_op jit(solution)/shard_map/ppermute | solution.py:472
  104.8 1.9 %collective-permute-done.19.refs_4_ = bf16[32,512]{1,0:T(8,128)(2,1)S(1)} collective-permute-done((bf16[32,512]{1,0:T(8,128)(2,1)S(1)}, bf16[32,512]{1,0:T(8,128)(2,1)S(1)}, u32[]{:S(2)}, u32[]{:S(2)}) %collective-permute-start.19) | collective-permute-done | bytes 32800 | tf_op jit(solution)/shard_map/ppermute | solution.py:472
  106.7 0.9 outer_sync.1
  107.6 8.6 %all-to-all-start = ((bf16[16,32,512]{2,1,0:T(8,128)(2,1)}), bf16[16,32,512]{2,1,0:T(8,128)(2,1)S(1)}, u32[]{:S(2)}, u32[]{:S(2)}) async-start(bf16[16,32,512]{2,1,0:T(8,128)(2,1)} %get-tuple-element.130), calls=%async_computation | async-start | bytes 1048576 | tf_op jit(solution)/shard_map/all_to_all | solution.py:468
  116.3 2.1 %collective-permute-done.21.refs_1_ = bf16[16,32,512]{2,1,0:T(8,128)(2,1)S(1)} collective-permute-done((bf16[16,32,512]{2,1,0:T(8,128)(2,1)}, bf16[16,32,512]{2,1,0:T(8,128)(2,1)S(1)}, u32[]{:S(2)}, u32[]{:S(2)}) %collective-permute-start.21) | collective-permute-done | bytes 524320 | tf_op jit(solution)/shard_map/ppermute | solution.py:472
  118.5 13.3 %all-to-all-done.refs_2_ = bf16[16,32,512]{2,1,0:T(8,128)(2,1)S(1)} async-done(((bf16[16,32,512]{2,1,0:T(8,128)(2,1)}), bf16[16,32,512]{2,1,0:T(8,128)(2,1)S(1)}, u32[]{:S(2)}, u32[]{:S(2)}) %all-to-all-start) | async-done | bytes 524320 | tf_op jit(solution)/shard_map/all_to_all | solution.py:468
  131.9 0.8 copy-done
  132.7 3.6 %all-to-all-start.1 = ((bf16[16,32,512]{2,1,0:T(8,128)(2,1)}), bf16[16,32,512]{2,1,0:T(8,128)(2,1)S(1)}, u32[]{:S(2)}, u32[]{:S(2)}) async-start(bf16[16,32,512]{2,1,0:T(8,128)(2,1)} %copy-done), calls=%async_computation.1 | async-start | bytes 1048576 | tf_op jit(solution)/shard_map/all_to_all | solution.py:468
  136.4 1.9 %collective-permute-done.20.refs_3_ = bf16[16,32,512]{2,1,0:T(8,128)(2,1)S(1)} collective-permute-done((bf16[16,32,512]{2,1,0:T(8,128)(2,1)S(1)}, bf16[16,32,512]{2,1,0:T(8,128)(2,1)S(1)}, u32[]{:S(2)}, u32[]{:S(2)}) %collective-permute-start.20) | collective-permute-done | bytes 524320 | tf_op jit(solution)/shard_map/ppermute | solution.py:472
  138.3 1.4 mix.1
  139.7 12.5 %all-to-all-done.1.refs_2_ = bf16[16,32,512]{2,1,0:T(8,128)(2,1)S(1)} async-done(((bf16[16,32,512]{2,1,0:T(8,128)(2,1)}), bf16[16,32,512]{2,1,0:T(8,128)(2,1)S(1)}, u32[]{:S(2)}, u32[]{:S(2)}) %all-to-all-start.1) | async-done | bytes 524320 | tf_op jit(solution)/shard_map/all_to_all | solution.py:468
  152.2 0.7 outer_other.1
  (38 shorter events, 5.6 us)
Async XLA Ops:
  1.3 22.2 %slice-start = ((s8[8388608]{0:T(1024)(128)(4,1)}), s8[4194304]{0:T(1024)(128)(4,1)S(1)}, s32[]{:S(2)}) async-start(s8[8388608]{0:T(1024)(128)(4,1)} %bitcast.3), calls=%async_computation.2 | async-start | bytes 8388608
  2.8 20.7 %collective-permute-start = (bf16[256,1536]{1,0:T(8,128)(2,1)S(1)}, bf16[256,1536]{1,0:T(8,128)(2,1)S(1)}, u32[]{:S(2)}, u32[]{:S(2)}) collective-permute-start(bf16[256,1536]{1,0:T(8,128)(2,1)S(1)} %get-tuple-element.74), channel_id=1, source_target_pairs={{0,1},{1,0},{2,3},{3,2},{4,5},{5,4},{6,7},{7,6},{8,9},{9,8},{10,11... | collective-permute-start | bytes 2359304 | tf_op jit(solution)/shard_map/ppermute | solution.py:472
  5.1 20.5 %collective-permute-start.2 = (bf16[256,1536]{1,0:T(8,128)(2,1)S(1)}, bf16[256,1536]{1,0:T(8,128)(2,1)S(1)}, u32[]{:S(2)}, u32[]{:S(2)}) collective-permute-start(bf16[256,1536]{1,0:T(8,128)(2,1)S(1)} %get-tuple-element.77), channel_id=1, source_target_pairs={{0,3},{1,2},{2,1},{3,0},{4,7},{5,6},{6,5},{7,4},{8,11},{9,10},{10,... | collective-permute-start | bytes 2359304 | tf_op jit(solution)/shard_map/ppermute | solution.py:472
  5.7 17.8 %slice-start.1 = ((s8[8388608]{0:T(1024)(128)(4,1)}), s8[4194304]{0:T(1024)(128)(4,1)S(1)}, s32[]{:S(2)}) async-start(s8[8388608]{0:T(1024)(128)(4,1)} %bitcast.3), calls=%async_computation.3 | async-start | bytes 8388608
  7.9 26.8 %collective-permute-start.1 = (bf16[256,1024]{1,0:T(8,128)(2,1)S(1)}, bf16[256,1024]{1,0:T(8,128)(2,1)S(1)}, u32[]{:S(2)}, u32[]{:S(2)}) collective-permute-start(bf16[256,1024]{1,0:T(8,128)(2,1)S(1)} %get-tuple-element.76), channel_id=1, source_target_pairs={{0,1},{1,0},{2,3},{3,2},{4,5},{5,4},{6,7},{7,6},{8,9},{9,8},{10,11... | collective-permute-start | bytes 1572872 | tf_op jit(solution)/shard_map/ppermute | solution.py:472
  9.4 27.5 %collective-permute-start.3 = (bf16[256,1024]{1,0:T(8,128)(2,1)S(1)}, bf16[256,1024]{1,0:T(8,128)(2,1)S(1)}, u32[]{:S(2)}, u32[]{:S(2)}) collective-permute-start(bf16[256,1024]{1,0:T(8,128)(2,1)S(1)} %get-tuple-element.78), channel_id=1, source_target_pairs={{0,3},{1,2},{2,1},{3,0},{4,7},{5,6},{6,5},{7,4},{8,11},{9,10},{10,... | collective-permute-start | bytes 1572872 | tf_op jit(solution)/shard_map/ppermute | solution.py:472
  10.1 42.9 %collective-permute-start.6 = (bf16[256,3584]{1,0:T(8,128)(2,1)S(1)}, bf16[256,3584]{1,0:T(8,128)(2,1)S(1)}, u32[]{:S(2)}, u32[]{:S(2)}) collective-permute-start(bf16[256,3584]{1,0:T(8,128)(2,1)S(1)} %get-tuple-element.92), channel_id=1, source_target_pairs={{0,4},{1,5},{2,6},{3,7},{4,0},{5,1},{6,2},{7,3},{8,12},{9,13},{10,... | collective-permute-start | bytes 5505032 | tf_op jit(solution)/shard_map/ppermute | solution.py:472
  26.2 19.8 %collective-permute-start.8 = (bf16[512,512]{1,0:T(8,128)(2,1)S(1)}, bf16[512,512]{1,0:T(8,128)(2,1)S(1)}, u32[]{:S(2)}, u32[]{:S(2)}) collective-permute-start(bf16[512,512]{1,0:T(8,128)(2,1)S(1)} %get-tuple-element.96), channel_id=1, source_target_pairs={{0,1},{1,0},{2,3},{3,2},{4,5},{5,4},{6,7},{7,6},{8,9},{9,8},{10,11... | collective-permute-start | bytes 1572872 | tf_op jit(solution)/shard_map/ppermute | solution.py:472
  27.6 20.4 %collective-permute-start.7 = (bf16[512,512]{1,0:T(8,128)(2,1)S(1)}, bf16[512,512]{1,0:T(8,128)(2,1)S(1)}, u32[]{:S(2)}, u32[]{:S(2)}) collective-permute-start(bf16[512,512]{1,0:T(8,128)(2,1)S(1)} %get-tuple-element.94), channel_id=1, source_target_pairs={{0,3},{1,2},{2,1},{3,0},{4,7},{5,6},{6,5},{7,4},{8,11},{9,10},{10,... | collective-permute-start | bytes 1572872 | tf_op jit(solution)/shard_map/ppermute | solution.py:472
  35.4 23.7 %collective-permute-start.4 = (bf16[512,512]{1,0:T(8,128)(2,1)S(1)}, bf16[512,512]{1,0:T(8,128)(2,1)S(1)}, u32[]{:S(2)}, u32[]{:S(2)}) collective-permute-start(bf16[512,512]{1,0:T(8,128)(2,1)S(1)} %get-tuple-element.87), channel_id=1, source_target_pairs={{0,3},{1,2},{2,1},{3,0},{4,7},{5,6},{6,5},{7,4},{8,11},{9,10},{10,... | collective-permute-start | bytes 1572872 | tf_op jit(solution)/shard_map/ppermute | solution.py:472
  37.5 21.6 %collective-permute-start.5 = (bf16[512,512]{1,0:T(8,128)(2,1)S(1)}, bf16[512,512]{1,0:T(8,128)(2,1)S(1)}, u32[]{:S(2)}, u32[]{:S(2)}) collective-permute-start(bf16[512,512]{1,0:T(8,128)(2,1)S(1)} %get-tuple-element.90), channel_id=1, source_target_pairs={{0,1},{1,0},{2,3},{3,2},{4,5},{5,4},{6,7},{7,6},{8,9},{9,8},{10,11... | collective-permute-start | bytes 1572872 | tf_op jit(solution)/shard_map/ppermute | solution.py:472
  48.3 24.8 %collective-permute-start.9 = (bf16[2,512,512]{2,1,0:T(8,128)(2,1)S(1)}, bf16[2,512,512]{2,1,0:T(8,128)(2,1)S(1)}, u32[]{:S(2)}, u32[]{:S(2)}) collective-permute-start(bf16[2,512,512]{2,1,0:T(8,128)(2,1)S(1)} %get-tuple-element.101), channel_id=1, source_target_pairs={{0,4},{1,5},{2,6},{3,7},{4,0},{5,1},{6,2},{7,3},{8,12},{9,13},{10,... | collective-permute-start | bytes 3145736 | tf_op jit(solution)/shard_map/ppermute | solution.py:472
  56.3 22.4 %collective-permute-start.12 = (bf16[2,256,1024]{2,1,0:T(8,128)(2,1)S(1)}, bf16[2,256,1024]{2,1,0:T(8,128)(2,1)S(1)}, u32[]{:S(2)}, u32[]{:S(2)}) collective-permute-start(bf16[2,256,1024]{2,1,0:T(8,128)(2,1)S(1)} %get-tuple-element.109), channel_id=1, source_target_pairs={{0,1},{1,0},{2,3},{3,2},{4,5},{5,4},{6,7},{7,6},{8,9},{9,8},{10,11... | collective-permute-start | bytes 3145736 | tf_op jit(solution)/shard_map/ppermute | solution.py:472
  57.5 21.7 %collective-permute-start.13 = (bf16[2,256,1024]{2,1,0:T(8,128)(2,1)S(1)}, bf16[2,256,1024]{2,1,0:T(8,128)(2,1)S(1)}, u32[]{:S(2)}, u32[]{:S(2)}) collective-permute-start(bf16[2,256,1024]{2,1,0:T(8,128)(2,1)S(1)} %get-tuple-element.111), channel_id=1, source_target_pairs={{0,3},{1,2},{2,1},{3,0},{4,7},{5,6},{6,5},{7,4},{8,11},{9,10},{10,... | collective-permute-start | bytes 3145736 | tf_op jit(solution)/shard_map/ppermute | solution.py:472
  75.0 2.0 %collective-permute-start.10 = (bf16[16,32,512]{2,1,0:T(8,128)(2,1)S(1)}, bf16[16,32,512]{2,1,0:T(8,128)(2,1)S(1)}, u32[]{:S(2)}, u32[]{:S(2)}) collective-permute-start(bf16[16,32,512]{2,1,0:T(8,128)(2,1)S(1)} %get-tuple-element.104), channel_id=1, source_target_pairs={{0,8},{8,0},{16,24},{24,16},{32,40},{40,32},{48,56},{56,48},{64,72... | collective-permute-start | bytes 1572872 | tf_op jit(solution)/shard_map/ppermute | solution.py:472
  75.1 20.2 %collective-permute-start.16 = (bf16[256,1024]{1,0:T(8,128)(2,1)S(1)}, bf16[256,1024]{1,0:T(8,128)(2,1)S(1)}, u32[]{:S(2)}, u32[]{:S(2)}) collective-permute-start(bf16[256,1024]{1,0:T(8,128)(2,1)S(1)} %get-tuple-element.119), channel_id=1, source_target_pairs={{0,4},{1,5},{2,6},{3,7},{4,0},{5,1},{6,2},{7,3},{8,12},{9,13},{10,... | collective-permute-start | bytes 1572872 | tf_op jit(solution)/shard_map/ppermute | solution.py:472
  77.1 8.4 %collective-permute-start.11 = (bf16[2,4,32,512]{3,2,1,0:T(8,128)(2,1)S(1)}, bf16[2,4,32,512]{3,2,1,0:T(8,128)(2,1)S(1)}, u32[]{:S(2)}, u32[]{:S(2)}) collective-permute-start(bf16[2,4,32,512]{3,2,1,0:T(8,128)(2,1)S(1)} %get-tuple-element.107), channel_id=1, source_target_pairs={{0,64},{8,72},{16,80},{24,88},{32,96},{40,104},{48,112},{56,120},{... | collective-permute-start | bytes 786440 | tf_op jit(solution)/shard_map/ppermute | solution.py:472
  79.4 17.0 %collective-permute-start.17 = (bf16[256,1024]{1,0:T(8,128)(2,1)S(1)}, bf16[256,1024]{1,0:T(8,128)(2,1)S(1)}, u32[]{:S(2)}, u32[]{:S(2)}) collective-permute-start(bf16[256,1024]{1,0:T(8,128)(2,1)S(1)} %get-tuple-element.122), channel_id=1, source_target_pairs={{0,3},{1,2},{2,1},{3,0},{4,7},{5,6},{6,5},{7,4},{8,11},{9,10},{10,... | collective-permute-start | bytes 1572872 | tf_op jit(solution)/shard_map/ppermute | solution.py:472
  81.2 15.2 %collective-permute-start.18 = (bf16[256,1024]{1,0:T(8,128)(2,1)S(1)}, bf16[256,1024]{1,0:T(8,128)(2,1)S(1)}, u32[]{:S(2)}, u32[]{:S(2)}) collective-permute-start(bf16[256,1024]{1,0:T(8,128)(2,1)S(1)} %get-tuple-element.124), channel_id=1, source_target_pairs={{0,1},{1,0},{2,3},{3,2},{4,5},{5,4},{6,7},{7,6},{8,9},{9,8},{10,11... | collective-permute-start | bytes 1572872 | tf_op jit(solution)/shard_map/ppermute | solution.py:472
  85.6 6.3 %collective-permute-start.14 = (bf16[4,32,512]{2,1,0:T(8,128)(2,1)S(1)}, bf16[4,32,512]{2,1,0:T(8,128)(2,1)S(1)}, u32[]{:S(2)}, u32[]{:S(2)}) collective-permute-start(bf16[4,32,512]{2,1,0:T(8,128)(2,1)S(1)} %get-tuple-element.115), channel_id=1, source_target_pairs={{0,192},{8,200},{16,208},{24,216},{32,224},{40,232},{48,240},{56,2... | collective-permute-start | bytes 393224 | tf_op jit(solution)/shard_map/ppermute | solution.py:472
  91.9 7.7 %collective-permute-start.15 = (bf16[2,32,512]{2,1,0:T(8,128)(2,1)S(1)}, bf16[2,32,512]{2,1,0:T(8,128)(2,1)S(1)}, u32[]{:S(2)}, u32[]{:S(2)}) collective-permute-start(bf16[2,32,512]{2,1,0:T(8,128)(2,1)S(1)} %get-tuple-element.118), channel_id=1, source_target_pairs={{0,16},{8,24},{16,0},{24,8},{32,48},{40,56},{48,32},{56,40},{64,80... | collective-permute-start | bytes 196616 | tf_op jit(solution)/shard_map/ppermute | solution.py:472
  99.6 0.8 copy-start.2
  100.4 6.3 %copy-start.1 = (f32[2,32,512]{2,1,0:T(8,128)S(1)}, f32[2,32,512]{2,1,0:T(8,128)}, u32[]{:S(2)}) copy-start(f32[2,32,512]{2,1,0:T(8,128)} %refs_1_.23) | copy-start | bytes 393220
  100.4 6.3 %copy-start.3 = (f32[32,512]{1,0:T(8,128)S(1)}, f32[32,512]{1,0:T(8,128)}, u32[]{:S(2)}) copy-start(f32[32,512]{1,0:T(8,128)} %refs_2_.5) | copy-start | bytes 196612
  100.4 6.3 %collective-permute-start.19 = (bf16[32,512]{1,0:T(8,128)(2,1)S(1)}, bf16[32,512]{1,0:T(8,128)(2,1)S(1)}, u32[]{:S(2)}, u32[]{:S(2)}) collective-permute-start(bf16[32,512]{1,0:T(8,128)(2,1)S(1)} %get-tuple-element.128), channel_id=1, source_target_pairs={{0,48},{8,56},{16,32},{24,40},{32,16},{40,24},{48,0},{56,8},{64,11... | collective-permute-start | bytes 98312 | tf_op jit(solution)/shard_map/ppermute | solution.py:472
  107.6 24.1 %all-to-all-start = ((bf16[16,32,512]{2,1,0:T(8,128)(2,1)}), bf16[16,32,512]{2,1,0:T(8,128)(2,1)S(1)}, u32[]{:S(2)}, u32[]{:S(2)}) async-start(bf16[16,32,512]{2,1,0:T(8,128)(2,1)} %get-tuple-element.130), calls=%async_computation | async-start | bytes 1048576 | tf_op jit(solution)/shard_map/all_to_all | solution.py:468
  116.2 2.2 %collective-permute-start.21 = (bf16[16,32,512]{2,1,0:T(8,128)(2,1)}, bf16[16,32,512]{2,1,0:T(8,128)(2,1)S(1)}, u32[]{:S(2)}, u32[]{:S(2)}) collective-permute-start(bf16[16,32,512]{2,1,0:T(8,128)(2,1)} %copy-done.2), channel_id=1, source_target_pairs={{0,8},{8,0},{16,24},{24,16},{32,40},{40,32},{48,56},{56,48},{64,72... | collective-permute-start | bytes 1572872 | tf_op jit(solution)/shard_map/ppermute | solution.py:472
  131.9 0.8 copy-start
  132.7 19.4 %all-to-all-start.1 = ((bf16[16,32,512]{2,1,0:T(8,128)(2,1)}), bf16[16,32,512]{2,1,0:T(8,128)(2,1)S(1)}, u32[]{:S(2)}, u32[]{:S(2)}) async-start(bf16[16,32,512]{2,1,0:T(8,128)(2,1)} %copy-done), calls=%async_computation.1 | async-start | bytes 1048576 | tf_op jit(solution)/shard_map/all_to_all | solution.py:468
  136.3 2.0 %collective-permute-start.20 = (bf16[16,32,512]{2,1,0:T(8,128)(2,1)S(1)}, bf16[16,32,512]{2,1,0:T(8,128)(2,1)S(1)}, u32[]{:S(2)}, u32[]{:S(2)}) collective-permute-start(bf16[16,32,512]{2,1,0:T(8,128)(2,1)S(1)} %all-to-all-done.refs_2_), channel_id=1, source_target_pairs={{0,8},{8,0},{16,24},{24,16},{32,40},{40,32},{48,56},{56,48},{64,72... | collective-permute-start | bytes 1572872 | tf_op jit(solution)/shard_map/ppermute | solution.py:472

commit v9 on v8

--- a/solution.py
+++ b/solution.py
@@ -368,13 +368,6 @@
     return call(to_z, (shape(2, 32, KV),) * 2, (keep, recv), [VM] * 2, [VM] * 2, name=name)
 
 
-def plane_sums(inner, recv, after):
-    def kernel(inner_ref, recv_ref, _, out_ref):
-        out_ref[...] = plus(inner_ref[:, place()[2]], recv_ref[...])
-
-    return call(kernel, (shape(16, 32, KV),), (inner, recv, after), [VM, VM, ANY], [VM], name="plane_sums")
-
-
 def outer_sync(plan, anchors, momentum, keep, recv):
     def kernel(plan_ref, anchor_ref, momentum_ref, a, b, new_ref, moment_ref, short_ref):
         s = lax.rem(plan_ref[0], 2)
@@ -399,16 +392,23 @@
     )
 
 
-def outer_other(plan, anchors, parts):
-    def kernel(plan_ref, anchor_ref, parts_ref, out_ref):
+def relay(value):
+    def kernel(value_ref, out_ref):
+        out_ref[...] = value_ref[...]
+
+    return call(kernel, (shape(*value.shape),), (value,), [VM], [VM], name="relay")
+
+
+def outer_other(plan, anchors, keep, recv):
+    def kernel(plan_ref, anchor_ref, a, b, out_ref):
         other = 1 - lax.rem(plan_ref[0], 2)
-        out_ref[...] = anchor_ref[other] - sum(parts_ref[i].astype(F32) for i in range(16)) / 32
+        out_ref[...] = anchor_ref[other] - (a[...].astype(F32) + b[...].astype(F32)) / 32
 
     return call(
         kernel,
         (shape(32, KV, dtype=F32),),
-        (plan, anchors, parts),
-        [SM] + [VM] * 2,
+        (plan, anchors, keep, recv),
+        [SM] + [VM] * 3,
         [VM],
         name="outer_other",
     )
@@ -542,12 +542,19 @@
     core_o = swap(send_o, "core")
     send, keep = halve("sync_z3", (32, KV), keep, recv, LONG)
     recv = swap(send, "z3")
+    send_o, keep_o = sum_x(inner_o, core_o, "other_x1")
+    recv_o = swap(send_o, "x1")
     anchor_new, momentum_new, short = outer_sync(plan, anchors, momentum, keep, recv)
     block = exchange(short)
-    block_far = swap(block, "core")
-    parts = exchange(plane_sums(inner_o, core_o, block))
-    new = mix(plan, inner_s, block, block_far, new)
-    pending = outer_other(plan, anchors, parts)
+    send_o, keep_o = halve("other_x3", QUAD, keep_o, recv_o, LONG)
+    recv_o = swap(send_o, "x3")
+    send_o, keep_o = sum_z(keep_o, recv_o, "other_z1")
+    recv_o = swap(send_o, "z1")
+    block = relay(block)
+    send_o, keep_o = halve("other_z3", (32, KV), keep_o, recv_o, LONG)
+    recv_o = swap(send_o, "z3")
+    new = mix(plan, inner_s, block, swap(block, "core"), new)
+    pending = outer_other(plan, anchors, keep_o, recv_o)
     return (new.reshape(1, 2, ROWS, KV), anchor_new, momentum_new, pending)
 
 

time: 154 us -> 143 us (0.929)
  waiting for transfers between devices: 80.6 us -> 67.4 us
  starting transfers between devices: 47 us -> 50.5 us
  local copies, waits for them, and re-layouts: 1.62 us -> 0.02 us
    all_to_all x2 -> x1, waiting for transfers between devices: 25.8 us -> 7.61 us  [exchange(): lax.all_to_all(value, 'worker', 0, 0, axis_index_groups=PLANES, tiled=True)]
    ppermute x22 -> x26, starting transfers between devices: 34.9 us -> 42.1 us  [swap(): return lax.ppermute(value, *MOVES[move])]
    ppermute x22 -> x26, waiting for transfers between devices: 54.7 us -> 59.8 us  [swap(): return lax.ppermute(value, *MOVES[move])]
    all_to_all x2 -> x1, starting transfers between devices: 12.2 us -> 8.39 us  [exchange(): lax.all_to_all(value, 'worker', 0, 0, axis_index_groups=PLANES, tiled=True)]
    unnamed x12 -> x8, local copies, waits for them, and re-layouts: 1.62 us -> 0.02 us
    pallas_call x25 -> x29, Pallas kernels: 22.2 us -> 22.2 us  [call(): pl.pallas_call(chained, out_shape=outs + [in_hbm(8, 128)], in_specs=list(...]
  transfers between devices with their start and end apart: 24 -> 27, of which waited for: 16 -> 16; matrix products, arithmetic and copies ran while one was open for 0% -> 0% of each run, Pallas kernels for 12% -> 14%
where the time goes in v9:
time: 143 us; the launch traced here: 142 us
  waiting for transfers between devices  67.4 us (47%)
  starting transfers between devices  50.5 us (35%)
  Pallas kernels  22.2 us (16%)
  between operations  1.57 us (1%)
    ppermute x26, waiting for transfers between devices, swap(): return lax.ppermute(value, *MOVES[move])  59.8 us
    ppermute x26, starting transfers between devices, swap(): return lax.ppermute(value, *MOVES[move])  42.1 us
    pallas_call x29, Pallas kernels, call(): pl.pallas_call(chained, out_shape=outs + [in_hbm(8, 128)], in_specs=list(...  22.2 us
    all_to_all x1, starting transfers between devices, exchange(): lax.all_to_all(value, 'worker', 0, 0, axis_index_groups=PLANES, tiled=True)  8.39 us
    all_to_all x1, waiting for transfers between devices, exchange(): lax.all_to_all(value, 'worker', 0, 0, axis_index_groups=PLANES, tiled=True)  7.61 us
  transfers between devices with their start and end apart: 27, of which 16 were waited for; matrix products, arithmetic and copies ran while one was open for 0% of the time, Pallas kernels for 14%

profile of v9, /device:TPU:8, one launch (start us, length us, event | category | flops | bytes accessed | tf_op | source)
XLA Modules:
  0.0 141.7 jit_solution(7290076453587979830)
XLA Ops:
  1.3 1.5 %pack_1.1 = (bf16[256,1536]{1,0:T(8,128)(2,1)S(1)}, bf16[256,1536]{1,0:T(8,128)(2,1)S(1)}, bf16[512,256]{1,0:T(8,128)(2,1)S(1)}, bf16[8,128]{1,0:T(8,128)(2,1)}) custom-call(s32[1]{0:T(128)S(6)} %copy.13.refs_0_, s32[1,256]{1,0:T(1,128)} %bitcast.8, bf16[2,256,8192]{2,1,0:T(8,128)(2,1)} %refs_1_.21, bf16[2,256,512]{2,1,0:T(8,128)(2,1)} %refs_3_.3), custom_call_target="tpu_custom_call" | custom-call | tf_op jit(solution)/shard_map/pack_1/pallas_call | solution.py:70
  2.8 2.3 %collective-permute-start = (bf16[256,1536]{1,0:T(8,128)(2,1)S(1)}, bf16[256,1536]{1,0:T(8,128)(2,1)S(1)}, u32[]{:S(2)}, u32[]{:S(2)}) collective-permute-start(bf16[256,1536]{1,0:T(8,128)(2,1)S(1)} %get-tuple-element.86), channel_id=1, source_target_pairs={{0,1},{1,0},{2,3},{3,2},{4,5},{5,4},{6,7},{7,6},{8,9},{9,8},{10,11... | collective-permute-start | bytes 2359304 | tf_op jit(solution)/shard_map/ppermute | solution.py:472
  5.1 0.7 collective-permute-start.2
  5.7 2.2 %pack_2.1 = (bf16[256,3584]{1,0:T(8,128)(2,1)S(1)}, bf16[256,1024]{1,0:T(8,128)(2,1)S(1)}, bf16[256,1024]{1,0:T(8,128)(2,1)S(1)}, bf16[256,1024]{1,0:T(8,128)(2,...) custom-call(s32[1]{0:T(128)S(6)} %copy.13.refs_0_, s32[1,256]{1,0:T(1,128)} %bitcast.9, ...), custom_call_target="tpu_custom_call" | custom-call | tf_op jit(solution)/shard_map/pack_2/pallas_call | solution.py:70
  7.9 1.4 %collective-permute-start.1 = (bf16[256,1024]{1,0:T(8,128)(2,1)S(1)}, bf16[256,1024]{1,0:T(8,128)(2,1)S(1)}, u32[]{:S(2)}, u32[]{:S(2)}) collective-permute-start(bf16[256,1024]{1,0:T(8,128)(2,1)S(1)} %get-tuple-element.88), channel_id=1, source_target_pairs={{0,1},{1,0},{2,3},{3,2},{4,5},{5,4},{6,7},{7,6},{8,9},{9,8},{10,11... | collective-permute-start | bytes 1572872 | tf_op jit(solution)/shard_map/ppermute | solution.py:472
  9.4 0.7 collective-permute-start.3
  10.1 1.7 %collective-permute-start.6 = (bf16[256,3584]{1,0:T(8,128)(2,1)S(1)}, bf16[256,3584]{1,0:T(8,128)(2,1)S(1)}, u32[]{:S(2)}, u32[]{:S(2)}) collective-permute-start(bf16[256,3584]{1,0:T(8,128)(2,1)S(1)} %get-tuple-element.104), channel_id=1, source_target_pairs={{0,4},{1,5},{2,6},{3,7},{4,0},{5,1},{6,2},{7,3},{8,12},{9,13},{10,... | collective-permute-start | bytes 5505032 | tf_op jit(solution)/shard_map/ppermute | solution.py:472
  11.7 11.8 %collective-permute-done.refs_3_ = bf16[256,1536]{1,0:T(8,128)(2,1)S(1)} collective-permute-done((bf16[256,1536]{1,0:T(8,128)(2,1)S(1)}, bf16[256,1536]{1,0:T(8,128)(2,1)S(1)}, u32[]{:S(2)}, u32[]{:S(2)}) %collective-permute-start) | collective-permute-done | bytes 786464 | tf_op jit(solution)/shard_map/ppermute | solution.py:472
  23.5 0.6 send_a1.1
  24.1 1.4 collective-permute-done.2.refs_3_
  26.2 1.4 collective-permute-start.8
  27.6 1.3 collective-permute-start.7
  29.5 0.6 keep_b1.1
  30.1 4.6 %collective-permute-done.1.refs_4_ = bf16[256,1024]{1,0:T(8,128)(2,1)S(1)} collective-permute-done((bf16[256,1024]{1,0:T(8,128)(2,1)S(1)}, bf16[256,1024]{1,0:T(8,128)(2,1)S(1)}, u32[]{:S(2)}, u32[]{:S(2)}) %collective-permute-start.1) | collective-permute-done | bytes 524320 | tf_op jit(solution)/shard_map/ppermute | solution.py:472
  34.7 0.6 send_a2.1
  35.4 1.5 %collective-permute-start.4 = (bf16[512,512]{1,0:T(8,128)(2,1)S(1)}, bf16[512,512]{1,0:T(8,128)(2,1)S(1)}, u32[]{:S(2)}, u32[]{:S(2)}) collective-permute-start(bf16[512,512]{1,0:T(8,128)(2,1)S(1)} %get-tuple-element.99), channel_id=1, source_target_pairs={{0,3},{1,2},{2,1},{3,0},{4,7},{5,6},{6,5},{7,4},{8,11},{9,10},{10,... | collective-permute-start | bytes 1572872 | tf_op jit(solution)/shard_map/ppermute | solution.py:472
  37.5 2.0 %collective-permute-start.5 = (bf16[512,512]{1,0:T(8,128)(2,1)S(1)}, bf16[512,512]{1,0:T(8,128)(2,1)S(1)}, u32[]{:S(2)}, u32[]{:S(2)}) collective-permute-start(bf16[512,512]{1,0:T(8,128)(2,1)S(1)} %get-tuple-element.102), channel_id=1, source_target_pairs={{0,1},{1,0},{2,3},{3,2},{4,5},{5,4},{6,7},{7,6},{8,9},{9,8},{10,11... | collective-permute-start | bytes 1572872 | tf_op jit(solution)/shard_map/ppermute | solution.py:472
  40.1 0.6 keep_b2.1
  40.7 5.3 %collective-permute-done.8.refs_3_ = bf16[512,512]{1,0:T(8,128)(2,1)S(1)} collective-permute-done((bf16[512,512]{1,0:T(8,128)(2,1)S(1)}, bf16[512,512]{1,0:T(8,128)(2,1)S(1)}, u32[]{:S(2)}, u32[]{:S(2)}) %collective-permute-start.8) | collective-permute-done | bytes 524320 | tf_op jit(solution)/shard_map/ppermute | solution.py:472
  46.0 2.0 %collective-permute-done.7.refs_1_ = bf16[512,512]{1,0:T(8,128)(2,1)S(1)} collective-permute-done((bf16[512,512]{1,0:T(8,128)(2,1)S(1)}, bf16[512,512]{1,0:T(8,128)(2,1)S(1)}, u32[]{:S(2)}, u32[]{:S(2)}) %collective-permute-start.7) | collective-permute-done | bytes 524320 | tf_op jit(solution)/shard_map/ppermute | solution.py:472
  48.9 4.2 %collective-permute-done.6.refs_3_ = bf16[256,3584]{1,0:T(8,128)(2,1)S(1)} collective-permute-done((bf16[256,3584]{1,0:T(8,128)(2,1)S(1)}, bf16[256,3584]{1,0:T(8,128)(2,1)S(1)}, u32[]{:S(2)}, u32[]{:S(2)}) %collective-permute-start.6) | collective-permute-done | bytes 1835040 | tf_op jit(solution)/shard_map/ppermute | solution.py:472
  53.0 3.3 %other_1.1 = (bf16[2,256,1024]{2,1,0:T(8,128)(2,1)S(1)}, bf16[2,256,1024]{2,1,0:T(8,128)(2,1)S(1)}, bf16[256,1024]{1,0:T(8,128)(2,1)S(1)}, bf16[256,1024]{1,0:T(8,128)(2,1)S(1)}, bf16[8,128]{1,0:T(8,128)(2,1)}) custom-call(s32[1]{0:T(128)S(6)} %copy.13.refs_0_, bf16[2,256,8192]{2,1,0:T(8,128)(2,1)S(1)} %bitcast.4, ...), custom_call_target="tpu_custom_call" | custom-call | flops 20000000000 | tf_op jit(solution)/shard_map/other_1/pallas_call | solution.py:70
  56.3 1.1 collective-permute-start.12
  57.5 1.6 %collective-permute-start.13 = (bf16[2,256,1024]{2,1,0:T(8,128)(2,1)S(1)}, bf16[2,256,1024]{2,1,0:T(8,128)(2,1)S(1)}, u32[]{:S(2)}, u32[]{:S(2)}) collective-permute-start(bf16[2,256,1024]{2,1,0:T(8,128)(2,1)S(1)} %get-tuple-element.123), channel_id=1, source_target_pairs={{0,3},{1,2},{2,1},{3,0},{4,7},{5,6},{6,5},{7,4},{8,11},{9,10},{10,... | collective-permute-start | bytes 3145736 | tf_op jit(solution)/shard_map/ppermute | solution.py:472
  59.3 13.8 %collective-permute-done.9.refs_3_ = bf16[2,512,512]{2,1,0:T(8,128)(2,1)S(1)} collective-permute-done((bf16[2,512,512]{2,1,0:T(8,128)(2,1)S(1)}, bf16[2,512,512]{2,1,0:T(8,128)(2,1)S(1)}, u32[]{:S(2)}, u32[]{:S(2)}) %collective-permute-start.9) | collective-permute-done | bytes 1048608 | tf_op jit(solution)/shard_map/ppermute | solution.py:472
  73.1 1.9 %inner_sync.1 = (bf16[16,2,32,512]{3,2,1,0:T(8,128)(2,1)S(1)}, bf16[16,32,512]{2,1,0:T(8,128)(2,1)S(1)}, bf16[8,128]{1,0:T(8,128)(2,1)}) custom-call(s32[1]{0:T(128)S(6)} %copy.13.refs_0_, bf16[2,16,2,32,512]{4,3,2,1,0:T(8,128)(2,1)} %bitcast.5, bf16[2,512,512]{2,1,0:T(8,128)(2,1)S(1)} %get-tuple-element.112.refs_2_, ...), custom_call_target="tpu_custom_call" | custom-call | tf_op jit(solution)/shard_map/inner_sync/pallas_call | solution.py:70
  75.1 1.8 %collective-permute-start.16 = (bf16[256,1024]{1,0:T(8,128)(2,1)S(1)}, bf16[256,1024]{1,0:T(8,128)(2,1)S(1)}, u32[]{:S(2)}, u32[]{:S(2)}) collective-permute-start(bf16[256,1024]{1,0:T(8,128)(2,1)S(1)} %get-tuple-element.131), channel_id=1, source_target_pairs={{0,4},{1,5},{2,6},{3,7},{4,0},{5,1},{6,2},{7,3},{8,12},{9,13},{10,... | collective-permute-start | bytes 1572872 | tf_op jit(solution)/shard_map/ppermute | solution.py:472
  77.1 1.6 %collective-permute-start.11 = (bf16[2,4,32,512]{3,2,1,0:T(8,128)(2,1)S(1)}, bf16[2,4,32,512]{3,2,1,0:T(8,128)(2,1)S(1)}, u32[]{:S(2)}, u32[]{:S(2)}) collective-permute-start(bf16[2,4,32,512]{3,2,1,0:T(8,128)(2,1)S(1)} %get-tuple-element.119), channel_id=1, source_target_pairs={{0,64},{8,72},{16,80},{24,88},{32,96},{40,104},{48,112},{56,120},{... | collective-permute-start | bytes 786440 | tf_op jit(solution)/shard_map/ppermute | solution.py:472
  79.4 1.8 %collective-permute-start.17 = (bf16[256,1024]{1,0:T(8,128)(2,1)S(1)}, bf16[256,1024]{1,0:T(8,128)(2,1)S(1)}, u32[]{:S(2)}, u32[]{:S(2)}) collective-permute-start(bf16[256,1024]{1,0:T(8,128)(2,1)S(1)} %get-tuple-element.134), channel_id=1, source_target_pairs={{0,3},{1,2},{2,1},{3,0},{4,7},{5,6},{6,5},{7,4},{8,11},{9,10},{10,... | collective-permute-start | bytes 1572872 | tf_op jit(solution)/shard_map/ppermute | solution.py:472
  81.2 2.6 %collective-permute-start.18 = (bf16[256,1024]{1,0:T(8,128)(2,1)S(1)}, bf16[256,1024]{1,0:T(8,128)(2,1)S(1)}, u32[]{:S(2)}, u32[]{:S(2)}) collective-permute-start(bf16[256,1024]{1,0:T(8,128)(2,1)S(1)} %get-tuple-element.136), channel_id=1, source_target_pairs={{0,1},{1,0},{2,3},{3,2},{4,5},{5,4},{6,7},{7,6},{8,9},{9,8},{10,11... | collective-permute-start | bytes 1572872 | tf_op jit(solution)/shard_map/ppermute | solution.py:472
  83.8 1.7 %collective-permute-done.11.refs_1_.refs_3_ = bf16[2,4,32,512]{3,2,1,0:T(8,128)(2,1)S(1)} collective-permute-done((bf16[2,4,32,512]{3,2,1,0:T(8,128)(2,1)S(1)}, bf16[2,4,32,512]{3,2,1,0:T(8,128)(2,1)S(1)}, u32[]{:S(2)}, u32[]{:S(2)}) %collective-permute-start.11) | collective-permute-done | bytes 262176 | tf_op jit(solution)/shard_map/ppermute | solution.py:472
  85.6 2.8 %collective-permute-start.14 = (bf16[4,32,512]{2,1,0:T(8,128)(2,1)S(1)}, bf16[4,32,512]{2,1,0:T(8,128)(2,1)S(1)}, u32[]{:S(2)}, u32[]{:S(2)}) collective-permute-start(bf16[4,32,512]{2,1,0:T(8,128)(2,1)S(1)} %get-tuple-element.127), channel_id=1, source_target_pairs={{0,192},{8,200},{16,208},{24,216},{32,224},{40,232},{48,240},{56,2... | collective-permute-start | bytes 393224 | tf_op jit(solution)/shard_map/ppermute | solution.py:472
  88.5 3.4 %collective-permute-done.14.refs_1_ = bf16[4,32,512]{2,1,0:T(8,128)(2,1)S(1)} collective-permute-done((bf16[4,32,512]{2,1,0:T(8,128)(2,1)S(1)}, bf16[4,32,512]{2,1,0:T(8,128)(2,1)S(1)}, u32[]{:S(2)}, u32[]{:S(2)}) %collective-permute-start.14) | collective-permute-done | bytes 131104 | tf_op jit(solution)/shard_map/ppermute | solution.py:472
  91.9 3.4 %collective-permute-start.15 = (bf16[2,32,512]{2,1,0:T(8,128)(2,1)S(1)}, bf16[2,32,512]{2,1,0:T(8,128)(2,1)S(1)}, u32[]{:S(2)}, u32[]{:S(2)}) collective-permute-start(bf16[2,32,512]{2,1,0:T(8,128)(2,1)S(1)} %get-tuple-element.130), channel_id=1, source_target_pairs={{0,16},{8,24},{16,0},{24,8},{32,48},{40,56},{48,32},{56,40},{64,80... | collective-permute-start | bytes 196616 | tf_op jit(solution)/shard_map/ppermute | solution.py:472
  95.3 1.1 other_3.1
  96.4 3.1 %inner_other.1 = (bf16[16,2,32,512]{3,2,1,0:T(8,128)(2,1)S(1)}, bf16[16,32,512]{2,1,0:T(8,128)(2,1)S(1)}, bf16[2,16,2,32,512]{4,3,2,1,0:T(8,128)(2,1)}, bf16[8,128]{1,0:T(8,128)(2,1)}) custom-call(s32[1]{0:T(128)S(6)} %copy.13.refs_0_, bf16[2,16,2,32,512]{4,3,2,1,0:T(8,128)(2,1)} %bitcast.6, bf16[256,1024]{1,0:T(8,128)(2,1)S(1)} %get-tuple-element.133.refs_2_, ...), custom_call_target="tpu_custom_call" | custom-call | tf_op jit(solution)/shard_map/inner_other/pallas_call | solution.py:70
  99.7 4.4 %collective-permute-start.19 = (bf16[32,512]{1,0:T(8,128)(2,1)S(1)}, bf16[32,512]{1,0:T(8,128)(2,1)S(1)}, u32[]{:S(2)}, u32[]{:S(2)}) collective-permute-start(bf16[32,512]{1,0:T(8,128)(2,1)S(1)} %get-tuple-element.140), channel_id=1, source_target_pairs={{0,48},{8,56},{16,32},{24,40},{32,16},{40,24},{48,0},{56,8},{64,11... | collective-permute-start | bytes 98312 | tf_op jit(solution)/shard_map/ppermute | solution.py:472
  104.6 1.6 %collective-permute-done.19.refs_4_ = bf16[32,512]{1,0:T(8,128)(2,1)S(1)} collective-permute-done((bf16[32,512]{1,0:T(8,128)(2,1)S(1)}, bf16[32,512]{1,0:T(8,128)(2,1)S(1)}, u32[]{:S(2)}, u32[]{:S(2)}) %collective-permute-start.19) | collective-permute-done | bytes 32800 | tf_op jit(solution)/shard_map/ppermute | solution.py:472
  106.3 0.9 outer_sync.1
  107.2 8.4 %all-to-all-start = ((bf16[16,32,512]{2,1,0:T(8,128)(2,1)}), bf16[16,32,512]{2,1,0:T(8,128)(2,1)S(1)}, u32[]{:S(2)}, u32[]{:S(2)}) async-start(bf16[16,32,512]{2,1,0:T(8,128)(2,1)} %get-tuple-element.145), calls=%async_computation | async-start | bytes 1048576 | tf_op jit(solution)/shard_map/all_to_all | solution.py:468
  115.6 3.2 %collective-permute-start.22 = (bf16[4,32,512]{2,1,0:T(8,128)(2,1)S(1)}, bf16[4,32,512]{2,1,0:T(8,128)(2,1)S(1)}, u32[]{:S(2)}, u32[]{:S(2)}) collective-permute-start(bf16[4,32,512]{2,1,0:T(8,128)(2,1)S(1)} %get-tuple-element.150), channel_id=1, source_target_pairs={{0,192},{8,200},{16,208},{24,216},{32,224},{40,232},{48,240},{56,2... | collective-permute-start | bytes 393224 | tf_op jit(solution)/shard_map/ppermute | solution.py:472
  118.9 4.7 %collective-permute-done.22.refs_1_ = bf16[4,32,512]{2,1,0:T(8,128)(2,1)S(1)} collective-permute-done((bf16[4,32,512]{2,1,0:T(8,128)(2,1)S(1)}, bf16[4,32,512]{2,1,0:T(8,128)(2,1)S(1)}, u32[]{:S(2)}, u32[]{:S(2)}) %collective-permute-start.22) | collective-permute-done | bytes 131104 | tf_op jit(solution)/shard_map/ppermute | solution.py:472
  123.6 3.6 %collective-permute-start.24 = (bf16[2,32,512]{2,1,0:T(8,128)(2,1)S(1)}, bf16[2,32,512]{2,1,0:T(8,128)(2,1)S(1)}, u32[]{:S(2)}, u32[]{:S(2)}) collective-permute-start(bf16[2,32,512]{2,1,0:T(8,128)(2,1)S(1)} %get-tuple-element.156), channel_id=1, source_target_pairs={{0,16},{8,24},{16,0},{24,8},{32,48},{40,56},{48,32},{56,40},{64,80... | collective-permute-start | bytes 196616 | tf_op jit(solution)/shard_map/ppermute | solution.py:472
  127.2 7.6 %all-to-all-done.refs_0_ = bf16[16,32,512]{2,1,0:T(8,128)(2,1)S(1)} async-done(((bf16[16,32,512]{2,1,0:T(8,128)(2,1)}), bf16[16,32,512]{2,1,0:T(8,128)(2,1)S(1)}, u32[]{:S(2)}, u32[]{:S(2)}) %all-to-all-start) | async-done | bytes 524320 | tf_op jit(solution)/shard_map/all_to_all | solution.py:468
  135.1 1.8 %collective-permute-done.23.refs_3_ = bf16[16,32,512]{2,1,0:T(8,128)(2,1)S(1)} collective-permute-done((bf16[16,32,512]{2,1,0:T(8,128)(2,1)S(1)}, bf16[16,32,512]{2,1,0:T(8,128)(2,1)S(1)}, u32[]{:S(2)}, u32[]{:S(2)}) %collective-permute-start.23) | collective-permute-done | bytes 524320 | tf_op jit(solution)/shard_map/ppermute | solution.py:472
  136.8 1.4 mix.1
  138.2 2.9 %collective-permute-done.25.refs_3_ = bf16[32,512]{1,0:T(8,128)(2,1)S(1)} collective-permute-done((bf16[32,512]{1,0:T(8,128)(2,1)S(1)}, bf16[32,512]{1,0:T(8,128)(2,1)S(1)}, u32[]{:S(2)}, u32[]{:S(2)}) %collective-permute-start.25) | collective-permute-done | bytes 32800 | tf_op jit(solution)/shard_map/ppermute | solution.py:472
  141.1 0.6 outer_other.1
  (44 shorter events, 5.6 us)
Async XLA Ops:
  1.3 22.2 %slice-start = ((s8[8388608]{0:T(1024)(128)(4,1)}), s8[4194304]{0:T(1024)(128)(4,1)S(1)}, s32[]{:S(2)}) async-start(s8[8388608]{0:T(1024)(128)(4,1)} %bitcast.3), calls=%async_computation.1 | async-start | bytes 8388608
  2.8 20.7 %collective-permute-start = (bf16[256,1536]{1,0:T(8,128)(2,1)S(1)}, bf16[256,1536]{1,0:T(8,128)(2,1)S(1)}, u32[]{:S(2)}, u32[]{:S(2)}) collective-permute-start(bf16[256,1536]{1,0:T(8,128)(2,1)S(1)} %get-tuple-element.86), channel_id=1, source_target_pairs={{0,1},{1,0},{2,3},{3,2},{4,5},{5,4},{6,7},{7,6},{8,9},{9,8},{10,11... | collective-permute-start | bytes 2359304 | tf_op jit(solution)/shard_map/ppermute | solution.py:472
  5.1 20.5 %collective-permute-start.2 = (bf16[256,1536]{1,0:T(8,128)(2,1)S(1)}, bf16[256,1536]{1,0:T(8,128)(2,1)S(1)}, u32[]{:S(2)}, u32[]{:S(2)}) collective-permute-start(bf16[256,1536]{1,0:T(8,128)(2,1)S(1)} %get-tuple-element.89), channel_id=1, source_target_pairs={{0,3},{1,2},{2,1},{3,0},{4,7},{5,6},{6,5},{7,4},{8,11},{9,10},{10,... | collective-permute-start | bytes 2359304 | tf_op jit(solution)/shard_map/ppermute | solution.py:472
  5.7 17.8 %slice-start.1 = ((s8[8388608]{0:T(1024)(128)(4,1)}), s8[4194304]{0:T(1024)(128)(4,1)S(1)}, s32[]{:S(2)}) async-start(s8[8388608]{0:T(1024)(128)(4,1)} %bitcast.3), calls=%async_computation.2 | async-start | bytes 8388608
  7.9 26.8 %collective-permute-start.1 = (bf16[256,1024]{1,0:T(8,128)(2,1)S(1)}, bf16[256,1024]{1,0:T(8,128)(2,1)S(1)}, u32[]{:S(2)}, u32[]{:S(2)}) collective-permute-start(bf16[256,1024]{1,0:T(8,128)(2,1)S(1)} %get-tuple-element.88), channel_id=1, source_target_pairs={{0,1},{1,0},{2,3},{3,2},{4,5},{5,4},{6,7},{7,6},{8,9},{9,8},{10,11... | collective-permute-start | bytes 1572872 | tf_op jit(solution)/shard_map/ppermute | solution.py:472
  9.4 27.5 %collective-permute-start.3 = (bf16[256,1024]{1,0:T(8,128)(2,1)S(1)}, bf16[256,1024]{1,0:T(8,128)(2,1)S(1)}, u32[]{:S(2)}, u32[]{:S(2)}) collective-permute-start(bf16[256,1024]{1,0:T(8,128)(2,1)S(1)} %get-tuple-element.90), channel_id=1, source_target_pairs={{0,3},{1,2},{2,1},{3,0},{4,7},{5,6},{6,5},{7,4},{8,11},{9,10},{10,... | collective-permute-start | bytes 1572872 | tf_op jit(solution)/shard_map/ppermute | solution.py:472
  10.1 42.9 %collective-permute-start.6 = (bf16[256,3584]{1,0:T(8,128)(2,1)S(1)}, bf16[256,3584]{1,0:T(8,128)(2,1)S(1)}, u32[]{:S(2)}, u32[]{:S(2)}) collective-permute-start(bf16[256,3584]{1,0:T(8,128)(2,1)S(1)} %get-tuple-element.104), channel_id=1, source_target_pairs={{0,4},{1,5},{2,6},{3,7},{4,0},{5,1},{6,2},{7,3},{8,12},{9,13},{10,... | collective-permute-start | bytes 5505032 | tf_op jit(solution)/shard_map/ppermute | solution.py:472
  26.2 19.8 %collective-permute-start.8 = (bf16[512,512]{1,0:T(8,128)(2,1)S(1)}, bf16[512,512]{1,0:T(8,128)(2,1)S(1)}, u32[]{:S(2)}, u32[]{:S(2)}) collective-permute-start(bf16[512,512]{1,0:T(8,128)(2,1)S(1)} %get-tuple-element.108), channel_id=1, source_target_pairs={{0,1},{1,0},{2,3},{3,2},{4,5},{5,4},{6,7},{7,6},{8,9},{9,8},{10,11... | collective-permute-start | bytes 1572872 | tf_op jit(solution)/shard_map/ppermute | solution.py:472
  27.6 20.4 %collective-permute-start.7 = (bf16[512,512]{1,0:T(8,128)(2,1)S(1)}, bf16[512,512]{1,0:T(8,128)(2,1)S(1)}, u32[]{:S(2)}, u32[]{:S(2)}) collective-permute-start(bf16[512,512]{1,0:T(8,128)(2,1)S(1)} %get-tuple-element.106), channel_id=1, source_target_pairs={{0,3},{1,2},{2,1},{3,0},{4,7},{5,6},{6,5},{7,4},{8,11},{9,10},{10,... | collective-permute-start | bytes 1572872 | tf_op jit(solution)/shard_map/ppermute | solution.py:472
  35.4 23.7 %collective-permute-start.4 = (bf16[512,512]{1,0:T(8,128)(2,1)S(1)}, bf16[512,512]{1,0:T(8,128)(2,1)S(1)}, u32[]{:S(2)}, u32[]{:S(2)}) collective-permute-start(bf16[512,512]{1,0:T(8,128)(2,1)S(1)} %get-tuple-element.99), channel_id=1, source_target_pairs={{0,3},{1,2},{2,1},{3,0},{4,7},{5,6},{6,5},{7,4},{8,11},{9,10},{10,... | collective-permute-start | bytes 1572872 | tf_op jit(solution)/shard_map/ppermute | solution.py:472
  37.5 21.6 %collective-permute-start.5 = (bf16[512,512]{1,0:T(8,128)(2,1)S(1)}, bf16[512,512]{1,0:T(8,128)(2,1)S(1)}, u32[]{:S(2)}, u32[]{:S(2)}) collective-permute-start(bf16[512,512]{1,0:T(8,128)(2,1)S(1)} %get-tuple-element.102), channel_id=1, source_target_pairs={{0,1},{1,0},{2,3},{3,2},{4,5},{5,4},{6,7},{7,6},{8,9},{9,8},{10,11... | collective-permute-start | bytes 1572872 | tf_op jit(solution)/shard_map/ppermute | solution.py:472
  48.3 24.8 %collective-permute-start.9 = (bf16[2,512,512]{2,1,0:T(8,128)(2,1)S(1)}, bf16[2,512,512]{2,1,0:T(8,128)(2,1)S(1)}, u32[]{:S(2)}, u32[]{:S(2)}) collective-permute-start(bf16[2,512,512]{2,1,0:T(8,128)(2,1)S(1)} %get-tuple-element.113), channel_id=1, source_target_pairs={{0,4},{1,5},{2,6},{3,7},{4,0},{5,1},{6,2},{7,3},{8,12},{9,13},{10,... | collective-permute-start | bytes 3145736 | tf_op jit(solution)/shard_map/ppermute | solution.py:472
  56.3 22.4 %collective-permute-start.12 = (bf16[2,256,1024]{2,1,0:T(8,128)(2,1)S(1)}, bf16[2,256,1024]{2,1,0:T(8,128)(2,1)S(1)}, u32[]{:S(2)}, u32[]{:S(2)}) collective-permute-start(bf16[2,256,1024]{2,1,0:T(8,128)(2,1)S(1)} %get-tuple-element.121), channel_id=1, source_target_pairs={{0,1},{1,0},{2,3},{3,2},{4,5},{5,4},{6,7},{7,6},{8,9},{9,8},{10,11... | collective-permute-start | bytes 3145736 | tf_op jit(solution)/shard_map/ppermute | solution.py:472
  57.5 21.7 %collective-permute-start.13 = (bf16[2,256,1024]{2,1,0:T(8,128)(2,1)S(1)}, bf16[2,256,1024]{2,1,0:T(8,128)(2,1)S(1)}, u32[]{:S(2)}, u32[]{:S(2)}) collective-permute-start(bf16[2,256,1024]{2,1,0:T(8,128)(2,1)S(1)} %get-tuple-element.123), channel_id=1, source_target_pairs={{0,3},{1,2},{2,1},{3,0},{4,7},{5,6},{6,5},{7,4},{8,11},{9,10},{10,... | collective-permute-start | bytes 3145736 | tf_op jit(solution)/shard_map/ppermute | solution.py:472
  75.0 2.0 %collective-permute-start.10 = (bf16[16,32,512]{2,1,0:T(8,128)(2,1)S(1)}, bf16[16,32,512]{2,1,0:T(8,128)(2,1)S(1)}, u32[]{:S(2)}, u32[]{:S(2)}) collective-permute-start(bf16[16,32,512]{2,1,0:T(8,128)(2,1)S(1)} %get-tuple-element.116), channel_id=1, source_target_pairs={{0,8},{8,0},{16,24},{24,16},{32,40},{40,32},{48,56},{56,48},{64,72... | collective-permute-start | bytes 1572872 | tf_op jit(solution)/shard_map/ppermute | solution.py:472
  75.1 20.2 %collective-permute-start.16 = (bf16[256,1024]{1,0:T(8,128)(2,1)S(1)}, bf16[256,1024]{1,0:T(8,128)(2,1)S(1)}, u32[]{:S(2)}, u32[]{:S(2)}) collective-permute-start(bf16[256,1024]{1,0:T(8,128)(2,1)S(1)} %get-tuple-element.131), channel_id=1, source_target_pairs={{0,4},{1,5},{2,6},{3,7},{4,0},{5,1},{6,2},{7,3},{8,12},{9,13},{10,... | collective-permute-start | bytes 1572872 | tf_op jit(solution)/shard_map/ppermute | solution.py:472
  77.1 8.4 %collective-permute-start.11 = (bf16[2,4,32,512]{3,2,1,0:T(8,128)(2,1)S(1)}, bf16[2,4,32,512]{3,2,1,0:T(8,128)(2,1)S(1)}, u32[]{:S(2)}, u32[]{:S(2)}) collective-permute-start(bf16[2,4,32,512]{3,2,1,0:T(8,128)(2,1)S(1)} %get-tuple-element.119), channel_id=1, source_target_pairs={{0,64},{8,72},{16,80},{24,88},{32,96},{40,104},{48,112},{56,120},{... | collective-permute-start | bytes 786440 | tf_op jit(solution)/shard_map/ppermute | solution.py:472
  79.4 17.0 %collective-permute-start.17 = (bf16[256,1024]{1,0:T(8,128)(2,1)S(1)}, bf16[256,1024]{1,0:T(8,128)(2,1)S(1)}, u32[]{:S(2)}, u32[]{:S(2)}) collective-permute-start(bf16[256,1024]{1,0:T(8,128)(2,1)S(1)} %get-tuple-element.134), channel_id=1, source_target_pairs={{0,3},{1,2},{2,1},{3,0},{4,7},{5,6},{6,5},{7,4},{8,11},{9,10},{10,... | collective-permute-start | bytes 1572872 | tf_op jit(solution)/shard_map/ppermute | solution.py:472
  81.2 15.2 %collective-permute-start.18 = (bf16[256,1024]{1,0:T(8,128)(2,1)S(1)}, bf16[256,1024]{1,0:T(8,128)(2,1)S(1)}, u32[]{:S(2)}, u32[]{:S(2)}) collective-permute-start(bf16[256,1024]{1,0:T(8,128)(2,1)S(1)} %get-tuple-element.136), channel_id=1, source_target_pairs={{0,1},{1,0},{2,3},{3,2},{4,5},{5,4},{6,7},{7,6},{8,9},{9,8},{10,11... | collective-permute-start | bytes 1572872 | tf_op jit(solution)/shard_map/ppermute | solution.py:472
  85.6 6.3 %collective-permute-start.14 = (bf16[4,32,512]{2,1,0:T(8,128)(2,1)S(1)}, bf16[4,32,512]{2,1,0:T(8,128)(2,1)S(1)}, u32[]{:S(2)}, u32[]{:S(2)}) collective-permute-start(bf16[4,32,512]{2,1,0:T(8,128)(2,1)S(1)} %get-tuple-element.127), channel_id=1, source_target_pairs={{0,192},{8,200},{16,208},{24,216},{32,224},{40,232},{48,240},{56,2... | collective-permute-start | bytes 393224 | tf_op jit(solution)/shard_map/ppermute | solution.py:472
  91.9 7.8 %collective-permute-start.15 = (bf16[2,32,512]{2,1,0:T(8,128)(2,1)S(1)}, bf16[2,32,512]{2,1,0:T(8,128)(2,1)S(1)}, u32[]{:S(2)}, u32[]{:S(2)}) collective-permute-start(bf16[2,32,512]{2,1,0:T(8,128)(2,1)S(1)} %get-tuple-element.130), channel_id=1, source_target_pairs={{0,16},{8,24},{16,0},{24,8},{32,48},{40,56},{48,32},{56,40},{64,80... | collective-permute-start | bytes 196616 | tf_op jit(solution)/shard_map/ppermute | solution.py:472
  99.6 4.6 %collective-permute-start.20 = (bf16[16,32,512]{2,1,0:T(8,128)(2,1)S(1)}, bf16[16,32,512]{2,1,0:T(8,128)(2,1)S(1)}, u32[]{:S(2)}, u32[]{:S(2)}) collective-permute-start(bf16[16,32,512]{2,1,0:T(8,128)(2,1)S(1)} %get-tuple-element.142), channel_id=1, source_target_pairs={{0,8},{8,0},{16,24},{24,16},{32,40},{40,32},{48,56},{56,48},{64,72... | collective-permute-start | bytes 1572872 | tf_op jit(solution)/shard_map/ppermute | solution.py:472
  99.7 6.6 %copy-start = (f32[2,32,512]{2,1,0:T(8,128)S(1)}, f32[2,32,512]{2,1,0:T(8,128)}, u32[]{:S(2)}) copy-start(f32[2,32,512]{2,1,0:T(8,128)} %refs_1_.23) | copy-start | bytes 393220
  99.7 6.6 %copy-start.1 = (f32[32,512]{1,0:T(8,128)S(1)}, f32[32,512]{1,0:T(8,128)}, u32[]{:S(2)}) copy-start(f32[32,512]{1,0:T(8,128)} %refs_2_.5) | copy-start | bytes 196612
  99.7 6.5 %collective-permute-start.19 = (bf16[32,512]{1,0:T(8,128)(2,1)S(1)}, bf16[32,512]{1,0:T(8,128)(2,1)S(1)}, u32[]{:S(2)}, u32[]{:S(2)}) collective-permute-start(bf16[32,512]{1,0:T(8,128)(2,1)S(1)} %get-tuple-element.140), channel_id=1, source_target_pairs={{0,48},{8,56},{16,32},{24,40},{32,16},{40,24},{48,0},{56,8},{64,11... | collective-permute-start | bytes 98312 | tf_op jit(solution)/shard_map/ppermute | solution.py:472
  104.3 11.3 %collective-permute-start.21 = (bf16[2,4,32,512]{3,2,1,0:T(8,128)(2,1)S(1)}, bf16[2,4,32,512]{3,2,1,0:T(8,128)(2,1)S(1)}, u32[]{:S(2)}, u32[]{:S(2)}) collective-permute-start(bf16[2,4,32,512]{3,2,1,0:T(8,128)(2,1)S(1)} %get-tuple-element.147), channel_id=1, source_target_pairs={{0,64},{8,72},{16,80},{24,88},{32,96},{40,104},{48,112},{56,120},{... | collective-permute-start | bytes 786440 | tf_op jit(solution)/shard_map/ppermute | solution.py:472
  107.2 27.6 %all-to-all-start = ((bf16[16,32,512]{2,1,0:T(8,128)(2,1)}), bf16[16,32,512]{2,1,0:T(8,128)(2,1)S(1)}, u32[]{:S(2)}, u32[]{:S(2)}) async-start(bf16[16,32,512]{2,1,0:T(8,128)(2,1)} %get-tuple-element.145), calls=%async_computation | async-start | bytes 1048576 | tf_op jit(solution)/shard_map/all_to_all | solution.py:468
  115.6 7.9 %collective-permute-start.22 = (bf16[4,32,512]{2,1,0:T(8,128)(2,1)S(1)}, bf16[4,32,512]{2,1,0:T(8,128)(2,1)S(1)}, u32[]{:S(2)}, u32[]{:S(2)}) collective-permute-start(bf16[4,32,512]{2,1,0:T(8,128)(2,1)S(1)} %get-tuple-element.150), channel_id=1, source_target_pairs={{0,192},{8,200},{16,208},{24,216},{32,224},{40,232},{48,240},{56,2... | collective-permute-start | bytes 393224 | tf_op jit(solution)/shard_map/ppermute | solution.py:472
  123.6 11.3 %collective-permute-start.24 = (bf16[2,32,512]{2,1,0:T(8,128)(2,1)S(1)}, bf16[2,32,512]{2,1,0:T(8,128)(2,1)S(1)}, u32[]{:S(2)}, u32[]{:S(2)}) collective-permute-start(bf16[2,32,512]{2,1,0:T(8,128)(2,1)S(1)} %get-tuple-element.156), channel_id=1, source_target_pairs={{0,16},{8,24},{16,0},{24,8},{32,48},{40,56},{48,32},{56,40},{64,80... | collective-permute-start | bytes 196616 | tf_op jit(solution)/shard_map/ppermute | solution.py:472
  134.8 2.0 %collective-permute-start.23 = (bf16[16,32,512]{2,1,0:T(8,128)(2,1)S(1)}, bf16[16,32,512]{2,1,0:T(8,128)(2,1)S(1)}, u32[]{:S(2)}, u32[]{:S(2)}) collective-permute-start(bf16[16,32,512]{2,1,0:T(8,128)(2,1)S(1)} %get-tuple-element.153.refs_2_), channel_id=1, source_target_pairs={{0,8},{8,0},{16,24},{24,16},{32,40},{40,32},{48,56},{56,48},{64,72... | collective-permute-start | bytes 1572872 | tf_op jit(solution)/shard_map/ppermute | solution.py:472
  135.0 6.1 %collective-permute-start.25 = (bf16[32,512]{1,0:T(8,128)(2,1)S(1)}, bf16[32,512]{1,0:T(8,128)(2,1)S(1)}, u32[]{:S(2)}, u32[]{:S(2)}) collective-permute-start(bf16[32,512]{1,0:T(8,128)(2,1)S(1)} %get-tuple-element.163), channel_id=1, source_target_pairs={{0,48},{8,56},{16,32},{24,40},{32,16},{40,24},{48,0},{56,8},{64,11... | collective-permute-start | bytes 98312 | tf_op jit(solution)/shard_map/ppermute | solution.py:472

commit v10 on v9

--- a/solution.py
+++ b/solution.py
@@ -252,64 +252,90 @@
 WORKERS = (16, 2, 32, KV)
 
 
-def inner_sync(plan, w, near, across):
-    def kernel(plan_ref, w_ref, near_ref, z_ref, inner_ref, send_ref, wv, sem, sem2):
+def take(plan, w):
+    def kernel(plan_ref, w_ref, sync_ref, other_ref, sems):
         s = lax.rem(plan_ref[0], 2)
-        core = place()[2]
-        load = pltpu.make_async_copy(w_ref.at[s], wv, sem)
-        load.start()
-        load.wait()
+        copies = [
+            pltpu.make_async_copy(w_ref.at[layer], out, sems.at[i])
+            for i, (layer, out) in enumerate(((s, sync_ref), (1 - s, other_ref)))
+        ]
+        for c in copies:
+            c.start()
+        for c in copies:
+            c.wait()
+
+    return call(
+        kernel,
+        (in_vmem(*WORKERS),) * 2,
+        (plan, w),
+        [SM, HBM],
+        [VM] * 2,
+        [pltpu.SemaphoreType.DMA((2,))],
+        name="take",
+    )
+
+
+def inner_sync(w, near, across):
+    def kernel(w_ref, near_ref, z_ref, inner_ref, send_ref, sem):
         for h in range(2):
             for q in range(4):
                 cols = pl.ds(q * 128, 128)
                 i = h * 8 + q * 2
                 gradient = flip(near_ref[h, :, cols], z_ref[h, :, cols])
-                inner_ref[i : i + 2] = stepped(wv[i : i + 2].reshape(128, KV), gradient).reshape(2, 2, 32, KV)
-        out = pltpu.make_async_copy(inner_ref.at[:, 1 - core], send_ref, sem2)
+                inner_ref[i : i + 2] = stepped(w_ref[i : i + 2].reshape(128, KV), gradient).reshape(2, 2, 32, KV)
+        out = pltpu.make_async_copy(inner_ref.at[:, 1 - place()[2]], send_ref, sem)
         out.start()
         out.wait()
 
     return call(
         kernel,
         (shape(*WORKERS), shape(16, 32, KV)),
-        (plan, w, near, across),
-        [SM, HBM] + [VM] * 2,
+        (w, near, across),
+        [VM] * 3,
         [VM, ANY],
-        [pltpu.VMEM(WORKERS, BF16), pltpu.SemaphoreType.DMA, pltpu.SemaphoreType.DMA],
+        [pltpu.SemaphoreType.DMA],
         name="inner_sync",
     )
 
 
-def inner_other(plan, w, first, second):
-    def kernel(plan_ref, w_ref, *rest):
-        k0, r0, l0, k1, r1, l1, inner_ref, send_ref, new_ref, wv, sem, sem2 = rest
-        other = 1 - lax.rem(plan_ref[0], 2)
-        core = place()[2]
-        load = pltpu.make_async_copy(w_ref.at[other], wv, sem)
-        load.start()
-        load.wait()
+def inner_other(w, first, second):
+    def kernel(w_ref, k0, r0, l0, k1, r1, l1, inner_ref, send_ref, sem):
         for q in range(8):
             cols = pl.ds(q * 128, 128)
             i = q * 2
             gradient = jnp.concatenate(
                 [flip(k[:, cols], r[0, :, cols], l[:, cols]) for k, r, l in ((k0, r0, l0), (k1, r1, l1))], axis=1
             )
-            inner_ref[i : i + 2] = stepped(wv[i : i + 2].reshape(128, KV), gradient).reshape(2, 2, 32, KV)
-        out = pltpu.make_async_copy(inner_ref.at[:, 1 - core], send_ref, sem2.at[0])
-        keep = pltpu.make_async_copy(inner_ref, new_ref.at[other], sem2.at[1])
+            inner_ref[i : i + 2] = stepped(w_ref[i : i + 2].reshape(128, KV), gradient).reshape(2, 2, 32, KV)
+        out = pltpu.make_async_copy(inner_ref.at[:, 1 - place()[2]], send_ref, sem)
         out.start()
-        keep.start()
         out.wait()
-        keep.wait()
-
-    return call(
-        kernel,
-        (shape(*WORKERS), shape(16, 32, KV), shape(2, *WORKERS)),
-        (plan, w, *first, *second),
-        [SM, HBM] + [VM] * 6,
-        [VM, ANY, ANY],
-        [pltpu.VMEM(WORKERS, BF16), pltpu.SemaphoreType.DMA, pltpu.SemaphoreType.DMA((2,))],
+
+    return call(
+        kernel,
+        (shape(*WORKERS), shape(16, 32, KV)),
+        (w, *first, *second),
+        [VM] * 7,
+        [VM, ANY],
+        [pltpu.SemaphoreType.DMA],
         name="inner_other",
+    )
+
+
+def store(plan, inner):
+    def kernel(plan_ref, inner_ref, new_ref, sem):
+        out = pltpu.make_async_copy(inner_ref, new_ref.at[1 - lax.rem(plan_ref[0], 2)], sem)
+        out.start()
+        out.wait()
+
+    return call(
+        kernel,
+        (shape(2, *WORKERS),),
+        (plan, inner),
+        [SM, VM],
+        [ANY],
+        [pltpu.SemaphoreType.DMA],
+        name="store",
     )
 
 
@@ -411,30 +437,30 @@
         [SM] + [VM] * 3,
         [VM],
         name="outer_other",
-    )
-
-
-def mix(plan, inner, own, recv, new):
-    def kernel(plan_ref, inner_ref, own_ref, recv_ref, _, out_ref, stage, sems):
-        s = lax.rem(plan_ref[0], 2)
+        hint=LONG,
+    )
+
+
+def mix(plan, inner, rows, new, far):
+    def kernel(plan_ref, inner_ref, rows_ref, _, out_ref, stage, sem):
         core = place()[2]
-        for t, c in ((own_ref, core), (recv_ref, 1 - core)):
-            stage[:, c] = (
-                mix_weight * inner_ref[:, c].astype(F32) + (1.0 - mix_weight) * t[...].astype(F32)
-            ).astype(BF16)
-        out = pltpu.make_async_copy(stage, out_ref.at[s], sems)
+        c = 1 - core if far else core
+        stage[...] = (
+            mix_weight * inner_ref[:, c].astype(F32) + (1.0 - mix_weight) * rows_ref[...].astype(F32)
+        ).astype(BF16)
+        out = pltpu.make_async_copy(stage, out_ref.at[lax.rem(plan_ref[0], 2), :, c], sem)
         out.start()
         out.wait()
 
     return call(
         kernel,
         (shape(2, *WORKERS),),
-        (plan, inner, own, recv, new),
-        [SM, VM, VM, VM, ANY],
+        (plan, inner, rows, new),
+        [SM, VM, VM, ANY],
         [ANY],
-        [pltpu.VMEM(WORKERS, BF16), pltpu.SemaphoreType.DMA],
-        aliases={4: 0},
-        name="mix",
+        [pltpu.VMEM((16, 32, KV), BF16), pltpu.SemaphoreType.DMA],
+        aliases={3: 0},
+        name="mix_far" if far else "mix_own",
     )
 
 
@@ -527,7 +553,8 @@
     got_0, got_1 = swap(send_0, "a"), swap(send_1, "b")
     near = sums("near", [(2, KV, HALF)], [(keep_a2, near_a, None, None, 0, 0), (keep_b2, near_b, None, None, 0, 1)])
 
-    inner_s, send_s = inner_sync(plan, w, near, across)
+    w_s, w_o = take(plan, w)
+    inner_s, send_s = inner_sync(w_s, near, across)
     send, keep = sum_x(inner_s, swap(send_s, "core"), "sync_x1")
     recv = swap(send, "x1")
     last_0, last_1 = sums(
@@ -538,10 +565,11 @@
     send, keep = sum_z(keep, swap(send, "x3"), "sync_z1")
     recv = swap(send, "z1")
     mine_0, mine_1 = other("other_3", [dest(0, 1, 0, [(0, None, *lo), (1, None, *hi)])], [half, half], (got_z1, got_z3), SHORT)
-    inner_o, send_o, new = inner_other(plan, w, (mine_0, got_0, last_0), (mine_1, got_1, last_1))
+    inner_o, send_o = inner_other(w_o, (mine_0, got_0, last_0), (mine_1, got_1, last_1))
     core_o = swap(send_o, "core")
     send, keep = halve("sync_z3", (32, KV), keep, recv, LONG)
     recv = swap(send, "z3")
+    new = store(plan, inner_o)
     send_o, keep_o = sum_x(inner_o, core_o, "other_x1")
     recv_o = swap(send_o, "x1")
     anchor_new, momentum_new, short = outer_sync(plan, anchors, momentum, keep, recv)
@@ -550,11 +578,12 @@
     recv_o = swap(send_o, "x3")
     send_o, keep_o = sum_z(keep_o, recv_o, "other_z1")
     recv_o = swap(send_o, "z1")
+    send_o, keep_o = halve("other_z3", (32, KV), keep_o, recv_o)
+    recv_o = swap(send_o, "z3")
     block = relay(block)
-    send_o, keep_o = halve("other_z3", (32, KV), keep_o, recv_o, LONG)
-    recv_o = swap(send_o, "z3")
-    new = mix(plan, inner_s, block, swap(block, "core"), new)
+    new = mix(plan, inner_s, block, new, 0)
     pending = outer_other(plan, anchors, keep_o, recv_o)
+    new = mix(plan, inner_s, swap(block, "core"), new, 1)
     return (new.reshape(1, 2, ROWS, KV), anchor_new, momentum_new, pending)
 
 

time: 143 us -> 138 us (0.965)
  waiting for transfers between devices: 67.4 us -> 59.3 us
  starting transfers between devices: 50.5 us -> 53.5 us
    all_to_all x1, waiting for transfers between devices: 7.61 us -> 0.24 us  [exchange(): lax.all_to_all(value, 'worker', 0, 0, axis_index_groups=PLANES, tiled=True)]
    ppermute x26, starting transfers between devices: 42.1 us -> 44.3 us  [swap(): return lax.ppermute(value, *MOVES[move])]
    pallas_call x29 -> x32, Pallas kernels: 22.2 us -> 22 us  [call(): pl.pallas_call(chained, out_shape=outs + [in_hbm(8, 128)], in_specs=list(...]
  transfers between devices with their start and end apart: 27 -> 27, of which waited for: 16 -> 17; matrix products, arithmetic and copies ran while one was open for 0% -> 0% of each run, Pallas kernels for 14% -> 14%
where the time goes in v10:
time: 138 us; the launch traced here: 137 us
  waiting for transfers between devices  59.3 us (43%)
  starting transfers between devices  53.5 us (39%)
  Pallas kernels  22 us (16%)
  between operations  1.73 us (1%)
    ppermute x26, waiting for transfers between devices, swap(): return lax.ppermute(value, *MOVES[move])  59.1 us
    ppermute x26, starting transfers between devices, swap(): return lax.ppermute(value, *MOVES[move])  44.3 us
    pallas_call x32, Pallas kernels, call(): pl.pallas_call(chained, out_shape=outs + [in_hbm(8, 128)], in_specs=list(...  22 us
    all_to_all x1, starting transfers between devices, exchange(): lax.all_to_all(value, 'worker', 0, 0, axis_index_groups=PLANES, tiled=True)  9.18 us
  transfers between devices with their start and end apart: 27, of which 17 were waited for; matrix products, arithmetic and copies ran while one was open for 0% of the time, Pallas kernels for 14%

profile of v10, /device:TPU:8, one launch (start us, length us, event | category | flops | bytes accessed | tf_op | source)
XLA Modules:
  0.0 136.5 jit_solution(959670456499775990)
XLA Ops:
  1.3 1.5 %pack_1.1 = (bf16[256,1536]{1,0:T(8,128)(2,1)S(1)}, bf16[256,1536]{1,0:T(8,128)(2,1)S(1)}, bf16[512,256]{1,0:T(8,128)(2,1)S(1)}, bf16[8,128]{1,0:T(8,128)(2,1)}) custom-call(s32[1]{0:T(128)S(6)} %copy.15.refs_0_, s32[1,256]{1,0:T(1,128)} %bitcast.7, bf16[2,256,8192]{2,1,0:T(8,128)(2,1)} %refs_1_.21, bf16[2,256,512]{2,1,0:T(8,128)(2,1)} %refs_3_.3), custom_call_target="tpu_custom_call" | custom-call | tf_op jit(solution)/shard_map/pack_1/pallas_call | solution.py:70
  2.8 2.3 %collective-permute-start = (bf16[256,1536]{1,0:T(8,128)(2,1)S(1)}, bf16[256,1536]{1,0:T(8,128)(2,1)S(1)}, u32[]{:S(2)}, u32[]{:S(2)}) collective-permute-start(bf16[256,1536]{1,0:T(8,128)(2,1)S(1)} %get-tuple-element.92), channel_id=1, source_target_pairs={{0,1},{1,0},{2,3},{3,2},{4,5},{5,4},{6,7},{7,6},{8,9},{9,8},{10,11... | collective-permute-start | bytes 2359304 | tf_op jit(solution)/shard_map/ppermute | solution.py:498
  5.1 0.7 collective-permute-start.2
  5.7 2.2 %pack_2.1 = (bf16[256,3584]{1,0:T(8,128)(2,1)S(1)}, bf16[256,1024]{1,0:T(8,128)(2,1)S(1)}, bf16[256,1024]{1,0:T(8,128)(2,1)S(1)}, bf16[256,1024]{1,0:T(8,128)(2,...) custom-call(s32[1]{0:T(128)S(6)} %copy.15.refs_0_, s32[1,256]{1,0:T(1,128)} %bitcast.8, ...), custom_call_target="tpu_custom_call" | custom-call | tf_op jit(solution)/shard_map/pack_2/pallas_call | solution.py:70
  7.9 1.4 %collective-permute-start.1 = (bf16[256,1024]{1,0:T(8,128)(2,1)S(1)}, bf16[256,1024]{1,0:T(8,128)(2,1)S(1)}, u32[]{:S(2)}, u32[]{:S(2)}) collective-permute-start(bf16[256,1024]{1,0:T(8,128)(2,1)S(1)} %get-tuple-element.94), channel_id=1, source_target_pairs={{0,1},{1,0},{2,3},{3,2},{4,5},{5,4},{6,7},{7,6},{8,9},{9,8},{10,11... | collective-permute-start | bytes 1572872 | tf_op jit(solution)/shard_map/ppermute | solution.py:498
  9.4 0.7 collective-permute-start.3
  10.1 1.7 %collective-permute-start.6 = (bf16[256,3584]{1,0:T(8,128)(2,1)S(1)}, bf16[256,3584]{1,0:T(8,128)(2,1)S(1)}, u32[]{:S(2)}, u32[]{:S(2)}) collective-permute-start(bf16[256,3584]{1,0:T(8,128)(2,1)S(1)} %get-tuple-element.110), channel_id=1, source_target_pairs={{0,4},{1,5},{2,6},{3,7},{4,0},{5,1},{6,2},{7,3},{8,12},{9,13},{10,... | collective-permute-start | bytes 5505032 | tf_op jit(solution)/shard_map/ppermute | solution.py:498
  11.7 11.8 %collective-permute-done.refs_3_ = bf16[256,1536]{1,0:T(8,128)(2,1)S(1)} collective-permute-done((bf16[256,1536]{1,0:T(8,128)(2,1)S(1)}, bf16[256,1536]{1,0:T(8,128)(2,1)S(1)}, u32[]{:S(2)}, u32[]{:S(2)}) %collective-permute-start) | collective-permute-done | bytes 786464 | tf_op jit(solution)/shard_map/ppermute | solution.py:498
  24.1 1.4 %collective-permute-done.2.refs_3_ = bf16[256,1536]{1,0:T(8,128)(2,1)S(1)} collective-permute-done((bf16[256,1536]{1,0:T(8,128)(2,1)S(1)}, bf16[256,1536]{1,0:T(8,128)(2,1)S(1)}, u32[]{:S(2)}, u32[]{:S(2)}) %collective-permute-start.2) | collective-permute-done | bytes 786464 | tf_op jit(solution)/shard_map/ppermute | solution.py:498
  26.2 1.4 %collective-permute-start.8 = (bf16[512,512]{1,0:T(8,128)(2,1)S(1)}, bf16[512,512]{1,0:T(8,128)(2,1)S(1)}, u32[]{:S(2)}, u32[]{:S(2)}) collective-permute-start(bf16[512,512]{1,0:T(8,128)(2,1)S(1)} %get-tuple-element.114), channel_id=1, source_target_pairs={{0,1},{1,0},{2,3},{3,2},{4,5},{5,4},{6,7},{7,6},{8,9},{9,8},{10,11... | collective-permute-start | bytes 1572872 | tf_op jit(solution)/shard_map/ppermute | solution.py:498
  27.6 1.3 collective-permute-start.7
  29.5 0.6 keep_b1.1
  30.1 4.6 %collective-permute-done.1.refs_4_ = bf16[256,1024]{1,0:T(8,128)(2,1)S(1)} collective-permute-done((bf16[256,1024]{1,0:T(8,128)(2,1)S(1)}, bf16[256,1024]{1,0:T(8,128)(2,1)S(1)}, u32[]{:S(2)}, u32[]{:S(2)}) %collective-permute-start.1) | collective-permute-done | bytes 524320 | tf_op jit(solution)/shard_map/ppermute | solution.py:498
  35.4 1.5 %collective-permute-start.4 = (bf16[512,512]{1,0:T(8,128)(2,1)S(1)}, bf16[512,512]{1,0:T(8,128)(2,1)S(1)}, u32[]{:S(2)}, u32[]{:S(2)}) collective-permute-start(bf16[512,512]{1,0:T(8,128)(2,1)S(1)} %get-tuple-element.105), channel_id=1, source_target_pairs={{0,3},{1,2},{2,1},{3,0},{4,7},{5,6},{6,5},{7,4},{8,11},{9,10},{10,... | collective-permute-start | bytes 1572872 | tf_op jit(solution)/shard_map/ppermute | solution.py:498
  37.5 2.0 %collective-permute-start.5 = (bf16[512,512]{1,0:T(8,128)(2,1)S(1)}, bf16[512,512]{1,0:T(8,128)(2,1)S(1)}, u32[]{:S(2)}, u32[]{:S(2)}) collective-permute-start(bf16[512,512]{1,0:T(8,128)(2,1)S(1)} %get-tuple-element.108), channel_id=1, source_target_pairs={{0,1},{1,0},{2,3},{3,2},{4,5},{5,4},{6,7},{7,6},{8,9},{9,8},{10,11... | collective-permute-start | bytes 1572872 | tf_op jit(solution)/shard_map/ppermute | solution.py:498
  40.7 5.3 %collective-permute-done.8.refs_3_ = bf16[512,512]{1,0:T(8,128)(2,1)S(1)} collective-permute-done((bf16[512,512]{1,0:T(8,128)(2,1)S(1)}, bf16[512,512]{1,0:T(8,128)(2,1)S(1)}, u32[]{:S(2)}, u32[]{:S(2)}) %collective-permute-start.8) | collective-permute-done | bytes 524320 | tf_op jit(solution)/shard_map/ppermute | solution.py:498
  46.0 2.0 %collective-permute-done.7.refs_1_ = bf16[512,512]{1,0:T(8,128)(2,1)S(1)} collective-permute-done((bf16[512,512]{1,0:T(8,128)(2,1)S(1)}, bf16[512,512]{1,0:T(8,128)(2,1)S(1)}, u32[]{:S(2)}, u32[]{:S(2)}) %collective-permute-start.7) | collective-permute-done | bytes 524320 | tf_op jit(solution)/shard_map/ppermute | solution.py:498
  48.9 4.2 %collective-permute-done.6.refs_3_ = bf16[256,3584]{1,0:T(8,128)(2,1)S(1)} collective-permute-done((bf16[256,3584]{1,0:T(8,128)(2,1)S(1)}, bf16[256,3584]{1,0:T(8,128)(2,1)S(1)}, u32[]{:S(2)}, u32[]{:S(2)}) %collective-permute-start.6) | collective-permute-done | bytes 1835040 | tf_op jit(solution)/shard_map/ppermute | solution.py:498
  53.0 3.3 %other_1.1 = (bf16[2,256,1024]{2,1,0:T(8,128)(2,1)S(1)}, bf16[2,256,1024]{2,1,0:T(8,128)(2,1)S(1)}, bf16[256,1024]{1,0:T(8,128)(2,1)S(1)}, bf16[256,1024]{1,0:T(8,128)(2,1)S(1)}, bf16[8,128]{1,0:T(8,128)(2,1)}) custom-call(s32[1]{0:T(128)S(6)} %copy.15.refs_0_, bf16[2,256,8192]{2,1,0:T(8,128)(2,1)S(1)} %bitcast.4, ...), custom_call_target="tpu_custom_call" | custom-call | flops 20000000000 | tf_op jit(solution)/shard_map/other_1/pallas_call | solution.py:70
  56.3 1.1 collective-permute-start.12
  57.5 1.6 %collective-permute-start.13 = (bf16[2,256,1024]{2,1,0:T(8,128)(2,1)S(1)}, bf16[2,256,1024]{2,1,0:T(8,128)(2,1)S(1)}, u32[]{:S(2)}, u32[]{:S(2)}) collective-permute-start(bf16[2,256,1024]{2,1,0:T(8,128)(2,1)S(1)} %get-tuple-element.131), channel_id=1, source_target_pairs={{0,3},{1,2},{2,1},{3,0},{4,7},{5,6},{6,5},{7,4},{8,11},{9,10},{10,... | collective-permute-start | bytes 3145736 | tf_op jit(solution)/shard_map/ppermute | solution.py:498
  59.3 1.6 %take.1 = (bf16[16,2,32,512]{3,2,1,0:T(8,128)(2,1)S(1)}, bf16[16,2,32,512]{3,2,1,0:T(8,128)(2,1)S(1)}, bf16[8,128]{1,0:T(8,128)(2,1)}) custom-call(s32[1]{0:T(128)S(6)} %copy.15.refs_0_, bf16[2,16,2,32,512]{4,3,2,1,0:T(8,128)(2,1)} %bitcast.6, bf16[8,128]{1,0:T(8,128)(2,1)} %get-tuple-element.118.refs_2_), custom_call_target="tpu_custom_call" | custom-call | tf_op jit(solution)/shard_map/take/pallas_call | solution.py:70
  60.9 12.2 %collective-permute-done.9.refs_2_ = bf16[2,512,512]{2,1,0:T(8,128)(2,1)S(1)} collective-permute-done((bf16[2,512,512]{2,1,0:T(8,128)(2,1)S(1)}, bf16[2,512,512]{2,1,0:T(8,128)(2,1)S(1)}, u32[]{:S(2)}, u32[]{:S(2)}) %collective-permute-start.9) | collective-permute-done | bytes 1048608 | tf_op jit(solution)/shard_map/ppermute | solution.py:498
  73.1 0.7 inner_sync.1
  73.9 1.8 %collective-permute-start.16 = (bf16[256,1024]{1,0:T(8,128)(2,1)S(1)}, bf16[256,1024]{1,0:T(8,128)(2,1)S(1)}, u32[]{:S(2)}, u32[]{:S(2)}) collective-permute-start(bf16[256,1024]{1,0:T(8,128)(2,1)S(1)} %get-tuple-element.140), channel_id=1, source_target_pairs={{0,4},{1,5},{2,6},{3,7},{4,0},{5,1},{6,2},{7,3},{8,12},{9,13},{10,... | collective-permute-start | bytes 1572872 | tf_op jit(solution)/shard_map/ppermute | solution.py:498
  75.9 1.6 %collective-permute-start.11 = (bf16[2,4,32,512]{3,2,1,0:T(8,128)(2,1)S(1)}, bf16[2,4,32,512]{3,2,1,0:T(8,128)(2,1)S(1)}, u32[]{:S(2)}, u32[]{:S(2)}) collective-permute-start(bf16[2,4,32,512]{3,2,1,0:T(8,128)(2,1)S(1)} %get-tuple-element.127), channel_id=1, source_target_pairs={{0,64},{8,72},{16,80},{24,88},{32,96},{40,104},{48,112},{56,120},{... | collective-permute-start | bytes 786440 | tf_op jit(solution)/shard_map/ppermute | solution.py:498
  77.5 0.9 collective-permute-done.12.refs_1_.refs_2_
  78.3 0.8 collective-permute-done.13.refs_3_.refs_5_
  79.4 1.8 %collective-permute-start.17 = (bf16[256,1024]{1,0:T(8,128)(2,1)S(1)}, bf16[256,1024]{1,0:T(8,128)(2,1)S(1)}, u32[]{:S(2)}, u32[]{:S(2)}) collective-permute-start(bf16[256,1024]{1,0:T(8,128)(2,1)S(1)} %get-tuple-element.143), channel_id=1, source_target_pairs={{0,3},{1,2},{2,1},{3,0},{4,7},{5,6},{6,5},{7,4},{8,11},{9,10},{10,... | collective-permute-start | bytes 1572872 | tf_op jit(solution)/shard_map/ppermute | solution.py:498
  81.2 2.6 %collective-permute-start.18 = (bf16[256,1024]{1,0:T(8,128)(2,1)S(1)}, bf16[256,1024]{1,0:T(8,128)(2,1)S(1)}, u32[]{:S(2)}, u32[]{:S(2)}) collective-permute-start(bf16[256,1024]{1,0:T(8,128)(2,1)S(1)} %get-tuple-element.145), channel_id=1, source_target_pairs={{0,1},{1,0},{2,3},{3,2},{4,5},{5,4},{6,7},{7,6},{8,9},{9,8},{10,11... | collective-permute-start | bytes 1572872 | tf_op jit(solution)/shard_map/ppermute | solution.py:498
  84.4 2.8 %collective-permute-start.14 = (bf16[4,32,512]{2,1,0:T(8,128)(2,1)S(1)}, bf16[4,32,512]{2,1,0:T(8,128)(2,1)S(1)}, u32[]{:S(2)}, u32[]{:S(2)}) collective-permute-start(bf16[4,32,512]{2,1,0:T(8,128)(2,1)S(1)} %get-tuple-element.135), channel_id=1, source_target_pairs={{0,192},{8,200},{16,208},{24,216},{32,224},{40,232},{48,240},{56,2... | collective-permute-start | bytes 393224 | tf_op jit(solution)/shard_map/ppermute | solution.py:498
  87.2 3.4 %collective-permute-done.14.refs_1_ = bf16[4,32,512]{2,1,0:T(8,128)(2,1)S(1)} collective-permute-done((bf16[4,32,512]{2,1,0:T(8,128)(2,1)S(1)}, bf16[4,32,512]{2,1,0:T(8,128)(2,1)S(1)}, u32[]{:S(2)}, u32[]{:S(2)}) %collective-permute-start.14) | collective-permute-done | bytes 131104 | tf_op jit(solution)/shard_map/ppermute | solution.py:498
  90.7 3.4 %collective-permute-start.15 = (bf16[2,32,512]{2,1,0:T(8,128)(2,1)S(1)}, bf16[2,32,512]{2,1,0:T(8,128)(2,1)S(1)}, u32[]{:S(2)}, u32[]{:S(2)}) collective-permute-start(bf16[2,32,512]{2,1,0:T(8,128)(2,1)S(1)} %get-tuple-element.138), channel_id=1, source_target_pairs={{0,16},{8,24},{16,0},{24,8},{32,48},{40,56},{48,32},{56,40},{64,80... | collective-permute-start | bytes 196616 | tf_op jit(solution)/shard_map/ppermute | solution.py:498
  94.0 1.1 other_3.1
  95.2 0.9 inner_other.1
  96.3 6.0 %collective-permute-start.19 = (bf16[32,512]{1,0:T(8,128)(2,1)S(1)}, bf16[32,512]{1,0:T(8,128)(2,1)S(1)}, u32[]{:S(2)}, u32[]{:S(2)}) collective-permute-start(bf16[32,512]{1,0:T(8,128)(2,1)S(1)} %get-tuple-element.149), channel_id=1, source_target_pairs={{0,48},{8,56},{16,32},{24,40},{32,16},{40,24},{48,0},{56,8},{64,11... | collective-permute-start | bytes 98312 | tf_op jit(solution)/shard_map/ppermute | solution.py:498
  102.3 1.0 store.1
  104.2 0.9 outer_sync.1
  105.1 9.2 %all-to-all-start = ((bf16[16,32,512]{2,1,0:T(8,128)(2,1)}), bf16[16,32,512]{2,1,0:T(8,128)(2,1)S(1)}, u32[]{:S(2)}, u32[]{:S(2)}) async-start(bf16[16,32,512]{2,1,0:T(8,128)(2,1)} %get-tuple-element.155), calls=%async_computation | async-start | bytes 1048576 | tf_op jit(solution)/shard_map/all_to_all | solution.py:494
  114.4 3.2 %collective-permute-start.22 = (bf16[4,32,512]{2,1,0:T(8,128)(2,1)S(1)}, bf16[4,32,512]{2,1,0:T(8,128)(2,1)S(1)}, u32[]{:S(2)}, u32[]{:S(2)}) collective-permute-start(bf16[4,32,512]{2,1,0:T(8,128)(2,1)S(1)} %get-tuple-element.160), channel_id=1, source_target_pairs={{0,192},{8,200},{16,208},{24,216},{32,224},{40,232},{48,240},{56,2... | collective-permute-start | bytes 393224 | tf_op jit(solution)/shard_map/ppermute | solution.py:498
  117.6 5.1 %collective-permute-done.22.refs_1_ = bf16[4,32,512]{2,1,0:T(8,128)(2,1)S(1)} collective-permute-done((bf16[4,32,512]{2,1,0:T(8,128)(2,1)S(1)}, bf16[4,32,512]{2,1,0:T(8,128)(2,1)S(1)}, u32[]{:S(2)}, u32[]{:S(2)}) %collective-permute-start.22) | collective-permute-done | bytes 131104 | tf_op jit(solution)/shard_map/ppermute | solution.py:498
  122.7 1.7 %collective-permute-start.23 = (bf16[2,32,512]{2,1,0:T(8,128)(2,1)S(1)}, bf16[2,32,512]{2,1,0:T(8,128)(2,1)S(1)}, u32[]{:S(2)}, u32[]{:S(2)}) collective-permute-start(bf16[2,32,512]{2,1,0:T(8,128)(2,1)S(1)} %get-tuple-element.163), channel_id=1, source_target_pairs={{0,16},{8,24},{16,0},{24,8},{32,48},{40,56},{48,32},{56,40},{64,80... | collective-permute-start | bytes 196616 | tf_op jit(solution)/shard_map/ppermute | solution.py:498
  124.5 4.1 %collective-permute-done.23.refs_1_.refs_3_ = bf16[2,32,512]{2,1,0:T(8,128)(2,1)S(1)} collective-permute-done((bf16[2,32,512]{2,1,0:T(8,128)(2,1)S(1)}, bf16[2,32,512]{2,1,0:T(8,128)(2,1)S(1)}, u32[]{:S(2)}, u32[]{:S(2)}) %collective-permute-start.23) | collective-permute-done | bytes 65568 | tf_op jit(solution)/shard_map/ppermute | solution.py:498
  128.6 2.5 %collective-permute-start.25 = (bf16[32,512]{1,0:T(8,128)(2,1)S(1)}, bf16[32,512]{1,0:T(8,128)(2,1)S(1)}, u32[]{:S(2)}, u32[]{:S(2)}) collective-permute-start(bf16[32,512]{1,0:T(8,128)(2,1)S(1)} %get-tuple-element.171), channel_id=1, source_target_pairs={{0,48},{8,56},{16,32},{24,40},{32,16},{40,24},{48,0},{56,8},{64,11... | collective-permute-start | bytes 98312 | tf_op jit(solution)/shard_map/ppermute | solution.py:498
  131.5 1.0 mix_own.1
  132.5 2.2 %collective-permute-done.25.refs_3_ = bf16[32,512]{1,0:T(8,128)(2,1)S(1)} collective-permute-done((bf16[32,512]{1,0:T(8,128)(2,1)S(1)}, bf16[32,512]{1,0:T(8,128)(2,1)S(1)}, u32[]{:S(2)}, u32[]{:S(2)}) %collective-permute-start.25) | collective-permute-done | bytes 32800 | tf_op jit(solution)/shard_map/ppermute | solution.py:498
  134.7 0.6 outer_other.1
  135.4 1.0 mix_far.1
  (47 shorter events, 8.1 us)
Async XLA Ops:
  1.3 22.2 %slice-start = ((s8[8388608]{0:T(1024)(128)(4,1)}), s8[4194304]{0:T(1024)(128)(4,1)S(1)}, s32[]{:S(2)}) async-start(s8[8388608]{0:T(1024)(128)(4,1)} %bitcast.3), calls=%async_computation.1 | async-start | bytes 8388608
  2.8 20.7 %collective-permute-start = (bf16[256,1536]{1,0:T(8,128)(2,1)S(1)}, bf16[256,1536]{1,0:T(8,128)(2,1)S(1)}, u32[]{:S(2)}, u32[]{:S(2)}) collective-permute-start(bf16[256,1536]{1,0:T(8,128)(2,1)S(1)} %get-tuple-element.92), channel_id=1, source_target_pairs={{0,1},{1,0},{2,3},{3,2},{4,5},{5,4},{6,7},{7,6},{8,9},{9,8},{10,11... | collective-permute-start | bytes 2359304 | tf_op jit(solution)/shard_map/ppermute | solution.py:498
  5.1 20.5 %collective-permute-start.2 = (bf16[256,1536]{1,0:T(8,128)(2,1)S(1)}, bf16[256,1536]{1,0:T(8,128)(2,1)S(1)}, u32[]{:S(2)}, u32[]{:S(2)}) collective-permute-start(bf16[256,1536]{1,0:T(8,128)(2,1)S(1)} %get-tuple-element.95), channel_id=1, source_target_pairs={{0,3},{1,2},{2,1},{3,0},{4,7},{5,6},{6,5},{7,4},{8,11},{9,10},{10,... | collective-permute-start | bytes 2359304 | tf_op jit(solution)/shard_map/ppermute | solution.py:498
  5.7 17.8 %slice-start.1 = ((s8[8388608]{0:T(1024)(128)(4,1)}), s8[4194304]{0:T(1024)(128)(4,1)S(1)}, s32[]{:S(2)}) async-start(s8[8388608]{0:T(1024)(128)(4,1)} %bitcast.3), calls=%async_computation.2 | async-start | bytes 8388608
  7.9 26.8 %collective-permute-start.1 = (bf16[256,1024]{1,0:T(8,128)(2,1)S(1)}, bf16[256,1024]{1,0:T(8,128)(2,1)S(1)}, u32[]{:S(2)}, u32[]{:S(2)}) collective-permute-start(bf16[256,1024]{1,0:T(8,128)(2,1)S(1)} %get-tuple-element.94), channel_id=1, source_target_pairs={{0,1},{1,0},{2,3},{3,2},{4,5},{5,4},{6,7},{7,6},{8,9},{9,8},{10,11... | collective-permute-start | bytes 1572872 | tf_op jit(solution)/shard_map/ppermute | solution.py:498
  9.4 27.5 %collective-permute-start.3 = (bf16[256,1024]{1,0:T(8,128)(2,1)S(1)}, bf16[256,1024]{1,0:T(8,128)(2,1)S(1)}, u32[]{:S(2)}, u32[]{:S(2)}) collective-permute-start(bf16[256,1024]{1,0:T(8,128)(2,1)S(1)} %get-tuple-element.96), channel_id=1, source_target_pairs={{0,3},{1,2},{2,1},{3,0},{4,7},{5,6},{6,5},{7,4},{8,11},{9,10},{10,... | collective-permute-start | bytes 1572872 | tf_op jit(solution)/shard_map/ppermute | solution.py:498
  10.1 42.9 %collective-permute-start.6 = (bf16[256,3584]{1,0:T(8,128)(2,1)S(1)}, bf16[256,3584]{1,0:T(8,128)(2,1)S(1)}, u32[]{:S(2)}, u32[]{:S(2)}) collective-permute-start(bf16[256,3584]{1,0:T(8,128)(2,1)S(1)} %get-tuple-element.110), channel_id=1, source_target_pairs={{0,4},{1,5},{2,6},{3,7},{4,0},{5,1},{6,2},{7,3},{8,12},{9,13},{10,... | collective-permute-start | bytes 5505032 | tf_op jit(solution)/shard_map/ppermute | solution.py:498
  26.2 19.8 %collective-permute-start.8 = (bf16[512,512]{1,0:T(8,128)(2,1)S(1)}, bf16[512,512]{1,0:T(8,128)(2,1)S(1)}, u32[]{:S(2)}, u32[]{:S(2)}) collective-permute-start(bf16[512,512]{1,0:T(8,128)(2,1)S(1)} %get-tuple-element.114), channel_id=1, source_target_pairs={{0,1},{1,0},{2,3},{3,2},{4,5},{5,4},{6,7},{7,6},{8,9},{9,8},{10,11... | collective-permute-start | bytes 1572872 | tf_op jit(solution)/shard_map/ppermute | solution.py:498
  27.6 20.4 %collective-permute-start.7 = (bf16[512,512]{1,0:T(8,128)(2,1)S(1)}, bf16[512,512]{1,0:T(8,128)(2,1)S(1)}, u32[]{:S(2)}, u32[]{:S(2)}) collective-permute-start(bf16[512,512]{1,0:T(8,128)(2,1)S(1)} %get-tuple-element.112), channel_id=1, source_target_pairs={{0,3},{1,2},{2,1},{3,0},{4,7},{5,6},{6,5},{7,4},{8,11},{9,10},{10,... | collective-permute-start | bytes 1572872 | tf_op jit(solution)/shard_map/ppermute | solution.py:498
  35.4 23.7 %collective-permute-start.4 = (bf16[512,512]{1,0:T(8,128)(2,1)S(1)}, bf16[512,512]{1,0:T(8,128)(2,1)S(1)}, u32[]{:S(2)}, u32[]{:S(2)}) collective-permute-start(bf16[512,512]{1,0:T(8,128)(2,1)S(1)} %get-tuple-element.105), channel_id=1, source_target_pairs={{0,3},{1,2},{2,1},{3,0},{4,7},{5,6},{6,5},{7,4},{8,11},{9,10},{10,... | collective-permute-start | bytes 1572872 | tf_op jit(solution)/shard_map/ppermute | solution.py:498
  37.5 21.6 %collective-permute-start.5 = (bf16[512,512]{1,0:T(8,128)(2,1)S(1)}, bf16[512,512]{1,0:T(8,128)(2,1)S(1)}, u32[]{:S(2)}, u32[]{:S(2)}) collective-permute-start(bf16[512,512]{1,0:T(8,128)(2,1)S(1)} %get-tuple-element.108), channel_id=1, source_target_pairs={{0,1},{1,0},{2,3},{3,2},{4,5},{5,4},{6,7},{7,6},{8,9},{9,8},{10,11... | collective-permute-start | bytes 1572872 | tf_op jit(solution)/shard_map/ppermute | solution.py:498
  48.3 24.8 %collective-permute-start.9 = (bf16[2,512,512]{2,1,0:T(8,128)(2,1)S(1)}, bf16[2,512,512]{2,1,0:T(8,128)(2,1)S(1)}, u32[]{:S(2)}, u32[]{:S(2)}) collective-permute-start(bf16[2,512,512]{2,1,0:T(8,128)(2,1)S(1)} %get-tuple-element.121), channel_id=1, source_target_pairs={{0,4},{1,5},{2,6},{3,7},{4,0},{5,1},{6,2},{7,3},{8,12},{9,13},{10,... | collective-permute-start | bytes 3145736 | tf_op jit(solution)/shard_map/ppermute | solution.py:498
  56.3 22.0 %collective-permute-start.12 = (bf16[2,256,1024]{2,1,0:T(8,128)(2,1)S(1)}, bf16[2,256,1024]{2,1,0:T(8,128)(2,1)S(1)}, u32[]{:S(2)}, u32[]{:S(2)}) collective-permute-start(bf16[2,256,1024]{2,1,0:T(8,128)(2,1)S(1)} %get-tuple-element.129), channel_id=1, source_target_pairs={{0,1},{1,0},{2,3},{3,2},{4,5},{5,4},{6,7},{7,6},{8,9},{9,8},{10,11... | collective-permute-start | bytes 3145736 | tf_op jit(solution)/shard_map/ppermute | solution.py:498
  57.5 21.7 %collective-permute-start.13 = (bf16[2,256,1024]{2,1,0:T(8,128)(2,1)S(1)}, bf16[2,256,1024]{2,1,0:T(8,128)(2,1)S(1)}, u32[]{:S(2)}, u32[]{:S(2)}) collective-permute-start(bf16[2,256,1024]{2,1,0:T(8,128)(2,1)S(1)} %get-tuple-element.131), channel_id=1, source_target_pairs={{0,3},{1,2},{2,1},{3,0},{4,7},{5,6},{6,5},{7,4},{8,11},{9,10},{10,... | collective-permute-start | bytes 3145736 | tf_op jit(solution)/shard_map/ppermute | solution.py:498
  73.8 2.0 %collective-permute-start.10 = (bf16[16,32,512]{2,1,0:T(8,128)(2,1)S(1)}, bf16[16,32,512]{2,1,0:T(8,128)(2,1)S(1)}, u32[]{:S(2)}, u32[]{:S(2)}) collective-permute-start(bf16[16,32,512]{2,1,0:T(8,128)(2,1)S(1)} %get-tuple-element.124), channel_id=1, source_target_pairs={{0,8},{8,0},{16,24},{24,16},{32,40},{40,32},{48,56},{56,48},{64,72... | collective-permute-start | bytes 1572872 | tf_op jit(solution)/shard_map/ppermute | solution.py:498
  73.9 20.2 %collective-permute-start.16 = (bf16[256,1024]{1,0:T(8,128)(2,1)S(1)}, bf16[256,1024]{1,0:T(8,128)(2,1)S(1)}, u32[]{:S(2)}, u32[]{:S(2)}) collective-permute-start(bf16[256,1024]{1,0:T(8,128)(2,1)S(1)} %get-tuple-element.140), channel_id=1, source_target_pairs={{0,4},{1,5},{2,6},{3,7},{4,0},{5,1},{6,2},{7,3},{8,12},{9,13},{10,... | collective-permute-start | bytes 1572872 | tf_op jit(solution)/shard_map/ppermute | solution.py:498
  75.9 8.4 %collective-permute-start.11 = (bf16[2,4,32,512]{3,2,1,0:T(8,128)(2,1)S(1)}, bf16[2,4,32,512]{3,2,1,0:T(8,128)(2,1)S(1)}, u32[]{:S(2)}, u32[]{:S(2)}) collective-permute-start(bf16[2,4,32,512]{3,2,1,0:T(8,128)(2,1)S(1)} %get-tuple-element.127), channel_id=1, source_target_pairs={{0,64},{8,72},{16,80},{24,88},{32,96},{40,104},{48,112},{56,120},{... | collective-permute-start | bytes 786440 | tf_op jit(solution)/shard_map/ppermute | solution.py:498
  79.4 15.8 %collective-permute-start.17 = (bf16[256,1024]{1,0:T(8,128)(2,1)S(1)}, bf16[256,1024]{1,0:T(8,128)(2,1)S(1)}, u32[]{:S(2)}, u32[]{:S(2)}) collective-permute-start(bf16[256,1024]{1,0:T(8,128)(2,1)S(1)} %get-tuple-element.143), channel_id=1, source_target_pairs={{0,3},{1,2},{2,1},{3,0},{4,7},{5,6},{6,5},{7,4},{8,11},{9,10},{10,... | collective-permute-start | bytes 1572872 | tf_op jit(solution)/shard_map/ppermute | solution.py:498
  81.2 14.0 %collective-permute-start.18 = (bf16[256,1024]{1,0:T(8,128)(2,1)S(1)}, bf16[256,1024]{1,0:T(8,128)(2,1)S(1)}, u32[]{:S(2)}, u32[]{:S(2)}) collective-permute-start(bf16[256,1024]{1,0:T(8,128)(2,1)S(1)} %get-tuple-element.145), channel_id=1, source_target_pairs={{0,1},{1,0},{2,3},{3,2},{4,5},{5,4},{6,7},{7,6},{8,9},{9,8},{10,11... | collective-permute-start | bytes 1572872 | tf_op jit(solution)/shard_map/ppermute | solution.py:498
  84.4 6.3 %collective-permute-start.14 = (bf16[4,32,512]{2,1,0:T(8,128)(2,1)S(1)}, bf16[4,32,512]{2,1,0:T(8,128)(2,1)S(1)}, u32[]{:S(2)}, u32[]{:S(2)}) collective-permute-start(bf16[4,32,512]{2,1,0:T(8,128)(2,1)S(1)} %get-tuple-element.135), channel_id=1, source_target_pairs={{0,192},{8,200},{16,208},{24,216},{32,224},{40,232},{48,240},{56,2... | collective-permute-start | bytes 393224 | tf_op jit(solution)/shard_map/ppermute | solution.py:498
  90.7 5.6 %collective-permute-start.15 = (bf16[2,32,512]{2,1,0:T(8,128)(2,1)S(1)}, bf16[2,32,512]{2,1,0:T(8,128)(2,1)S(1)}, u32[]{:S(2)}, u32[]{:S(2)}) collective-permute-start(bf16[2,32,512]{2,1,0:T(8,128)(2,1)S(1)} %get-tuple-element.138), channel_id=1, source_target_pairs={{0,16},{8,24},{16,0},{24,8},{32,48},{40,56},{48,32},{56,40},{64,80... | collective-permute-start | bytes 196616 | tf_op jit(solution)/shard_map/ppermute | solution.py:498
  96.1 7.1 %collective-permute-start.20 = (bf16[16,32,512]{2,1,0:T(8,128)(2,1)S(1)}, bf16[16,32,512]{2,1,0:T(8,128)(2,1)S(1)}, u32[]{:S(2)}, u32[]{:S(2)}) collective-permute-start(bf16[16,32,512]{2,1,0:T(8,128)(2,1)S(1)} %get-tuple-element.151), channel_id=1, source_target_pairs={{0,8},{8,0},{16,24},{24,16},{32,40},{40,32},{48,56},{56,48},{64,72... | collective-permute-start | bytes 1572872 | tf_op jit(solution)/shard_map/ppermute | solution.py:498
  96.3 7.9 %copy-start = (f32[2,32,512]{2,1,0:T(8,128)S(1)}, f32[2,32,512]{2,1,0:T(8,128)}, u32[]{:S(2)}) copy-start(f32[2,32,512]{2,1,0:T(8,128)} %refs_1_.23) | copy-start | bytes 393220
  96.3 7.9 %copy-start.1 = (f32[32,512]{1,0:T(8,128)S(1)}, f32[32,512]{1,0:T(8,128)}, u32[]{:S(2)}) copy-start(f32[32,512]{1,0:T(8,128)} %refs_2_.5) | copy-start | bytes 196612
  96.3 7.9 %collective-permute-start.19 = (bf16[32,512]{1,0:T(8,128)(2,1)S(1)}, bf16[32,512]{1,0:T(8,128)(2,1)S(1)}, u32[]{:S(2)}, u32[]{:S(2)}) collective-permute-start(bf16[32,512]{1,0:T(8,128)(2,1)S(1)} %get-tuple-element.149), channel_id=1, source_target_pairs={{0,48},{8,56},{16,32},{24,40},{32,16},{40,24},{48,0},{56,8},{64,11... | collective-permute-start | bytes 98312 | tf_op jit(solution)/shard_map/ppermute | solution.py:498
  103.4 10.9 %collective-permute-start.21 = (bf16[2,4,32,512]{3,2,1,0:T(8,128)(2,1)S(1)}, bf16[2,4,32,512]{3,2,1,0:T(8,128)(2,1)S(1)}, u32[]{:S(2)}, u32[]{:S(2)}) collective-permute-start(bf16[2,4,32,512]{3,2,1,0:T(8,128)(2,1)S(1)} %get-tuple-element.157), channel_id=1, source_target_pairs={{0,64},{8,72},{16,80},{24,88},{32,96},{40,104},{48,112},{56,120},{... | collective-permute-start | bytes 786440 | tf_op jit(solution)/shard_map/ppermute | solution.py:498
  105.1 26.3 %all-to-all-start = ((bf16[16,32,512]{2,1,0:T(8,128)(2,1)}), bf16[16,32,512]{2,1,0:T(8,128)(2,1)S(1)}, u32[]{:S(2)}, u32[]{:S(2)}) async-start(bf16[16,32,512]{2,1,0:T(8,128)(2,1)} %get-tuple-element.155), calls=%async_computation | async-start | bytes 1048576 | tf_op jit(solution)/shard_map/all_to_all | solution.py:494
  114.4 8.3 %collective-permute-start.22 = (bf16[4,32,512]{2,1,0:T(8,128)(2,1)S(1)}, bf16[4,32,512]{2,1,0:T(8,128)(2,1)S(1)}, u32[]{:S(2)}, u32[]{:S(2)}) collective-permute-start(bf16[4,32,512]{2,1,0:T(8,128)(2,1)S(1)} %get-tuple-element.160), channel_id=1, source_target_pairs={{0,192},{8,200},{16,208},{24,216},{32,224},{40,232},{48,240},{56,2... | collective-permute-start | bytes 393224 | tf_op jit(solution)/shard_map/ppermute | solution.py:498
  122.7 5.9 %collective-permute-start.23 = (bf16[2,32,512]{2,1,0:T(8,128)(2,1)S(1)}, bf16[2,32,512]{2,1,0:T(8,128)(2,1)S(1)}, u32[]{:S(2)}, u32[]{:S(2)}) collective-permute-start(bf16[2,32,512]{2,1,0:T(8,128)(2,1)S(1)} %get-tuple-element.163), channel_id=1, source_target_pairs={{0,16},{8,24},{16,0},{24,8},{32,48},{40,56},{48,32},{56,40},{64,80... | collective-permute-start | bytes 196616 | tf_op jit(solution)/shard_map/ppermute | solution.py:498
  128.6 6.1 %collective-permute-start.25 = (bf16[32,512]{1,0:T(8,128)(2,1)S(1)}, bf16[32,512]{1,0:T(8,128)(2,1)S(1)}, u32[]{:S(2)}, u32[]{:S(2)}) collective-permute-start(bf16[32,512]{1,0:T(8,128)(2,1)S(1)} %get-tuple-element.171), channel_id=1, source_target_pairs={{0,48},{8,56},{16,32},{24,40},{32,16},{40,24},{48,0},{56,8},{64,11... | collective-permute-start | bytes 98312 | tf_op jit(solution)/shard_map/ppermute | solution.py:498
  131.4 4.0 %collective-permute-start.24 = (bf16[16,32,512]{2,1,0:T(8,128)(2,1)S(1)}, bf16[16,32,512]{2,1,0:T(8,128)(2,1)S(1)}, u32[]{:S(2)}, u32[]{:S(2)}) collective-permute-start(bf16[16,32,512]{2,1,0:T(8,128)(2,1)S(1)} %get-tuple-element.166.refs_2_), channel_id=1, source_target_pairs={{0,8},{8,0},{16,24},{24,16},{32,40},{40,32},{48,56},{56,48},{64,72... | collective-permute-start | bytes 1572872 | tf_op jit(solution)/shard_map/ppermute | solution.py:498

commit v11 on v10

--- a/solution.py
+++ b/solution.py
@@ -25,6 +25,7 @@
 MIB = 1024 * 1024
 BIG = 24
 LONG = 2 * 10**10
+MIDDLE = 125 * 10**8
 SHORT = 3 * 10**9
 
 
@@ -87,15 +88,11 @@
 
 def pack(name, fragment, plan, ids, x, g, outs, pieces, g_to):
     def kernel(plan_ref, ids_ref, x_ref, g_ref, *rest):
-        bufs, gt_ref = rest[: len(outs)], rest[len(outs)]
-        gin, tok, sems = rest[len(outs) + 1 :]
+        bufs = rest[: len(outs)]
+        sems = rest[-1]
         _, _, _, z, y = place()
         s = lax.rem(plan_ref[0], 2)
         layers = (s, 1 - s)
-        first = [
-            pltpu.make_async_copy(ids_ref, tok, sems.at[0]),
-            pltpu.make_async_copy(g_ref.at[layers[fragment]], gin, sems.at[1]),
-        ]
         copies = []
         for layer, start, width, out, at in pieces:
             col = pl.multiple_of(start(z, y), HALF)
@@ -106,29 +103,36 @@
                     sems.at[2 + len(copies)],
                 )
             )
-        for c in first + copies:
+        if fragment is not None:
+            gt_ref, gin, tok = rest[len(outs) : -1]
+            first = [
+                pltpu.make_async_copy(ids_ref, tok, sems.at[0]),
+                pltpu.make_async_copy(g_ref.at[layers[fragment]], gin, sems.at[1]),
+            ]
+            for c in first:
+                c.start()
+        for c in copies:
             c.start()
-        for c in first:
-            c.wait()
-        gt = (gin[...].astype(F32).T * (tok[...] != 0).astype(F32)).astype(BF16)
-        gt_ref[...] = gt
-        for out, at in g_to:
-            for h in range(2):
-                bufs[out][:, at + h * TOK : at + (h + 1) * TOK] = gt[h * TOK : (h + 1) * TOK]
+        if fragment is not None:
+            for c in first:
+                c.wait()
+            gt = (gin[...].astype(F32).T * (tok[...] != 0).astype(F32)).astype(BF16)
+            gt_ref[...] = gt
+            for out, at in g_to:
+                for h in range(2):
+                    bufs[out][:, at + h * TOK : at + (h + 1) * TOK] = gt[h * TOK : (h + 1) * TOK]
         for c in copies:
             c.wait()
 
-    return call(
-        kernel,
-        [in_vmem(TOK, n) for n in outs] + [in_vmem(KV, TOK)],
+    has = fragment is not None
+    return call(
+        kernel,
+        [in_vmem(TOK, n) for n in outs] + [in_vmem(KV, TOK)] * has,
         (plan, ids, x, g),
         [SM, HBM, HBM, HBM],
-        [VM] * (len(outs) + 1),
-        [
-            pltpu.VMEM((TOK, KV), BF16),
-            pltpu.VMEM((1, TOK), jnp.int32),
-            pltpu.SemaphoreType.DMA((2 + len(pieces),)),
-        ],
+        [VM] * (len(outs) + has),
+        [pltpu.VMEM((TOK, KV), BF16), pltpu.VMEM((1, TOK), jnp.int32)] * has
+        + [pltpu.SemaphoreType.DMA((2 + len(pieces),))],
         name=name,
         vmem=BIG,
     )
@@ -151,17 +155,10 @@
 
     wide, half = 2 * HALF + KV, 2 * HALF
     a1, b1, gt_s = pack("pack_1", 0, plan, ids, x, g, [wide, wide], pair(True, 0), [(0, half), (1, half)])
-    z1, a2, b2, z3, gt_o = pack(
-        "pack_2",
-        1,
-        plan,
-        ids,
-        x,
-        g,
-        [3 * ROWS + KV, half, half, ROWS],
-        [other(1, 0, 0), other(2, 0, 1), other(3, 0, 2), *pair(False, 1), other(0, 3, 0)],
-        [(0, 3 * ROWS)],
-    )
+    z1, gt_o = pack(
+        "pack_2", 1, plan, ids, x, g, [3 * ROWS + KV], [other(1, 0, 0), other(2, 0, 1), other(3, 0, 2)], [(0, 3 * ROWS)]
+    )
+    a2, b2, z3 = pack("pack_3", None, plan, ids, x, g, [half, half, ROWS], [*pair(False, 0), other(0, 2, 0)], [])
     return a1, b1, z1, a2, b2, z3, gt_s, gt_o
 
 
@@ -535,7 +532,7 @@
     near_a = swap(tile("send_a2", False, 3, 0, 1, (got_a1, got_a2)), "b")
     near_b = swap(tile("send_b2", False, 1, HALF, 1, (got_b1, got_b2)), "a")
     keep_a2 = tile("keep_a2", False, 0, 0, 0, (got_a1, got_a2))
-    keep_b2 = tile("keep_b2", False, 0, HALF, 0, (got_b1, got_b2), 2 * LONG)
+    keep_b2 = tile("keep_b2", False, 0, HALF, 0, (got_b1, got_b2), MIDDLE)
     across = swap(
         sums("far", [(2, KV, HALF)], [(keep_a1, far_a, None, None, 0, 0), (keep_b1, far_b, None, None, 0, 1)]), "z"
     )
@@ -562,9 +559,10 @@
     )
     last_0, last_1 = swap(last_0, "b"), swap(last_1, "a")
     send, keep = halve("sync_x3", QUAD, keep, recv)
-    send, keep = sum_z(keep, swap(send, "x3"), "sync_z1")
+    recv = swap(send, "x3")
+    mine_0, mine_1 = other("other_3", [dest(0, 1, 0, [(0, None, *lo), (1, None, *hi)])], [half, half], (got_z1, got_z3), SHORT)
+    send, keep = sum_z(keep, recv, "sync_z1")
     recv = swap(send, "z1")
-    mine_0, mine_1 = other("other_3", [dest(0, 1, 0, [(0, None, *lo), (1, None, *hi)])], [half, half], (got_z1, got_z3), SHORT)
     inner_o, send_o = inner_other(w_o, (mine_0, got_0, last_0), (mine_1, got_1, last_1))
     core_o = swap(send_o, "core")
     send, keep = halve("sync_z3", (32, KV), keep, recv, LONG)

time: 138 us -> 139 us (level)
  starting transfers between devices: 53.5 us -> 55.5 us
  waiting for transfers between devices: 59.3 us -> 57.8 us
    ppermute x26, starting transfers between devices: 44.3 us -> 46.9 us  [swap(): return lax.ppermute(value, *MOVES[move])]
    ppermute x26, waiting for transfers between devices: 59.1 us -> 57.5 us  [swap(): return lax.ppermute(value, *MOVES[move])]
    pallas_call x32 -> x33, Pallas kernels: 22 us -> 22.9 us  [call(): pl.pallas_call(chained, out_shape=outs + [in_hbm(8, 128)], in_specs=list(...]
  transfers between devices with their start and end apart: 27 -> 27, of which waited for: 17 -> 18; matrix products, arithmetic and copies ran while one was open for 0% -> 0% of each run, Pallas kernels for 14% -> 15%
where the time goes in v11:
time: 139 us; the launch traced here: 138 us
  waiting for transfers between devices  57.8 us (42%)
  starting transfers between devices  55.5 us (40%)
  Pallas kernels  22.9 us (16%)
  between operations  1.72 us (1%)
    ppermute x26, waiting for transfers between devices, swap(): return lax.ppermute(value, *MOVES[move])  57.5 us
    ppermute x26, starting transfers between devices, swap(): return lax.ppermute(value, *MOVES[move])  46.9 us
    pallas_call x33, Pallas kernels, call(): pl.pallas_call(chained, out_shape=outs + [in_hbm(8, 128)], in_specs=list(...  22.9 us
    all_to_all x1, starting transfers between devices, exchange(): lax.all_to_all(value, 'worker', 0, 0, axis_index_groups=PLANES, tiled=True)  8.6 us
  transfers between devices with their start and end apart: 27, of which 18 were waited for; matrix products, arithmetic and copies ran while one was open for 0% of the time, Pallas kernels for 15%

profile of v11, /device:TPU:8, one launch (start us, length us, event | category | flops | bytes accessed | tf_op | source)
XLA Modules:
  0.0 137.8 jit_solution(17853564321722485390)
XLA Ops:
  1.3 1.3 pack_1.1
  2.6 2.3 %collective-permute-start = (bf16[256,1536]{1,0:T(8,128)(2,1)S(1)}, bf16[256,1536]{1,0:T(8,128)(2,1)S(1)}, u32[]{:S(2)}, u32[]{:S(2)}) collective-permute-start(bf16[256,1536]{1,0:T(8,128)(2,1)S(1)} %get-tuple-element.93), channel_id=1, source_target_pairs={{0,1},{1,0},{2,3},{3,2},{4,5},{5,4},{6,7},{7,6},{8,9},{9,8},{10,11... | collective-permute-start | bytes 2359304 | tf_op jit(solution)/shard_map/ppermute | solution.py:495
  4.9 0.7 collective-permute-start.2
  5.6 1.6 %pack_2.1 = (bf16[256,3584]{1,0:T(8,128)(2,1)S(1)}, bf16[512,256]{1,0:T(8,128)(2,1)S(1)}, bf16[8,128]{1,0:T(8,128)(2,1)}) custom-call(s32[1]{0:T(128)S(6)} %copy.15.refs_0_, s32[1,256]{1,0:T(1,128)} %bitcast.8, bf16[2,256,8192]{2,1,0:T(8,128)(2,1)} %refs_1_.21, bf16[2,256,512]{2,1,0:T(8,128)(2,1)} %refs_3_.5, bf16[8,128]{1,0:T(8,128)(2,1)} %get-tuple-element.94.refs_4_), custom_call_target="tpu_custom_call" | custom-call | tf_op jit(solution)/shard_map/pack_2/pallas_call | solution.py:71
  7.2 2.0 %collective-permute-start.6 = (bf16[256,3584]{1,0:T(8,128)(2,1)S(1)}, bf16[256,3584]{1,0:T(8,128)(2,1)S(1)}, u32[]{:S(2)}, u32[]{:S(2)}) collective-permute-start(bf16[256,3584]{1,0:T(8,128)(2,1)S(1)} %get-tuple-element.112), channel_id=1, source_target_pairs={{0,4},{1,5},{2,6},{3,7},{4,0},{5,1},{6,2},{7,3},{8,12},{9,13},{10,... | collective-permute-start | bytes 5505032 | tf_op jit(solution)/shard_map/ppermute | solution.py:495
  9.2 1.6 %pack_3.1 = (bf16[256,1024]{1,0:T(8,128)(2,1)S(1)}, bf16[256,1024]{1,0:T(8,128)(2,1)S(1)}, bf16[256,1024]{1,0:T(8,128)(2,1)S(1)}, bf16[8,128]{1,0:T(8,128)(2,1)}) custom-call(s32[1]{0:T(128)S(6)} %copy.15.refs_0_, s32[1,256]{1,0:T(1,128)} %bitcast.9, bf16[2,256,8192]{2,1,0:T(8,128)(2,1)} %refs_1_.21, bf16[2,256,512]{2,1,0:T(8,128)(2,1)} %refs_3_.5, ...), custom_call_target="tpu_custom_call" | custom-call | tf_op jit(solution)/shard_map/pack_3/pallas_call | solution.py:71
  10.8 1.4 %collective-permute-start.1 = (bf16[256,1024]{1,0:T(8,128)(2,1)S(1)}, bf16[256,1024]{1,0:T(8,128)(2,1)S(1)}, u32[]{:S(2)}, u32[]{:S(2)}) collective-permute-start(bf16[256,1024]{1,0:T(8,128)(2,1)S(1)} %get-tuple-element.96), channel_id=1, source_target_pairs={{0,1},{1,0},{2,3},{3,2},{4,5},{5,4},{6,7},{7,6},{8,9},{9,8},{10,11... | collective-permute-start | bytes 1572872 | tf_op jit(solution)/shard_map/ppermute | solution.py:495
  12.7 10.6 %collective-permute-done.refs_3_ = bf16[256,1536]{1,0:T(8,128)(2,1)S(1)} collective-permute-done((bf16[256,1536]{1,0:T(8,128)(2,1)S(1)}, bf16[256,1536]{1,0:T(8,128)(2,1)S(1)}, u32[]{:S(2)}, u32[]{:S(2)}) %collective-permute-start) | collective-permute-done | bytes 786464 | tf_op jit(solution)/shard_map/ppermute | solution.py:495
  24.0 1.4 %collective-permute-done.2.refs_3_ = bf16[256,1536]{1,0:T(8,128)(2,1)S(1)} collective-permute-done((bf16[256,1536]{1,0:T(8,128)(2,1)S(1)}, bf16[256,1536]{1,0:T(8,128)(2,1)S(1)}, u32[]{:S(2)}, u32[]{:S(2)}) %collective-permute-start.2) | collective-permute-done | bytes 786464 | tf_op jit(solution)/shard_map/ppermute | solution.py:495
  26.0 1.4 %collective-permute-start.8 = (bf16[512,512]{1,0:T(8,128)(2,1)S(1)}, bf16[512,512]{1,0:T(8,128)(2,1)S(1)}, u32[]{:S(2)}, u32[]{:S(2)}) collective-permute-start(bf16[512,512]{1,0:T(8,128)(2,1)S(1)} %get-tuple-element.116), channel_id=1, source_target_pairs={{0,1},{1,0},{2,3},{3,2},{4,5},{5,4},{6,7},{7,6},{8,9},{9,8},{10,11... | collective-permute-start | bytes 1572872 | tf_op jit(solution)/shard_map/ppermute | solution.py:495
  27.4 1.3 collective-permute-start.7
  30.0 4.6 %collective-permute-done.1.refs_4_ = bf16[256,1024]{1,0:T(8,128)(2,1)S(1)} collective-permute-done((bf16[256,1024]{1,0:T(8,128)(2,1)S(1)}, bf16[256,1024]{1,0:T(8,128)(2,1)S(1)}, u32[]{:S(2)}, u32[]{:S(2)}) %collective-permute-start.1) | collective-permute-done | bytes 524320 | tf_op jit(solution)/shard_map/ppermute | solution.py:495
  35.2 1.5 %collective-permute-start.4 = (bf16[512,512]{1,0:T(8,128)(2,1)S(1)}, bf16[512,512]{1,0:T(8,128)(2,1)S(1)}, u32[]{:S(2)}, u32[]{:S(2)}) collective-permute-start(bf16[512,512]{1,0:T(8,128)(2,1)S(1)} %get-tuple-element.107), channel_id=1, source_target_pairs={{0,3},{1,2},{2,1},{3,0},{4,7},{5,6},{6,5},{7,4},{8,11},{9,10},{10,... | collective-permute-start | bytes 1572872 | tf_op jit(solution)/shard_map/ppermute | solution.py:495
  37.3 2.0 %collective-permute-start.5 = (bf16[512,512]{1,0:T(8,128)(2,1)S(1)}, bf16[512,512]{1,0:T(8,128)(2,1)S(1)}, u32[]{:S(2)}, u32[]{:S(2)}) collective-permute-start(bf16[512,512]{1,0:T(8,128)(2,1)S(1)} %get-tuple-element.110), channel_id=1, source_target_pairs={{0,1},{1,0},{2,3},{3,2},{4,5},{5,4},{6,7},{7,6},{8,9},{9,8},{10,11... | collective-permute-start | bytes 1572872 | tf_op jit(solution)/shard_map/ppermute | solution.py:495
  40.5 5.3 %collective-permute-done.8.refs_3_ = bf16[512,512]{1,0:T(8,128)(2,1)S(1)} collective-permute-done((bf16[512,512]{1,0:T(8,128)(2,1)S(1)}, bf16[512,512]{1,0:T(8,128)(2,1)S(1)}, u32[]{:S(2)}, u32[]{:S(2)}) %collective-permute-start.8) | collective-permute-done | bytes 524320 | tf_op jit(solution)/shard_map/ppermute | solution.py:495
  45.8 2.0 %collective-permute-done.7.refs_1_ = bf16[512,512]{1,0:T(8,128)(2,1)S(1)} collective-permute-done((bf16[512,512]{1,0:T(8,128)(2,1)S(1)}, bf16[512,512]{1,0:T(8,128)(2,1)S(1)}, u32[]{:S(2)}, u32[]{:S(2)}) %collective-permute-start.7) | collective-permute-done | bytes 524320 | tf_op jit(solution)/shard_map/ppermute | solution.py:495
  48.7 1.2 collective-permute-done.6.refs_3_
  49.9 3.3 %other_1.1 = (bf16[2,256,1024]{2,1,0:T(8,128)(2,1)S(1)}, bf16[2,256,1024]{2,1,0:T(8,128)(2,1)S(1)}, bf16[256,1024]{1,0:T(8,128)(2,1)S(1)}, bf16[256,1024]{1,0:T(8,128)(2,1)S(1)}, bf16[8,128]{1,0:T(8,128)(2,1)}) custom-call(s32[1]{0:T(128)S(6)} %copy.15.refs_0_, bf16[2,256,8192]{2,1,0:T(8,128)(2,1)S(1)} %bitcast.4, ...), custom_call_target="tpu_custom_call" | custom-call | flops 20000000000 | tf_op jit(solution)/shard_map/other_1/pallas_call | solution.py:71
  53.3 1.3 collective-permute-start.12
  54.5 1.6 %collective-permute-start.13 = (bf16[2,256,1024]{2,1,0:T(8,128)(2,1)S(1)}, bf16[2,256,1024]{2,1,0:T(8,128)(2,1)S(1)}, u32[]{:S(2)}, u32[]{:S(2)}) collective-permute-start(bf16[2,256,1024]{2,1,0:T(8,128)(2,1)S(1)} %get-tuple-element.133), channel_id=1, source_target_pairs={{0,3},{1,2},{2,1},{3,0},{4,7},{5,6},{6,5},{7,4},{8,11},{9,10},{10,... | collective-permute-start | bytes 3145736 | tf_op jit(solution)/shard_map/ppermute | solution.py:495
  56.1 2.6 %collective-permute-done.4.refs_1_ = bf16[512,512]{1,0:T(8,128)(2,1)S(1)} collective-permute-done((bf16[512,512]{1,0:T(8,128)(2,1)S(1)}, bf16[512,512]{1,0:T(8,128)(2,1)S(1)}, u32[]{:S(2)}, u32[]{:S(2)}) %collective-permute-start.4) | collective-permute-done | bytes 524320 | tf_op jit(solution)/shard_map/ppermute | solution.py:495
  59.0 1.6 %take.1 = (bf16[16,2,32,512]{3,2,1,0:T(8,128)(2,1)S(1)}, bf16[16,2,32,512]{3,2,1,0:T(8,128)(2,1)S(1)}, bf16[8,128]{1,0:T(8,128)(2,1)}) custom-call(s32[1]{0:T(128)S(6)} %copy.15.refs_0_, bf16[2,16,2,32,512]{4,3,2,1,0:T(8,128)(2,1)} %bitcast.6, bf16[8,128]{1,0:T(8,128)(2,1)} %get-tuple-element.120.refs_2_), custom_call_target="tpu_custom_call" | custom-call | tf_op jit(solution)/shard_map/take/pallas_call | solution.py:71
  60.5 10.6 %collective-permute-done.9.refs_2_ = bf16[2,512,512]{2,1,0:T(8,128)(2,1)S(1)} collective-permute-done((bf16[2,512,512]{2,1,0:T(8,128)(2,1)S(1)}, bf16[2,512,512]{2,1,0:T(8,128)(2,1)S(1)}, u32[]{:S(2)}, u32[]{:S(2)}) %collective-permute-start.9) | collective-permute-done | bytes 1048608 | tf_op jit(solution)/shard_map/ppermute | solution.py:495
  71.9 1.8 %collective-permute-start.15 = (bf16[256,1024]{1,0:T(8,128)(2,1)S(1)}, bf16[256,1024]{1,0:T(8,128)(2,1)S(1)}, u32[]{:S(2)}, u32[]{:S(2)}) collective-permute-start(bf16[256,1024]{1,0:T(8,128)(2,1)S(1)} %get-tuple-element.138), channel_id=1, source_target_pairs={{0,4},{1,5},{2,6},{3,7},{4,0},{5,1},{6,2},{7,3},{8,12},{9,13},{10,... | collective-permute-start | bytes 1572872 | tf_op jit(solution)/shard_map/ppermute | solution.py:495
  74.0 1.6 %collective-permute-start.11 = (bf16[2,4,32,512]{3,2,1,0:T(8,128)(2,1)S(1)}, bf16[2,4,32,512]{3,2,1,0:T(8,128)(2,1)S(1)}, u32[]{:S(2)}, u32[]{:S(2)}) collective-permute-start(bf16[2,4,32,512]{3,2,1,0:T(8,128)(2,1)S(1)} %get-tuple-element.129), channel_id=1, source_target_pairs={{0,64},{8,72},{16,80},{24,88},{32,96},{40,104},{48,112},{56,120},{... | collective-permute-start | bytes 786440 | tf_op jit(solution)/shard_map/ppermute | solution.py:495
  75.5 2.6 %collective-permute-done.12.refs_1_.refs_2_ = bf16[2,256,1024]{2,1,0:T(8,128)(2,1)S(1)} collective-permute-done((bf16[2,256,1024]{2,1,0:T(8,128)(2,1)S(1)}, bf16[2,256,1024]{2,1,0:T(8,128)(2,1)S(1)}, u32[]{:S(2)}, u32[]{:S(2)}) %collective-permute-start.12) | collective-permute-done | bytes 1048608 | tf_op jit(solution)/shard_map/ppermute | solution.py:495
  78.2 0.8 collective-permute-done.13.refs_3_.refs_5_
  79.3 1.8 %collective-permute-start.17 = (bf16[256,1024]{1,0:T(8,128)(2,1)S(1)}, bf16[256,1024]{1,0:T(8,128)(2,1)S(1)}, u32[]{:S(2)}, u32[]{:S(2)}) collective-permute-start(bf16[256,1024]{1,0:T(8,128)(2,1)S(1)} %get-tuple-element.145), channel_id=1, source_target_pairs={{0,3},{1,2},{2,1},{3,0},{4,7},{5,6},{6,5},{7,4},{8,11},{9,10},{10,... | collective-permute-start | bytes 1572872 | tf_op jit(solution)/shard_map/ppermute | solution.py:495
  81.1 2.6 %collective-permute-start.18 = (bf16[256,1024]{1,0:T(8,128)(2,1)S(1)}, bf16[256,1024]{1,0:T(8,128)(2,1)S(1)}, u32[]{:S(2)}, u32[]{:S(2)}) collective-permute-start(bf16[256,1024]{1,0:T(8,128)(2,1)S(1)} %get-tuple-element.147), channel_id=1, source_target_pairs={{0,1},{1,0},{2,3},{3,2},{4,5},{5,4},{6,7},{7,6},{8,9},{9,8},{10,11... | collective-permute-start | bytes 1572872 | tf_op jit(solution)/shard_map/ppermute | solution.py:495
  83.7 2.8 %collective-permute-start.14 = (bf16[4,32,512]{2,1,0:T(8,128)(2,1)S(1)}, bf16[4,32,512]{2,1,0:T(8,128)(2,1)S(1)}, u32[]{:S(2)}, u32[]{:S(2)}) collective-permute-start(bf16[4,32,512]{2,1,0:T(8,128)(2,1)S(1)} %get-tuple-element.137), channel_id=1, source_target_pairs={{0,192},{8,200},{16,208},{24,216},{32,224},{40,232},{48,240},{56,2... | collective-permute-start | bytes 393224 | tf_op jit(solution)/shard_map/ppermute | solution.py:495
  86.6 1.1 other_3.1
  87.7 2.3 %collective-permute-done.14.refs_1_ = bf16[4,32,512]{2,1,0:T(8,128)(2,1)S(1)} collective-permute-done((bf16[4,32,512]{2,1,0:T(8,128)(2,1)S(1)}, bf16[4,32,512]{2,1,0:T(8,128)(2,1)S(1)}, u32[]{:S(2)}, u32[]{:S(2)}) %collective-permute-start.14) | collective-permute-done | bytes 131104 | tf_op jit(solution)/shard_map/ppermute | solution.py:495
  90.0 3.4 %collective-permute-start.16 = (bf16[2,32,512]{2,1,0:T(8,128)(2,1)S(1)}, bf16[2,32,512]{2,1,0:T(8,128)(2,1)S(1)}, u32[]{:S(2)}, u32[]{:S(2)}) collective-permute-start(bf16[2,32,512]{2,1,0:T(8,128)(2,1)S(1)} %get-tuple-element.142), channel_id=1, source_target_pairs={{0,16},{8,24},{16,0},{24,8},{32,48},{40,56},{48,32},{56,40},{64,80... | collective-permute-start | bytes 196616 | tf_op jit(solution)/shard_map/ppermute | solution.py:495
  93.4 0.7 collective-permute-done.18.refs_6_
  94.1 0.9 inner_other.1
  95.7 6.1 %collective-permute-start.19 = (bf16[32,512]{1,0:T(8,128)(2,1)S(1)}, bf16[32,512]{1,0:T(8,128)(2,1)S(1)}, u32[]{:S(2)}, u32[]{:S(2)}) collective-permute-start(bf16[32,512]{1,0:T(8,128)(2,1)S(1)} %get-tuple-element.151), channel_id=1, source_target_pairs={{0,48},{8,56},{16,32},{24,40},{32,16},{40,24},{48,0},{56,8},{64,11... | collective-permute-start | bytes 98312 | tf_op jit(solution)/shard_map/ppermute | solution.py:495
  101.8 1.0 store.1
  102.9 1.3 collective-permute-start.21
  104.3 0.9 outer_sync.1
  105.2 8.6 %all-to-all-start = ((bf16[16,32,512]{2,1,0:T(8,128)(2,1)}), bf16[16,32,512]{2,1,0:T(8,128)(2,1)S(1)}, u32[]{:S(2)}, u32[]{:S(2)}) async-start(bf16[16,32,512]{2,1,0:T(8,128)(2,1)} %get-tuple-element.157), calls=%async_computation | async-start | bytes 1048576 | tf_op jit(solution)/shard_map/all_to_all | solution.py:491
  113.9 3.2 %collective-permute-start.22 = (bf16[4,32,512]{2,1,0:T(8,128)(2,1)S(1)}, bf16[4,32,512]{2,1,0:T(8,128)(2,1)S(1)}, u32[]{:S(2)}, u32[]{:S(2)}) collective-permute-start(bf16[4,32,512]{2,1,0:T(8,128)(2,1)S(1)} %get-tuple-element.162), channel_id=1, source_target_pairs={{0,192},{8,200},{16,208},{24,216},{32,224},{40,232},{48,240},{56,2... | collective-permute-start | bytes 393224 | tf_op jit(solution)/shard_map/ppermute | solution.py:495
  117.1 4.4 %collective-permute-done.22.refs_1_ = bf16[4,32,512]{2,1,0:T(8,128)(2,1)S(1)} collective-permute-done((bf16[4,32,512]{2,1,0:T(8,128)(2,1)S(1)}, bf16[4,32,512]{2,1,0:T(8,128)(2,1)S(1)}, u32[]{:S(2)}, u32[]{:S(2)}) %collective-permute-start.22) | collective-permute-done | bytes 131104 | tf_op jit(solution)/shard_map/ppermute | solution.py:495
  121.6 3.1 %collective-permute-start.23 = (bf16[2,32,512]{2,1,0:T(8,128)(2,1)S(1)}, bf16[2,32,512]{2,1,0:T(8,128)(2,1)S(1)}, u32[]{:S(2)}, u32[]{:S(2)}) collective-permute-start(bf16[2,32,512]{2,1,0:T(8,128)(2,1)S(1)} %get-tuple-element.165), channel_id=1, source_target_pairs={{0,16},{8,24},{16,0},{24,8},{32,48},{40,56},{48,32},{56,40},{64,80... | collective-permute-start | bytes 196616 | tf_op jit(solution)/shard_map/ppermute | solution.py:495
  124.7 5.2 %collective-permute-done.23.refs_1_.refs_3_ = bf16[2,32,512]{2,1,0:T(8,128)(2,1)S(1)} collective-permute-done((bf16[2,32,512]{2,1,0:T(8,128)(2,1)S(1)}, bf16[2,32,512]{2,1,0:T(8,128)(2,1)S(1)}, u32[]{:S(2)}, u32[]{:S(2)}) %collective-permute-start.23) | collective-permute-done | bytes 65568 | tf_op jit(solution)/shard_map/ppermute | solution.py:495
  129.9 2.3 %collective-permute-start.25 = (bf16[32,512]{1,0:T(8,128)(2,1)S(1)}, bf16[32,512]{1,0:T(8,128)(2,1)S(1)}, u32[]{:S(2)}, u32[]{:S(2)}) collective-permute-start(bf16[32,512]{1,0:T(8,128)(2,1)S(1)} %get-tuple-element.173), channel_id=1, source_target_pairs={{0,48},{8,56},{16,32},{24,40},{32,16},{40,24},{48,0},{56,8},{64,11... | collective-permute-start | bytes 98312 | tf_op jit(solution)/shard_map/ppermute | solution.py:495
  132.6 1.0 mix_own.1
  133.6 2.4 %collective-permute-done.25.refs_3_ = bf16[32,512]{1,0:T(8,128)(2,1)S(1)} collective-permute-done((bf16[32,512]{1,0:T(8,128)(2,1)S(1)}, bf16[32,512]{1,0:T(8,128)(2,1)S(1)}, u32[]{:S(2)}, u32[]{:S(2)}) %collective-permute-start.25) | collective-permute-done | bytes 32800 | tf_op jit(solution)/shard_map/ppermute | solution.py:495
  136.7 1.0 mix_far.1
  (48 shorter events, 9.7 us)
Async XLA Ops:
  2.6 20.7 %collective-permute-start = (bf16[256,1536]{1,0:T(8,128)(2,1)S(1)}, bf16[256,1536]{1,0:T(8,128)(2,1)S(1)}, u32[]{:S(2)}, u32[]{:S(2)}) collective-permute-start(bf16[256,1536]{1,0:T(8,128)(2,1)S(1)} %get-tuple-element.93), channel_id=1, source_target_pairs={{0,1},{1,0},{2,3},{3,2},{4,5},{5,4},{6,7},{7,6},{8,9},{9,8},{10,11... | collective-permute-start | bytes 2359304 | tf_op jit(solution)/shard_map/ppermute | solution.py:495
  4.9 20.5 %collective-permute-start.2 = (bf16[256,1536]{1,0:T(8,128)(2,1)S(1)}, bf16[256,1536]{1,0:T(8,128)(2,1)S(1)}, u32[]{:S(2)}, u32[]{:S(2)}) collective-permute-start(bf16[256,1536]{1,0:T(8,128)(2,1)S(1)} %get-tuple-element.97), channel_id=1, source_target_pairs={{0,3},{1,2},{2,1},{3,0},{4,7},{5,6},{6,5},{7,4},{8,11},{9,10},{10,... | collective-permute-start | bytes 2359304 | tf_op jit(solution)/shard_map/ppermute | solution.py:495
  5.6 17.8 %slice-start = ((s8[8388608]{0:T(1024)(128)(4,1)}), s8[4194304]{0:T(1024)(128)(4,1)S(1)}, s32[]{:S(2)}) async-start(s8[8388608]{0:T(1024)(128)(4,1)} %bitcast.3), calls=%async_computation.1 | async-start | bytes 8388608
  7.2 42.7 %collective-permute-start.6 = (bf16[256,3584]{1,0:T(8,128)(2,1)S(1)}, bf16[256,3584]{1,0:T(8,128)(2,1)S(1)}, u32[]{:S(2)}, u32[]{:S(2)}) collective-permute-start(bf16[256,3584]{1,0:T(8,128)(2,1)S(1)} %get-tuple-element.112), channel_id=1, source_target_pairs={{0,4},{1,5},{2,6},{3,7},{4,0},{5,1},{6,2},{7,3},{8,12},{9,13},{10,... | collective-permute-start | bytes 5505032 | tf_op jit(solution)/shard_map/ppermute | solution.py:495
  9.2 14.1 %slice-start.1 = ((s8[8388608]{0:T(1024)(128)(4,1)}), s8[4194304]{0:T(1024)(128)(4,1)S(1)}, s32[]{:S(2)}) async-start(s8[8388608]{0:T(1024)(128)(4,1)} %bitcast.3), calls=%async_computation.2 | async-start | bytes 8388608
  10.8 23.7 %collective-permute-start.1 = (bf16[256,1024]{1,0:T(8,128)(2,1)S(1)}, bf16[256,1024]{1,0:T(8,128)(2,1)S(1)}, u32[]{:S(2)}, u32[]{:S(2)}) collective-permute-start(bf16[256,1024]{1,0:T(8,128)(2,1)S(1)} %get-tuple-element.96), channel_id=1, source_target_pairs={{0,1},{1,0},{2,3},{3,2},{4,5},{5,4},{6,7},{7,6},{8,9},{9,8},{10,11... | collective-permute-start | bytes 1572872 | tf_op jit(solution)/shard_map/ppermute | solution.py:495
  12.3 24.4 %collective-permute-start.3 = (bf16[256,1024]{1,0:T(8,128)(2,1)S(1)}, bf16[256,1024]{1,0:T(8,128)(2,1)S(1)}, u32[]{:S(2)}, u32[]{:S(2)}) collective-permute-start(bf16[256,1024]{1,0:T(8,128)(2,1)S(1)} %get-tuple-element.98), channel_id=1, source_target_pairs={{0,3},{1,2},{2,1},{3,0},{4,7},{5,6},{6,5},{7,4},{8,11},{9,10},{10,... | collective-permute-start | bytes 1572872 | tf_op jit(solution)/shard_map/ppermute | solution.py:495
  26.0 19.8 %collective-permute-start.8 = (bf16[512,512]{1,0:T(8,128)(2,1)S(1)}, bf16[512,512]{1,0:T(8,128)(2,1)S(1)}, u32[]{:S(2)}, u32[]{:S(2)}) collective-permute-start(bf16[512,512]{1,0:T(8,128)(2,1)S(1)} %get-tuple-element.116), channel_id=1, source_target_pairs={{0,1},{1,0},{2,3},{3,2},{4,5},{5,4},{6,7},{7,6},{8,9},{9,8},{10,11... | collective-permute-start | bytes 1572872 | tf_op jit(solution)/shard_map/ppermute | solution.py:495
  27.4 20.4 %collective-permute-start.7 = (bf16[512,512]{1,0:T(8,128)(2,1)S(1)}, bf16[512,512]{1,0:T(8,128)(2,1)S(1)}, u32[]{:S(2)}, u32[]{:S(2)}) collective-permute-start(bf16[512,512]{1,0:T(8,128)(2,1)S(1)} %get-tuple-element.114), channel_id=1, source_target_pairs={{0,3},{1,2},{2,1},{3,0},{4,7},{5,6},{6,5},{7,4},{8,11},{9,10},{10,... | collective-permute-start | bytes 1572872 | tf_op jit(solution)/shard_map/ppermute | solution.py:495
  35.2 23.5 %collective-permute-start.4 = (bf16[512,512]{1,0:T(8,128)(2,1)S(1)}, bf16[512,512]{1,0:T(8,128)(2,1)S(1)}, u32[]{:S(2)}, u32[]{:S(2)}) collective-permute-start(bf16[512,512]{1,0:T(8,128)(2,1)S(1)} %get-tuple-element.107), channel_id=1, source_target_pairs={{0,3},{1,2},{2,1},{3,0},{4,7},{5,6},{6,5},{7,4},{8,11},{9,10},{10,... | collective-permute-start | bytes 1572872 | tf_op jit(solution)/shard_map/ppermute | solution.py:495
  37.3 21.4 %collective-permute-start.5 = (bf16[512,512]{1,0:T(8,128)(2,1)S(1)}, bf16[512,512]{1,0:T(8,128)(2,1)S(1)}, u32[]{:S(2)}, u32[]{:S(2)}) collective-permute-start(bf16[512,512]{1,0:T(8,128)(2,1)S(1)} %get-tuple-element.110), channel_id=1, source_target_pairs={{0,1},{1,0},{2,3},{3,2},{4,5},{5,4},{6,7},{7,6},{8,9},{9,8},{10,11... | collective-permute-start | bytes 1572872 | tf_op jit(solution)/shard_map/ppermute | solution.py:495
  48.1 23.1 %collective-permute-start.9 = (bf16[2,512,512]{2,1,0:T(8,128)(2,1)S(1)}, bf16[2,512,512]{2,1,0:T(8,128)(2,1)S(1)}, u32[]{:S(2)}, u32[]{:S(2)}) collective-permute-start(bf16[2,512,512]{2,1,0:T(8,128)(2,1)S(1)} %get-tuple-element.123), channel_id=1, source_target_pairs={{0,4},{1,5},{2,6},{3,7},{4,0},{5,1},{6,2},{7,3},{8,12},{9,13},{10,... | collective-permute-start | bytes 3145736 | tf_op jit(solution)/shard_map/ppermute | solution.py:495
  53.3 24.9 %collective-permute-start.12 = (bf16[2,256,1024]{2,1,0:T(8,128)(2,1)S(1)}, bf16[2,256,1024]{2,1,0:T(8,128)(2,1)S(1)}, u32[]{:S(2)}, u32[]{:S(2)}) collective-permute-start(bf16[2,256,1024]{2,1,0:T(8,128)(2,1)S(1)} %get-tuple-element.131), channel_id=1, source_target_pairs={{0,1},{1,0},{2,3},{3,2},{4,5},{5,4},{6,7},{7,6},{8,9},{9,8},{10,11... | collective-permute-start | bytes 3145736 | tf_op jit(solution)/shard_map/ppermute | solution.py:495
  54.5 24.5 %collective-permute-start.13 = (bf16[2,256,1024]{2,1,0:T(8,128)(2,1)S(1)}, bf16[2,256,1024]{2,1,0:T(8,128)(2,1)S(1)}, u32[]{:S(2)}, u32[]{:S(2)}) collective-permute-start(bf16[2,256,1024]{2,1,0:T(8,128)(2,1)S(1)} %get-tuple-element.133), channel_id=1, source_target_pairs={{0,3},{1,2},{2,1},{3,0},{4,7},{5,6},{6,5},{7,4},{8,11},{9,10},{10,... | collective-permute-start | bytes 3145736 | tf_op jit(solution)/shard_map/ppermute | solution.py:495
  71.8 2.0 %collective-permute-start.10 = (bf16[16,32,512]{2,1,0:T(8,128)(2,1)S(1)}, bf16[16,32,512]{2,1,0:T(8,128)(2,1)S(1)}, u32[]{:S(2)}, u32[]{:S(2)}) collective-permute-start(bf16[16,32,512]{2,1,0:T(8,128)(2,1)S(1)} %get-tuple-element.126), channel_id=1, source_target_pairs={{0,8},{8,0},{16,24},{24,16},{32,40},{40,32},{48,56},{56,48},{64,72... | collective-permute-start | bytes 1572872 | tf_op jit(solution)/shard_map/ppermute | solution.py:495
  71.9 14.6 %collective-permute-start.15 = (bf16[256,1024]{1,0:T(8,128)(2,1)S(1)}, bf16[256,1024]{1,0:T(8,128)(2,1)S(1)}, u32[]{:S(2)}, u32[]{:S(2)}) collective-permute-start(bf16[256,1024]{1,0:T(8,128)(2,1)S(1)} %get-tuple-element.138), channel_id=1, source_target_pairs={{0,4},{1,5},{2,6},{3,7},{4,0},{5,1},{6,2},{7,3},{8,12},{9,13},{10,... | collective-permute-start | bytes 1572872 | tf_op jit(solution)/shard_map/ppermute | solution.py:495
  74.0 9.7 %collective-permute-start.11 = (bf16[2,4,32,512]{3,2,1,0:T(8,128)(2,1)S(1)}, bf16[2,4,32,512]{3,2,1,0:T(8,128)(2,1)S(1)}, u32[]{:S(2)}, u32[]{:S(2)}) collective-permute-start(bf16[2,4,32,512]{3,2,1,0:T(8,128)(2,1)S(1)} %get-tuple-element.129), channel_id=1, source_target_pairs={{0,64},{8,72},{16,80},{24,88},{32,96},{40,104},{48,112},{56,120},{... | collective-permute-start | bytes 786440 | tf_op jit(solution)/shard_map/ppermute | solution.py:495
  79.3 14.1 %collective-permute-start.17 = (bf16[256,1024]{1,0:T(8,128)(2,1)S(1)}, bf16[256,1024]{1,0:T(8,128)(2,1)S(1)}, u32[]{:S(2)}, u32[]{:S(2)}) collective-permute-start(bf16[256,1024]{1,0:T(8,128)(2,1)S(1)} %get-tuple-element.145), channel_id=1, source_target_pairs={{0,3},{1,2},{2,1},{3,0},{4,7},{5,6},{6,5},{7,4},{8,11},{9,10},{10,... | collective-permute-start | bytes 1572872 | tf_op jit(solution)/shard_map/ppermute | solution.py:495
  81.1 13.0 %collective-permute-start.18 = (bf16[256,1024]{1,0:T(8,128)(2,1)S(1)}, bf16[256,1024]{1,0:T(8,128)(2,1)S(1)}, u32[]{:S(2)}, u32[]{:S(2)}) collective-permute-start(bf16[256,1024]{1,0:T(8,128)(2,1)S(1)} %get-tuple-element.147), channel_id=1, source_target_pairs={{0,1},{1,0},{2,3},{3,2},{4,5},{5,4},{6,7},{7,6},{8,9},{9,8},{10,11... | collective-permute-start | bytes 1572872 | tf_op jit(solution)/shard_map/ppermute | solution.py:495
  83.7 6.3 %collective-permute-start.14 = (bf16[4,32,512]{2,1,0:T(8,128)(2,1)S(1)}, bf16[4,32,512]{2,1,0:T(8,128)(2,1)S(1)}, u32[]{:S(2)}, u32[]{:S(2)}) collective-permute-start(bf16[4,32,512]{2,1,0:T(8,128)(2,1)S(1)} %get-tuple-element.137), channel_id=1, source_target_pairs={{0,192},{8,200},{16,208},{24,216},{32,224},{40,232},{48,240},{56,2... | collective-permute-start | bytes 393224 | tf_op jit(solution)/shard_map/ppermute | solution.py:495
  90.0 5.6 %collective-permute-start.16 = (bf16[2,32,512]{2,1,0:T(8,128)(2,1)S(1)}, bf16[2,32,512]{2,1,0:T(8,128)(2,1)S(1)}, u32[]{:S(2)}, u32[]{:S(2)}) collective-permute-start(bf16[2,32,512]{2,1,0:T(8,128)(2,1)S(1)} %get-tuple-element.142), channel_id=1, source_target_pairs={{0,16},{8,24},{16,0},{24,8},{32,48},{40,56},{48,32},{56,40},{64,80... | collective-permute-start | bytes 196616 | tf_op jit(solution)/shard_map/ppermute | solution.py:495
  95.0 7.8 %collective-permute-start.20 = (bf16[16,32,512]{2,1,0:T(8,128)(2,1)S(1)}, bf16[16,32,512]{2,1,0:T(8,128)(2,1)S(1)}, u32[]{:S(2)}, u32[]{:S(2)}) collective-permute-start(bf16[16,32,512]{2,1,0:T(8,128)(2,1)S(1)} %get-tuple-element.153), channel_id=1, source_target_pairs={{0,8},{8,0},{16,24},{24,16},{32,40},{40,32},{48,56},{56,48},{64,72... | collective-permute-start | bytes 1572872 | tf_op jit(solution)/shard_map/ppermute | solution.py:495
  95.6 8.6 %copy-start = (f32[2,32,512]{2,1,0:T(8,128)S(1)}, f32[2,32,512]{2,1,0:T(8,128)}, u32[]{:S(2)}) copy-start(f32[2,32,512]{2,1,0:T(8,128)} %refs_1_.23) | copy-start | bytes 393220
  95.7 8.6 %copy-start.1 = (f32[32,512]{1,0:T(8,128)S(1)}, f32[32,512]{1,0:T(8,128)}, u32[]{:S(2)}) copy-start(f32[32,512]{1,0:T(8,128)} %refs_2_.7) | copy-start | bytes 196612
  95.7 8.6 %collective-permute-start.19 = (bf16[32,512]{1,0:T(8,128)(2,1)S(1)}, bf16[32,512]{1,0:T(8,128)(2,1)S(1)}, u32[]{:S(2)}, u32[]{:S(2)}) collective-permute-start(bf16[32,512]{1,0:T(8,128)(2,1)S(1)} %get-tuple-element.151), channel_id=1, source_target_pairs={{0,48},{8,56},{16,32},{24,40},{32,16},{40,24},{48,0},{56,8},{64,11... | collective-permute-start | bytes 98312 | tf_op jit(solution)/shard_map/ppermute | solution.py:495
  102.9 10.9 %collective-permute-start.21 = (bf16[2,4,32,512]{3,2,1,0:T(8,128)(2,1)S(1)}, bf16[2,4,32,512]{3,2,1,0:T(8,128)(2,1)S(1)}, u32[]{:S(2)}, u32[]{:S(2)}) collective-permute-start(bf16[2,4,32,512]{3,2,1,0:T(8,128)(2,1)S(1)} %get-tuple-element.159), channel_id=1, source_target_pairs={{0,64},{8,72},{16,80},{24,88},{32,96},{40,104},{48,112},{56,120},{... | collective-permute-start | bytes 786440 | tf_op jit(solution)/shard_map/ppermute | solution.py:495
  105.2 27.3 %all-to-all-start = ((bf16[16,32,512]{2,1,0:T(8,128)(2,1)}), bf16[16,32,512]{2,1,0:T(8,128)(2,1)S(1)}, u32[]{:S(2)}, u32[]{:S(2)}) async-start(bf16[16,32,512]{2,1,0:T(8,128)(2,1)} %get-tuple-element.157), calls=%async_computation | async-start | bytes 1048576 | tf_op jit(solution)/shard_map/all_to_all | solution.py:491
  113.9 7.7 %collective-permute-start.22 = (bf16[4,32,512]{2,1,0:T(8,128)(2,1)S(1)}, bf16[4,32,512]{2,1,0:T(8,128)(2,1)S(1)}, u32[]{:S(2)}, u32[]{:S(2)}) collective-permute-start(bf16[4,32,512]{2,1,0:T(8,128)(2,1)S(1)} %get-tuple-element.162), channel_id=1, source_target_pairs={{0,192},{8,200},{16,208},{24,216},{32,224},{40,232},{48,240},{56,2... | collective-permute-start | bytes 393224 | tf_op jit(solution)/shard_map/ppermute | solution.py:495
  121.6 8.3 %collective-permute-start.23 = (bf16[2,32,512]{2,1,0:T(8,128)(2,1)S(1)}, bf16[2,32,512]{2,1,0:T(8,128)(2,1)S(1)}, u32[]{:S(2)}, u32[]{:S(2)}) collective-permute-start(bf16[2,32,512]{2,1,0:T(8,128)(2,1)S(1)} %get-tuple-element.165), channel_id=1, source_target_pairs={{0,16},{8,24},{16,0},{24,8},{32,48},{40,56},{48,32},{56,40},{64,80... | collective-permute-start | bytes 196616 | tf_op jit(solution)/shard_map/ppermute | solution.py:495
  129.9 6.1 %collective-permute-start.25 = (bf16[32,512]{1,0:T(8,128)(2,1)S(1)}, bf16[32,512]{1,0:T(8,128)(2,1)S(1)}, u32[]{:S(2)}, u32[]{:S(2)}) collective-permute-start(bf16[32,512]{1,0:T(8,128)(2,1)S(1)} %get-tuple-element.173), channel_id=1, source_target_pairs={{0,48},{8,56},{16,32},{24,40},{32,16},{40,24},{48,0},{56,8},{64,11... | collective-permute-start | bytes 98312 | tf_op jit(solution)/shard_map/ppermute | solution.py:495
  132.5 4.2 %collective-permute-start.24 = (bf16[16,32,512]{2,1,0:T(8,128)(2,1)S(1)}, bf16[16,32,512]{2,1,0:T(8,128)(2,1)S(1)}, u32[]{:S(2)}, u32[]{:S(2)}) collective-permute-start(bf16[16,32,512]{2,1,0:T(8,128)(2,1)S(1)} %get-tuple-element.168.refs_2_), channel_id=1, source_target_pairs={{0,8},{8,0},{16,24},{24,16},{32,40},{40,32},{48,56},{56,48},{64,72... | collective-permute-start | bytes 1572872 | tf_op jit(solution)/shard_map/ppermute | solution.py:495

commit v12 on v11

--- a/solution.py
+++ b/solution.py
@@ -563,15 +563,15 @@
     mine_0, mine_1 = other("other_3", [dest(0, 1, 0, [(0, None, *lo), (1, None, *hi)])], [half, half], (got_z1, got_z3), SHORT)
     send, keep = sum_z(keep, recv, "sync_z1")
     recv = swap(send, "z1")
+    send, keep = halve("sync_z3", (32, KV), keep, recv)
+    recv = swap(send, "z3")
     inner_o, send_o = inner_other(w_o, (mine_0, got_0, last_0), (mine_1, got_1, last_1))
     core_o = swap(send_o, "core")
-    send, keep = halve("sync_z3", (32, KV), keep, recv, LONG)
-    recv = swap(send, "z3")
+    anchor_new, momentum_new, short = outer_sync(plan, anchors, momentum, keep, recv)
+    block = exchange(short)
     new = store(plan, inner_o)
     send_o, keep_o = sum_x(inner_o, core_o, "other_x1")
     recv_o = swap(send_o, "x1")
-    anchor_new, momentum_new, short = outer_sync(plan, anchors, momentum, keep, recv)
-    block = exchange(short)
     send_o, keep_o = halve("other_x3", QUAD, keep_o, recv_o, LONG)
     recv_o = swap(send_o, "x3")
     send_o, keep_o = sum_z(keep_o, recv_o, "other_z1")

time: 139 us -> 139 us (level)
  starting transfers between devices: 55.5 us -> 57.7 us
  waiting for transfers between devices: 57.8 us -> 56.4 us
    all_to_all x1, starting transfers between devices: 8.6 us -> 10.4 us  [exchange(): lax.all_to_all(value, 'worker', 0, 0, axis_index_groups=PLANES, tiled=True)]
  transfers between devices with their start and end apart: 27 -> 27, of which waited for: 18 -> 17; matrix products, arithmetic and copies ran while one was open for 0% -> 0% of each run, Pallas kernels for 15% -> 15%
where the time goes in v12:
time: 139 us
  starting transfers between devices  57.7 us (42%)
  waiting for transfers between devices  56.4 us (41%)
  Pallas kernels  22.9 us (16%)
  between operations  1.71 us (1%)
    ppermute x26, waiting for transfers between devices, swap(): return lax.ppermute(value, *MOVES[move])  56.4 us
    ppermute x26, starting transfers between devices, swap(): return lax.ppermute(value, *MOVES[move])  47.3 us
    pallas_call x33, Pallas kernels, call(): pl.pallas_call(chained, out_shape=outs + [in_hbm(8, 128)], in_specs=list(...  22.9 us
    all_to_all x1, starting transfers between devices, exchange(): lax.all_to_all(value, 'worker', 0, 0, axis_index_groups=PLANES, tiled=True)  10.4 us
  transfers between devices with their start and end apart: 27, of which 17 were waited for; matrix products, arithmetic and copies ran while one was open for 0% of the time, Pallas kernels for 15%

profile of v12, /device:TPU:8, one launch (start us, length us, event | category | flops | bytes accessed | tf_op | source)
XLA Modules:
  0.0 138.7 jit_solution(14631928701766261372)
XLA Ops:
  1.3 1.3 pack_1.1
  2.6 2.3 %collective-permute-start = (bf16[256,1536]{1,0:T(8,128)(2,1)S(1)}, bf16[256,1536]{1,0:T(8,128)(2,1)S(1)}, u32[]{:S(2)}, u32[]{:S(2)}) collective-permute-start(bf16[256,1536]{1,0:T(8,128)(2,1)S(1)} %get-tuple-element.93), channel_id=1, source_target_pairs={{0,1},{1,0},{2,3},{3,2},{4,5},{5,4},{6,7},{7,6},{8,9},{9,8},{10,11... | collective-permute-start | bytes 2359304 | tf_op jit(solution)/shard_map/ppermute | solution.py:495
  4.9 0.7 collective-permute-start.2
  5.6 1.6 %pack_2.1 = (bf16[256,3584]{1,0:T(8,128)(2,1)S(1)}, bf16[512,256]{1,0:T(8,128)(2,1)S(1)}, bf16[8,128]{1,0:T(8,128)(2,1)}) custom-call(s32[1]{0:T(128)S(6)} %copy.15.refs_0_, s32[1,256]{1,0:T(1,128)} %bitcast.8, bf16[2,256,8192]{2,1,0:T(8,128)(2,1)} %refs_1_.21, bf16[2,256,512]{2,1,0:T(8,128)(2,1)} %refs_3_.5, bf16[8,128]{1,0:T(8,128)(2,1)} %get-tuple-element.94.refs_4_), custom_call_target="tpu_custom_call" | custom-call | tf_op jit(solution)/shard_map/pack_2/pallas_call | solution.py:71
  7.2 2.0 %collective-permute-start.6 = (bf16[256,3584]{1,0:T(8,128)(2,1)S(1)}, bf16[256,3584]{1,0:T(8,128)(2,1)S(1)}, u32[]{:S(2)}, u32[]{:S(2)}) collective-permute-start(bf16[256,3584]{1,0:T(8,128)(2,1)S(1)} %get-tuple-element.112), channel_id=1, source_target_pairs={{0,4},{1,5},{2,6},{3,7},{4,0},{5,1},{6,2},{7,3},{8,12},{9,13},{10,... | collective-permute-start | bytes 5505032 | tf_op jit(solution)/shard_map/ppermute | solution.py:495
  9.2 1.6 %pack_3.1 = (bf16[256,1024]{1,0:T(8,128)(2,1)S(1)}, bf16[256,1024]{1,0:T(8,128)(2,1)S(1)}, bf16[256,1024]{1,0:T(8,128)(2,1)S(1)}, bf16[8,128]{1,0:T(8,128)(2,1)}) custom-call(s32[1]{0:T(128)S(6)} %copy.15.refs_0_, s32[1,256]{1,0:T(1,128)} %bitcast.9, bf16[2,256,8192]{2,1,0:T(8,128)(2,1)} %refs_1_.21, bf16[2,256,512]{2,1,0:T(8,128)(2,1)} %refs_3_.5, ...), custom_call_target="tpu_custom_call" | custom-call | tf_op jit(solution)/shard_map/pack_3/pallas_call | solution.py:71
  10.8 1.4 %collective-permute-start.1 = (bf16[256,1024]{1,0:T(8,128)(2,1)S(1)}, bf16[256,1024]{1,0:T(8,128)(2,1)S(1)}, u32[]{:S(2)}, u32[]{:S(2)}) collective-permute-start(bf16[256,1024]{1,0:T(8,128)(2,1)S(1)} %get-tuple-element.96), channel_id=1, source_target_pairs={{0,1},{1,0},{2,3},{3,2},{4,5},{5,4},{6,7},{7,6},{8,9},{9,8},{10,11... | collective-permute-start | bytes 1572872 | tf_op jit(solution)/shard_map/ppermute | solution.py:495
  12.7 10.6 %collective-permute-done.refs_3_ = bf16[256,1536]{1,0:T(8,128)(2,1)S(1)} collective-permute-done((bf16[256,1536]{1,0:T(8,128)(2,1)S(1)}, bf16[256,1536]{1,0:T(8,128)(2,1)S(1)}, u32[]{:S(2)}, u32[]{:S(2)}) %collective-permute-start) | collective-permute-done | bytes 786464 | tf_op jit(solution)/shard_map/ppermute | solution.py:495
  24.0 1.4 %collective-permute-done.2.refs_3_ = bf16[256,1536]{1,0:T(8,128)(2,1)S(1)} collective-permute-done((bf16[256,1536]{1,0:T(8,128)(2,1)S(1)}, bf16[256,1536]{1,0:T(8,128)(2,1)S(1)}, u32[]{:S(2)}, u32[]{:S(2)}) %collective-permute-start.2) | collective-permute-done | bytes 786464 | tf_op jit(solution)/shard_map/ppermute | solution.py:495
  26.0 1.4 %collective-permute-start.8 = (bf16[512,512]{1,0:T(8,128)(2,1)S(1)}, bf16[512,512]{1,0:T(8,128)(2,1)S(1)}, u32[]{:S(2)}, u32[]{:S(2)}) collective-permute-start(bf16[512,512]{1,0:T(8,128)(2,1)S(1)} %get-tuple-element.116), channel_id=1, source_target_pairs={{0,1},{1,0},{2,3},{3,2},{4,5},{5,4},{6,7},{7,6},{8,9},{9,8},{10,11... | collective-permute-start | bytes 1572872 | tf_op jit(solution)/shard_map/ppermute | solution.py:495
  27.4 1.3 collective-permute-start.7
  30.0 4.6 %collective-permute-done.1.refs_4_ = bf16[256,1024]{1,0:T(8,128)(2,1)S(1)} collective-permute-done((bf16[256,1024]{1,0:T(8,128)(2,1)S(1)}, bf16[256,1024]{1,0:T(8,128)(2,1)S(1)}, u32[]{:S(2)}, u32[]{:S(2)}) %collective-permute-start.1) | collective-permute-done | bytes 524320 | tf_op jit(solution)/shard_map/ppermute | solution.py:495
  35.2 1.5 %collective-permute-start.4 = (bf16[512,512]{1,0:T(8,128)(2,1)S(1)}, bf16[512,512]{1,0:T(8,128)(2,1)S(1)}, u32[]{:S(2)}, u32[]{:S(2)}) collective-permute-start(bf16[512,512]{1,0:T(8,128)(2,1)S(1)} %get-tuple-element.107), channel_id=1, source_target_pairs={{0,3},{1,2},{2,1},{3,0},{4,7},{5,6},{6,5},{7,4},{8,11},{9,10},{10,... | collective-permute-start | bytes 1572872 | tf_op jit(solution)/shard_map/ppermute | solution.py:495
  37.3 2.0 %collective-permute-start.5 = (bf16[512,512]{1,0:T(8,128)(2,1)S(1)}, bf16[512,512]{1,0:T(8,128)(2,1)S(1)}, u32[]{:S(2)}, u32[]{:S(2)}) collective-permute-start(bf16[512,512]{1,0:T(8,128)(2,1)S(1)} %get-tuple-element.110), channel_id=1, source_target_pairs={{0,1},{1,0},{2,3},{3,2},{4,5},{5,4},{6,7},{7,6},{8,9},{9,8},{10,11... | collective-permute-start | bytes 1572872 | tf_op jit(solution)/shard_map/ppermute | solution.py:495
  40.5 5.3 %collective-permute-done.8.refs_3_ = bf16[512,512]{1,0:T(8,128)(2,1)S(1)} collective-permute-done((bf16[512,512]{1,0:T(8,128)(2,1)S(1)}, bf16[512,512]{1,0:T(8,128)(2,1)S(1)}, u32[]{:S(2)}, u32[]{:S(2)}) %collective-permute-start.8) | collective-permute-done | bytes 524320 | tf_op jit(solution)/shard_map/ppermute | solution.py:495
  45.8 2.0 %collective-permute-done.7.refs_1_ = bf16[512,512]{1,0:T(8,128)(2,1)S(1)} collective-permute-done((bf16[512,512]{1,0:T(8,128)(2,1)S(1)}, bf16[512,512]{1,0:T(8,128)(2,1)S(1)}, u32[]{:S(2)}, u32[]{:S(2)}) %collective-permute-start.7) | collective-permute-done | bytes 524320 | tf_op jit(solution)/shard_map/ppermute | solution.py:495
  48.7 1.2 collective-permute-done.6.refs_3_
  49.9 3.3 %other_1.1 = (bf16[2,256,1024]{2,1,0:T(8,128)(2,1)S(1)}, bf16[2,256,1024]{2,1,0:T(8,128)(2,1)S(1)}, bf16[256,1024]{1,0:T(8,128)(2,1)S(1)}, bf16[256,1024]{1,0:T(8,128)(2,1)S(1)}, bf16[8,128]{1,0:T(8,128)(2,1)}) custom-call(s32[1]{0:T(128)S(6)} %copy.15.refs_0_, bf16[2,256,8192]{2,1,0:T(8,128)(2,1)S(1)} %bitcast.4, ...), custom_call_target="tpu_custom_call" | custom-call | flops 20000000000 | tf_op jit(solution)/shard_map/other_1/pallas_call | solution.py:71
  53.3 1.3 collective-permute-start.12
  54.5 1.6 %collective-permute-start.13 = (bf16[2,256,1024]{2,1,0:T(8,128)(2,1)S(1)}, bf16[2,256,1024]{2,1,0:T(8,128)(2,1)S(1)}, u32[]{:S(2)}, u32[]{:S(2)}) collective-permute-start(bf16[2,256,1024]{2,1,0:T(8,128)(2,1)S(1)} %get-tuple-element.133), channel_id=1, source_target_pairs={{0,3},{1,2},{2,1},{3,0},{4,7},{5,6},{6,5},{7,4},{8,11},{9,10},{10,... | collective-permute-start | bytes 3145736 | tf_op jit(solution)/shard_map/ppermute | solution.py:495
  56.1 2.6 %collective-permute-done.4.refs_1_ = bf16[512,512]{1,0:T(8,128)(2,1)S(1)} collective-permute-done((bf16[512,512]{1,0:T(8,128)(2,1)S(1)}, bf16[512,512]{1,0:T(8,128)(2,1)S(1)}, u32[]{:S(2)}, u32[]{:S(2)}) %collective-permute-start.4) | collective-permute-done | bytes 524320 | tf_op jit(solution)/shard_map/ppermute | solution.py:495
  59.0 1.6 %take.1 = (bf16[16,2,32,512]{3,2,1,0:T(8,128)(2,1)S(1)}, bf16[16,2,32,512]{3,2,1,0:T(8,128)(2,1)S(1)}, bf16[8,128]{1,0:T(8,128)(2,1)}) custom-call(s32[1]{0:T(128)S(6)} %copy.15.refs_0_, bf16[2,16,2,32,512]{4,3,2,1,0:T(8,128)(2,1)} %bitcast.6, bf16[8,128]{1,0:T(8,128)(2,1)} %get-tuple-element.120.refs_2_), custom_call_target="tpu_custom_call" | custom-call | tf_op jit(solution)/shard_map/take/pallas_call | solution.py:71
  60.5 10.6 %collective-permute-done.9.refs_2_ = bf16[2,512,512]{2,1,0:T(8,128)(2,1)S(1)} collective-permute-done((bf16[2,512,512]{2,1,0:T(8,128)(2,1)S(1)}, bf16[2,512,512]{2,1,0:T(8,128)(2,1)S(1)}, u32[]{:S(2)}, u32[]{:S(2)}) %collective-permute-start.9) | collective-permute-done | bytes 1048608 | tf_op jit(solution)/shard_map/ppermute | solution.py:495
  71.9 1.8 %collective-permute-start.15 = (bf16[256,1024]{1,0:T(8,128)(2,1)S(1)}, bf16[256,1024]{1,0:T(8,128)(2,1)S(1)}, u32[]{:S(2)}, u32[]{:S(2)}) collective-permute-start(bf16[256,1024]{1,0:T(8,128)(2,1)S(1)} %get-tuple-element.138), channel_id=1, source_target_pairs={{0,4},{1,5},{2,6},{3,7},{4,0},{5,1},{6,2},{7,3},{8,12},{9,13},{10,... | collective-permute-start | bytes 1572872 | tf_op jit(solution)/shard_map/ppermute | solution.py:495
  74.0 1.6 %collective-permute-start.11 = (bf16[2,4,32,512]{3,2,1,0:T(8,128)(2,1)S(1)}, bf16[2,4,32,512]{3,2,1,0:T(8,128)(2,1)S(1)}, u32[]{:S(2)}, u32[]{:S(2)}) collective-permute-start(bf16[2,4,32,512]{3,2,1,0:T(8,128)(2,1)S(1)} %get-tuple-element.129), channel_id=1, source_target_pairs={{0,64},{8,72},{16,80},{24,88},{32,96},{40,104},{48,112},{56,120},{... | collective-permute-start | bytes 786440 | tf_op jit(solution)/shard_map/ppermute | solution.py:495
  75.5 2.6 %collective-permute-done.12.refs_1_.refs_2_ = bf16[2,256,1024]{2,1,0:T(8,128)(2,1)S(1)} collective-permute-done((bf16[2,256,1024]{2,1,0:T(8,128)(2,1)S(1)}, bf16[2,256,1024]{2,1,0:T(8,128)(2,1)S(1)}, u32[]{:S(2)}, u32[]{:S(2)}) %collective-permute-start.12) | collective-permute-done | bytes 1048608 | tf_op jit(solution)/shard_map/ppermute | solution.py:495
  78.2 0.8 collective-permute-done.13.refs_3_.refs_5_
  79.3 1.8 %collective-permute-start.18 = (bf16[256,1024]{1,0:T(8,128)(2,1)S(1)}, bf16[256,1024]{1,0:T(8,128)(2,1)S(1)}, u32[]{:S(2)}, u32[]{:S(2)}) collective-permute-start(bf16[256,1024]{1,0:T(8,128)(2,1)S(1)} %get-tuple-element.148), channel_id=1, source_target_pairs={{0,3},{1,2},{2,1},{3,0},{4,7},{5,6},{6,5},{7,4},{8,11},{9,10},{10,... | collective-permute-start | bytes 1572872 | tf_op jit(solution)/shard_map/ppermute | solution.py:495
  81.1 2.6 %collective-permute-start.19 = (bf16[256,1024]{1,0:T(8,128)(2,1)S(1)}, bf16[256,1024]{1,0:T(8,128)(2,1)S(1)}, u32[]{:S(2)}, u32[]{:S(2)}) collective-permute-start(bf16[256,1024]{1,0:T(8,128)(2,1)S(1)} %get-tuple-element.150), channel_id=1, source_target_pairs={{0,1},{1,0},{2,3},{3,2},{4,5},{5,4},{6,7},{7,6},{8,9},{9,8},{10,11... | collective-permute-start | bytes 1572872 | tf_op jit(solution)/shard_map/ppermute | solution.py:495
  83.7 2.8 %collective-permute-start.14 = (bf16[4,32,512]{2,1,0:T(8,128)(2,1)S(1)}, bf16[4,32,512]{2,1,0:T(8,128)(2,1)S(1)}, u32[]{:S(2)}, u32[]{:S(2)}) collective-permute-start(bf16[4,32,512]{2,1,0:T(8,128)(2,1)S(1)} %get-tuple-element.137), channel_id=1, source_target_pairs={{0,192},{8,200},{16,208},{24,216},{32,224},{40,232},{48,240},{56,2... | collective-permute-start | bytes 393224 | tf_op jit(solution)/shard_map/ppermute | solution.py:495
  86.6 1.1 other_3.1
  87.7 2.3 %collective-permute-done.14.refs_1_ = bf16[4,32,512]{2,1,0:T(8,128)(2,1)S(1)} collective-permute-done((bf16[4,32,512]{2,1,0:T(8,128)(2,1)S(1)}, bf16[4,32,512]{2,1,0:T(8,128)(2,1)S(1)}, u32[]{:S(2)}, u32[]{:S(2)}) %collective-permute-start.14) | collective-permute-done | bytes 131104 | tf_op jit(solution)/shard_map/ppermute | solution.py:495
  90.0 3.4 %collective-permute-start.16 = (bf16[2,32,512]{2,1,0:T(8,128)(2,1)S(1)}, bf16[2,32,512]{2,1,0:T(8,128)(2,1)S(1)}, u32[]{:S(2)}, u32[]{:S(2)}) collective-permute-start(bf16[2,32,512]{2,1,0:T(8,128)(2,1)S(1)} %get-tuple-element.142), channel_id=1, source_target_pairs={{0,16},{8,24},{16,0},{24,8},{32,48},{40,56},{48,32},{56,40},{64,80... | collective-permute-start | bytes 196616 | tf_op jit(solution)/shard_map/ppermute | solution.py:495
  93.4 2.2 %collective-permute-done.16.refs_1_.refs_3_ = bf16[2,32,512]{2,1,0:T(8,128)(2,1)S(1)} collective-permute-done((bf16[2,32,512]{2,1,0:T(8,128)(2,1)S(1)}, bf16[2,32,512]{2,1,0:T(8,128)(2,1)S(1)}, u32[]{:S(2)}, u32[]{:S(2)}) %collective-permute-start.16) | collective-permute-done | bytes 65568 | tf_op jit(solution)/shard_map/ppermute | solution.py:495
  95.6 6.1 %collective-permute-start.17 = (bf16[32,512]{1,0:T(8,128)(2,1)S(1)}, bf16[32,512]{1,0:T(8,128)(2,1)S(1)}, u32[]{:S(2)}, u32[]{:S(2)}) collective-permute-start(bf16[32,512]{1,0:T(8,128)(2,1)S(1)} %get-tuple-element.145), channel_id=1, source_target_pairs={{0,48},{8,56},{16,32},{24,40},{32,16},{40,24},{48,0},{56,8},{64,11... | collective-permute-start | bytes 98312 | tf_op jit(solution)/shard_map/ppermute | solution.py:495
  101.8 0.9 inner_other.1
  102.8 0.9 collective-permute-done.17.refs_4_
  103.7 0.9 outer_sync.1
  104.6 1.0 store.1
  106.1 10.4 %all-to-all-start = ((bf16[16,32,512]{2,1,0:T(8,128)(2,1)}), bf16[16,32,512]{2,1,0:T(8,128)(2,1)S(1)}, u32[]{:S(2)}, u32[]{:S(2)}) async-start(bf16[16,32,512]{2,1,0:T(8,128)(2,1)} %get-tuple-element.153), calls=%async_computation | async-start | bytes 1048576 | tf_op jit(solution)/shard_map/all_to_all | solution.py:491
  116.5 3.2 %collective-permute-start.22 = (bf16[4,32,512]{2,1,0:T(8,128)(2,1)S(1)}, bf16[4,32,512]{2,1,0:T(8,128)(2,1)S(1)}, u32[]{:S(2)}, u32[]{:S(2)}) collective-permute-start(bf16[4,32,512]{2,1,0:T(8,128)(2,1)S(1)} %get-tuple-element.162), channel_id=1, source_target_pairs={{0,192},{8,200},{16,208},{24,216},{32,224},{40,232},{48,240},{56,2... | collective-permute-start | bytes 393224 | tf_op jit(solution)/shard_map/ppermute | solution.py:495
  119.8 5.3 %collective-permute-done.22.refs_1_ = bf16[4,32,512]{2,1,0:T(8,128)(2,1)S(1)} collective-permute-done((bf16[4,32,512]{2,1,0:T(8,128)(2,1)S(1)}, bf16[4,32,512]{2,1,0:T(8,128)(2,1)S(1)}, u32[]{:S(2)}, u32[]{:S(2)}) %collective-permute-start.22) | collective-permute-done | bytes 131104 | tf_op jit(solution)/shard_map/ppermute | solution.py:495
  125.1 3.2 %collective-permute-start.23 = (bf16[2,32,512]{2,1,0:T(8,128)(2,1)S(1)}, bf16[2,32,512]{2,1,0:T(8,128)(2,1)S(1)}, u32[]{:S(2)}, u32[]{:S(2)}) collective-permute-start(bf16[2,32,512]{2,1,0:T(8,128)(2,1)S(1)} %get-tuple-element.165), channel_id=1, source_target_pairs={{0,16},{8,24},{16,0},{24,8},{32,48},{40,56},{48,32},{56,40},{64,80... | collective-permute-start | bytes 196616 | tf_op jit(solution)/shard_map/ppermute | solution.py:495
  128.3 2.5 %collective-permute-done.23.refs_1_.refs_3_ = bf16[2,32,512]{2,1,0:T(8,128)(2,1)S(1)} collective-permute-done((bf16[2,32,512]{2,1,0:T(8,128)(2,1)S(1)}, bf16[2,32,512]{2,1,0:T(8,128)(2,1)S(1)}, u32[]{:S(2)}, u32[]{:S(2)}) %collective-permute-start.23) | collective-permute-done | bytes 65568 | tf_op jit(solution)/shard_map/ppermute | solution.py:495
  130.8 3.7 %collective-permute-start.25 = (bf16[32,512]{1,0:T(8,128)(2,1)S(1)}, bf16[32,512]{1,0:T(8,128)(2,1)S(1)}, u32[]{:S(2)}, u32[]{:S(2)}) collective-permute-start(bf16[32,512]{1,0:T(8,128)(2,1)S(1)} %get-tuple-element.173), channel_id=1, source_target_pairs={{0,48},{8,56},{16,32},{24,40},{32,16},{40,24},{48,0},{56,8},{64,11... | collective-permute-start | bytes 98312 | tf_op jit(solution)/shard_map/ppermute | solution.py:495
  134.6 1.0 mix_own.1
  135.6 1.3 collective-permute-done.25.refs_3_
  137.5 1.0 mix_far.1
  (48 shorter events, 9.3 us)
Async XLA Ops:
  2.6 20.7 %collective-permute-start = (bf16[256,1536]{1,0:T(8,128)(2,1)S(1)}, bf16[256,1536]{1,0:T(8,128)(2,1)S(1)}, u32[]{:S(2)}, u32[]{:S(2)}) collective-permute-start(bf16[256,1536]{1,0:T(8,128)(2,1)S(1)} %get-tuple-element.93), channel_id=1, source_target_pairs={{0,1},{1,0},{2,3},{3,2},{4,5},{5,4},{6,7},{7,6},{8,9},{9,8},{10,11... | collective-permute-start | bytes 2359304 | tf_op jit(solution)/shard_map/ppermute | solution.py:495
  4.9 20.5 %collective-permute-start.2 = (bf16[256,1536]{1,0:T(8,128)(2,1)S(1)}, bf16[256,1536]{1,0:T(8,128)(2,1)S(1)}, u32[]{:S(2)}, u32[]{:S(2)}) collective-permute-start(bf16[256,1536]{1,0:T(8,128)(2,1)S(1)} %get-tuple-element.97), channel_id=1, source_target_pairs={{0,3},{1,2},{2,1},{3,0},{4,7},{5,6},{6,5},{7,4},{8,11},{9,10},{10,... | collective-permute-start | bytes 2359304 | tf_op jit(solution)/shard_map/ppermute | solution.py:495
  5.6 17.8 %slice-start = ((s8[8388608]{0:T(1024)(128)(4,1)}), s8[4194304]{0:T(1024)(128)(4,1)S(1)}, s32[]{:S(2)}) async-start(s8[8388608]{0:T(1024)(128)(4,1)} %bitcast.3), calls=%async_computation.1 | async-start | bytes 8388608
  7.2 42.7 %collective-permute-start.6 = (bf16[256,3584]{1,0:T(8,128)(2,1)S(1)}, bf16[256,3584]{1,0:T(8,128)(2,1)S(1)}, u32[]{:S(2)}, u32[]{:S(2)}) collective-permute-start(bf16[256,3584]{1,0:T(8,128)(2,1)S(1)} %get-tuple-element.112), channel_id=1, source_target_pairs={{0,4},{1,5},{2,6},{3,7},{4,0},{5,1},{6,2},{7,3},{8,12},{9,13},{10,... | collective-permute-start | bytes 5505032 | tf_op jit(solution)/shard_map/ppermute | solution.py:495
  9.2 14.1 %slice-start.1 = ((s8[8388608]{0:T(1024)(128)(4,1)}), s8[4194304]{0:T(1024)(128)(4,1)S(1)}, s32[]{:S(2)}) async-start(s8[8388608]{0:T(1024)(128)(4,1)} %bitcast.3), calls=%async_computation.2 | async-start | bytes 8388608
  10.8 23.7 %collective-permute-start.1 = (bf16[256,1024]{1,0:T(8,128)(2,1)S(1)}, bf16[256,1024]{1,0:T(8,128)(2,1)S(1)}, u32[]{:S(2)}, u32[]{:S(2)}) collective-permute-start(bf16[256,1024]{1,0:T(8,128)(2,1)S(1)} %get-tuple-element.96), channel_id=1, source_target_pairs={{0,1},{1,0},{2,3},{3,2},{4,5},{5,4},{6,7},{7,6},{8,9},{9,8},{10,11... | collective-permute-start | bytes 1572872 | tf_op jit(solution)/shard_map/ppermute | solution.py:495
  12.3 24.4 %collective-permute-start.3 = (bf16[256,1024]{1,0:T(8,128)(2,1)S(1)}, bf16[256,1024]{1,0:T(8,128)(2,1)S(1)}, u32[]{:S(2)}, u32[]{:S(2)}) collective-permute-start(bf16[256,1024]{1,0:T(8,128)(2,1)S(1)} %get-tuple-element.98), channel_id=1, source_target_pairs={{0,3},{1,2},{2,1},{3,0},{4,7},{5,6},{6,5},{7,4},{8,11},{9,10},{10,... | collective-permute-start | bytes 1572872 | tf_op jit(solution)/shard_map/ppermute | solution.py:495
  26.0 19.8 %collective-permute-start.8 = (bf16[512,512]{1,0:T(8,128)(2,1)S(1)}, bf16[512,512]{1,0:T(8,128)(2,1)S(1)}, u32[]{:S(2)}, u32[]{:S(2)}) collective-permute-start(bf16[512,512]{1,0:T(8,128)(2,1)S(1)} %get-tuple-element.116), channel_id=1, source_target_pairs={{0,1},{1,0},{2,3},{3,2},{4,5},{5,4},{6,7},{7,6},{8,9},{9,8},{10,11... | collective-permute-start | bytes 1572872 | tf_op jit(solution)/shard_map/ppermute | solution.py:495
  27.4 20.4 %collective-permute-start.7 = (bf16[512,512]{1,0:T(8,128)(2,1)S(1)}, bf16[512,512]{1,0:T(8,128)(2,1)S(1)}, u32[]{:S(2)}, u32[]{:S(2)}) collective-permute-start(bf16[512,512]{1,0:T(8,128)(2,1)S(1)} %get-tuple-element.114), channel_id=1, source_target_pairs={{0,3},{1,2},{2,1},{3,0},{4,7},{5,6},{6,5},{7,4},{8,11},{9,10},{10,... | collective-permute-start | bytes 1572872 | tf_op jit(solution)/shard_map/ppermute | solution.py:495
  35.2 23.5 %collective-permute-start.4 = (bf16[512,512]{1,0:T(8,128)(2,1)S(1)}, bf16[512,512]{1,0:T(8,128)(2,1)S(1)}, u32[]{:S(2)}, u32[]{:S(2)}) collective-permute-start(bf16[512,512]{1,0:T(8,128)(2,1)S(1)} %get-tuple-element.107), channel_id=1, source_target_pairs={{0,3},{1,2},{2,1},{3,0},{4,7},{5,6},{6,5},{7,4},{8,11},{9,10},{10,... | collective-permute-start | bytes 1572872 | tf_op jit(solution)/shard_map/ppermute | solution.py:495
  37.3 21.4 %collective-permute-start.5 = (bf16[512,512]{1,0:T(8,128)(2,1)S(1)}, bf16[512,512]{1,0:T(8,128)(2,1)S(1)}, u32[]{:S(2)}, u32[]{:S(2)}) collective-permute-start(bf16[512,512]{1,0:T(8,128)(2,1)S(1)} %get-tuple-element.110), channel_id=1, source_target_pairs={{0,1},{1,0},{2,3},{3,2},{4,5},{5,4},{6,7},{7,6},{8,9},{9,8},{10,11... | collective-permute-start | bytes 1572872 | tf_op jit(solution)/shard_map/ppermute | solution.py:495
  48.1 23.1 %collective-permute-start.9 = (bf16[2,512,512]{2,1,0:T(8,128)(2,1)S(1)}, bf16[2,512,512]{2,1,0:T(8,128)(2,1)S(1)}, u32[]{:S(2)}, u32[]{:S(2)}) collective-permute-start(bf16[2,512,512]{2,1,0:T(8,128)(2,1)S(1)} %get-tuple-element.123), channel_id=1, source_target_pairs={{0,4},{1,5},{2,6},{3,7},{4,0},{5,1},{6,2},{7,3},{8,12},{9,13},{10,... | collective-permute-start | bytes 3145736 | tf_op jit(solution)/shard_map/ppermute | solution.py:495
  53.3 24.9 %collective-permute-start.12 = (bf16[2,256,1024]{2,1,0:T(8,128)(2,1)S(1)}, bf16[2,256,1024]{2,1,0:T(8,128)(2,1)S(1)}, u32[]{:S(2)}, u32[]{:S(2)}) collective-permute-start(bf16[2,256,1024]{2,1,0:T(8,128)(2,1)S(1)} %get-tuple-element.131), channel_id=1, source_target_pairs={{0,1},{1,0},{2,3},{3,2},{4,5},{5,4},{6,7},{7,6},{8,9},{9,8},{10,11... | collective-permute-start | bytes 3145736 | tf_op jit(solution)/shard_map/ppermute | solution.py:495
  54.5 24.5 %collective-permute-start.13 = (bf16[2,256,1024]{2,1,0:T(8,128)(2,1)S(1)}, bf16[2,256,1024]{2,1,0:T(8,128)(2,1)S(1)}, u32[]{:S(2)}, u32[]{:S(2)}) collective-permute-start(bf16[2,256,1024]{2,1,0:T(8,128)(2,1)S(1)} %get-tuple-element.133), channel_id=1, source_target_pairs={{0,3},{1,2},{2,1},{3,0},{4,7},{5,6},{6,5},{7,4},{8,11},{9,10},{10,... | collective-permute-start | bytes 3145736 | tf_op jit(solution)/shard_map/ppermute | solution.py:495
  71.8 2.0 %collective-permute-start.10 = (bf16[16,32,512]{2,1,0:T(8,128)(2,1)S(1)}, bf16[16,32,512]{2,1,0:T(8,128)(2,1)S(1)}, u32[]{:S(2)}, u32[]{:S(2)}) collective-permute-start(bf16[16,32,512]{2,1,0:T(8,128)(2,1)S(1)} %get-tuple-element.126), channel_id=1, source_target_pairs={{0,8},{8,0},{16,24},{24,16},{32,40},{40,32},{48,56},{56,48},{64,72... | collective-permute-start | bytes 1572872 | tf_op jit(solution)/shard_map/ppermute | solution.py:495
  71.9 14.6 %collective-permute-start.15 = (bf16[256,1024]{1,0:T(8,128)(2,1)S(1)}, bf16[256,1024]{1,0:T(8,128)(2,1)S(1)}, u32[]{:S(2)}, u32[]{:S(2)}) collective-permute-start(bf16[256,1024]{1,0:T(8,128)(2,1)S(1)} %get-tuple-element.138), channel_id=1, source_target_pairs={{0,4},{1,5},{2,6},{3,7},{4,0},{5,1},{6,2},{7,3},{8,12},{9,13},{10,... | collective-permute-start | bytes 1572872 | tf_op jit(solution)/shard_map/ppermute | solution.py:495
  74.0 9.7 %collective-permute-start.11 = (bf16[2,4,32,512]{3,2,1,0:T(8,128)(2,1)S(1)}, bf16[2,4,32,512]{3,2,1,0:T(8,128)(2,1)S(1)}, u32[]{:S(2)}, u32[]{:S(2)}) collective-permute-start(bf16[2,4,32,512]{3,2,1,0:T(8,128)(2,1)S(1)} %get-tuple-element.129), channel_id=1, source_target_pairs={{0,64},{8,72},{16,80},{24,88},{32,96},{40,104},{48,112},{56,120},{... | collective-permute-start | bytes 786440 | tf_op jit(solution)/shard_map/ppermute | solution.py:495
  79.3 22.5 %collective-permute-start.18 = (bf16[256,1024]{1,0:T(8,128)(2,1)S(1)}, bf16[256,1024]{1,0:T(8,128)(2,1)S(1)}, u32[]{:S(2)}, u32[]{:S(2)}) collective-permute-start(bf16[256,1024]{1,0:T(8,128)(2,1)S(1)} %get-tuple-element.148), channel_id=1, source_target_pairs={{0,3},{1,2},{2,1},{3,0},{4,7},{5,6},{6,5},{7,4},{8,11},{9,10},{10,... | collective-permute-start | bytes 1572872 | tf_op jit(solution)/shard_map/ppermute | solution.py:495
  81.1 20.7 %collective-permute-start.19 = (bf16[256,1024]{1,0:T(8,128)(2,1)S(1)}, bf16[256,1024]{1,0:T(8,128)(2,1)S(1)}, u32[]{:S(2)}, u32[]{:S(2)}) collective-permute-start(bf16[256,1024]{1,0:T(8,128)(2,1)S(1)} %get-tuple-element.150), channel_id=1, source_target_pairs={{0,1},{1,0},{2,3},{3,2},{4,5},{5,4},{6,7},{7,6},{8,9},{9,8},{10,11... | collective-permute-start | bytes 1572872 | tf_op jit(solution)/shard_map/ppermute | solution.py:495
  83.7 6.3 %collective-permute-start.14 = (bf16[4,32,512]{2,1,0:T(8,128)(2,1)S(1)}, bf16[4,32,512]{2,1,0:T(8,128)(2,1)S(1)}, u32[]{:S(2)}, u32[]{:S(2)}) collective-permute-start(bf16[4,32,512]{2,1,0:T(8,128)(2,1)S(1)} %get-tuple-element.137), channel_id=1, source_target_pairs={{0,192},{8,200},{16,208},{24,216},{32,224},{40,232},{48,240},{56,2... | collective-permute-start | bytes 393224 | tf_op jit(solution)/shard_map/ppermute | solution.py:495
  90.0 5.6 %collective-permute-start.16 = (bf16[2,32,512]{2,1,0:T(8,128)(2,1)S(1)}, bf16[2,32,512]{2,1,0:T(8,128)(2,1)S(1)}, u32[]{:S(2)}, u32[]{:S(2)}) collective-permute-start(bf16[2,32,512]{2,1,0:T(8,128)(2,1)S(1)} %get-tuple-element.142), channel_id=1, source_target_pairs={{0,16},{8,24},{16,0},{24,8},{32,48},{40,56},{48,32},{56,40},{64,80... | collective-permute-start | bytes 196616 | tf_op jit(solution)/shard_map/ppermute | solution.py:495
  95.6 8.0 %collective-permute-start.17 = (bf16[32,512]{1,0:T(8,128)(2,1)S(1)}, bf16[32,512]{1,0:T(8,128)(2,1)S(1)}, u32[]{:S(2)}, u32[]{:S(2)}) collective-permute-start(bf16[32,512]{1,0:T(8,128)(2,1)S(1)} %get-tuple-element.145), channel_id=1, source_target_pairs={{0,48},{8,56},{16,32},{24,40},{32,16},{40,24},{48,0},{56,8},{64,11... | collective-permute-start | bytes 98312 | tf_op jit(solution)/shard_map/ppermute | solution.py:495
  101.8 1.9 %copy-start = (f32[2,32,512]{2,1,0:T(8,128)S(1)}, f32[2,32,512]{2,1,0:T(8,128)}, u32[]{:S(2)}) copy-start(f32[2,32,512]{2,1,0:T(8,128)} %refs_1_.23) | copy-start | bytes 393220
  101.8 1.9 %copy-start.1 = (f32[32,512]{1,0:T(8,128)S(1)}, f32[32,512]{1,0:T(8,128)}, u32[]{:S(2)}) copy-start(f32[32,512]{1,0:T(8,128)} %refs_2_.7) | copy-start | bytes 196612
  102.7 2.8 %collective-permute-start.20 = (bf16[16,32,512]{2,1,0:T(8,128)(2,1)S(1)}, bf16[16,32,512]{2,1,0:T(8,128)(2,1)S(1)}, u32[]{:S(2)}, u32[]{:S(2)}) collective-permute-start(bf16[16,32,512]{2,1,0:T(8,128)(2,1)S(1)} %get-tuple-element.155), channel_id=1, source_target_pairs={{0,8},{8,0},{16,24},{24,16},{32,40},{40,32},{48,56},{56,48},{64,72... | collective-permute-start | bytes 1572872 | tf_op jit(solution)/shard_map/ppermute | solution.py:495
  105.7 10.7 %collective-permute-start.21 = (bf16[2,4,32,512]{3,2,1,0:T(8,128)(2,1)S(1)}, bf16[2,4,32,512]{3,2,1,0:T(8,128)(2,1)S(1)}, u32[]{:S(2)}, u32[]{:S(2)}) collective-permute-start(bf16[2,4,32,512]{3,2,1,0:T(8,128)(2,1)S(1)} %get-tuple-element.159), channel_id=1, source_target_pairs={{0,64},{8,72},{16,80},{24,88},{32,96},{40,104},{48,112},{56,120},{... | collective-permute-start | bytes 786440 | tf_op jit(solution)/shard_map/ppermute | solution.py:495
  106.1 28.4 %all-to-all-start = ((bf16[16,32,512]{2,1,0:T(8,128)(2,1)}), bf16[16,32,512]{2,1,0:T(8,128)(2,1)S(1)}, u32[]{:S(2)}, u32[]{:S(2)}) async-start(bf16[16,32,512]{2,1,0:T(8,128)(2,1)} %get-tuple-element.153), calls=%async_computation | async-start | bytes 1048576 | tf_op jit(solution)/shard_map/all_to_all | solution.py:491
  116.5 8.5 %collective-permute-start.22 = (bf16[4,32,512]{2,1,0:T(8,128)(2,1)S(1)}, bf16[4,32,512]{2,1,0:T(8,128)(2,1)S(1)}, u32[]{:S(2)}, u32[]{:S(2)}) collective-permute-start(bf16[4,32,512]{2,1,0:T(8,128)(2,1)S(1)} %get-tuple-element.162), channel_id=1, source_target_pairs={{0,192},{8,200},{16,208},{24,216},{32,224},{40,232},{48,240},{56,2... | collective-permute-start | bytes 393224 | tf_op jit(solution)/shard_map/ppermute | solution.py:495
  125.1 5.7 %collective-permute-start.23 = (bf16[2,32,512]{2,1,0:T(8,128)(2,1)S(1)}, bf16[2,32,512]{2,1,0:T(8,128)(2,1)S(1)}, u32[]{:S(2)}, u32[]{:S(2)}) collective-permute-start(bf16[2,32,512]{2,1,0:T(8,128)(2,1)S(1)} %get-tuple-element.165), channel_id=1, source_target_pairs={{0,16},{8,24},{16,0},{24,8},{32,48},{40,56},{48,32},{56,40},{64,80... | collective-permute-start | bytes 196616 | tf_op jit(solution)/shard_map/ppermute | solution.py:495
  130.8 6.1 %collective-permute-start.25 = (bf16[32,512]{1,0:T(8,128)(2,1)S(1)}, bf16[32,512]{1,0:T(8,128)(2,1)S(1)}, u32[]{:S(2)}, u32[]{:S(2)}) collective-permute-start(bf16[32,512]{1,0:T(8,128)(2,1)S(1)} %get-tuple-element.173), channel_id=1, source_target_pairs={{0,48},{8,56},{16,32},{24,40},{32,16},{40,24},{48,0},{56,8},{64,11... | collective-permute-start | bytes 98312 | tf_op jit(solution)/shard_map/ppermute | solution.py:495
  134.5 3.0 %collective-permute-start.24 = (bf16[16,32,512]{2,1,0:T(8,128)(2,1)S(1)}, bf16[16,32,512]{2,1,0:T(8,128)(2,1)S(1)}, u32[]{:S(2)}, u32[]{:S(2)}) collective-permute-start(bf16[16,32,512]{2,1,0:T(8,128)(2,1)S(1)} %get-tuple-element.168.refs_2_), channel_id=1, source_target_pairs={{0,8},{8,0},{16,24},{24,16},{32,40},{40,32},{48,56},{56,48},{64,72... | collective-permute-start | bytes 1572872 | tf_op jit(solution)/shard_map/ppermute | solution.py:495

commit v13 on v10

--- a/solution.py
+++ b/solution.py
@@ -562,20 +562,21 @@
     )
     last_0, last_1 = swap(last_0, "b"), swap(last_1, "a")
     send, keep = halve("sync_x3", QUAD, keep, recv)
-    send, keep = sum_z(keep, swap(send, "x3"), "sync_z1")
+    recv = swap(send, "x3")
+    mine_0, mine_1 = other("other_3", [dest(0, 1, 0, [(0, None, *lo), (1, None, *hi)])], [half, half], (got_z1, got_z3), SHORT)
+    send, keep = sum_z(keep, recv, "sync_z1")
     recv = swap(send, "z1")
-    mine_0, mine_1 = other("other_3", [dest(0, 1, 0, [(0, None, *lo), (1, None, *hi)])], [half, half], (got_z1, got_z3), SHORT)
     inner_o, send_o = inner_other(w_o, (mine_0, got_0, last_0), (mine_1, got_1, last_1))
     core_o = swap(send_o, "core")
     send, keep = halve("sync_z3", (32, KV), keep, recv, LONG)
     recv = swap(send, "z3")
-    new = store(plan, inner_o)
     send_o, keep_o = sum_x(inner_o, core_o, "other_x1")
     recv_o = swap(send_o, "x1")
     anchor_new, momentum_new, short = outer_sync(plan, anchors, momentum, keep, recv)
     block = exchange(short)
     send_o, keep_o = halve("other_x3", QUAD, keep_o, recv_o, LONG)
     recv_o = swap(send_o, "x3")
+    new = store(plan, inner_o)
     send_o, keep_o = sum_z(keep_o, recv_o, "other_z1")
     recv_o = swap(send_o, "z1")
     send_o, keep_o = halve("other_z3", (32, KV), keep_o, recv_o)

time: 138 us -> 138 us (level)
  waiting for transfers between devices: 59.3 us -> 56.4 us
  starting transfers between devices: 53.5 us -> 55.7 us
    ppermute x26, waiting for transfers between devices: 59.1 us -> 56.4 us  [swap(): return lax.ppermute(value, *MOVES[move])]
    ppermute x26, starting transfers between devices: 44.3 us -> 46.5 us  [swap(): return lax.ppermute(value, *MOVES[move])]
  transfers between devices with their start and end apart: 27 -> 27, of which waited for: 17 -> 18; matrix products, arithmetic and copies ran while one was open for 0% -> 0% of each run, Pallas kernels for 14% -> 14%
where the time goes in v13:
time: 138 us; the launch traced here: 136 us
  waiting for transfers between devices  56.4 us (41%)
  starting transfers between devices  55.7 us (40%)
  Pallas kernels  22 us (16%)
  between operations  1.69 us (1%)
    ppermute x26, waiting for transfers between devices, swap(): return lax.ppermute(value, *MOVES[move])  56.4 us
    ppermute x26, starting transfers between devices, swap(): return lax.ppermute(value, *MOVES[move])  46.5 us
    pallas_call x32, Pallas kernels, call(): pl.pallas_call(chained, out_shape=outs + [in_hbm(8, 128)], in_specs=list(...  22 us
    all_to_all x1, starting transfers between devices, exchange(): lax.all_to_all(value, 'worker', 0, 0, axis_index_groups=PLANES, tiled=True)  9.19 us
  transfers between devices with their start and end apart: 27, of which 18 were waited for; matrix products, arithmetic and copies ran while one was open for 0% of the time, Pallas kernels for 14%

profile of v13, /device:TPU:8, one launch (start us, length us, event | category | flops | bytes accessed | tf_op | source)
XLA Modules:
  0.0 135.8 jit_solution(4327802347793919035)
XLA Ops:
  1.3 1.5 %pack_1.1 = (bf16[256,1536]{1,0:T(8,128)(2,1)S(1)}, bf16[256,1536]{1,0:T(8,128)(2,1)S(1)}, bf16[512,256]{1,0:T(8,128)(2,1)S(1)}, bf16[8,128]{1,0:T(8,128)(2,1)}) custom-call(s32[1]{0:T(128)S(6)} %copy.15.refs_0_, s32[1,256]{1,0:T(1,128)} %bitcast.7, bf16[2,256,8192]{2,1,0:T(8,128)(2,1)} %refs_1_.21, bf16[2,256,512]{2,1,0:T(8,128)(2,1)} %refs_3_.3), custom_call_target="tpu_custom_call" | custom-call | tf_op jit(solution)/shard_map/pack_1/pallas_call | solution.py:70
  2.8 2.3 %collective-permute-start = (bf16[256,1536]{1,0:T(8,128)(2,1)S(1)}, bf16[256,1536]{1,0:T(8,128)(2,1)S(1)}, u32[]{:S(2)}, u32[]{:S(2)}) collective-permute-start(bf16[256,1536]{1,0:T(8,128)(2,1)S(1)} %get-tuple-element.92), channel_id=1, source_target_pairs={{0,1},{1,0},{2,3},{3,2},{4,5},{5,4},{6,7},{7,6},{8,9},{9,8},{10,11... | collective-permute-start | bytes 2359304 | tf_op jit(solution)/shard_map/ppermute | solution.py:498
  5.1 0.7 collective-permute-start.2
  5.7 2.2 %pack_2.1 = (bf16[256,3584]{1,0:T(8,128)(2,1)S(1)}, bf16[256,1024]{1,0:T(8,128)(2,1)S(1)}, bf16[256,1024]{1,0:T(8,128)(2,1)S(1)}, bf16[256,1024]{1,0:T(8,128)(2,...) custom-call(s32[1]{0:T(128)S(6)} %copy.15.refs_0_, s32[1,256]{1,0:T(1,128)} %bitcast.8, ...), custom_call_target="tpu_custom_call" | custom-call | tf_op jit(solution)/shard_map/pack_2/pallas_call | solution.py:70
  7.9 1.4 %collective-permute-start.1 = (bf16[256,1024]{1,0:T(8,128)(2,1)S(1)}, bf16[256,1024]{1,0:T(8,128)(2,1)S(1)}, u32[]{:S(2)}, u32[]{:S(2)}) collective-permute-start(bf16[256,1024]{1,0:T(8,128)(2,1)S(1)} %get-tuple-element.94), channel_id=1, source_target_pairs={{0,1},{1,0},{2,3},{3,2},{4,5},{5,4},{6,7},{7,6},{8,9},{9,8},{10,11... | collective-permute-start | bytes 1572872 | tf_op jit(solution)/shard_map/ppermute | solution.py:498
  9.4 0.7 collective-permute-start.3
  10.1 1.7 %collective-permute-start.6 = (bf16[256,3584]{1,0:T(8,128)(2,1)S(1)}, bf16[256,3584]{1,0:T(8,128)(2,1)S(1)}, u32[]{:S(2)}, u32[]{:S(2)}) collective-permute-start(bf16[256,3584]{1,0:T(8,128)(2,1)S(1)} %get-tuple-element.110), channel_id=1, source_target_pairs={{0,4},{1,5},{2,6},{3,7},{4,0},{5,1},{6,2},{7,3},{8,12},{9,13},{10,... | collective-permute-start | bytes 5505032 | tf_op jit(solution)/shard_map/ppermute | solution.py:498
  11.7 11.8 %collective-permute-done.refs_3_ = bf16[256,1536]{1,0:T(8,128)(2,1)S(1)} collective-permute-done((bf16[256,1536]{1,0:T(8,128)(2,1)S(1)}, bf16[256,1536]{1,0:T(8,128)(2,1)S(1)}, u32[]{:S(2)}, u32[]{:S(2)}) %collective-permute-start) | collective-permute-done | bytes 786464 | tf_op jit(solution)/shard_map/ppermute | solution.py:498
  24.1 1.4 %collective-permute-done.2.refs_3_ = bf16[256,1536]{1,0:T(8,128)(2,1)S(1)} collective-permute-done((bf16[256,1536]{1,0:T(8,128)(2,1)S(1)}, bf16[256,1536]{1,0:T(8,128)(2,1)S(1)}, u32[]{:S(2)}, u32[]{:S(2)}) %collective-permute-start.2) | collective-permute-done | bytes 786464 | tf_op jit(solution)/shard_map/ppermute | solution.py:498
  26.2 1.4 %collective-permute-start.8 = (bf16[512,512]{1,0:T(8,128)(2,1)S(1)}, bf16[512,512]{1,0:T(8,128)(2,1)S(1)}, u32[]{:S(2)}, u32[]{:S(2)}) collective-permute-start(bf16[512,512]{1,0:T(8,128)(2,1)S(1)} %get-tuple-element.114), channel_id=1, source_target_pairs={{0,1},{1,0},{2,3},{3,2},{4,5},{5,4},{6,7},{7,6},{8,9},{9,8},{10,11... | collective-permute-start | bytes 1572872 | tf_op jit(solution)/shard_map/ppermute | solution.py:498
  27.6 1.3 collective-permute-start.7
  30.1 4.6 %collective-permute-done.1.refs_4_ = bf16[256,1024]{1,0:T(8,128)(2,1)S(1)} collective-permute-done((bf16[256,1024]{1,0:T(8,128)(2,1)S(1)}, bf16[256,1024]{1,0:T(8,128)(2,1)S(1)}, u32[]{:S(2)}, u32[]{:S(2)}) %collective-permute-start.1) | collective-permute-done | bytes 524320 | tf_op jit(solution)/shard_map/ppermute | solution.py:498
  35.4 1.5 %collective-permute-start.4 = (bf16[512,512]{1,0:T(8,128)(2,1)S(1)}, bf16[512,512]{1,0:T(8,128)(2,1)S(1)}, u32[]{:S(2)}, u32[]{:S(2)}) collective-permute-start(bf16[512,512]{1,0:T(8,128)(2,1)S(1)} %get-tuple-element.105), channel_id=1, source_target_pairs={{0,3},{1,2},{2,1},{3,0},{4,7},{5,6},{6,5},{7,4},{8,11},{9,10},{10,... | collective-permute-start | bytes 1572872 | tf_op jit(solution)/shard_map/ppermute | solution.py:498
  37.5 2.0 %collective-permute-start.5 = (bf16[512,512]{1,0:T(8,128)(2,1)S(1)}, bf16[512,512]{1,0:T(8,128)(2,1)S(1)}, u32[]{:S(2)}, u32[]{:S(2)}) collective-permute-start(bf16[512,512]{1,0:T(8,128)(2,1)S(1)} %get-tuple-element.108), channel_id=1, source_target_pairs={{0,1},{1,0},{2,3},{3,2},{4,5},{5,4},{6,7},{7,6},{8,9},{9,8},{10,11... | collective-permute-start | bytes 1572872 | tf_op jit(solution)/shard_map/ppermute | solution.py:498
  40.7 5.3 %collective-permute-done.8.refs_3_ = bf16[512,512]{1,0:T(8,128)(2,1)S(1)} collective-permute-done((bf16[512,512]{1,0:T(8,128)(2,1)S(1)}, bf16[512,512]{1,0:T(8,128)(2,1)S(1)}, u32[]{:S(2)}, u32[]{:S(2)}) %collective-permute-start.8) | collective-permute-done | bytes 524320 | tf_op jit(solution)/shard_map/ppermute | solution.py:498
  46.0 2.0 %collective-permute-done.7.refs_1_ = bf16[512,512]{1,0:T(8,128)(2,1)S(1)} collective-permute-done((bf16[512,512]{1,0:T(8,128)(2,1)S(1)}, bf16[512,512]{1,0:T(8,128)(2,1)S(1)}, u32[]{:S(2)}, u32[]{:S(2)}) %collective-permute-start.7) | collective-permute-done | bytes 524320 | tf_op jit(solution)/shard_map/ppermute | solution.py:498
  48.9 4.2 %collective-permute-done.6.refs_3_ = bf16[256,3584]{1,0:T(8,128)(2,1)S(1)} collective-permute-done((bf16[256,3584]{1,0:T(8,128)(2,1)S(1)}, bf16[256,3584]{1,0:T(8,128)(2,1)S(1)}, u32[]{:S(2)}, u32[]{:S(2)}) %collective-permute-start.6) | collective-permute-done | bytes 1835040 | tf_op jit(solution)/shard_map/ppermute | solution.py:498
  53.0 3.3 %other_1.1 = (bf16[2,256,1024]{2,1,0:T(8,128)(2,1)S(1)}, bf16[2,256,1024]{2,1,0:T(8,128)(2,1)S(1)}, bf16[256,1024]{1,0:T(8,128)(2,1)S(1)}, bf16[256,1024]{1,0:T(8,128)(2,1)S(1)}, bf16[8,128]{1,0:T(8,128)(2,1)}) custom-call(s32[1]{0:T(128)S(6)} %copy.15.refs_0_, bf16[2,256,8192]{2,1,0:T(8,128)(2,1)S(1)} %bitcast.4, ...), custom_call_target="tpu_custom_call" | custom-call | flops 20000000000 | tf_op jit(solution)/shard_map/other_1/pallas_call | solution.py:70
  56.3 1.1 collective-permute-start.12
  57.5 1.6 %collective-permute-start.13 = (bf16[2,256,1024]{2,1,0:T(8,128)(2,1)S(1)}, bf16[2,256,1024]{2,1,0:T(8,128)(2,1)S(1)}, u32[]{:S(2)}, u32[]{:S(2)}) collective-permute-start(bf16[2,256,1024]{2,1,0:T(8,128)(2,1)S(1)} %get-tuple-element.131), channel_id=1, source_target_pairs={{0,3},{1,2},{2,1},{3,0},{4,7},{5,6},{6,5},{7,4},{8,11},{9,10},{10,... | collective-permute-start | bytes 3145736 | tf_op jit(solution)/shard_map/ppermute | solution.py:498
  59.3 1.6 %take.1 = (bf16[16,2,32,512]{3,2,1,0:T(8,128)(2,1)S(1)}, bf16[16,2,32,512]{3,2,1,0:T(8,128)(2,1)S(1)}, bf16[8,128]{1,0:T(8,128)(2,1)}) custom-call(s32[1]{0:T(128)S(6)} %copy.15.refs_0_, bf16[2,16,2,32,512]{4,3,2,1,0:T(8,128)(2,1)} %bitcast.6, bf16[8,128]{1,0:T(8,128)(2,1)} %get-tuple-element.118.refs_2_), custom_call_target="tpu_custom_call" | custom-call | tf_op jit(solution)/shard_map/take/pallas_call | solution.py:70
  60.9 12.2 %collective-permute-done.9.refs_2_ = bf16[2,512,512]{2,1,0:T(8,128)(2,1)S(1)} collective-permute-done((bf16[2,512,512]{2,1,0:T(8,128)(2,1)S(1)}, bf16[2,512,512]{2,1,0:T(8,128)(2,1)S(1)}, u32[]{:S(2)}, u32[]{:S(2)}) %collective-permute-start.9) | collective-permute-done | bytes 1048608 | tf_op jit(solution)/shard_map/ppermute | solution.py:498
  73.9 1.8 %collective-permute-start.15 = (bf16[256,1024]{1,0:T(8,128)(2,1)S(1)}, bf16[256,1024]{1,0:T(8,128)(2,1)S(1)}, u32[]{:S(2)}, u32[]{:S(2)}) collective-permute-start(bf16[256,1024]{1,0:T(8,128)(2,1)S(1)} %get-tuple-element.136), channel_id=1, source_target_pairs={{0,4},{1,5},{2,6},{3,7},{4,0},{5,1},{6,2},{7,3},{8,12},{9,13},{10,... | collective-permute-start | bytes 1572872 | tf_op jit(solution)/shard_map/ppermute | solution.py:498
  75.9 1.6 %collective-permute-start.11 = (bf16[2,4,32,512]{3,2,1,0:T(8,128)(2,1)S(1)}, bf16[2,4,32,512]{3,2,1,0:T(8,128)(2,1)S(1)}, u32[]{:S(2)}, u32[]{:S(2)}) collective-permute-start(bf16[2,4,32,512]{3,2,1,0:T(8,128)(2,1)S(1)} %get-tuple-element.127), channel_id=1, source_target_pairs={{0,64},{8,72},{16,80},{24,88},{32,96},{40,104},{48,112},{56,120},{... | collective-permute-start | bytes 786440 | tf_op jit(solution)/shard_map/ppermute | solution.py:498
  77.5 0.9 collective-permute-done.12.refs_1_.refs_2_
  78.3 0.8 collective-permute-done.13.refs_3_.refs_5_
  79.4 1.8 %collective-permute-start.17 = (bf16[256,1024]{1,0:T(8,128)(2,1)S(1)}, bf16[256,1024]{1,0:T(8,128)(2,1)S(1)}, u32[]{:S(2)}, u32[]{:S(2)}) collective-permute-start(bf16[256,1024]{1,0:T(8,128)(2,1)S(1)} %get-tuple-element.143), channel_id=1, source_target_pairs={{0,3},{1,2},{2,1},{3,0},{4,7},{5,6},{6,5},{7,4},{8,11},{9,10},{10,... | collective-permute-start | bytes 1572872 | tf_op jit(solution)/shard_map/ppermute | solution.py:498
  81.2 2.6 %collective-permute-start.18 = (bf16[256,1024]{1,0:T(8,128)(2,1)S(1)}, bf16[256,1024]{1,0:T(8,128)(2,1)S(1)}, u32[]{:S(2)}, u32[]{:S(2)}) collective-permute-start(bf16[256,1024]{1,0:T(8,128)(2,1)S(1)} %get-tuple-element.145), channel_id=1, source_target_pairs={{0,1},{1,0},{2,3},{3,2},{4,5},{5,4},{6,7},{7,6},{8,9},{9,8},{10,11... | collective-permute-start | bytes 1572872 | tf_op jit(solution)/shard_map/ppermute | solution.py:498
  84.4 2.8 %collective-permute-start.14 = (bf16[4,32,512]{2,1,0:T(8,128)(2,1)S(1)}, bf16[4,32,512]{2,1,0:T(8,128)(2,1)S(1)}, u32[]{:S(2)}, u32[]{:S(2)}) collective-permute-start(bf16[4,32,512]{2,1,0:T(8,128)(2,1)S(1)} %get-tuple-element.135), channel_id=1, source_target_pairs={{0,192},{8,200},{16,208},{24,216},{32,224},{40,232},{48,240},{56,2... | collective-permute-start | bytes 393224 | tf_op jit(solution)/shard_map/ppermute | solution.py:498
  87.2 1.0 collective-permute-done.15.refs_4_
  88.2 1.1 other_3.1
  89.4 1.3 collective-permute-done.14.refs_1_
  90.7 3.4 %collective-permute-start.16 = (bf16[2,32,512]{2,1,0:T(8,128)(2,1)S(1)}, bf16[2,32,512]{2,1,0:T(8,128)(2,1)S(1)}, u32[]{:S(2)}, u32[]{:S(2)}) collective-permute-start(bf16[2,32,512]{2,1,0:T(8,128)(2,1)S(1)} %get-tuple-element.140), channel_id=1, source_target_pairs={{0,16},{8,24},{16,0},{24,8},{32,48},{40,56},{48,32},{56,40},{64,80... | collective-permute-start | bytes 196616 | tf_op jit(solution)/shard_map/ppermute | solution.py:498
  94.0 0.9 inner_other.1
  95.1 1.2 collective-permute-done.16.refs_1_.refs_3_
  96.3 6.0 %collective-permute-start.19 = (bf16[32,512]{1,0:T(8,128)(2,1)S(1)}, bf16[32,512]{1,0:T(8,128)(2,1)S(1)}, u32[]{:S(2)}, u32[]{:S(2)}) collective-permute-start(bf16[32,512]{1,0:T(8,128)(2,1)S(1)} %get-tuple-element.149), channel_id=1, source_target_pairs={{0,48},{8,56},{16,32},{24,40},{32,16},{40,24},{48,0},{56,8},{64,11... | collective-permute-start | bytes 98312 | tf_op jit(solution)/shard_map/ppermute | solution.py:498
  102.8 1.4 %collective-permute-done.19.refs_4_ = bf16[32,512]{1,0:T(8,128)(2,1)S(1)} collective-permute-done((bf16[32,512]{1,0:T(8,128)(2,1)S(1)}, bf16[32,512]{1,0:T(8,128)(2,1)S(1)}, u32[]{:S(2)}, u32[]{:S(2)}) %collective-permute-start.19) | collective-permute-done | bytes 32800 | tf_op jit(solution)/shard_map/ppermute | solution.py:498
  104.2 0.9 outer_sync.1
  105.1 9.2 %all-to-all-start = ((bf16[16,32,512]{2,1,0:T(8,128)(2,1)}), bf16[16,32,512]{2,1,0:T(8,128)(2,1)S(1)}, u32[]{:S(2)}, u32[]{:S(2)}) async-start(bf16[16,32,512]{2,1,0:T(8,128)(2,1)} %get-tuple-element.154), calls=%async_computation | async-start | bytes 1048576 | tf_op jit(solution)/shard_map/all_to_all | solution.py:494
  114.4 3.2 %collective-permute-start.22 = (bf16[4,32,512]{2,1,0:T(8,128)(2,1)S(1)}, bf16[4,32,512]{2,1,0:T(8,128)(2,1)S(1)}, u32[]{:S(2)}, u32[]{:S(2)}) collective-permute-start(bf16[4,32,512]{2,1,0:T(8,128)(2,1)S(1)} %get-tuple-element.159), channel_id=1, source_target_pairs={{0,192},{8,200},{16,208},{24,216},{32,224},{40,232},{48,240},{56,2... | collective-permute-start | bytes 393224 | tf_op jit(solution)/shard_map/ppermute | solution.py:498
  117.6 1.0 store.1
  118.6 3.8 %collective-permute-done.22.refs_1_ = bf16[4,32,512]{2,1,0:T(8,128)(2,1)S(1)} collective-permute-done((bf16[4,32,512]{2,1,0:T(8,128)(2,1)S(1)}, bf16[4,32,512]{2,1,0:T(8,128)(2,1)S(1)}, u32[]{:S(2)}, u32[]{:S(2)}) %collective-permute-start.22) | collective-permute-done | bytes 131104 | tf_op jit(solution)/shard_map/ppermute | solution.py:498
  122.4 3.1 %collective-permute-start.23 = (bf16[2,32,512]{2,1,0:T(8,128)(2,1)S(1)}, bf16[2,32,512]{2,1,0:T(8,128)(2,1)S(1)}, u32[]{:S(2)}, u32[]{:S(2)}) collective-permute-start(bf16[2,32,512]{2,1,0:T(8,128)(2,1)S(1)} %get-tuple-element.163), channel_id=1, source_target_pairs={{0,16},{8,24},{16,0},{24,8},{32,48},{40,56},{48,32},{56,40},{64,80... | collective-permute-start | bytes 196616 | tf_op jit(solution)/shard_map/ppermute | solution.py:498
  125.5 2.4 %collective-permute-done.23.refs_1_.refs_3_ = bf16[2,32,512]{2,1,0:T(8,128)(2,1)S(1)} collective-permute-done((bf16[2,32,512]{2,1,0:T(8,128)(2,1)S(1)}, bf16[2,32,512]{2,1,0:T(8,128)(2,1)S(1)}, u32[]{:S(2)}, u32[]{:S(2)}) %collective-permute-start.23) | collective-permute-done | bytes 65568 | tf_op jit(solution)/shard_map/ppermute | solution.py:498
  127.9 3.4 %collective-permute-start.25 = (bf16[32,512]{1,0:T(8,128)(2,1)S(1)}, bf16[32,512]{1,0:T(8,128)(2,1)S(1)}, u32[]{:S(2)}, u32[]{:S(2)}) collective-permute-start(bf16[32,512]{1,0:T(8,128)(2,1)S(1)} %get-tuple-element.171), channel_id=1, source_target_pairs={{0,48},{8,56},{16,32},{24,40},{32,16},{40,24},{48,0},{56,8},{64,11... | collective-permute-start | bytes 98312 | tf_op jit(solution)/shard_map/ppermute | solution.py:498
  131.4 1.0 mix_own.1
  132.4 1.6 %collective-permute-done.25.refs_3_ = bf16[32,512]{1,0:T(8,128)(2,1)S(1)} collective-permute-done((bf16[32,512]{1,0:T(8,128)(2,1)S(1)}, bf16[32,512]{1,0:T(8,128)(2,1)S(1)}, u32[]{:S(2)}, u32[]{:S(2)}) %collective-permute-start.25) | collective-permute-done | bytes 32800 | tf_op jit(solution)/shard_map/ppermute | solution.py:498
  134.7 1.0 mix_far.1
  (47 shorter events, 9.4 us)
Async XLA Ops:
  1.3 22.2 %slice-start = ((s8[8388608]{0:T(1024)(128)(4,1)}), s8[4194304]{0:T(1024)(128)(4,1)S(1)}, s32[]{:S(2)}) async-start(s8[8388608]{0:T(1024)(128)(4,1)} %bitcast.3), calls=%async_computation.1 | async-start | bytes 8388608
  2.8 20.7 %collective-permute-start = (bf16[256,1536]{1,0:T(8,128)(2,1)S(1)}, bf16[256,1536]{1,0:T(8,128)(2,1)S(1)}, u32[]{:S(2)}, u32[]{:S(2)}) collective-permute-start(bf16[256,1536]{1,0:T(8,128)(2,1)S(1)} %get-tuple-element.92), channel_id=1, source_target_pairs={{0,1},{1,0},{2,3},{3,2},{4,5},{5,4},{6,7},{7,6},{8,9},{9,8},{10,11... | collective-permute-start | bytes 2359304 | tf_op jit(solution)/shard_map/ppermute | solution.py:498
  5.1 20.5 %collective-permute-start.2 = (bf16[256,1536]{1,0:T(8,128)(2,1)S(1)}, bf16[256,1536]{1,0:T(8,128)(2,1)S(1)}, u32[]{:S(2)}, u32[]{:S(2)}) collective-permute-start(bf16[256,1536]{1,0:T(8,128)(2,1)S(1)} %get-tuple-element.95), channel_id=1, source_target_pairs={{0,3},{1,2},{2,1},{3,0},{4,7},{5,6},{6,5},{7,4},{8,11},{9,10},{10,... | collective-permute-start | bytes 2359304 | tf_op jit(solution)/shard_map/ppermute | solution.py:498
  5.7 17.8 %slice-start.1 = ((s8[8388608]{0:T(1024)(128)(4,1)}), s8[4194304]{0:T(1024)(128)(4,1)S(1)}, s32[]{:S(2)}) async-start(s8[8388608]{0:T(1024)(128)(4,1)} %bitcast.3), calls=%async_computation.2 | async-start | bytes 8388608
  7.9 26.8 %collective-permute-start.1 = (bf16[256,1024]{1,0:T(8,128)(2,1)S(1)}, bf16[256,1024]{1,0:T(8,128)(2,1)S(1)}, u32[]{:S(2)}, u32[]{:S(2)}) collective-permute-start(bf16[256,1024]{1,0:T(8,128)(2,1)S(1)} %get-tuple-element.94), channel_id=1, source_target_pairs={{0,1},{1,0},{2,3},{3,2},{4,5},{5,4},{6,7},{7,6},{8,9},{9,8},{10,11... | collective-permute-start | bytes 1572872 | tf_op jit(solution)/shard_map/ppermute | solution.py:498
  9.4 27.5 %collective-permute-start.3 = (bf16[256,1024]{1,0:T(8,128)(2,1)S(1)}, bf16[256,1024]{1,0:T(8,128)(2,1)S(1)}, u32[]{:S(2)}, u32[]{:S(2)}) collective-permute-start(bf16[256,1024]{1,0:T(8,128)(2,1)S(1)} %get-tuple-element.96), channel_id=1, source_target_pairs={{0,3},{1,2},{2,1},{3,0},{4,7},{5,6},{6,5},{7,4},{8,11},{9,10},{10,... | collective-permute-start | bytes 1572872 | tf_op jit(solution)/shard_map/ppermute | solution.py:498
  10.1 42.9 %collective-permute-start.6 = (bf16[256,3584]{1,0:T(8,128)(2,1)S(1)}, bf16[256,3584]{1,0:T(8,128)(2,1)S(1)}, u32[]{:S(2)}, u32[]{:S(2)}) collective-permute-start(bf16[256,3584]{1,0:T(8,128)(2,1)S(1)} %get-tuple-element.110), channel_id=1, source_target_pairs={{0,4},{1,5},{2,6},{3,7},{4,0},{5,1},{6,2},{7,3},{8,12},{9,13},{10,... | collective-permute-start | bytes 5505032 | tf_op jit(solution)/shard_map/ppermute | solution.py:498
  26.2 19.8 %collective-permute-start.8 = (bf16[512,512]{1,0:T(8,128)(2,1)S(1)}, bf16[512,512]{1,0:T(8,128)(2,1)S(1)}, u32[]{:S(2)}, u32[]{:S(2)}) collective-permute-start(bf16[512,512]{1,0:T(8,128)(2,1)S(1)} %get-tuple-element.114), channel_id=1, source_target_pairs={{0,1},{1,0},{2,3},{3,2},{4,5},{5,4},{6,7},{7,6},{8,9},{9,8},{10,11... | collective-permute-start | bytes 1572872 | tf_op jit(solution)/shard_map/ppermute | solution.py:498
  27.6 20.4 %collective-permute-start.7 = (bf16[512,512]{1,0:T(8,128)(2,1)S(1)}, bf16[512,512]{1,0:T(8,128)(2,1)S(1)}, u32[]{:S(2)}, u32[]{:S(2)}) collective-permute-start(bf16[512,512]{1,0:T(8,128)(2,1)S(1)} %get-tuple-element.112), channel_id=1, source_target_pairs={{0,3},{1,2},{2,1},{3,0},{4,7},{5,6},{6,5},{7,4},{8,11},{9,10},{10,... | collective-permute-start | bytes 1572872 | tf_op jit(solution)/shard_map/ppermute | solution.py:498
  35.4 23.7 %collective-permute-start.4 = (bf16[512,512]{1,0:T(8,128)(2,1)S(1)}, bf16[512,512]{1,0:T(8,128)(2,1)S(1)}, u32[]{:S(2)}, u32[]{:S(2)}) collective-permute-start(bf16[512,512]{1,0:T(8,128)(2,1)S(1)} %get-tuple-element.105), channel_id=1, source_target_pairs={{0,3},{1,2},{2,1},{3,0},{4,7},{5,6},{6,5},{7,4},{8,11},{9,10},{10,... | collective-permute-start | bytes 1572872 | tf_op jit(solution)/shard_map/ppermute | solution.py:498
  37.5 21.6 %collective-permute-start.5 = (bf16[512,512]{1,0:T(8,128)(2,1)S(1)}, bf16[512,512]{1,0:T(8,128)(2,1)S(1)}, u32[]{:S(2)}, u32[]{:S(2)}) collective-permute-start(bf16[512,512]{1,0:T(8,128)(2,1)S(1)} %get-tuple-element.108), channel_id=1, source_target_pairs={{0,1},{1,0},{2,3},{3,2},{4,5},{5,4},{6,7},{7,6},{8,9},{9,8},{10,11... | collective-permute-start | bytes 1572872 | tf_op jit(solution)/shard_map/ppermute | solution.py:498
  48.3 24.8 %collective-permute-start.9 = (bf16[2,512,512]{2,1,0:T(8,128)(2,1)S(1)}, bf16[2,512,512]{2,1,0:T(8,128)(2,1)S(1)}, u32[]{:S(2)}, u32[]{:S(2)}) collective-permute-start(bf16[2,512,512]{2,1,0:T(8,128)(2,1)S(1)} %get-tuple-element.121), channel_id=1, source_target_pairs={{0,4},{1,5},{2,6},{3,7},{4,0},{5,1},{6,2},{7,3},{8,12},{9,13},{10,... | collective-permute-start | bytes 3145736 | tf_op jit(solution)/shard_map/ppermute | solution.py:498
  56.3 22.0 %collective-permute-start.12 = (bf16[2,256,1024]{2,1,0:T(8,128)(2,1)S(1)}, bf16[2,256,1024]{2,1,0:T(8,128)(2,1)S(1)}, u32[]{:S(2)}, u32[]{:S(2)}) collective-permute-start(bf16[2,256,1024]{2,1,0:T(8,128)(2,1)S(1)} %get-tuple-element.129), channel_id=1, source_target_pairs={{0,1},{1,0},{2,3},{3,2},{4,5},{5,4},{6,7},{7,6},{8,9},{9,8},{10,11... | collective-permute-start | bytes 3145736 | tf_op jit(solution)/shard_map/ppermute | solution.py:498
  57.5 21.7 %collective-permute-start.13 = (bf16[2,256,1024]{2,1,0:T(8,128)(2,1)S(1)}, bf16[2,256,1024]{2,1,0:T(8,128)(2,1)S(1)}, u32[]{:S(2)}, u32[]{:S(2)}) collective-permute-start(bf16[2,256,1024]{2,1,0:T(8,128)(2,1)S(1)} %get-tuple-element.131), channel_id=1, source_target_pairs={{0,3},{1,2},{2,1},{3,0},{4,7},{5,6},{6,5},{7,4},{8,11},{9,10},{10,... | collective-permute-start | bytes 3145736 | tf_op jit(solution)/shard_map/ppermute | solution.py:498
  73.8 2.0 %collective-permute-start.10 = (bf16[16,32,512]{2,1,0:T(8,128)(2,1)S(1)}, bf16[16,32,512]{2,1,0:T(8,128)(2,1)S(1)}, u32[]{:S(2)}, u32[]{:S(2)}) collective-permute-start(bf16[16,32,512]{2,1,0:T(8,128)(2,1)S(1)} %get-tuple-element.124), channel_id=1, source_target_pairs={{0,8},{8,0},{16,24},{24,16},{32,40},{40,32},{48,56},{56,48},{64,72... | collective-permute-start | bytes 1572872 | tf_op jit(solution)/shard_map/ppermute | solution.py:498
  73.9 14.3 %collective-permute-start.15 = (bf16[256,1024]{1,0:T(8,128)(2,1)S(1)}, bf16[256,1024]{1,0:T(8,128)(2,1)S(1)}, u32[]{:S(2)}, u32[]{:S(2)}) collective-permute-start(bf16[256,1024]{1,0:T(8,128)(2,1)S(1)} %get-tuple-element.136), channel_id=1, source_target_pairs={{0,4},{1,5},{2,6},{3,7},{4,0},{5,1},{6,2},{7,3},{8,12},{9,13},{10,... | collective-permute-start | bytes 1572872 | tf_op jit(solution)/shard_map/ppermute | solution.py:498
  75.9 8.4 %collective-permute-start.11 = (bf16[2,4,32,512]{3,2,1,0:T(8,128)(2,1)S(1)}, bf16[2,4,32,512]{3,2,1,0:T(8,128)(2,1)S(1)}, u32[]{:S(2)}, u32[]{:S(2)}) collective-permute-start(bf16[2,4,32,512]{3,2,1,0:T(8,128)(2,1)S(1)} %get-tuple-element.127), channel_id=1, source_target_pairs={{0,64},{8,72},{16,80},{24,88},{32,96},{40,104},{48,112},{56,120},{... | collective-permute-start | bytes 786440 | tf_op jit(solution)/shard_map/ppermute | solution.py:498
  79.4 14.6 %collective-permute-start.17 = (bf16[256,1024]{1,0:T(8,128)(2,1)S(1)}, bf16[256,1024]{1,0:T(8,128)(2,1)S(1)}, u32[]{:S(2)}, u32[]{:S(2)}) collective-permute-start(bf16[256,1024]{1,0:T(8,128)(2,1)S(1)} %get-tuple-element.143), channel_id=1, source_target_pairs={{0,3},{1,2},{2,1},{3,0},{4,7},{5,6},{6,5},{7,4},{8,11},{9,10},{10,... | collective-permute-start | bytes 1572872 | tf_op jit(solution)/shard_map/ppermute | solution.py:498
  81.2 12.8 %collective-permute-start.18 = (bf16[256,1024]{1,0:T(8,128)(2,1)S(1)}, bf16[256,1024]{1,0:T(8,128)(2,1)S(1)}, u32[]{:S(2)}, u32[]{:S(2)}) collective-permute-start(bf16[256,1024]{1,0:T(8,128)(2,1)S(1)} %get-tuple-element.145), channel_id=1, source_target_pairs={{0,1},{1,0},{2,3},{3,2},{4,5},{5,4},{6,7},{7,6},{8,9},{9,8},{10,11... | collective-permute-start | bytes 1572872 | tf_op jit(solution)/shard_map/ppermute | solution.py:498
  84.4 6.3 %collective-permute-start.14 = (bf16[4,32,512]{2,1,0:T(8,128)(2,1)S(1)}, bf16[4,32,512]{2,1,0:T(8,128)(2,1)S(1)}, u32[]{:S(2)}, u32[]{:S(2)}) collective-permute-start(bf16[4,32,512]{2,1,0:T(8,128)(2,1)S(1)} %get-tuple-element.135), channel_id=1, source_target_pairs={{0,192},{8,200},{16,208},{24,216},{32,224},{40,232},{48,240},{56,2... | collective-permute-start | bytes 393224 | tf_op jit(solution)/shard_map/ppermute | solution.py:498
  90.7 5.6 %collective-permute-start.16 = (bf16[2,32,512]{2,1,0:T(8,128)(2,1)S(1)}, bf16[2,32,512]{2,1,0:T(8,128)(2,1)S(1)}, u32[]{:S(2)}, u32[]{:S(2)}) collective-permute-start(bf16[2,32,512]{2,1,0:T(8,128)(2,1)S(1)} %get-tuple-element.140), channel_id=1, source_target_pairs={{0,16},{8,24},{16,0},{24,8},{32,48},{40,56},{48,32},{56,40},{64,80... | collective-permute-start | bytes 196616 | tf_op jit(solution)/shard_map/ppermute | solution.py:498
  95.0 7.3 %collective-permute-start.20 = (bf16[16,32,512]{2,1,0:T(8,128)(2,1)S(1)}, bf16[16,32,512]{2,1,0:T(8,128)(2,1)S(1)}, u32[]{:S(2)}, u32[]{:S(2)}) collective-permute-start(bf16[16,32,512]{2,1,0:T(8,128)(2,1)S(1)} %get-tuple-element.151), channel_id=1, source_target_pairs={{0,8},{8,0},{16,24},{24,16},{32,40},{40,32},{48,56},{56,48},{64,72... | collective-permute-start | bytes 1572872 | tf_op jit(solution)/shard_map/ppermute | solution.py:498
  96.3 7.9 %copy-start = (f32[2,32,512]{2,1,0:T(8,128)S(1)}, f32[2,32,512]{2,1,0:T(8,128)}, u32[]{:S(2)}) copy-start(f32[2,32,512]{2,1,0:T(8,128)} %refs_1_.23) | copy-start | bytes 393220
  96.3 7.9 %copy-start.1 = (f32[32,512]{1,0:T(8,128)S(1)}, f32[32,512]{1,0:T(8,128)}, u32[]{:S(2)}) copy-start(f32[32,512]{1,0:T(8,128)} %refs_2_.5) | copy-start | bytes 196612
  96.3 7.9 %collective-permute-start.19 = (bf16[32,512]{1,0:T(8,128)(2,1)S(1)}, bf16[32,512]{1,0:T(8,128)(2,1)S(1)}, u32[]{:S(2)}, u32[]{:S(2)}) collective-permute-start(bf16[32,512]{1,0:T(8,128)(2,1)S(1)} %get-tuple-element.149), channel_id=1, source_target_pairs={{0,48},{8,56},{16,32},{24,40},{32,16},{40,24},{48,0},{56,8},{64,11... | collective-permute-start | bytes 98312 | tf_op jit(solution)/shard_map/ppermute | solution.py:498
  102.4 11.9 %collective-permute-start.21 = (bf16[2,4,32,512]{3,2,1,0:T(8,128)(2,1)S(1)}, bf16[2,4,32,512]{3,2,1,0:T(8,128)(2,1)S(1)}, u32[]{:S(2)}, u32[]{:S(2)}) collective-permute-start(bf16[2,4,32,512]{3,2,1,0:T(8,128)(2,1)S(1)} %get-tuple-element.156), channel_id=1, source_target_pairs={{0,64},{8,72},{16,80},{24,88},{32,96},{40,104},{48,112},{56,120},{... | collective-permute-start | bytes 786440 | tf_op jit(solution)/shard_map/ppermute | solution.py:498
  105.1 26.2 %all-to-all-start = ((bf16[16,32,512]{2,1,0:T(8,128)(2,1)}), bf16[16,32,512]{2,1,0:T(8,128)(2,1)S(1)}, u32[]{:S(2)}, u32[]{:S(2)}) async-start(bf16[16,32,512]{2,1,0:T(8,128)(2,1)} %get-tuple-element.154), calls=%async_computation | async-start | bytes 1048576 | tf_op jit(solution)/shard_map/all_to_all | solution.py:494
  114.4 8.0 %collective-permute-start.22 = (bf16[4,32,512]{2,1,0:T(8,128)(2,1)S(1)}, bf16[4,32,512]{2,1,0:T(8,128)(2,1)S(1)}, u32[]{:S(2)}, u32[]{:S(2)}) collective-permute-start(bf16[4,32,512]{2,1,0:T(8,128)(2,1)S(1)} %get-tuple-element.159), channel_id=1, source_target_pairs={{0,192},{8,200},{16,208},{24,216},{32,224},{40,232},{48,240},{56,2... | collective-permute-start | bytes 393224 | tf_op jit(solution)/shard_map/ppermute | solution.py:498
  122.4 5.5 %collective-permute-start.23 = (bf16[2,32,512]{2,1,0:T(8,128)(2,1)S(1)}, bf16[2,32,512]{2,1,0:T(8,128)(2,1)S(1)}, u32[]{:S(2)}, u32[]{:S(2)}) collective-permute-start(bf16[2,32,512]{2,1,0:T(8,128)(2,1)S(1)} %get-tuple-element.163), channel_id=1, source_target_pairs={{0,16},{8,24},{16,0},{24,8},{32,48},{40,56},{48,32},{56,40},{64,80... | collective-permute-start | bytes 196616 | tf_op jit(solution)/shard_map/ppermute | solution.py:498
  127.9 6.1 %collective-permute-start.25 = (bf16[32,512]{1,0:T(8,128)(2,1)S(1)}, bf16[32,512]{1,0:T(8,128)(2,1)S(1)}, u32[]{:S(2)}, u32[]{:S(2)}) collective-permute-start(bf16[32,512]{1,0:T(8,128)(2,1)S(1)} %get-tuple-element.171), channel_id=1, source_target_pairs={{0,48},{8,56},{16,32},{24,40},{32,16},{40,24},{48,0},{56,8},{64,11... | collective-permute-start | bytes 98312 | tf_op jit(solution)/shard_map/ppermute | solution.py:498
  131.3 3.3 %collective-permute-start.24 = (bf16[16,32,512]{2,1,0:T(8,128)(2,1)S(1)}, bf16[16,32,512]{2,1,0:T(8,128)(2,1)S(1)}, u32[]{:S(2)}, u32[]{:S(2)}) collective-permute-start(bf16[16,32,512]{2,1,0:T(8,128)(2,1)S(1)} %get-tuple-element.166.refs_2_), channel_id=1, source_target_pairs={{0,8},{8,0},{16,24},{24,16},{32,40},{40,32},{48,56},{56,48},{64,72... | collective-permute-start | bytes 1572872 | tf_op jit(solution)/shard_map/ppermute | solution.py:498
